TPU v7x, 32 devices: a whole 2x2x4 slice. The times are simulated.
32 devices in a mesh: groups: 2 (over y), sec: 4 (over z), strip: 4 (over x, core).
Axes of the slice: x: 2, y: 2, z: 4, core: 2. Of those that a mesh axis runs over, the one named last changes fastest.
Arguments:
- sections: bfloat16 [4, 256, 1024], P('sec', 'strip', 'groups'), parts along dimension 2, may hold values from -40 to 40
- mask_fine: int32 [4, 8, 32], P('sec', 'strip', 'groups'), parts along dimension 2, may hold values 0 or 1
- mask_coarse: int32 [4, 4, 16], P('sec', 'strip', 'groups'), parts along dimension 2, may hold values 0 or 1
Outputs:
- corr_fine: float32 [4, 2, 8, 32, 1024], P('sec', None, 'strip', 'groups'), parts along dimension 3
- corr_coarse: float32 [4, 2, 4, 16, 1024], P('sec', None, 'strip', 'groups'), parts along dimension 3
There are 2 independent parts, one for each index of `groups`. A program takes and returns all parts, laid end to end along the dimension named above; each array names one. Nothing has to cross between parts.
All inputs are finite; a program needn't handle non-finite values. No bound on the sum of `mask_fine` or of `mask_coarse` on one device may be relied on, other than what follows from the above.
Results may differ from a plain program's by a relative error of at most 0.0039.
Values may be sent and summed in bfloat16 or wider, within the bound.
No kernel may reach another device: no remote copies, remote signals or barrier semaphores. Data moves between devices by JAX's collectives and lax.ppermute only.
A program may use at most 64 MiB of HBM per device.

v0:
```python
import functools

import jax
import jax.numpy as jnp
import numpy as np
from jax import lax
from jax.experimental import pallas as pl
from jax.experimental.pallas import tpu as pltpu
from jax.sharding import PartitionSpec as P

PATCH = 64
STRIDE = 32
WINDOW = 32
HALF = PATCH // 2
LANES = 128
NYQ = 16

f32 = jnp.float32
bf16 = jnp.bfloat16


def from_device(value, sec_steps, strip_steps):
    secs, strips = lax.axis_size("sec"), lax.axis_size("strip")
    pairs = []
    for sec in range(secs - sec_steps):
        for strip in range(strips - strip_steps):
            pairs.append(((sec + sec_steps) * strips + strip + strip_steps, sec * strips + strip))
    return lax.ppermute(value, ("sec", "strip"), pairs)


def wave(phase):
    turns = np.arange(PATCH) * (2 * np.pi / PATCH)
    cos = np.round(np.cos(turns), 14)
    sin = np.round(np.sin(turns), 14)
    phase = np.mod(phase, PATCH)
    return cos[phase], sin[phase]


def split_table(table):
    high = table.astype(jnp.bfloat16)
    low = (table - high.astype(np.float64)).astype(jnp.bfloat16)
    return high, low


def stacked(table):
    return np.concatenate(split_table(table), axis=0)


def fine_table():
    c, s = wave(np.arange(PATCH)[:, None] * np.arange(PATCH)[None, :])
    table = np.zeros((2, 2, PATCH, 2, 2, PATCH))
    for p in range(2):
        table[0, p, :, 0, p] = c
        table[1, p, :, 0, p] = -s
        table[0, p, :, 1, p] = -s
        table[1, p, :, 1, p] = -c
    return stacked(table.reshape(4 * PATCH, 4 * PATCH))


def coarse_table():
    c, s = wave((np.arange(2 * PATCH) // 2)[:, None] * np.arange(PATCH)[None, :])
    table = np.zeros((2, 2, 2 * PATCH, 2, 2, PATCH))
    for p in range(2):
        table[p, 0, :, 0, p] = 0.5 * c
        table[p, 1, :, 0, p] = -0.5 * s
        table[p, 0, :, 1, p] = -0.5 * s
        table[p, 1, :, 1, p] = -0.5 * c
    return stacked(table.reshape(8 * PATCH, 4 * PATCH))


def shift_table():
    t = np.arange(WINDOW) - WINDOW // 2
    c, s = wave(np.arange(PATCH)[:, None] * t[None, :])
    table = np.zeros((2, 2, 2, PATCH, 2, 4, WINDOW))
    for odd in range(2):
        for p in range(2):
            table[odd, 0, p, :, 0, 2 * p + odd] = c
            table[odd, 1, p, :, 0, 2 * p + odd] = -s
            table[odd, 0, p, :, 1, 2 * p + odd] = s
            table[odd, 1, p, :, 1, 2 * p + odd] = c
    return stacked(table.reshape(8 * PATCH, 8 * WINDOW))


def map_table(blocks):
    shift = np.arange(WINDOW) - WINDOW // 2
    c, s = wave(shift[:, None] * np.arange(HALF)[None, :])
    weight = np.where(np.arange(HALF) == 0, 1.0, 2.0) / PATCH**3
    rows = []
    for block in range(blocks):
        nyquist = np.zeros((WINDOW, NYQ))
        nyquist[:, block] = wave(HALF * shift)[0] / PATCH**3
        high, low = split_table(np.concatenate([c * weight, -s * weight, nyquist], axis=1))
        rows += [np.concatenate([high, high], axis=1), np.concatenate([low, np.zeros_like(low)], axis=1)]
    return np.concatenate(rows)


def all_tables(blocks):
    tables = [fine_table(), coarse_table(), shift_table(), map_table(blocks)]
    width = max(table.shape[1] for table in tables)
    places = np.cumsum([0] + [table.shape[0] for table in tables])
    padded = [np.pad(table, ((0, 0), (0, width - table.shape[1]))) for table in tables]
    return np.concatenate(padded), [int(place) for place in places]


def split(value):
    high = value.astype(bf16)
    return high, (value - high.astype(f32)).astype(bf16)


def dot(left, right):
    return jnp.dot(left, right, preferred_element_type=f32)


def dot3(high, low, table_ref, at):
    depth = high.shape[1]
    table_high = table_ref[at : at + depth]
    table_low = table_ref[at + depth : at + 2 * depth]
    return dot(
        jnp.concatenate([high, low, high], axis=1),
        jnp.concatenate([table_high, table_high, table_low], axis=0))


def cosine(turns):
    turns = turns + PATCH // 4
    part = (turns & (HALF - 1)) - PATCH // 4
    angle = part.astype(f32) * (2 * np.pi / PATCH)
    square = angle * angle
    value = jnp.full(square.shape, 1.0 / 479001600, f32)
    for term in (-1.0 / 3628800, 1.0 / 40320, -1.0 / 720, 1.0 / 24, -0.5, 1.0):
        value = value * square + term
    return jnp.where((turns & HALF) == 0, value, -value)


def write_row_table(row_ref, fine, coarse):
    ext = row_ref.shape[1] // 2
    half_rows = row_ref.shape[0] // 2
    blocks = [(b * HALF, b * STRIDE, 0) for b in range(fine)]
    blocks += [(fine * HALF + NYQ + b * HALF, b * 2 * STRIDE, 1) for b in range(coarse)]

    def put(at, value):
        high, low = split(value)
        row_ref[at : at + value.shape[0], :ext] = high
        row_ref[at : at + value.shape[0], ext:] = low

    k = lax.broadcasted_iota(jnp.int32, (HALF, ext), 0)
    column = lax.broadcasted_iota(jnp.int32, (HALF, ext), 1)
    row = lax.broadcasted_iota(jnp.int32, (NYQ, ext), 0)
    nyquist = jnp.zeros((NYQ, ext), f32)
    for number, (at, first, pool) in enumerate(blocks):
        x = column - first
        kept = jnp.where((x >= 0) & (x < PATCH << pool), 1.0 / (1 << pool), 0.0)
        turns = k * (x >> pool)
        put(at, cosine(turns) * kept)
        put(half_rows + at, cosine(turns - PATCH // 4) * kept)
        wave_half = cosine((x[:NYQ] >> pool) * HALF) * kept[:NYQ]
        nyquist = jnp.where(row == number, wave_half, nyquist)
    put(fine * HALF, nyquist)
    put(half_rows + fine * HALF, jnp.zeros((NYQ, ext), f32))


def all_rows(value):
    for step in (4, 2, 1):
        value = value + pltpu.roll(value, step, 0)
    return value


class Level:
    def __init__(self, blocks, quads, first, nyquist, number, start, table):
        self.blocks, self.quads, self.tiles = blocks, quads, 2 * quads
        self.first, self.nyquist, self.number = first, nyquist, number
        self.rows = blocks * HALF + NYQ
        self.start = start
        self.table = table


def levels_of(fine, coarse, width, places):
    fine_at, coarse_at = places[0], places[1]
    return [
        Level(fine, width // STRIDE // 4, 0, fine * HALF, 0, 0, fine_at),
        Level(coarse, width // (2 * STRIDE) // 4, NYQ, 0, fine, fine * HALF, coarse_at),
    ]


def transform_rows(x, row_ref, t_ref, halves):
    width = x.shape[1]
    t_ref[...] = dot(row_ref[...], jnp.concatenate([x, x], axis=0))
    for r in range(0, t_ref.shape[0], 16):
        for ref, half in zip(halves, split(t_ref[r : r + 16])):
            ref[r : r + 16, :width] = half
            ref[r : r + 16, width:] = jnp.zeros((16, LANES), bf16)


def transform_columns(level, pool, halves, left, f_ref, spec_ref, table_ref):
    half_rows = halves[0].shape[0] // 2
    rows, size = level.rows, pool * LANES
    for source, target in zip(halves, left):
        for tile in range(level.tiles):
            for p in range(pool):
                at = size * (tile // 2) + LANES * p + pool * STRIDE * (tile % 2)
                for half in range(2):
                    target[tile * rows : (tile + 1) * rows, (2 * p + half) * LANES : (2 * p + half + 1) * LANES] = (
                        source[half * half_rows + level.start : half * half_rows + level.start + rows, at : at + LANES])
    f_ref[...] = dot3(left[0][...], left[1][...], table_ref, level.table)

    sub = lax.broadcasted_iota(jnp.int32, (8, LANES), 0)
    lane = lax.broadcasted_iota(jnp.int32, (8, LANES), 1)
    dc = (sub == 0) & (lane % PATCH == 0)
    dc_both = jnp.concatenate([dc, dc], axis=1)
    group = lax.broadcasted_iota(jnp.int32, (LANES, LANES), 0) // PATCH
    same = group == lax.broadcasted_iota(jnp.int32, (LANES, LANES), 1) // PATCH
    ones = jnp.where(same, 1.0, 0.0).astype(bf16)
    sums = []
    for tile in range(level.tiles):
        base = tile * rows
        for b in range(level.blocks):
            total = None
            for r in range(0, HALF, 8):
                at = base + level.first + b * HALF + r
                re, im = f_ref[at : at + 8, :LANES], f_ref[at : at + 8, LANES:]
                part = re * re + im * im
                if r == 0:
                    part = jnp.where(dc, 0.0, part)
                    head = jnp.where(sub == 0, part, 0.0)
                total = part if total is None else total + part
            at = base + level.nyquist
            re, im = f_ref[at : at + 8, :LANES], f_ref[at : at + 8, LANES:]
            tail = jnp.where(sub == level.number + b, re * re + im * im, 0.0)
            sums.append(2.0 * total - head + tail)
    high, low = split(jnp.concatenate(sums, axis=0))
    sums = dot(jnp.concatenate([high, low], axis=1), jnp.concatenate([ones, ones], axis=0))
    for tile in range(level.tiles):
        base = tile * rows
        at = base + level.nyquist
        nyq = f_ref[at : at + 8]
        scaled = jnp.zeros_like(nyq)
        for b in range(level.blocks):
            number = (tile * level.blocks + b) * 8
            scale = lax.rsqrt(all_rows(sums[number : number + 8]) * (1.0 / PATCH**4) + 1e-05)
            scale = jnp.concatenate([scale, scale], axis=1)
            first = level.first + b * HALF
            for r in range(0, HALF, 16):
                at = base + first + r
                head = f_ref[at : at + 8]
                if r == 0:
                    head = jnp.where(dc_both, 0.0, head)
                both = jnp.concatenate([head * scale, f_ref[at + 8 : at + 16] * scale], axis=0)
                spec_ref[at : at + 16] = both.astype(bf16)
            scaled = jnp.where(sub[:, :1] == level.number + b, nyq * scale, scaled)
        at = base + level.nyquist
        spec_ref[at : at + 16] = jnp.concatenate([scaled, jnp.zeros_like(scaled)], axis=0).astype(bf16)


def correlate_pair(levels, own_specs, other_specs, masks, table_ref, shift_at, map_at, scratch, outs):
    high_ref, low_ref, y_ref, maps_ref, rows_ref = scratch[:5]
    stacks = scratch[5:]
    base = 0
    for level, own, other in zip(levels, own_specs, other_specs):
        for tile in range(level.tiles):
            quad, odd = divmod(tile, 2)
            for r in range(0, level.rows, 16):
                at = tile * level.rows + r
                a, b = own[at : at + 16].astype(f32), other[at : at + 16].astype(f32)
                ar, ai, br, bi = a[:, :LANES], a[:, LANES:], b[:, :LANES], b[:, LANES:]
                cross = jnp.concatenate([ar * br + ai * bi, ar * bi - ai * br], axis=1)
                to = base + quad * level.rows + r
                for ref, half in zip((high_ref, low_ref), split(cross)):
                    ref[to : to + 16, 2 * odd * LANES : 2 * (odd + 1) * LANES] = half
        base += level.quads * level.rows
    y_ref[...] = dot3(high_ref[...], low_ref[...], table_ref, shift_at)
    base = tile = 0
    starts = {}
    for index, level in enumerate(levels):
        for b in range(level.blocks):
            stack_ref = stacks[level.number + b]
            for quad in range(level.quads):
                row = base + quad * level.rows
                top, nyq = row + level.first + b * HALF, row + level.nyquist
                for at, value in (
                    (0, y_ref[top : top + HALF, :LANES]),
                    (HALF, y_ref[top : top + HALF, LANES:]),
                    (2 * HALF, y_ref[nyq : nyq + NYQ, :LANES]),
                ):
                    for half, part in enumerate(split(value)):
                        to = half * (2 * HALF + NYQ) + at
                        stack_ref[to : to + value.shape[0], quad * LANES : (quad + 1) * LANES] = part
            table = map_at + 2 * WINDOW * (level.number + b)
            depth, columns = stack_ref.shape
            both = dot(table_ref[table : table + 2 * WINDOW, :depth], stack_ref[...])
            maps = both[:WINDOW] + both[WINDOW:]
            for quad in range(level.quads):
                maps_ref[tile + quad] = maps[:, quad * LANES : (quad + 1) * LANES]
            starts[index, b] = tile
            tile += level.quads
        base += level.quads * level.rows
    kept = [jnp.transpose(mask) for mask in masks]
    lanes = lax.broadcasted_iota(jnp.int32, (tile, LANES), 1) // WINDOW
    for big in range(WINDOW // 4):
        rows = [maps_ref[:, 4 * big + r, :] for r in range(4)]
        for g in range(4):
            value = None
            for r in range(4):
                moved = rows[r] if r == g else pltpu.roll(rows[r], (WINDOW * (r - g)) % LANES, 1)
                value = moved if value is None else jnp.where(lanes == r, moved, value)
            rows_ref[big, pl.ds(g, tile, stride=4), :] = value
        for index, (level, out) in enumerate(zip(levels, outs)):
            for b in range(level.blocks):
                column = kept[index][: 4 * level.quads, b : b + 1]
                at = 4 * starts[index, b]
                out[b, :, big * LANES : (big + 1) * LANES] = rows_ref[big, at : at + 4 * level.quads] * column


def mask_tile(mask_ref, pad_ref):
    pad_ref[...] = jnp.zeros(pad_ref.shape, f32)
    pad_ref[: mask_ref.shape[1], : mask_ref.shape[2]] = mask_ref[0].astype(f32)
    return pad_ref[...]


def near_kernel(
    fine, coarse, places,
    own_hbm, near, rim, rim_near, mask_hbm, mask_coarse_hbm, table_hbm,
    row_ref, table_ref, own_fine, own_coarse, map_fine, map_coarse,
    own, mask, mask_coarse, pad, pad_coarse, t_ref, t_high, t_low, left_high, left_low, coarse_high, coarse_low,
    f_fine, f_coarse, near_fine, near_coarse, *rest,
):
    sems = rest[-1]
    loads = [
        pltpu.make_async_copy(own_hbm, own, sems.at[0]),
        pltpu.make_async_copy(mask_hbm, mask, sems.at[1]),
        pltpu.make_async_copy(mask_coarse_hbm, mask_coarse, sems.at[2]),
    ]
    fine_at, coarse_at, shift_at, map_at, end = places
    for i, (first, last) in enumerate(((fine_at, coarse_at), (coarse_at, shift_at), (shift_at, end))):
        piece = pl.ds(first, last - first)
        loads.append(pltpu.make_async_copy(table_hbm.at[piece], table_ref.at[piece], sems.at[3 + i]))
    for load in loads:
        load.start()
    write_row_table(row_ref, fine, coarse)
    levels = levels_of(fine, coarse, near.shape[2], places)
    specs = ((near_fine, near_coarse), (own_fine, own_coarse))
    for z in range(2):
        if z == 1:
            loads[0].wait()
        strips = ((near, rim_near), (own, rim))[z]
        x = jnp.concatenate([strips[0][0], strips[1][0]], axis=0)
        transform_rows(x, row_ref, t_ref.at[z], (t_high.at[z], t_low.at[z]))
    loads[3].wait()
    for z in range(2):
        transform_columns(
            levels[0], 1, (t_high.at[z], t_low.at[z]), (left_high.at[z], left_low.at[z]), f_fine.at[z],
            specs[z][0], table_ref)
    loads[4].wait()
    for z in range(2):
        transform_columns(
            levels[1], 2, (t_high.at[z], t_low.at[z]), (coarse_high.at[z], coarse_low.at[z]), f_coarse.at[z],
            specs[z][1], table_ref)
    loads[5].wait()
    loads[1].wait()
    loads[2].wait()
    correlate_pair(
        levels, specs[1], specs[0], (mask_tile(mask, pad), mask_tile(mask_coarse, pad_coarse)),
        table_ref, shift_at, map_at, rest[:-1], (map_fine, map_coarse))


def far_kernel(
    fine, coarse, places,
    far, row_ref, table_ref, own_fine, own_coarse, map_fine, map_coarse, mask_hbm, mask_coarse_hbm,
    out_fine, out_coarse,
    mask, mask_coarse, pad, pad_coarse, t_ref, t_high, t_low, left_high, left_low, coarse_high, coarse_low,
    f_fine, f_coarse, far_fine, far_coarse, last_fine, last_coarse, *rest,
):
    sems = rest[-1]
    loads = [
        pltpu.make_async_copy(mask_hbm, mask, sems.at[0]),
        pltpu.make_async_copy(mask_coarse_hbm, mask_coarse, sems.at[1]),
    ]
    stores = [
        pltpu.make_async_copy(map_fine, out_fine.at[0, 0], sems.at[2]),
        pltpu.make_async_copy(map_coarse, out_coarse.at[0, 0], sems.at[3]),
    ]
    for copy in loads + stores:
        copy.start()
    fine_at, coarse_at, shift_at, map_at, end = places
    levels = levels_of(fine, coarse, far.shape[2], places)
    x = jnp.concatenate([far[0], far[1]], axis=0)
    transform_rows(x, row_ref, t_ref.at[0], (t_high.at[0], t_low.at[0]))
    transform_columns(
        levels[0], 1, (t_high.at[0], t_low.at[0]), (left_high.at[0], left_low.at[0]), f_fine.at[0], far_fine, table_ref)
    transform_columns(
        levels[1], 2, (t_high.at[0], t_low.at[0]), (coarse_high.at[0], coarse_low.at[0]), f_coarse.at[0],
        far_coarse, table_ref)
    for load in loads:
        load.wait()
    correlate_pair(
        levels, (own_fine, own_coarse), (far_fine, far_coarse),
        (mask_tile(mask, pad), mask_tile(mask_coarse, pad_coarse)),
        table_ref, shift_at, map_at, rest[:-1], (last_fine, last_coarse))
    last = [
        pltpu.make_async_copy(last_fine, out_fine.at[0, 1], sems.at[4]),
        pltpu.make_async_copy(last_coarse, out_coarse.at[0, 1], sems.at[5]),
    ]
    for copy in last:
        copy.start()
    for copy in stores + last:
        copy.wait()


def correlate(own, near, rim, rim_near, far, mask_fine, mask_coarse):
    strip_rows, width = own.shape[1:]
    fine, coarse = mask_fine.shape[1], mask_coarse.shape[1]
    ext = strip_rows + PATCH
    table, places = all_tables(fine + coarse)
    levels = levels_of(fine, coarse, width, places)
    half_rows = (fine + coarse) * HALF + NYQ
    tiles = sum(level.blocks * level.quads for level in levels)
    spec_shapes = [(level.tiles * level.rows, 2 * LANES) for level in levels]
    map_shapes = [(level.blocks, 4 * level.quads, WINDOW * WINDOW) for level in levels]
    cross_rows = sum(level.quads * level.rows for level in levels)

    def scratch(sections):
        def many(shape, dtype):
            return pltpu.VMEM((sections,) + shape, dtype)

        return [
            many((2 * half_rows, width), f32),
            many((2 * half_rows, width + LANES), bf16),
            many((2 * half_rows, width + LANES), bf16),
            many(spec_shapes[0], bf16),
            many(spec_shapes[0], bf16),
            many((spec_shapes[1][0], 4 * LANES), bf16),
            many((spec_shapes[1][0], 4 * LANES), bf16),
            many(spec_shapes[0], f32),
            many(spec_shapes[1], f32),
            pltpu.VMEM(spec_shapes[0], bf16),
            pltpu.VMEM(spec_shapes[1], bf16),
        ]

    pair_scratch = [
        pltpu.VMEM((cross_rows, 4 * LANES), bf16),
        pltpu.VMEM((cross_rows, 4 * LANES), bf16),
        pltpu.VMEM((cross_rows, 2 * LANES), f32),
        pltpu.VMEM((tiles, WINDOW, LANES), f32),
        pltpu.VMEM((WINDOW // 4, 4 * tiles, LANES), f32),
        *(pltpu.VMEM((4 * HALF + 2 * NYQ, level.quads * LANES), bf16) for level in levels for _ in range(level.blocks)),
        pltpu.SemaphoreType.DMA((6,)),
    ]
    mask_scratch = [
        pltpu.VMEM(mask_fine.shape, jnp.int32),
        pltpu.VMEM(mask_coarse.shape, jnp.int32),
        pltpu.VMEM((8, LANES), f32),
        pltpu.VMEM((8, LANES), f32),
    ]
    hbm = pl.BlockSpec(memory_space=pltpu.HBM)
    vmem = pl.BlockSpec(memory_space=pltpu.VMEM)
    params = pltpu.CompilerParams(vmem_limit_bytes=24 * 1024 * 1024)
    own, table, mask_fine, mask_coarse = (
        pltpu.with_memory_space_constraint(value, pltpu.HBM)
        for value in (own, jnp.asarray(table), mask_fine, mask_coarse))

    handed = pl.pallas_call(
        functools.partial(near_kernel, fine, coarse, places),
        out_shape=(
            jax.ShapeDtypeStruct((2 * half_rows, 2 * ext), bf16),
            jax.ShapeDtypeStruct(table.shape, bf16),
            *(jax.ShapeDtypeStruct(shape, bf16) for shape in spec_shapes),
            *(jax.ShapeDtypeStruct(shape, f32) for shape in map_shapes),
        ),
        in_specs=[hbm, vmem, vmem, vmem, hbm, hbm, hbm],
        out_specs=(vmem,) * 6,
        scratch_shapes=[pltpu.VMEM(own.shape, bf16), *mask_scratch, *scratch(2), *pair_scratch],
        compiler_params=params,
        cost_estimate=pl.CostEstimate(flops=4 * 10**9, bytes_accessed=4 * 10**6, transcendentals=0),
        name="near_maps",
    )(own, near, rim, rim_near, mask_fine, mask_coarse, table)
    return pl.pallas_call(
        functools.partial(far_kernel, fine, coarse, places),
        out_shape=tuple(jax.ShapeDtypeStruct((1, 2) + shape, f32) for shape in map_shapes),
        in_specs=[vmem] * 7 + [hbm, hbm],
        out_specs=(hbm, hbm),
        scratch_shapes=[
            *mask_scratch, *scratch(1), *(pltpu.VMEM(shape, f32) for shape in map_shapes), *pair_scratch],
        compiler_params=params,
        cost_estimate=pl.CostEstimate(flops=3 * 10**9, bytes_accessed=4 * 10**6, transcendentals=0),
        name="far_maps",
    )(far, *handed, mask_fine, mask_coarse)


def local(sections, mask_fine, mask_coarse):
    near = from_device(sections, 1, 0)
    rim_near = from_device(sections, 1, 1)
    rim = from_device(sections, 0, 1)
    far = from_device(jnp.concatenate([near, rim_near], axis=0), 1, 0)
    return correlate(sections, near, rim, rim_near, far, mask_fine, mask_coarse)


def solution(mesh):
    in_specs = (
        P("sec", "strip", "groups"),
        P("sec", "strip", "groups"),
        P("sec", "strip", "groups"),
    )
    out_specs = (P("sec", None, "strip", "groups", None), P("sec", None, "strip", "groups", None))
    return jax.shard_map(local, mesh=mesh, in_specs=in_specs, out_specs=out_specs, check_vma=False)
```

profile of v0, /device:TPU:0, one launch (start us, length us, event | category | flops | bytes accessed | tf_op | source)
XLA Modules:
  0.0 20.9 jit_solution(2809318886304926922)
XLA Ops:
  0.6 1.3 %collective-permute-start.1 = (bf16[1,64,512]{2,1,0:T(8,128)(2,1)}, bf16[1,64,512]{2,1,0:T(8,128)(2,1)S(1)}, u32[]{:S(2)}, u32[]{:S(2)}) collective-permute-start(bf16[1,64,512]{2,1,0:T(8,128)(2,1)} %own_hbm.1), channel_id=1, source_target_pairs={{5,0},{6,1},{7,2},{9,4},{10,5},{11,6},{13,8},{14,9},{15,10},{21,16... | collective-permute-start | bytes 196616 | tf_op jit(solution)/shard_map/ppermute | solution.py:28
  1.9 1.3 %collective-permute-start = (bf16[1,64,512]{2,1,0:T(8,128)(2,1)}, bf16[1,64,512]{2,1,0:T(8,128)(2,1)S(1)}, u32[]{:S(2)}, u32[]{:S(2)}) collective-permute-start(bf16[1,64,512]{2,1,0:T(8,128)(2,1)} %own_hbm.1), channel_id=1, source_target_pairs={{4,0},{5,1},{6,2},{7,3},{8,4},{9,5},{10,6},{11,7},{12,8},{13,9},{1... | collective-permute-start | bytes 196616 | tf_op jit(solution)/shard_map/ppermute | solution.py:28
  3.2 1.3 %collective-permute-start.3 = (bf16[1,64,512]{2,1,0:T(8,128)(2,1)}, bf16[1,64,512]{2,1,0:T(8,128)(2,1)S(1)}, u32[]{:S(2)}, u32[]{:S(2)}) collective-permute-start(bf16[1,64,512]{2,1,0:T(8,128)(2,1)} %own_hbm.1), channel_id=1, source_target_pairs={{1,0},{2,1},{3,2},{5,4},{6,5},{7,6},{9,8},{10,9},{11,10},{13,12},{... | collective-permute-start | bytes 196616 | tf_op jit(solution)/shard_map/ppermute | solution.py:28
  4.5 2.6 %collective-permute-done.1.rim_near = bf16[1,64,512]{2,1,0:T(8,128)(2,1)S(1)} collective-permute-done((bf16[1,64,512]{2,1,0:T(8,128)(2,1)}, bf16[1,64,512]{2,1,0:T(8,128)(2,1)S(1)}, u32[]{:S(2)}, u32[]{:S(2)}) %collective-permute-start.1) | collective-permute-done | bytes 65568 | tf_op jit(solution)/shard_map/ppermute | solution.py:28
  7.2 2.6 %collective-permute-done.near = bf16[1,64,512]{2,1,0:T(8,128)(2,1)S(1)} collective-permute-done((bf16[1,64,512]{2,1,0:T(8,128)(2,1)}, bf16[1,64,512]{2,1,0:T(8,128)(2,1)S(1)}, u32[]{:S(2)}, u32[]{:S(2)}) %collective-permute-start) | collective-permute-done | bytes 65568 | tf_op jit(solution)/shard_map/ppermute | solution.py:28
  9.8 1.3 %collective-permute-start.2 = (bf16[2,64,512]{2,1,0:T(8,128)(2,1)S(1)}, bf16[2,64,512]{2,1,0:T(8,128)(2,1)S(1)}, u32[]{:S(2)}, u32[]{:S(2)}) collective-permute-start(bf16[2,64,512]{2,1,0:T(8,128)(2,1)S(1)} %pad_maximum_fusion), channel_id=1, source_target_pairs={{4,0},{5,1},{6,2},{7,3},{8,4},{9,5},{10,6},{11,7},{12,8},{13,9},{1... | collective-permute-start | bytes 393224 | tf_op jit(solution)/shard_map/ppermute | solution.py:28
  11.1 0.0 collective-permute-done.3.rim
  11.1 4.8 %near_maps.1 = (bf16[224,256]{1,0:T(8,128)(2,1)S(1)}, bf16[2752,256]{1,0:T(8,128)(2,1)S(1)}, bf16[640,256]{1,0:T(8,128)(2,1)S(1)}, bf16[192,256]{1,0:T(8,128)(2,...) custom-call(bf16[1,64,512]{2,1,0:T(8,128)(2,1)} %own_hbm.1, ...), custom_call_target="tpu_custom_call" | custom-call | flops 4000000000 | bytes 4000000 | tf_op jit(solution)/shard_map/near_maps/pallas_call | solution.py:459
  15.9 1.8 %collective-permute-done.2.far = bf16[2,64,512]{2,1,0:T(8,128)(2,1)S(1)} collective-permute-done((bf16[2,64,512]{2,1,0:T(8,128)(2,1)S(1)}, bf16[2,64,512]{2,1,0:T(8,128)(2,1)S(1)}, u32[]{:S(2)}, u32[]{:S(2)}) %collective-permute-start.2) | collective-permute-done | bytes 131104 | tf_op jit(solution)/shard_map/ppermute | solution.py:28
  17.7 3.2 %far_maps.1 = (f32[1,2,2,16,1024]{4,3,2,1,0:T(8,128)}, f32[1,2,1,8,1024]{4,3,2,1,0:T(8,128)}) custom-call(bf16[2,64,512]{2,1,0:T(8,128)(2,1)S(1)} %collective-permute-done.2.far, bf16[224,256]{1,0:T(8,128)(2,1)S(1)} %get-tuple-element.8.row_ref, bf16[2752,256]{1,0:T(8,128)(2,1)S(1)} %get-tuple-element.9.table_ref, ...), custom_call_target="tpu_custom_call" | custom-call | flops 3000000000 | bytes 4000000 | tf_op jit(solution)/shard_map/far_maps/pallas_call | solution.py:474
  (1 shorter events, 0.0 us)
Async XLA Ops:
  0.6 6.5 %collective-permute-start.1 = (bf16[1,64,512]{2,1,0:T(8,128)(2,1)}, bf16[1,64,512]{2,1,0:T(8,128)(2,1)S(1)}, u32[]{:S(2)}, u32[]{:S(2)}) collective-permute-start(bf16[1,64,512]{2,1,0:T(8,128)(2,1)} %own_hbm.1), channel_id=1, source_target_pairs={{5,0},{6,1},{7,2},{9,4},{10,5},{11,6},{13,8},{14,9},{15,10},{21,16... | collective-permute-start | bytes 196616 | tf_op jit(solution)/shard_map/ppermute | solution.py:28
  1.9 7.9 %collective-permute-start = (bf16[1,64,512]{2,1,0:T(8,128)(2,1)}, bf16[1,64,512]{2,1,0:T(8,128)(2,1)S(1)}, u32[]{:S(2)}, u32[]{:S(2)}) collective-permute-start(bf16[1,64,512]{2,1,0:T(8,128)(2,1)} %own_hbm.1), channel_id=1, source_target_pairs={{4,0},{5,1},{6,2},{7,3},{8,4},{9,5},{10,6},{11,7},{12,8},{13,9},{1... | collective-permute-start | bytes 196616 | tf_op jit(solution)/shard_map/ppermute | solution.py:28
  3.2 7.9 %collective-permute-start.3 = (bf16[1,64,512]{2,1,0:T(8,128)(2,1)}, bf16[1,64,512]{2,1,0:T(8,128)(2,1)S(1)}, u32[]{:S(2)}, u32[]{:S(2)}) collective-permute-start(bf16[1,64,512]{2,1,0:T(8,128)(2,1)} %own_hbm.1), channel_id=1, source_target_pairs={{1,0},{2,1},{3,2},{5,4},{6,5},{7,6},{9,8},{10,9},{11,10},{13,12},{... | collective-permute-start | bytes 196616 | tf_op jit(solution)/shard_map/ppermute | solution.py:28
  9.8 7.9 %collective-permute-start.2 = (bf16[2,64,512]{2,1,0:T(8,128)(2,1)S(1)}, bf16[2,64,512]{2,1,0:T(8,128)(2,1)S(1)}, u32[]{:S(2)}, u32[]{:S(2)}) collective-permute-start(bf16[2,64,512]{2,1,0:T(8,128)(2,1)S(1)} %pad_maximum_fusion), channel_id=1, source_target_pairs={{4,0},{5,1},{6,2},{7,3},{8,4},{9,5},{10,6},{11,7},{12,8},{13,9},{1... | collective-permute-start | bytes 393224 | tf_op jit(solution)/shard_map/ppermute | solution.py:28
where the time goes:
time: 21.1 us; the launch traced here: 20.9 us
  Pallas kernels  8.02 us (38%)
  waiting for transfers between devices  7.03 us (33%)
  starting transfers between devices  5.17 us (25%)
  between operations  0.68 us (3%)
    ppermute x4, waiting for transfers between devices, from_device(): return lax.ppermute(value, ('sec', 'strip'), pairs)  7.03 us
    ppermute x4, starting transfers between devices, from_device(): return lax.ppermute(value, ('sec', 'strip'), pairs)  5.17 us
    pallas_call x1, Pallas kernels, correlate(): pl.pallas_call(functools.partial(near_kernel, fine, coarse, places), out_...  4.77 us
    pallas_call x1, Pallas kernels, correlate(): pl.pallas_call(functools.partial(far_kernel, fine, coarse, places), out_s...  3.25 us
  transfers between devices with their start and end apart: 4, of which 3 were waited for; matrix products, arithmetic and copies ran while one was open for 0% of the time, Pallas kernels for 23%

commit v1 on v0

--- a/solution.py
+++ b/solution.py
@@ -165,7 +165,8 @@
 
 
 class Level:
-    def __init__(self, blocks, quads, first, nyquist, number, start, table):
+    def __init__(self, pool, blocks, quads, first, nyquist, number, start, table):
+        self.pool = pool
         self.blocks, self.quads, self.tiles = blocks, quads, 2 * quads
         self.first, self.nyquist, self.number = first, nyquist, number
         self.rows = blocks * HALF + NYQ
@@ -176,8 +177,8 @@
 def levels_of(fine, coarse, width, places):
     fine_at, coarse_at = places[0], places[1]
     return [
-        Level(fine, width // STRIDE // 4, 0, fine * HALF, 0, 0, fine_at),
-        Level(coarse, width // (2 * STRIDE) // 4, NYQ, 0, fine, fine * HALF, coarse_at),
+        Level(1, fine, width // STRIDE // 4, 0, fine * HALF, 0, 0, fine_at),
+        Level(2, coarse, width // (2 * STRIDE) // 4, NYQ, 0, fine, fine * HALF, coarse_at),
     ]
 
 
@@ -190,28 +191,28 @@
             ref[r : r + 16, width:] = jnp.zeros((16, LANES), bf16)
 
 
-def transform_columns(level, pool, halves, left, f_ref, spec_ref, table_ref):
+def gather_windows(level, halves, left):
     half_rows = halves[0].shape[0] // 2
-    rows, size = level.rows, pool * LANES
+    rows, pool = level.rows, level.pool
     for source, target in zip(halves, left):
         for tile in range(level.tiles):
             for p in range(pool):
-                at = size * (tile // 2) + LANES * p + pool * STRIDE * (tile % 2)
+                at = pool * LANES * (tile // 2) + LANES * p + pool * STRIDE * (tile % 2)
                 for half in range(2):
                     target[tile * rows : (tile + 1) * rows, (2 * p + half) * LANES : (2 * p + half + 1) * LANES] = (
                         source[half * half_rows + level.start : half * half_rows + level.start + rows, at : at + LANES])
-    f_ref[...] = dot3(left[0][...], left[1][...], table_ref, level.table)
-
+
+
+def spectrum_power(level, f_ref):
     sub = lax.broadcasted_iota(jnp.int32, (8, LANES), 0)
     lane = lax.broadcasted_iota(jnp.int32, (8, LANES), 1)
     dc = (sub == 0) & (lane % PATCH == 0)
-    dc_both = jnp.concatenate([dc, dc], axis=1)
     group = lax.broadcasted_iota(jnp.int32, (LANES, LANES), 0) // PATCH
     same = group == lax.broadcasted_iota(jnp.int32, (LANES, LANES), 1) // PATCH
     ones = jnp.where(same, 1.0, 0.0).astype(bf16)
     sums = []
     for tile in range(level.tiles):
-        base = tile * rows
+        base = tile * level.rows
         for b in range(level.blocks):
             total = None
             for r in range(0, HALF, 8):
@@ -227,9 +228,15 @@
             tail = jnp.where(sub == level.number + b, re * re + im * im, 0.0)
             sums.append(2.0 * total - head + tail)
     high, low = split(jnp.concatenate(sums, axis=0))
-    sums = dot(jnp.concatenate([high, low], axis=1), jnp.concatenate([ones, ones], axis=0))
+    return dot(jnp.concatenate([high, low], axis=1), jnp.concatenate([ones, ones], axis=0))
+
+
+def scale_spectrum(level, f_ref, sums, spec_ref):
+    sub = lax.broadcasted_iota(jnp.int32, (8, 2 * LANES), 0)
+    lane = lax.broadcasted_iota(jnp.int32, (8, 2 * LANES), 1)
+    dc = (sub == 0) & (lane % PATCH == 0)
     for tile in range(level.tiles):
-        base = tile * rows
+        base = tile * level.rows
         at = base + level.nyquist
         nyq = f_ref[at : at + 8]
         scaled = jnp.zeros_like(nyq)
@@ -237,17 +244,31 @@
             number = (tile * level.blocks + b) * 8
             scale = lax.rsqrt(all_rows(sums[number : number + 8]) * (1.0 / PATCH**4) + 1e-05)
             scale = jnp.concatenate([scale, scale], axis=1)
-            first = level.first + b * HALF
             for r in range(0, HALF, 16):
-                at = base + first + r
+                at = base + level.first + b * HALF + r
                 head = f_ref[at : at + 8]
                 if r == 0:
-                    head = jnp.where(dc_both, 0.0, head)
+                    head = jnp.where(dc, 0.0, head)
                 both = jnp.concatenate([head * scale, f_ref[at + 8 : at + 16] * scale], axis=0)
                 spec_ref[at : at + 16] = both.astype(bf16)
-            scaled = jnp.where(sub[:, :1] == level.number + b, nyq * scale, scaled)
+            scaled = jnp.where(sub == level.number + b, nyq * scale, scaled)
         at = base + level.nyquist
         spec_ref[at : at + 16] = jnp.concatenate([scaled, jnp.zeros_like(scaled)], axis=0).astype(bf16)
+
+
+def transform(levels, x, row_ref, table_ref, tables_ready, scratch, specs):
+    t_ref, *halves = scratch[:3]
+    lefts, f_refs = (scratch[3:5], scratch[5:7]), scratch[7:9]
+    transform_rows(x, row_ref, t_ref, halves)
+    for level, left in zip(levels, lefts):
+        gather_windows(level, halves, left)
+    sums = []
+    for level, left, f_ref, ready in zip(levels, lefts, f_refs, tables_ready):
+        ready()
+        f_ref[...] = dot3(left[0][...], left[1][...], table_ref, level.table)
+        sums.append(spectrum_power(level, f_ref))
+    for level, f_ref, total, spec_ref in zip(levels, f_refs, sums, specs):
+        scale_spectrum(level, f_ref, total, spec_ref)
 
 
 def correlate_pair(levels, own_specs, other_specs, masks, table_ref, shift_at, map_at, scratch, outs):
@@ -315,85 +336,75 @@
     return pad_ref[...]
 
 
-def near_kernel(
+def own_kernel(
     fine, coarse, places,
-    own_hbm, near, rim, rim_near, mask_hbm, mask_coarse_hbm, table_hbm,
-    row_ref, table_ref, own_fine, own_coarse, map_fine, map_coarse,
-    own, mask, mask_coarse, pad, pad_coarse, t_ref, t_high, t_low, left_high, left_low, coarse_high, coarse_low,
-    f_fine, f_coarse, near_fine, near_coarse, *rest,
+    own_hbm, rim, table_hbm,
+    row_ref, table_ref, own_fine, own_coarse,
+    own, *rest,
 ):
-    sems = rest[-1]
-    loads = [
-        pltpu.make_async_copy(own_hbm, own, sems.at[0]),
-        pltpu.make_async_copy(mask_hbm, mask, sems.at[1]),
-        pltpu.make_async_copy(mask_coarse_hbm, mask_coarse, sems.at[2]),
-    ]
+    *scratch, sems = rest
     fine_at, coarse_at, shift_at, map_at, end = places
+    loads = [pltpu.make_async_copy(own_hbm, own, sems.at[0])]
     for i, (first, last) in enumerate(((fine_at, coarse_at), (coarse_at, shift_at), (shift_at, end))):
         piece = pl.ds(first, last - first)
-        loads.append(pltpu.make_async_copy(table_hbm.at[piece], table_ref.at[piece], sems.at[3 + i]))
+        loads.append(pltpu.make_async_copy(table_hbm.at[piece], table_ref.at[piece], sems.at[1 + i]))
     for load in loads:
         load.start()
     write_row_table(row_ref, fine, coarse)
-    levels = levels_of(fine, coarse, near.shape[2], places)
-    specs = ((near_fine, near_coarse), (own_fine, own_coarse))
-    for z in range(2):
-        if z == 1:
-            loads[0].wait()
-        strips = ((near, rim_near), (own, rim))[z]
-        x = jnp.concatenate([strips[0][0], strips[1][0]], axis=0)
-        transform_rows(x, row_ref, t_ref.at[z], (t_high.at[z], t_low.at[z]))
+    levels = levels_of(fine, coarse, rim.shape[2], places)
+    loads[0].wait()
+    x = jnp.concatenate([own[0], rim[0]], axis=0)
+    transform(levels, x, row_ref, table_ref, (loads[1].wait, loads[2].wait), scratch, (own_fine, own_coarse))
     loads[3].wait()
-    for z in range(2):
-        transform_columns(
-            levels[0], 1, (t_high.at[z], t_low.at[z]), (left_high.at[z], left_low.at[z]), f_fine.at[z],
-            specs[z][0], table_ref)
-    loads[4].wait()
-    for z in range(2):
-        transform_columns(
-            levels[1], 2, (t_high.at[z], t_low.at[z]), (coarse_high.at[z], coarse_low.at[z]), f_coarse.at[z],
-            specs[z][1], table_ref)
-    loads[5].wait()
-    loads[1].wait()
-    loads[2].wait()
+
+
+def other_maps(fine, coarse, places, other, row_ref, table_ref, own_specs, mask_hbms, outs, scratch, sems):
+    mask, mask_coarse, pad, pad_coarse = scratch[:4]
+    transform_scratch, specs, pair_scratch = scratch[4:13], scratch[13:15], scratch[15:]
+    fine_at, coarse_at, shift_at, map_at, end = places
+    loads = [
+        pltpu.make_async_copy(source, target, sems.at[i])
+        for i, (source, target) in enumerate(zip(mask_hbms, (mask, mask_coarse)))]
+    for load in loads:
+        load.start()
+    levels = levels_of(fine, coarse, other.shape[2], places)
+    x = jnp.concatenate([other[0], other[1]], axis=0)
+    transform(levels, x, row_ref, table_ref, (lambda: None,) * 2, transform_scratch, specs)
+    for load in loads:
+        load.wait()
     correlate_pair(
-        levels, specs[1], specs[0], (mask_tile(mask, pad), mask_tile(mask_coarse, pad_coarse)),
-        table_ref, shift_at, map_at, rest[:-1], (map_fine, map_coarse))
+        levels, own_specs, specs, (mask_tile(mask, pad), mask_tile(mask_coarse, pad_coarse)),
+        table_ref, shift_at, map_at, pair_scratch, outs)
+
+
+def near_kernel(
+    fine, coarse, places,
+    near, row_ref, table_ref, own_fine, own_coarse, mask_hbm, mask_coarse_hbm,
+    map_fine, map_coarse,
+    *rest,
+):
+    *scratch, sems = rest
+    other_maps(
+        fine, coarse, places, near, row_ref, table_ref, (own_fine, own_coarse), (mask_hbm, mask_coarse_hbm),
+        (map_fine, map_coarse), scratch, sems)
 
 
 def far_kernel(
     fine, coarse, places,
-    far, row_ref, table_ref, own_fine, own_coarse, map_fine, map_coarse, mask_hbm, mask_coarse_hbm,
+    far, row_ref, table_ref, own_fine, own_coarse, mask_hbm, mask_coarse_hbm, map_fine, map_coarse,
     out_fine, out_coarse,
-    mask, mask_coarse, pad, pad_coarse, t_ref, t_high, t_low, left_high, left_low, coarse_high, coarse_low,
-    f_fine, f_coarse, far_fine, far_coarse, last_fine, last_coarse, *rest,
+    last_fine, last_coarse, *rest,
 ):
-    sems = rest[-1]
-    loads = [
-        pltpu.make_async_copy(mask_hbm, mask, sems.at[0]),
-        pltpu.make_async_copy(mask_coarse_hbm, mask_coarse, sems.at[1]),
-    ]
+    *scratch, sems = rest
     stores = [
         pltpu.make_async_copy(map_fine, out_fine.at[0, 0], sems.at[2]),
         pltpu.make_async_copy(map_coarse, out_coarse.at[0, 0], sems.at[3]),
     ]
-    for copy in loads + stores:
+    for copy in stores:
         copy.start()
-    fine_at, coarse_at, shift_at, map_at, end = places
-    levels = levels_of(fine, coarse, far.shape[2], places)
-    x = jnp.concatenate([far[0], far[1]], axis=0)
-    transform_rows(x, row_ref, t_ref.at[0], (t_high.at[0], t_low.at[0]))
-    transform_columns(
-        levels[0], 1, (t_high.at[0], t_low.at[0]), (left_high.at[0], left_low.at[0]), f_fine.at[0], far_fine, table_ref)
-    transform_columns(
-        levels[1], 2, (t_high.at[0], t_low.at[0]), (coarse_high.at[0], coarse_low.at[0]), f_coarse.at[0],
-        far_coarse, table_ref)
-    for load in loads:
-        load.wait()
-    correlate_pair(
-        levels, (own_fine, own_coarse), (far_fine, far_coarse),
-        (mask_tile(mask, pad), mask_tile(mask_coarse, pad_coarse)),
-        table_ref, shift_at, map_at, rest[:-1], (last_fine, last_coarse))
+    other_maps(
+        fine, coarse, places, far, row_ref, table_ref, (own_fine, own_coarse), (mask_hbm, mask_coarse_hbm),
+        (last_fine, last_coarse), scratch, sems)
     last = [
         pltpu.make_async_copy(last_fine, out_fine.at[0, 1], sems.at[4]),
         pltpu.make_async_copy(last_coarse, out_coarse.at[0, 1], sems.at[5]),
@@ -404,7 +415,7 @@
         copy.wait()
 
 
-def correlate(own, near, rim, rim_near, far, mask_fine, mask_coarse):
+def correlate(own, rim, near, far_of, mask_fine, mask_coarse):
     strip_rows, width = own.shape[1:]
     fine, coarse = mask_fine.shape[1], mask_coarse.shape[1]
     ext = strip_rows + PATCH
@@ -413,28 +424,24 @@
     half_rows = (fine + coarse) * HALF + NYQ
     tiles = sum(level.blocks * level.quads for level in levels)
     spec_shapes = [(level.tiles * level.rows, 2 * LANES) for level in levels]
+    left_shapes = [(level.tiles * level.rows, 2 * level.pool * LANES) for level in levels]
     map_shapes = [(level.blocks, 4 * level.quads, WINDOW * WINDOW) for level in levels]
     cross_rows = sum(level.quads * level.rows for level in levels)
 
-    def scratch(sections):
-        def many(shape, dtype):
-            return pltpu.VMEM((sections,) + shape, dtype)
-
-        return [
-            many((2 * half_rows, width), f32),
-            many((2 * half_rows, width + LANES), bf16),
-            many((2 * half_rows, width + LANES), bf16),
-            many(spec_shapes[0], bf16),
-            many(spec_shapes[0], bf16),
-            many((spec_shapes[1][0], 4 * LANES), bf16),
-            many((spec_shapes[1][0], 4 * LANES), bf16),
-            many(spec_shapes[0], f32),
-            many(spec_shapes[1], f32),
-            pltpu.VMEM(spec_shapes[0], bf16),
-            pltpu.VMEM(spec_shapes[1], bf16),
-        ]
-
-    pair_scratch = [
+    transform_scratch = [
+        pltpu.VMEM((2 * half_rows, width), f32),
+        pltpu.VMEM((2 * half_rows, width + LANES), bf16),
+        pltpu.VMEM((2 * half_rows, width + LANES), bf16),
+        *(pltpu.VMEM(shape, bf16) for shape in left_shapes for _ in range(2)),
+        *(pltpu.VMEM(shape, f32) for shape in spec_shapes),
+    ]
+    other_scratch = [
+        pltpu.VMEM(mask_fine.shape, jnp.int32),
+        pltpu.VMEM(mask_coarse.shape, jnp.int32),
+        pltpu.VMEM((8, LANES), f32),
+        pltpu.VMEM((8, LANES), f32),
+        *transform_scratch,
+        *(pltpu.VMEM(shape, bf16) for shape in spec_shapes),
         pltpu.VMEM((cross_rows, 4 * LANES), bf16),
         pltpu.VMEM((cross_rows, 4 * LANES), bf16),
         pltpu.VMEM((cross_rows, 2 * LANES), f32),
@@ -443,53 +450,58 @@
         *(pltpu.VMEM((4 * HALF + 2 * NYQ, level.quads * LANES), bf16) for level in levels for _ in range(level.blocks)),
         pltpu.SemaphoreType.DMA((6,)),
     ]
-    mask_scratch = [
-        pltpu.VMEM(mask_fine.shape, jnp.int32),
-        pltpu.VMEM(mask_coarse.shape, jnp.int32),
-        pltpu.VMEM((8, LANES), f32),
-        pltpu.VMEM((8, LANES), f32),
-    ]
     hbm = pl.BlockSpec(memory_space=pltpu.HBM)
     vmem = pl.BlockSpec(memory_space=pltpu.VMEM)
     params = pltpu.CompilerParams(vmem_limit_bytes=24 * 1024 * 1024)
+
+    def cost(flops):
+        return pl.CostEstimate(flops=flops, bytes_accessed=4 * 10**6, transcendentals=0)
+
     own, table, mask_fine, mask_coarse = (
         pltpu.with_memory_space_constraint(value, pltpu.HBM)
         for value in (own, jnp.asarray(table), mask_fine, mask_coarse))
-
     handed = pl.pallas_call(
-        functools.partial(near_kernel, fine, coarse, places),
+        functools.partial(own_kernel, fine, coarse, places),
         out_shape=(
             jax.ShapeDtypeStruct((2 * half_rows, 2 * ext), bf16),
             jax.ShapeDtypeStruct(table.shape, bf16),
             *(jax.ShapeDtypeStruct(shape, bf16) for shape in spec_shapes),
-            *(jax.ShapeDtypeStruct(shape, f32) for shape in map_shapes),
         ),
-        in_specs=[hbm, vmem, vmem, vmem, hbm, hbm, hbm],
-        out_specs=(vmem,) * 6,
-        scratch_shapes=[pltpu.VMEM(own.shape, bf16), *mask_scratch, *scratch(2), *pair_scratch],
+        in_specs=[hbm, vmem, hbm],
+        out_specs=(vmem,) * 4,
+        scratch_shapes=[pltpu.VMEM(own.shape, bf16), *transform_scratch, pltpu.SemaphoreType.DMA((4,))],
         compiler_params=params,
-        cost_estimate=pl.CostEstimate(flops=4 * 10**9, bytes_accessed=4 * 10**6, transcendentals=0),
+        cost_estimate=cost(2 * 10**9),
+        name="own_spectra",
+    )(own, rim, table)
+    near, handed = lax.optimization_barrier((near, handed))
+    far = far_of(near)
+    maps = pl.pallas_call(
+        functools.partial(near_kernel, fine, coarse, places),
+        out_shape=tuple(jax.ShapeDtypeStruct(shape, f32) for shape in map_shapes),
+        in_specs=[vmem] * 5 + [hbm, hbm],
+        out_specs=(vmem, vmem),
+        scratch_shapes=other_scratch,
+        compiler_params=params,
+        cost_estimate=cost(3 * 10**9),
         name="near_maps",
-    )(own, near, rim, rim_near, mask_fine, mask_coarse, table)
+    )(near, *handed, mask_fine, mask_coarse)
     return pl.pallas_call(
         functools.partial(far_kernel, fine, coarse, places),
         out_shape=tuple(jax.ShapeDtypeStruct((1, 2) + shape, f32) for shape in map_shapes),
-        in_specs=[vmem] * 7 + [hbm, hbm],
+        in_specs=[vmem] * 5 + [hbm, hbm, vmem, vmem],
         out_specs=(hbm, hbm),
-        scratch_shapes=[
-            *mask_scratch, *scratch(1), *(pltpu.VMEM(shape, f32) for shape in map_shapes), *pair_scratch],
+        scratch_shapes=[*(pltpu.VMEM(shape, f32) for shape in map_shapes), *other_scratch],
         compiler_params=params,
-        cost_estimate=pl.CostEstimate(flops=3 * 10**9, bytes_accessed=4 * 10**6, transcendentals=0),
+        cost_estimate=cost(3 * 10**9),
         name="far_maps",
-    )(far, *handed, mask_fine, mask_coarse)
+    )(far, *handed, mask_fine, mask_coarse, *maps)
 
 
 def local(sections, mask_fine, mask_coarse):
-    near = from_device(sections, 1, 0)
-    rim_near = from_device(sections, 1, 1)
     rim = from_device(sections, 0, 1)
-    far = from_device(jnp.concatenate([near, rim_near], axis=0), 1, 0)
-    return correlate(sections, near, rim, rim_near, far, mask_fine, mask_coarse)
+    near = jnp.concatenate([from_device(sections, 1, 0), from_device(sections, 1, 1)], axis=0)
+    return correlate(sections, rim, near, lambda value: from_device(value, 1, 0), mask_fine, mask_coarse)
 
 
 def solution(mesh):

time: 21.1 us -> 24 us (1.14)
  the two profiles are of different devices: /device:TPU:0 before, /device:TPU:1 now
where the time goes in v1:
time: 24 us; the launch traced here: 23.6 us
  Pallas kernels  8.62 us (36%)
  waiting for transfers between devices  8.45 us (35%)
  starting transfers between devices  5.84 us (24%)
  between operations  0.68 us (3%)
    ppermute x4, waiting for transfers between devices, from_device(): return lax.ppermute(value, ('sec', 'strip'), pairs)  8.45 us
    ppermute x4, starting transfers between devices, from_device(): return lax.ppermute(value, ('sec', 'strip'), pairs)  5.84 us
    pallas_call x1, Pallas kernels, correlate(): pl.pallas_call(functools.partial(far_kernel, fine, coarse, places), out_s...  3.25 us
    pallas_call x1, Pallas kernels, correlate(): pl.pallas_call(functools.partial(own_kernel, fine, coarse, places), out_s...  2.74 us
    pallas_call x1, Pallas kernels, correlate(): pl.pallas_call(functools.partial(near_kernel, fine, coarse, places), out_...  2.64 us
  transfers between devices with their start and end apart: 4, of which 4 were waited for; matrix products, arithmetic and copies ran while one was open for 0% of the time, Pallas kernels for 11%

profile of v1, /device:TPU:1, one launch (start us, length us, event | category | flops | bytes accessed | tf_op | source)
XLA Modules:
  0.0 23.6 jit_solution(18147790965543623267)
XLA Ops:
  0.6 1.3 %collective-permute-start.1 = (bf16[1,64,512]{2,1,0:T(8,128)(2,1)}, bf16[1,64,512]{2,1,0:T(8,128)(2,1)S(1)}, u32[]{:S(2)}, u32[]{:S(2)}) collective-permute-start(bf16[1,64,512]{2,1,0:T(8,128)(2,1)} %own_hbm.1), channel_id=1, source_target_pairs={{5,0},{6,1},{7,2},{9,4},{10,5},{11,6},{13,8},{14,9},{15,10},{21,16... | collective-permute-start | bytes 196616 | tf_op jit(solution)/shard_map/ppermute | solution.py:28
  1.9 1.3 %collective-permute-start = (bf16[1,64,512]{2,1,0:T(8,128)(2,1)}, bf16[1,64,512]{2,1,0:T(8,128)(2,1)S(1)}, u32[]{:S(2)}, u32[]{:S(2)}) collective-permute-start(bf16[1,64,512]{2,1,0:T(8,128)(2,1)} %own_hbm.1), channel_id=1, source_target_pairs={{4,0},{5,1},{6,2},{7,3},{8,4},{9,5},{10,6},{11,7},{12,8},{13,9},{1... | collective-permute-start | bytes 196616 | tf_op jit(solution)/shard_map/ppermute | solution.py:28
  3.2 2.0 %collective-permute-start.2 = (bf16[1,64,512]{2,1,0:T(8,128)(2,1)}, bf16[1,64,512]{2,1,0:T(8,128)(2,1)S(1)}, u32[]{:S(2)}, u32[]{:S(2)}) collective-permute-start(bf16[1,64,512]{2,1,0:T(8,128)(2,1)} %own_hbm.1), channel_id=1, source_target_pairs={{1,0},{2,1},{3,2},{5,4},{6,5},{7,6},{9,8},{10,9},{11,10},{13,12},{... | collective-permute-start | bytes 196616 | tf_op jit(solution)/shard_map/ppermute | solution.py:28
  5.2 3.7 %collective-permute-done.1 = bf16[1,64,512]{2,1,0:T(8,128)(2,1)S(1)} collective-permute-done((bf16[1,64,512]{2,1,0:T(8,128)(2,1)}, bf16[1,64,512]{2,1,0:T(8,128)(2,1)S(1)}, u32[]{:S(2)}, u32[]{:S(2)}) %collective-permute-start.1) | collective-permute-done | bytes 65568 | tf_op jit(solution)/shard_map/ppermute | solution.py:28
  8.9 0.4 %collective-permute-done = bf16[1,64,512]{2,1,0:T(8,128)(2,1)S(1)} collective-permute-done((bf16[1,64,512]{2,1,0:T(8,128)(2,1)}, bf16[1,64,512]{2,1,0:T(8,128)(2,1)S(1)}, u32[]{:S(2)}, u32[]{:S(2)}) %collective-permute-start) | collective-permute-done | bytes 65568 | tf_op jit(solution)/shard_map/ppermute | solution.py:28
  9.2 0.6 %collective-permute-done.2.rim = bf16[1,64,512]{2,1,0:T(8,128)(2,1)S(1)} collective-permute-done((bf16[1,64,512]{2,1,0:T(8,128)(2,1)}, bf16[1,64,512]{2,1,0:T(8,128)(2,1)S(1)}, u32[]{:S(2)}, u32[]{:S(2)}) %collective-permute-start.2) | collective-permute-done | bytes 65568 | tf_op jit(solution)/shard_map/ppermute | solution.py:28
  9.9 2.7 %own_spectra.1 = (bf16[224,256]{1,0:T(8,128)(2,1)S(1)}, bf16[2752,256]{1,0:T(8,128)(2,1)S(1)}, bf16[640,256]{1,0:T(8,128)(2,1)S(1)}, bf16[192,256]{1,0:T(8,128)(2,1)S(1)}) custom-call(bf16[1,64,512]{2,1,0:T(8,128)(2,1)} %own_hbm.1, bf16[1,64,512]{2,1,0:T(8,128)(2,1)S(1)} %collective-permute-done.2.rim, bf16[2752,256]{1,0:T(8,128)(2,1)} %constant.2.clone.table_hbm), custom_call_target="tpu_custom_call" | custom-call | flops 2000000000 | bytes 4000000 | tf_op jit(solution)/shard_map/own_spectra/pallas_call | solution.py:463
  12.6 1.3 %collective-permute-start.3 = (bf16[2,64,512]{2,1,0:T(8,128)(2,1)S(1)}, bf16[2,64,512]{2,1,0:T(8,128)(2,1)S(1)}, u32[]{:S(2)}, u32[]{:S(2)}) collective-permute-start(bf16[2,64,512]{2,1,0:T(8,128)(2,1)S(1)} %pad_maximum_fusion.near), channel_id=1, source_target_pairs={{4,0},{5,1},{6,2},{7,3},{8,4},{9,5},{10,6},{11,7},{12,8},{13,9},{1... | collective-permute-start | bytes 393224 | tf_op jit(solution)/shard_map/ppermute | solution.py:28
  13.9 2.6 %near_maps.1 = (f32[2,16,1024]{2,1,0:T(8,128)S(1)}, f32[1,8,1024]{2,1,0:T(8,128)S(1)}) custom-call(bf16[2,64,512]{2,1,0:T(8,128)(2,1)S(1)} %pad_maximum_fusion.near, bf16[224,256]{1,0:T(8,128)(2,1)S(1)} %get-tuple-element.18.row_ref, bf16[2752,256]{1,0:T(8,128)(2,1)S(1)} %get-tuple-element.19.table_ref, bf16[640,256]{1,0:T(8,128)(2,1)S(1)} %get-tuple-element.20.own_fine, ...), custom_call_target="tpu_custom_call" | custom-call | flops 3000000000 | bytes 4000000 | tf_op jit(solution)/shard_map/near_maps/pallas_call | solution.py:479
  16.6 3.8 %collective-permute-done.3.far = bf16[2,64,512]{2,1,0:T(8,128)(2,1)S(1)} collective-permute-done((bf16[2,64,512]{2,1,0:T(8,128)(2,1)S(1)}, bf16[2,64,512]{2,1,0:T(8,128)(2,1)S(1)}, u32[]{:S(2)}, u32[]{:S(2)}) %collective-permute-start.3) | collective-permute-done | bytes 131104 | tf_op jit(solution)/shard_map/ppermute | solution.py:28
  20.4 3.2 %far_maps.1 = (f32[1,2,2,16,1024]{4,3,2,1,0:T(8,128)}, f32[1,2,1,8,1024]{4,3,2,1,0:T(8,128)}) custom-call(bf16[2,64,512]{2,1,0:T(8,128)(2,1)S(1)} %collective-permute-done.3.far, bf16[224,256]{1,0:T(8,128)(2,1)S(1)} %get-tuple-element.18.row_ref, bf16[2752,256]{1,0:T(8,128)(2,1)S(1)} %get-tuple-element.19.table_ref, ...), custom_call_target="tpu_custom_call" | custom-call | flops 3000000000 | bytes 4000000 | tf_op jit(solution)/shard_map/far_maps/pallas_call | solution.py:489
  (1 shorter events, 0.0 us)
Async XLA Ops:
  0.6 8.2 %collective-permute-start.1 = (bf16[1,64,512]{2,1,0:T(8,128)(2,1)}, bf16[1,64,512]{2,1,0:T(8,128)(2,1)S(1)}, u32[]{:S(2)}, u32[]{:S(2)}) collective-permute-start(bf16[1,64,512]{2,1,0:T(8,128)(2,1)} %own_hbm.1), channel_id=1, source_target_pairs={{5,0},{6,1},{7,2},{9,4},{10,5},{11,6},{13,8},{14,9},{15,10},{21,16... | collective-permute-start | bytes 196616 | tf_op jit(solution)/shard_map/ppermute | solution.py:28
  1.9 7.3 %collective-permute-start = (bf16[1,64,512]{2,1,0:T(8,128)(2,1)}, bf16[1,64,512]{2,1,0:T(8,128)(2,1)S(1)}, u32[]{:S(2)}, u32[]{:S(2)}) collective-permute-start(bf16[1,64,512]{2,1,0:T(8,128)(2,1)} %own_hbm.1), channel_id=1, source_target_pairs={{4,0},{5,1},{6,2},{7,3},{8,4},{9,5},{10,6},{11,7},{12,8},{13,9},{1... | collective-permute-start | bytes 196616 | tf_op jit(solution)/shard_map/ppermute | solution.py:28
  3.2 6.7 %collective-permute-start.2 = (bf16[1,64,512]{2,1,0:T(8,128)(2,1)}, bf16[1,64,512]{2,1,0:T(8,128)(2,1)S(1)}, u32[]{:S(2)}, u32[]{:S(2)}) collective-permute-start(bf16[1,64,512]{2,1,0:T(8,128)(2,1)} %own_hbm.1), channel_id=1, source_target_pairs={{1,0},{2,1},{3,2},{5,4},{6,5},{7,6},{9,8},{10,9},{11,10},{13,12},{... | collective-permute-start | bytes 196616 | tf_op jit(solution)/shard_map/ppermute | solution.py:28
  12.6 7.7 %collective-permute-start.3 = (bf16[2,64,512]{2,1,0:T(8,128)(2,1)S(1)}, bf16[2,64,512]{2,1,0:T(8,128)(2,1)S(1)}, u32[]{:S(2)}, u32[]{:S(2)}) collective-permute-start(bf16[2,64,512]{2,1,0:T(8,128)(2,1)S(1)} %pad_maximum_fusion.near), channel_id=1, source_target_pairs={{4,0},{5,1},{6,2},{7,3},{8,4},{9,5},{10,6},{11,7},{12,8},{13,9},{1... | collective-permute-start | bytes 393224 | tf_op jit(solution)/shard_map/ppermute | solution.py:28

commit v2 on v1

--- a/solution.py
+++ b/solution.py
@@ -180,15 +180,6 @@
         Level(1, fine, width // STRIDE // 4, 0, fine * HALF, 0, 0, fine_at),
         Level(2, coarse, width // (2 * STRIDE) // 4, NYQ, 0, fine, fine * HALF, coarse_at),
     ]
-
-
-def transform_rows(x, row_ref, t_ref, halves):
-    width = x.shape[1]
-    t_ref[...] = dot(row_ref[...], jnp.concatenate([x, x], axis=0))
-    for r in range(0, t_ref.shape[0], 16):
-        for ref, half in zip(halves, split(t_ref[r : r + 16])):
-            ref[r : r + 16, :width] = half
-            ref[r : r + 16, width:] = jnp.zeros((16, LANES), bf16)
 
 
 def gather_windows(level, halves, left):
@@ -256,22 +247,35 @@
         spec_ref[at : at + 16] = jnp.concatenate([scaled, jnp.zeros_like(scaled)], axis=0).astype(bf16)
 
 
-def transform(levels, x, row_ref, table_ref, tables_ready, scratch, specs):
+def transform(levels, strips, row_ref, table_ref, ready, scratch, specs):
     t_ref, *halves = scratch[:3]
     lefts, f_refs = (scratch[3:5], scratch[5:7]), scratch[7:9]
-    transform_rows(x, row_ref, t_ref, halves)
+    ready[0]()
+    x = jnp.concatenate([strip[0] for strip in strips], axis=0)
+    t_ref[...] = dot(row_ref[...], jnp.concatenate([x, x], axis=0))
+    yield
+    width = x.shape[1]
+    for r in range(0, t_ref.shape[0], 16):
+        for ref, half in zip(halves, split(t_ref[r : r + 16])):
+            ref[r : r + 16, :width] = half
+            ref[r : r + 16, width:] = jnp.zeros((16, LANES), bf16)
     for level, left in zip(levels, lefts):
         gather_windows(level, halves, left)
+        yield
     sums = []
-    for level, left, f_ref, ready in zip(levels, lefts, f_refs, tables_ready):
-        ready()
+    for level, left, f_ref, wait in zip(levels, lefts, f_refs, ready[1:]):
+        wait()
         f_ref[...] = dot3(left[0][...], left[1][...], table_ref, level.table)
+        yield
+    for level, f_ref in zip(levels, f_refs):
         sums.append(spectrum_power(level, f_ref))
+    yield
     for level, f_ref, total, spec_ref in zip(levels, f_refs, sums, specs):
         scale_spectrum(level, f_ref, total, spec_ref)
-
-
-def correlate_pair(levels, own_specs, other_specs, masks, table_ref, shift_at, map_at, scratch, outs):
+        yield
+
+
+def correlate_pair(levels, own_specs, other_specs, masks, table_ref, shift_at, map_at, ready, scratch, outs):
     high_ref, low_ref, y_ref, maps_ref, rows_ref = scratch[:5]
     stacks = scratch[5:]
     base = 0
@@ -287,7 +291,10 @@
                 for ref, half in zip((high_ref, low_ref), split(cross)):
                     ref[to : to + 16, 2 * odd * LANES : 2 * (odd + 1) * LANES] = half
         base += level.quads * level.rows
+        yield
+    ready()
     y_ref[...] = dot3(high_ref[...], low_ref[...], table_ref, shift_at)
+    yield
     base = tile = 0
     starts = {}
     for index, level in enumerate(levels):
@@ -312,8 +319,9 @@
                 maps_ref[tile + quad] = maps[:, quad * LANES : (quad + 1) * LANES]
             starts[index, b] = tile
             tile += level.quads
+            yield
         base += level.quads * level.rows
-    kept = [jnp.transpose(mask) for mask in masks]
+    kept = [jnp.transpose(mask()) for mask in masks]
     lanes = lax.broadcasted_iota(jnp.int32, (tile, LANES), 1) // WINDOW
     for big in range(WINDOW // 4):
         rows = [maps_ref[:, 4 * big + r, :] for r in range(4)]
@@ -336,86 +344,95 @@
     return pad_ref[...]
 
 
-def own_kernel(
+def run_staggered(tasks):
+    done = set()
+    waiting = list(tasks)
+    active = []
+    while waiting or active:
+        for task in waiting:
+            if task[2] <= done:
+                active.append(task)
+                waiting.remove(task)
+                break
+        for task in list(active):
+            if next(task[1], done) is done:
+                active.remove(task)
+                done.add(task[0])
+
+
+def maps_kernel(
     fine, coarse, places,
-    own_hbm, rim, table_hbm,
-    row_ref, table_ref, own_fine, own_coarse,
-    own, *rest,
+    own_hbm, near, far, rim, rim_near, rim_far, mask_hbm, mask_coarse_hbm, table_hbm,
+    out_fine, out_coarse,
+    own, mask, mask_coarse, pad, pad_coarse, row_ref, table_ref, *rest,
 ):
     *scratch, sems = rest
     fine_at, coarse_at, shift_at, map_at, end = places
-    loads = [pltpu.make_async_copy(own_hbm, own, sems.at[0])]
-    for i, (first, last) in enumerate(((fine_at, coarse_at), (coarse_at, shift_at), (shift_at, end))):
-        piece = pl.ds(first, last - first)
-        loads.append(pltpu.make_async_copy(table_hbm.at[piece], table_ref.at[piece], sems.at[1 + i]))
-    for load in loads:
-        load.start()
+    copies = {}
+
+    def load(name, source, target):
+        copies[name] = pltpu.make_async_copy(source, target, sems.at[len(copies)])
+        copies[name].start()
+
+    def table(name, first, last):
+        load(name, table_hbm.at[pl.ds(first, last - first)], table_ref.at[pl.ds(first, last - first)])
+
+    def once(name):
+        def wait():
+            copy = copies.pop(name, None)
+            if copy is not None:
+                copy.wait()
+
+        return wait
+
+    table("fine", fine_at, coarse_at)
+    load("own", own_hbm, own)
+    table("coarse", coarse_at, shift_at)
+    table("shift", shift_at, end)
+    load("mask", mask_hbm, mask)
+    load("mask_coarse", mask_coarse_hbm, mask_coarse)
+    waits = {name: once(name) for name in list(copies)}
+
+    def mask_of(name, source, target):
+        waits[name]()
+        return mask_tile(source, target)
+
     write_row_table(row_ref, fine, coarse)
-    levels = levels_of(fine, coarse, rim.shape[2], places)
-    loads[0].wait()
-    x = jnp.concatenate([own[0], rim[0]], axis=0)
-    transform(levels, x, row_ref, table_ref, (loads[1].wait, loads[2].wait), scratch, (own_fine, own_coarse))
-    loads[3].wait()
-
-
-def other_maps(fine, coarse, places, other, row_ref, table_ref, own_specs, mask_hbms, outs, scratch, sems):
-    mask, mask_coarse, pad, pad_coarse = scratch[:4]
-    transform_scratch, specs, pair_scratch = scratch[4:13], scratch[13:15], scratch[15:]
-    fine_at, coarse_at, shift_at, map_at, end = places
-    loads = [
-        pltpu.make_async_copy(source, target, sems.at[i])
-        for i, (source, target) in enumerate(zip(mask_hbms, (mask, mask_coarse)))]
-    for load in loads:
-        load.start()
-    levels = levels_of(fine, coarse, other.shape[2], places)
-    x = jnp.concatenate([other[0], other[1]], axis=0)
-    transform(levels, x, row_ref, table_ref, (lambda: None,) * 2, transform_scratch, specs)
-    for load in loads:
-        load.wait()
-    correlate_pair(
-        levels, own_specs, specs, (mask_tile(mask, pad), mask_tile(mask_coarse, pad_coarse)),
-        table_ref, shift_at, map_at, pair_scratch, outs)
-
-
-def near_kernel(
-    fine, coarse, places,
-    near, row_ref, table_ref, own_fine, own_coarse, mask_hbm, mask_coarse_hbm,
-    map_fine, map_coarse,
-    *rest,
-):
-    *scratch, sems = rest
-    other_maps(
-        fine, coarse, places, near, row_ref, table_ref, (own_fine, own_coarse), (mask_hbm, mask_coarse_hbm),
-        (map_fine, map_coarse), scratch, sems)
-
-
-def far_kernel(
-    fine, coarse, places,
-    far, row_ref, table_ref, own_fine, own_coarse, mask_hbm, mask_coarse_hbm, map_fine, map_coarse,
-    out_fine, out_coarse,
-    last_fine, last_coarse, *rest,
-):
-    *scratch, sems = rest
-    stores = [
-        pltpu.make_async_copy(map_fine, out_fine.at[0, 0], sems.at[2]),
-        pltpu.make_async_copy(map_coarse, out_coarse.at[0, 0], sems.at[3]),
-    ]
-    for copy in stores:
-        copy.start()
-    other_maps(
-        fine, coarse, places, far, row_ref, table_ref, (own_fine, own_coarse), (mask_hbm, mask_coarse_hbm),
-        (last_fine, last_coarse), scratch, sems)
-    last = [
-        pltpu.make_async_copy(last_fine, out_fine.at[0, 1], sems.at[4]),
-        pltpu.make_async_copy(last_coarse, out_coarse.at[0, 1], sems.at[5]),
-    ]
-    for copy in last:
-        copy.start()
-    for copy in stores + last:
-        copy.wait()
-
-
-def correlate(own, rim, near, far_of, mask_fine, mask_coarse):
+    levels = levels_of(fine, coarse, near.shape[2], places)
+    sections = [scratch[i * 11 : (i + 1) * 11] for i in range(3)]
+    rest = scratch[33:]
+    half = len(rest) // 2
+    pairs = [rest[:half], rest[half:]]
+    specs = [section[9:] for section in sections]
+    masks = (lambda: mask_of("mask", mask, pad), lambda: mask_of("mask_coarse", mask_coarse, pad_coarse))
+    tables = (waits["fine"], waits["coarse"])
+
+    def section(z, strips, first=lambda: None):
+        return transform(levels, strips, row_ref, table_ref, (first,) + tables, sections[z][:9], specs[z])
+
+    def pair(d):
+        *pair_scratch, last_fine, last_coarse = pairs[d - 1]
+        yield from correlate_pair(
+            levels, specs[0], specs[d], masks, table_ref, shift_at, map_at, waits["shift"], pair_scratch,
+            (last_fine, last_coarse))
+        for i, (source, target) in enumerate(((last_fine, out_fine), (last_coarse, out_coarse))):
+            store = pltpu.make_async_copy(source, target.at[0, d - 1], sems.at[6 + 2 * (d - 1) + i])
+            store.start()
+            stores.append(store)
+
+    stores = []
+    run_staggered([
+        ("near", section(1, (near, rim_near)), set()),
+        ("own", section(0, (own, rim), waits["own"]), set()),
+        ("far", section(2, (far, rim_far)), set()),
+        ("first", pair(1), {"near", "own"}),
+        ("second", pair(2), {"far", "own"}),
+    ])
+    for store in stores:
+        store.wait()
+
+
+def correlate(own, near, far, rim, rim_near, rim_far, mask_fine, mask_coarse):
     strip_rows, width = own.shape[1:]
     fine, coarse = mask_fine.shape[1], mask_coarse.shape[1]
     ext = strip_rows + PATCH
@@ -428,80 +445,55 @@
     map_shapes = [(level.blocks, 4 * level.quads, WINDOW * WINDOW) for level in levels]
     cross_rows = sum(level.quads * level.rows for level in levels)
 
-    transform_scratch = [
+    section_scratch = [
         pltpu.VMEM((2 * half_rows, width), f32),
         pltpu.VMEM((2 * half_rows, width + LANES), bf16),
         pltpu.VMEM((2 * half_rows, width + LANES), bf16),
         *(pltpu.VMEM(shape, bf16) for shape in left_shapes for _ in range(2)),
         *(pltpu.VMEM(shape, f32) for shape in spec_shapes),
+        *(pltpu.VMEM(shape, bf16) for shape in spec_shapes),
     ]
-    other_scratch = [
-        pltpu.VMEM(mask_fine.shape, jnp.int32),
-        pltpu.VMEM(mask_coarse.shape, jnp.int32),
-        pltpu.VMEM((8, LANES), f32),
-        pltpu.VMEM((8, LANES), f32),
-        *transform_scratch,
-        *(pltpu.VMEM(shape, bf16) for shape in spec_shapes),
+    pair_scratch = [
         pltpu.VMEM((cross_rows, 4 * LANES), bf16),
         pltpu.VMEM((cross_rows, 4 * LANES), bf16),
         pltpu.VMEM((cross_rows, 2 * LANES), f32),
         pltpu.VMEM((tiles, WINDOW, LANES), f32),
         pltpu.VMEM((WINDOW // 4, 4 * tiles, LANES), f32),
         *(pltpu.VMEM((4 * HALF + 2 * NYQ, level.quads * LANES), bf16) for level in levels for _ in range(level.blocks)),
-        pltpu.SemaphoreType.DMA((6,)),
+        *(pltpu.VMEM(shape, f32) for shape in map_shapes),
     ]
     hbm = pl.BlockSpec(memory_space=pltpu.HBM)
     vmem = pl.BlockSpec(memory_space=pltpu.VMEM)
-    params = pltpu.CompilerParams(vmem_limit_bytes=24 * 1024 * 1024)
-
-    def cost(flops):
-        return pl.CostEstimate(flops=flops, bytes_accessed=4 * 10**6, transcendentals=0)
-
     own, table, mask_fine, mask_coarse = (
         pltpu.with_memory_space_constraint(value, pltpu.HBM)
         for value in (own, jnp.asarray(table), mask_fine, mask_coarse))
-    handed = pl.pallas_call(
-        functools.partial(own_kernel, fine, coarse, places),
-        out_shape=(
-            jax.ShapeDtypeStruct((2 * half_rows, 2 * ext), bf16),
-            jax.ShapeDtypeStruct(table.shape, bf16),
-            *(jax.ShapeDtypeStruct(shape, bf16) for shape in spec_shapes),
-        ),
-        in_specs=[hbm, vmem, hbm],
-        out_specs=(vmem,) * 4,
-        scratch_shapes=[pltpu.VMEM(own.shape, bf16), *transform_scratch, pltpu.SemaphoreType.DMA((4,))],
-        compiler_params=params,
-        cost_estimate=cost(2 * 10**9),
-        name="own_spectra",
-    )(own, rim, table)
-    near, handed = lax.optimization_barrier((near, handed))
-    far = far_of(near)
-    maps = pl.pallas_call(
-        functools.partial(near_kernel, fine, coarse, places),
-        out_shape=tuple(jax.ShapeDtypeStruct(shape, f32) for shape in map_shapes),
-        in_specs=[vmem] * 5 + [hbm, hbm],
-        out_specs=(vmem, vmem),
-        scratch_shapes=other_scratch,
-        compiler_params=params,
-        cost_estimate=cost(3 * 10**9),
-        name="near_maps",
-    )(near, *handed, mask_fine, mask_coarse)
     return pl.pallas_call(
-        functools.partial(far_kernel, fine, coarse, places),
+        functools.partial(maps_kernel, fine, coarse, places),
         out_shape=tuple(jax.ShapeDtypeStruct((1, 2) + shape, f32) for shape in map_shapes),
-        in_specs=[vmem] * 5 + [hbm, hbm, vmem, vmem],
+        in_specs=[hbm] + [vmem] * 5 + [hbm] * 3,
         out_specs=(hbm, hbm),
-        scratch_shapes=[*(pltpu.VMEM(shape, f32) for shape in map_shapes), *other_scratch],
-        compiler_params=params,
-        cost_estimate=cost(3 * 10**9),
-        name="far_maps",
-    )(far, *handed, mask_fine, mask_coarse, *maps)
+        scratch_shapes=[
+            pltpu.VMEM(own.shape, bf16),
+            pltpu.VMEM(mask_fine.shape, jnp.int32),
+            pltpu.VMEM(mask_coarse.shape, jnp.int32),
+            pltpu.VMEM((8, LANES), f32),
+            pltpu.VMEM((8, LANES), f32),
+            pltpu.VMEM((2 * half_rows, 2 * ext), bf16),
+            pltpu.VMEM(table.shape, bf16),
+            *section_scratch * 3,
+            *pair_scratch * 2,
+            pltpu.SemaphoreType.DMA((10,)),
+        ],
+        compiler_params=pltpu.CompilerParams(vmem_limit_bytes=36 * 1024 * 1024),
+        name="maps",
+    )(own, near, far, rim, rim_near, rim_far, mask_fine, mask_coarse, table)
 
 
 def local(sections, mask_fine, mask_coarse):
-    rim = from_device(sections, 0, 1)
-    near = jnp.concatenate([from_device(sections, 1, 0), from_device(sections, 1, 1)], axis=0)
-    return correlate(sections, rim, near, lambda value: from_device(value, 1, 0), mask_fine, mask_coarse)
+    far = from_device(sections, 2, 0)
+    near = from_device(sections, 1, 0)
+    rims = [from_device(sections, z, 1) for z in range(3)]
+    return correlate(sections, near, far, *rims, mask_fine, mask_coarse)
 
 
 def solution(mesh):

time: 24 us -> 26.4 us (1.100)
  waiting for transfers between devices: 8.45 us -> 11.1 us
  Pallas kernels: 8.62 us -> 7.22 us
  starting transfers between devices: 5.84 us -> 7.13 us
    ppermute x4 -> x5, waiting for transfers between devices: 8.45 us -> 11.1 us  [from_device(): return lax.ppermute(value, ('sec', 'strip'), pairs)]
    pallas_call x3 -> x1, Pallas kernels: 8.62 us -> 7.22 us  [correlate(): pl.pallas_call(functools.partial(maps_kernel, fine, coarse, places), out_...]
    ppermute x4 -> x5, starting transfers between devices: 5.84 us -> 7.13 us  [from_device(): return lax.ppermute(value, ('sec', 'strip'), pairs)]
  transfers between devices with their start and end apart: 4 -> 5, of which waited for: 4 -> 5; matrix products, arithmetic and copies ran while one was open for 0% -> 0% of each run, Pallas kernels for 11% -> 0%
where the time goes in v2:
time: 26.4 us; the launch traced here: 26.2 us
  waiting for transfers between devices  11.1 us (42%)
  Pallas kernels  7.22 us (27%)
  starting transfers between devices  7.13 us (27%)
  between operations  0.67 us (3%)
    ppermute x5, waiting for transfers between devices, from_device(): return lax.ppermute(value, ('sec', 'strip'), pairs)  11.1 us
    pallas_call x1, Pallas kernels, correlate(): pl.pallas_call(functools.partial(maps_kernel, fine, coarse, places), out_...  7.22 us
    ppermute x5, starting transfers between devices, from_device(): return lax.ppermute(value, ('sec', 'strip'), pairs)  7.13 us
  transfers between devices with their start and end apart: 5, of which 5 were waited for; matrix products, arithmetic and copies ran while one was open for 0% of the time, Pallas kernels for 0%

profile of v2, /device:TPU:1, one launch (start us, length us, event | category | flops | bytes accessed | tf_op | source)
XLA Modules:
  0.0 26.2 jit_solution(9820207341327109967)
XLA Ops:
  0.6 1.3 %collective-permute-start.3 = (bf16[1,64,512]{2,1,0:T(8,128)(2,1)}, bf16[1,64,512]{2,1,0:T(8,128)(2,1)S(1)}, u32[]{:S(2)}, u32[]{:S(2)}) collective-permute-start(bf16[1,64,512]{2,1,0:T(8,128)(2,1)} %own_hbm.1), channel_id=1, source_target_pairs={{5,0},{6,1},{7,2},{9,4},{10,5},{11,6},{13,8},{14,9},{15,10},{21,16... | collective-permute-start | bytes 196616 | tf_op jit(solution)/shard_map/ppermute | solution.py:28
  1.9 2.0 %collective-permute-start.2 = (bf16[1,64,512]{2,1,0:T(8,128)(2,1)}, bf16[1,64,512]{2,1,0:T(8,128)(2,1)S(1)}, u32[]{:S(2)}, u32[]{:S(2)}) collective-permute-start(bf16[1,64,512]{2,1,0:T(8,128)(2,1)} %own_hbm.1), channel_id=1, source_target_pairs={{1,0},{2,1},{3,2},{5,4},{6,5},{7,6},{9,8},{10,9},{11,10},{13,12},{... | collective-permute-start | bytes 196616 | tf_op jit(solution)/shard_map/ppermute | solution.py:28
  3.9 1.3 %collective-permute-start.1 = (bf16[1,64,512]{2,1,0:T(8,128)(2,1)}, bf16[1,64,512]{2,1,0:T(8,128)(2,1)S(1)}, u32[]{:S(2)}, u32[]{:S(2)}) collective-permute-start(bf16[1,64,512]{2,1,0:T(8,128)(2,1)} %own_hbm.1), channel_id=1, source_target_pairs={{8,0},{9,1},{10,2},{11,3},{12,4},{13,5},{14,6},{15,7},{24,16},{25,... | collective-permute-start | bytes 196616 | tf_op jit(solution)/shard_map/ppermute | solution.py:28
  5.2 1.3 %collective-permute-start = (bf16[1,64,512]{2,1,0:T(8,128)(2,1)}, bf16[1,64,512]{2,1,0:T(8,128)(2,1)S(1)}, u32[]{:S(2)}, u32[]{:S(2)}) collective-permute-start(bf16[1,64,512]{2,1,0:T(8,128)(2,1)} %own_hbm.1), channel_id=1, source_target_pairs={{4,0},{5,1},{6,2},{7,3},{8,4},{9,5},{10,6},{11,7},{12,8},{13,9},{1... | collective-permute-start | bytes 196616 | tf_op jit(solution)/shard_map/ppermute | solution.py:28
  6.5 1.3 %collective-permute-start.4 = (bf16[1,64,512]{2,1,0:T(8,128)(2,1)}, bf16[1,64,512]{2,1,0:T(8,128)(2,1)S(1)}, u32[]{:S(2)}, u32[]{:S(2)}) collective-permute-start(bf16[1,64,512]{2,1,0:T(8,128)(2,1)} %own_hbm.1), channel_id=1, source_target_pairs={{9,0},{10,1},{11,2},{13,4},{14,5},{15,6},{25,16},{26,17},{27,18},{... | collective-permute-start | bytes 196616 | tf_op jit(solution)/shard_map/ppermute | solution.py:28
  7.8 1.2 %collective-permute-done.3.rim_near = bf16[1,64,512]{2,1,0:T(8,128)(2,1)S(1)} collective-permute-done((bf16[1,64,512]{2,1,0:T(8,128)(2,1)}, bf16[1,64,512]{2,1,0:T(8,128)(2,1)S(1)}, u32[]{:S(2)}, u32[]{:S(2)}) %collective-permute-start.3) | collective-permute-done | bytes 65568 | tf_op jit(solution)/shard_map/ppermute | solution.py:28
  9.0 0.2 collective-permute-done.2.rim
  9.1 2.4 %collective-permute-done.1.far = bf16[1,64,512]{2,1,0:T(8,128)(2,1)S(1)} collective-permute-done((bf16[1,64,512]{2,1,0:T(8,128)(2,1)}, bf16[1,64,512]{2,1,0:T(8,128)(2,1)S(1)}, u32[]{:S(2)}, u32[]{:S(2)}) %collective-permute-start.1) | collective-permute-done | bytes 65568 | tf_op jit(solution)/shard_map/ppermute | solution.py:28
  11.6 1.1 %collective-permute-done.near = bf16[1,64,512]{2,1,0:T(8,128)(2,1)S(1)} collective-permute-done((bf16[1,64,512]{2,1,0:T(8,128)(2,1)}, bf16[1,64,512]{2,1,0:T(8,128)(2,1)S(1)}, u32[]{:S(2)}, u32[]{:S(2)}) %collective-permute-start) | collective-permute-done | bytes 65568 | tf_op jit(solution)/shard_map/ppermute | solution.py:28
  12.7 6.3 %collective-permute-done.4.rim_far = bf16[1,64,512]{2,1,0:T(8,128)(2,1)S(1)} collective-permute-done((bf16[1,64,512]{2,1,0:T(8,128)(2,1)}, bf16[1,64,512]{2,1,0:T(8,128)(2,1)S(1)}, u32[]{:S(2)}, u32[]{:S(2)}) %collective-permute-start.4) | collective-permute-done | bytes 65568 | tf_op jit(solution)/shard_map/ppermute | solution.py:28
  18.9 7.2 %maps.1 = (f32[1,2,2,16,1024]{4,3,2,1,0:T(8,128)}, f32[1,2,1,8,1024]{4,3,2,1,0:T(8,128)}) custom-call(bf16[1,64,512]{2,1,0:T(8,128)(2,1)} %own_hbm.1, bf16[1,64,512]{2,1,0:T(8,128)(2,1)S(1)} %collective-permute-done.near, bf16[1,64,512]{2,1,0:T(8,128)(2,1)S(1)} %collective-permute-done.1.far, bf16[1,64,512]{2,1,0:T(8,128)(2,1)S(1)} %collective-permute-done.2.rim, ...), custom_call_target="tpu_custom_call" | custom-call | tf_op jit(solution)/shard_map/maps/pallas_call | solution.py:470
Async XLA Ops:
  0.6 8.3 %collective-permute-start.3 = (bf16[1,64,512]{2,1,0:T(8,128)(2,1)}, bf16[1,64,512]{2,1,0:T(8,128)(2,1)S(1)}, u32[]{:S(2)}, u32[]{:S(2)}) collective-permute-start(bf16[1,64,512]{2,1,0:T(8,128)(2,1)} %own_hbm.1), channel_id=1, source_target_pairs={{5,0},{6,1},{7,2},{9,4},{10,5},{11,6},{13,8},{14,9},{15,10},{21,16... | collective-permute-start | bytes 196616 | tf_op jit(solution)/shard_map/ppermute | solution.py:28
  1.9 7.2 %collective-permute-start.2 = (bf16[1,64,512]{2,1,0:T(8,128)(2,1)}, bf16[1,64,512]{2,1,0:T(8,128)(2,1)S(1)}, u32[]{:S(2)}, u32[]{:S(2)}) collective-permute-start(bf16[1,64,512]{2,1,0:T(8,128)(2,1)} %own_hbm.1), channel_id=1, source_target_pairs={{1,0},{2,1},{3,2},{5,4},{6,5},{7,6},{9,8},{10,9},{11,10},{13,12},{... | collective-permute-start | bytes 196616 | tf_op jit(solution)/shard_map/ppermute | solution.py:28
  3.9 7.7 %collective-permute-start.1 = (bf16[1,64,512]{2,1,0:T(8,128)(2,1)}, bf16[1,64,512]{2,1,0:T(8,128)(2,1)S(1)}, u32[]{:S(2)}, u32[]{:S(2)}) collective-permute-start(bf16[1,64,512]{2,1,0:T(8,128)(2,1)} %own_hbm.1), channel_id=1, source_target_pairs={{8,0},{9,1},{10,2},{11,3},{12,4},{13,5},{14,6},{15,7},{24,16},{25,... | collective-permute-start | bytes 196616 | tf_op jit(solution)/shard_map/ppermute | solution.py:28
  5.2 7.5 %collective-permute-start = (bf16[1,64,512]{2,1,0:T(8,128)(2,1)}, bf16[1,64,512]{2,1,0:T(8,128)(2,1)S(1)}, u32[]{:S(2)}, u32[]{:S(2)}) collective-permute-start(bf16[1,64,512]{2,1,0:T(8,128)(2,1)} %own_hbm.1), channel_id=1, source_target_pairs={{4,0},{5,1},{6,2},{7,3},{8,4},{9,5},{10,6},{11,7},{12,8},{13,9},{1... | collective-permute-start | bytes 196616 | tf_op jit(solution)/shard_map/ppermute | solution.py:28
  6.5 12.4 %collective-permute-start.4 = (bf16[1,64,512]{2,1,0:T(8,128)(2,1)}, bf16[1,64,512]{2,1,0:T(8,128)(2,1)S(1)}, u32[]{:S(2)}, u32[]{:S(2)}) collective-permute-start(bf16[1,64,512]{2,1,0:T(8,128)(2,1)} %own_hbm.1), channel_id=1, source_target_pairs={{9,0},{10,1},{11,2},{13,4},{14,5},{15,6},{25,16},{26,17},{27,18},{... | collective-permute-start | bytes 196616 | tf_op jit(solution)/shard_map/ppermute | solution.py:28

commit v3 on v2

v3 whole, which is shorter than its diff:
```python
import functools

import jax
import jax.numpy as jnp
import numpy as np
from jax import lax
from jax.experimental import pallas as pl
from jax.experimental.pallas import tpu as pltpu
from jax.sharding import PartitionSpec as P

PATCH = 64
STRIDE = 32
WINDOW = 32
HALF = PATCH // 2
LANES = 128
NYQ = 16

f32 = jnp.float32
bf16 = jnp.bfloat16


def from_device(value, sec_steps, strip_steps):
    secs, strips = lax.axis_size("sec"), lax.axis_size("strip")
    pairs = []
    for sec in range(secs - sec_steps):
        for strip in range(strips - strip_steps):
            pairs.append(((sec + sec_steps) * strips + strip + strip_steps, sec * strips + strip))
    return lax.ppermute(value, ("sec", "strip"), pairs)


def wave(phase):
    turns = np.arange(PATCH) * (2 * np.pi / PATCH)
    cos = np.round(np.cos(turns), 14)
    sin = np.round(np.sin(turns), 14)
    phase = np.mod(phase, PATCH)
    return cos[phase], sin[phase]


def split_table(table):
    high = table.astype(jnp.bfloat16)
    low = (table - high.astype(np.float64)).astype(jnp.bfloat16)
    return high, low


def stacked(table):
    return np.concatenate(split_table(table), axis=0)


def fine_table():
    c, s = wave(np.arange(PATCH)[:, None] * np.arange(PATCH)[None, :])
    table = np.zeros((2, 2, PATCH, 2, 2, PATCH))
    for p in range(2):
        table[0, p, :, 0, p] = c
        table[1, p, :, 0, p] = -s
        table[0, p, :, 1, p] = -s
        table[1, p, :, 1, p] = -c
    return stacked(table.reshape(4 * PATCH, 4 * PATCH))


def coarse_table():
    c, s = wave((np.arange(2 * PATCH) // 2)[:, None] * np.arange(PATCH)[None, :])
    table = np.zeros((2, 2, 2 * PATCH, 2, 2, PATCH))
    for p in range(2):
        table[p, 0, :, 0, p] = 0.5 * c
        table[p, 1, :, 0, p] = -0.5 * s
        table[p, 0, :, 1, p] = -0.5 * s
        table[p, 1, :, 1, p] = -0.5 * c
    return stacked(table.reshape(8 * PATCH, 4 * PATCH))


def shift_tables():
    spread = 1.869545
    t = np.arange(WINDOW) - WINDOW // 2
    c, s = wave(np.arange(PATCH)[:, None] * t[None, :])
    table = np.zeros((2, 2, 2, PATCH, 2, 4, WINDOW))
    for odd in range(2):
        for p in range(2):
            table[odd, 0, p, :, 0, 2 * p + odd] = c
            table[odd, 1, p, :, 0, 2 * p + odd] = -s
            table[odd, 0, p, :, 1, 2 * p + odd] = s
            table[odd, 1, p, :, 1, 2 * p + odd] = c
    along_t = (spread * table.reshape(8 * PATCH, 8 * WINDOW)).astype(jnp.bfloat16)
    c, s = wave(t[:, None] * np.arange(HALF)[None, :])
    weight = np.where(np.arange(HALF) == 0, 1.0, 2.0)
    nyquist = np.repeat(wave(HALF * t)[0][:, None], NYQ, axis=1)
    along_s = np.concatenate([c * weight, -s * weight, nyquist], axis=1) / (spread * PATCH**3)
    high, low = split_table(along_s)
    along_s = np.concatenate(
        [np.concatenate([high, high], axis=1), np.concatenate([low, np.zeros_like(low)], axis=1)], axis=0)
    return along_t, along_s


class Level:
    def __init__(self, pool, blocks, width, table):
        self.pool, self.first, self.blocks, self.table = pool, blocks[0], len(blocks), table
        self.quads = width // (4 * pool * STRIDE)
        self.tiles = 2 * self.quads
        self.body = self.blocks * HALF
        self.half = -(-self.quads * self.blocks // 8) * 8
        self.rows = self.tiles * self.body + 2 * self.half
        self.cross_body = self.quads * self.body
        self.cross_rows = self.cross_body + -(-self.half // 16) * 16

    def window(self, tile, p):
        quad, odd = divmod(tile, 2)
        return self.pool * LANES * quad + LANES * p + self.pool * STRIDE * odd

    def nyquist_row(self, tile, b):
        quad, odd = divmod(tile, 2)
        return odd * self.half + quad * self.blocks + b


def row_places(levels):
    at, places = 0, []
    for level in levels:
        places.append([at, at + level.body])
        at += level.body + 2 * level.half
    for level, place in zip(levels, places):
        place.append(at)
        at += level.body
    return places, at


def row_table(levels, ext):
    places, size = row_places(levels)
    table = np.zeros((size, ext))
    k = np.arange(HALF)[:, None]
    for level, (cos_at, nyquist_at, sin_at) in zip(levels, places):
        pool = level.pool
        x = np.arange(pool * PATCH) // pool
        c, s = wave(k * x[None, :])
        for b in range(level.blocks):
            first = (level.first + b) * pool * STRIDE
            columns = slice(first, first + x.size)
            table[cos_at + b * HALF : cos_at + (b + 1) * HALF, columns] = c / pool
            table[sin_at + b * HALF : sin_at + (b + 1) * HALF, columns] = s / pool
            for tile in range(level.tiles):
                table[nyquist_at + level.nyquist_row(tile, b), columns] = wave(HALF * x)[0] / pool
    return np.concatenate(split_table(table), axis=1)


def split(value):
    high = value.astype(bf16)
    return high, (value - high.astype(f32)).astype(bf16)


def dot(left, right):
    return jnp.dot(left, right, preferred_element_type=f32)


def dot3(high, low, table_ref, at):
    depth = high.shape[1]
    table_high = table_ref[at : at + depth]
    table_low = table_ref[at + depth : at + 2 * depth]
    return dot(
        jnp.concatenate([high, low, high], axis=1),
        jnp.concatenate([table_high, table_high, table_low], axis=0))


def cosine(turns):
    turns = turns + PATCH // 4
    part = (turns & (HALF - 1)) - PATCH // 4
    angle = part.astype(f32) * (2 * np.pi / PATCH)
    square = angle * angle
    value = jnp.full(square.shape, 1.0 / 479001600, f32)
    for term in (-1.0 / 3628800, 1.0 / 40320, -1.0 / 720, 1.0 / 24, -0.5, 1.0):
        value = value * square + term
    return jnp.where((turns & HALF) == 0, value, -value)


def write_row_table(row_ref, level):
    (cos_at, nyquist_at, sin_at), = row_places([level])[0]
    ext = row_ref.shape[1] // 2

    def put(at, value):
        high, low = split(value)
        row_ref[at : at + value.shape[0], :ext] = high
        row_ref[at : at + value.shape[0], ext:] = low

    def inside(x):
        return jnp.where((x >= 0) & (x < PATCH), 1.0, 0.0)

    k = lax.broadcasted_iota(jnp.int32, (HALF, ext), 0)
    for b in range(level.blocks):
        x = lax.broadcasted_iota(jnp.int32, (HALF, ext), 1) - (level.first + b) * STRIDE
        put(cos_at + b * HALF, cosine(k * x) * inside(x))
        put(sin_at + b * HALF, cosine(k * x - PATCH // 4) * inside(x))
    row = lax.broadcasted_iota(jnp.int32, (2 * level.half, ext), 0)
    x = lax.broadcasted_iota(jnp.int32, (2 * level.half, ext), 1)
    x = x - (level.first + lax.rem(lax.rem(row, level.half), level.blocks)) * STRIDE
    put(nyquist_at, cosine(x * HALF) * inside(x))


def all_rows(value):
    for step in (4, 2, 1):
        value = value + pltpu.roll(value, step, 0)
    return value


def gather_windows(level, place, t_ref, halves, left):
    cos_at, nyquist_at, sin_at = place
    body, end = level.body, level.tiles * level.body
    for p in range(level.pool):
        for source, target in zip(halves, left):
            for tile in range(level.tiles):
                at = level.window(tile, p)
                for half, start in enumerate((cos_at, sin_at)):
                    target[tile * body : (tile + 1) * body, (2 * p + half) * LANES : (2 * p + half + 1) * LANES] = (
                        source[start : start + body, at : at + LANES])
        row = lax.broadcasted_iota(jnp.int32, (2 * level.half, LANES), 0)
        nyquist = jnp.zeros((2 * level.half, LANES), f32)
        for tile in range(level.tiles):
            at, first = level.window(tile, p), level.nyquist_row(tile, 0)
            value = t_ref[nyquist_at : nyquist_at + 2 * level.half, at : at + LANES]
            nyquist = jnp.where((row >= first) & (row < first + level.blocks), value, nyquist)
        for target, part in zip(left, split(nyquist)):
            target[end:, 2 * p * LANES : (2 * p + 1) * LANES] = part
            target[end:, (2 * p + 1) * LANES : (2 * p + 2) * LANES] = jnp.zeros(part.shape, bf16)


def spectrum_power(level, f_ref):
    sub = lax.broadcasted_iota(jnp.int32, (8, LANES), 0)
    lane = lax.broadcasted_iota(jnp.int32, (8, LANES), 1)
    dc = (sub == 0) & (lane % PATCH == 0)
    group = lax.broadcasted_iota(jnp.int32, (LANES, LANES), 0) // PATCH
    same = group == lax.broadcasted_iota(jnp.int32, (LANES, LANES), 1) // PATCH
    ones = jnp.where(same, 1.0, 0.0).astype(bf16)

    def square(at):
        re, im = f_ref[at : at + 8, :LANES], f_ref[at : at + 8, LANES:]
        return re * re + im * im

    tails = [square(level.tiles * level.body + at) for at in range(0, 2 * level.half, 8)]
    sums = []
    for tile in range(level.tiles):
        for b in range(level.blocks):
            base = tile * level.body + b * HALF
            total = jnp.where(dc, 0.0, square(base))
            head = jnp.where(sub == 0, total, 0.0)
            for r in range(8, HALF, 8):
                total = total + square(base + r)
            row = level.nyquist_row(tile, b)
            sums.append(2.0 * total - head + jnp.where(sub == row % 8, tails[row // 8], 0.0))
    if len(sums) % 2:
        sums.append(jnp.zeros_like(sums[0]))
    high, low = split(jnp.concatenate(sums, axis=0))
    return dot(jnp.concatenate([high, low], axis=1), jnp.concatenate([ones, ones], axis=0))


def scale_spectrum(level, f_ref, sums, spec_ref):
    sub = lax.broadcasted_iota(jnp.int32, (8, 2 * LANES), 0)
    lane = lax.broadcasted_iota(jnp.int32, (8, 2 * LANES), 1)
    dc = (sub == 0) & (lane % PATCH == 0)
    end = level.tiles * level.body
    tails = [f_ref[end + at : end + at + 8] for at in range(0, 2 * level.half, 8)]
    scaled = [jnp.zeros_like(tail) for tail in tails]
    for tile in range(level.tiles):
        for b in range(level.blocks):
            number = (tile * level.blocks + b) * 8
            scale = lax.rsqrt(all_rows(sums[number : number + 8]) * (1.0 / PATCH**4) + 1e-05)
            scale = jnp.concatenate([scale, scale], axis=1)
            for r in range(0, HALF, 16):
                at = tile * level.body + b * HALF + r
                head = f_ref[at : at + 8]
                if r == 0:
                    head = jnp.where(dc, 0.0, head)
                both = jnp.concatenate([head * scale, f_ref[at + 8 : at + 16] * scale], axis=0)
                spec_ref[at : at + 16] = both.astype(bf16)
            row = level.nyquist_row(tile, b)
            scaled[row // 8] = jnp.where(sub == row % 8, tails[row // 8] * scale, scaled[row // 8])
    spec_ref[end:] = jnp.concatenate(scaled, axis=0).astype(bf16)


def transform(levels, strips, row_ref, table_ref, ready, scratch, specs):
    count = len(levels)
    t_ref, *halves = scratch[:3]
    lefts = [scratch[3 + 2 * i : 5 + 2 * i] for i in range(count)]
    f_refs = scratch[3 + 2 * count : 3 + 3 * count]
    places, size = row_places(levels)
    ready[0]()
    x = jnp.concatenate([strip[0] for strip in strips], axis=0)
    width = x.shape[1]
    t_ref[:, :width] = dot(row_ref[...], jnp.concatenate([x, x], axis=0))
    t_ref[:, width:] = jnp.zeros((size, LANES), f32)
    yield
    for level, place in zip(levels, places):
        for start in (place[0], place[2]):
            for r in range(start, start + level.body, 16):
                for ref, half in zip(halves, split(t_ref[r : r + 16])):
                    ref[r : r + 16] = half
    for level, place, left in zip(levels, places, lefts):
        gather_windows(level, place, t_ref, halves, left)
        yield
    for level, left, f_ref, wait in zip(levels, lefts, f_refs, ready[1:]):
        wait()
        f_ref[...] = dot3(left[0][...], left[1][...], table_ref, level.table)
        yield
    sums = []
    for level, f_ref in zip(levels, f_refs):
        sums.append(spectrum_power(level, f_ref))
        yield
    for level, f_ref, total, spec_ref in zip(levels, f_refs, sums, specs):
        scale_spectrum(level, f_ref, total, spec_ref)
        yield


def run_staggered(tasks):
    active, waiting = [], list(tasks)
    while waiting or active:
        if waiting:
            active.append(waiting.pop(0))
        for task in list(active):
            if next(task, True):
                active.remove(task)


def write_maps(levels, specs, masks, table_ref, shift_at, map_at, scratch, outs):
    cross_ref, y_ref, maps_ref, rows_ref, *stacks = scratch
    pairs = len(specs) - 1
    base = 0
    for index, level in enumerate(levels):
        for d in range(pairs):
            own, other = specs[0][index], specs[d + 1][index]

            def cross(at, rows):
                a, b = own[at : at + rows].astype(f32), other[at : at + rows].astype(f32)
                ar, ai, br, bi = a[:, :LANES], a[:, LANES:], b[:, :LANES], b[:, LANES:]
                return jnp.concatenate([ar * br + ai * bi, ar * bi - ai * br], axis=1)

            for tile in range(level.tiles):
                quad, odd = divmod(tile, 2)
                for r in range(0, level.body, 16):
                    to = base + quad * level.body + r
                    cross_ref[to : to + 16, 2 * odd * LANES : 2 * (odd + 1) * LANES] = (
                        cross(tile * level.body + r, 16).astype(bf16))
            nyquist = cross(level.tiles * level.body, 2 * level.half)
            nyquist = jnp.concatenate([nyquist[: level.half], nyquist[level.half :]], axis=1)
            to = base + level.cross_body
            spare = level.cross_rows - level.cross_body - level.half
            if spare:
                nyquist = jnp.concatenate([nyquist, jnp.zeros((spare, 4 * LANES), f32)], axis=0)
            cross_ref[to : base + level.cross_rows] = nyquist.astype(bf16)
            base += level.cross_rows
    y_ref[...] = dot(cross_ref[...], table_ref[shift_at : shift_at + 4 * LANES])
    base = tile = 0
    starts = {}
    row = lax.broadcasted_iota(jnp.int32, (NYQ, LANES), 0)
    for index, level in enumerate(levels):
        for b in range(level.blocks):
            stack_ref = stacks[index]
            for d in range(pairs):
                first = base + d * level.cross_rows
                nyq_at = first + level.cross_body
                nyquist = y_ref[nyq_at : nyq_at + NYQ, :LANES]
                for quad in range(level.quads):
                    top = first + quad * level.body + b * HALF
                    column = (d * level.quads + quad) * LANES
                    for at, value in (
                        (0, y_ref[top : top + HALF, :LANES]),
                        (HALF, y_ref[top : top + HALF, LANES:]),
                        (2 * HALF, jnp.where(row == quad * level.blocks + b, nyquist, 0.0)),
                    ):
                        for half, part in enumerate(split(value)):
                            to = half * (2 * HALF + NYQ) + at
                            stack_ref[to : to + value.shape[0], column : column + LANES] = part
            both = dot(table_ref[map_at : map_at + 2 * WINDOW, : stack_ref.shape[0]], stack_ref[...])
            maps = both[:WINDOW] + both[WINDOW:]
            for d in range(pairs):
                starts[index, d, b] = tile
                for quad in range(level.quads):
                    column = (d * level.quads + quad) * LANES
                    maps_ref[tile] = maps[:, column : column + LANES]
                    tile += 1
        base += pairs * level.cross_rows
    kept = [jnp.transpose(mask()) for mask in masks]
    lanes = lax.broadcasted_iota(jnp.int32, (tile, LANES), 1) // WINDOW
    for big in range(WINDOW // 4):
        rows = [maps_ref[:, 4 * big + r, :] for r in range(4)]
        for g in range(4):
            value = None
            for r in range(4):
                moved = rows[r] if r == g else pltpu.roll(rows[r], (WINDOW * (r - g)) % LANES, 1)
                value = moved if value is None else jnp.where(lanes == r, moved, value)
            rows_ref[big, pl.ds(g, tile, stride=4), :] = value
        for index, (level, out) in enumerate(zip(levels, outs)):
            for b in range(level.blocks):
                column = kept[index][: 4 * level.quads, level.first + b : level.first + b + 1]
                for d in range(pairs):
                    at = 4 * starts[index, d, b]
                    out[d, b, :, big * LANES : (big + 1) * LANES] = rows_ref[big, at : at + 4 * level.quads] * column


def mask_tile(mask_ref, pad_ref):
    pad_ref[...] = jnp.zeros(pad_ref.shape, f32)
    pad_ref[: mask_ref.shape[1], : mask_ref.shape[2]] = mask_ref[0].astype(f32)
    return pad_ref[...]


def section_scratch(levels, width):
    size = row_places(levels)[1]
    return [
        pltpu.VMEM((size, width + LANES), f32),
        pltpu.VMEM((size, width + LANES), bf16),
        pltpu.VMEM((size, width + LANES), bf16),
        *(pltpu.VMEM((level.rows, 2 * level.pool * LANES), bf16) for level in levels for _ in range(2)),
        *(pltpu.VMEM((level.rows, 2 * LANES), f32) for level in levels),
        *(pltpu.VMEM((level.rows, 2 * LANES), bf16) for level in levels),
    ]


def pair_scratch(levels):
    rows = sum(2 * level.cross_rows for level in levels)
    tiles = sum(2 * level.blocks * level.quads for level in levels)
    return [
        pltpu.VMEM((rows, 4 * LANES), bf16),
        pltpu.VMEM((rows, 2 * LANES), f32),
        pltpu.VMEM((tiles, WINDOW, LANES), f32),
        pltpu.VMEM((WINDOW // 4, 4 * tiles, LANES), f32),
        *(pltpu.VMEM((4 * HALF + 2 * NYQ, 2 * level.quads * LANES), bf16) for level in levels),
    ]


def all_maps(levels, strips, first_ready, row_ref, table_ref, tables_ready, shift_ready, places, masks, scratch, outs):
    size = 3 + 4 * len(levels)
    sections = [scratch[z * size : (z + 1) * size] for z in range(3)]
    specs = [section[size - len(levels) :] for section in sections]
    run_staggered([
        transform(
            levels, strips[z], row_ref, table_ref, (first_ready if z == 0 else lambda: None,) + tables_ready,
            sections[z], specs[z])
        for z in (1, 2, 0)])
    shift_ready()
    write_maps(levels, specs, masks, table_ref, *places, scratch[3 * size :], outs)


def copier(sems):
    used = []

    def start(source, target):
        copy = pltpu.make_async_copy(source, target, sems.at[len(used)])
        used.append(copy)
        copy.start()
        return copy.wait

    return start


def inner_kernel(
    levels, cuts,
    own_hbm, near, far, mask_hbm, table_hbm,
    maps, table_ref,
    own, mask, pad, row_ref, *rest,
):
    *scratch, sems = rest
    start = copier(sems)

    def table(first, last):
        piece = pl.ds(first, last - first)
        return start(table_hbm.at[piece], table_ref.at[piece])

    fine_at, shift_at, map_at, coarse_at, end = cuts
    fine_ready = table(fine_at, shift_at)
    own_ready = start(own_hbm, own)
    shift_ready = table(shift_at, coarse_at)
    mask_ready = start(mask_hbm, mask)
    coarse_ready = table(coarse_at, end)
    write_row_table(row_ref, levels[0])
    waited = []

    def fine_once():
        if not waited:
            fine_ready()
            waited.append(True)

    def mask_rows():
        mask_ready()
        return mask_tile(mask, pad)

    all_maps(
        levels, ((own,), (near,), (far,)), own_ready, row_ref, table_ref, (fine_once,), shift_ready,
        (shift_at, map_at), (mask_rows,), scratch, (maps,))
    coarse_ready()


def outer_kernel(
    levels, cuts, inner, row_at,
    own_hbm, near, far, rim, rim_near, rim_far, mask_hbm, mask_coarse_hbm, table_ref, inner_maps,
    out_fine, out_coarse,
    own, mask, mask_coarse, pad, pad_coarse, maps, maps_coarse, *rest,
):
    *scratch, sems = rest
    start = copier(sems)
    own_ready = start(own_hbm, own)
    mask_ready = start(mask_hbm, mask)
    mask_coarse_ready = start(mask_coarse_hbm, mask_coarse)
    stores = [start(inner_maps.at[d], out_fine.at[0, d, pl.ds(0, inner)]) for d in range(2)]

    def mask_rows():
        mask_ready()
        return mask_tile(mask, pad)

    def mask_coarse_rows():
        mask_coarse_ready()
        return mask_tile(mask_coarse, pad_coarse)

    fine_at, shift_at, map_at, coarse_at, end = cuts
    row_ref = table_ref.at[pl.ds(row_at, row_places(levels)[1])]
    all_maps(
        levels, ((own, rim), (near, rim_near), (far, rim_far)), own_ready, row_ref, table_ref,
        (lambda: None,) * 2, lambda: None, (shift_at, map_at), (mask_rows, mask_coarse_rows), scratch,
        (maps, maps_coarse))
    for d in range(2):
        stores.append(start(maps.at[d], out_fine.at[0, d, pl.ds(inner, levels[0].blocks)]))
        stores.append(start(maps_coarse.at[d], out_coarse.at[0, d]))
    for wait in stores:
        wait()


def correlate(own, near, far, rim, rim_near, rim_far, mask_fine, mask_coarse):
    strip_rows, width = own.shape[1:]
    fine, coarse = mask_fine.shape[1], mask_coarse.shape[1]
    inner = fine - 1
    shift, map_ = shift_tables()
    tables = [fine_table(), shift, map_, coarse_table()]
    cuts = [int(at) for at in np.cumsum([0] + [table.shape[0] for table in tables])]
    inner_levels = [Level(1, range(inner), width, cuts[0])]
    outer_levels = [Level(1, range(inner, fine), width, cuts[0]), Level(2, range(coarse), width, cuts[3])]
    row_at = cuts[4]
    tables.append(row_table(outer_levels, strip_rows + PATCH))
    columns = max(table.shape[1] for table in tables)
    table = np.concatenate([np.pad(table, ((0, 0), (0, columns - table.shape[1]))) for table in tables])
    cuts[4] = table.shape[0]

    shifts = WINDOW * WINDOW
    hbm = pl.BlockSpec(memory_space=pltpu.HBM)
    vmem = pl.BlockSpec(memory_space=pltpu.VMEM)
    params = pltpu.CompilerParams(vmem_limit_bytes=28 * 1024 * 1024)
    own, table, mask_fine, mask_coarse = (
        pltpu.with_memory_space_constraint(value, pltpu.HBM)
        for value in (own, jnp.asarray(table), mask_fine, mask_coarse))

    def cost(flops):
        return pl.CostEstimate(flops=flops, bytes_accessed=4 * 10**6, transcendentals=0)

    maps, handed = pl.pallas_call(
        functools.partial(inner_kernel, inner_levels, cuts),
        out_shape=(
            jax.ShapeDtypeStruct((2, inner, 4 * inner_levels[0].quads, shifts), f32),
            jax.ShapeDtypeStruct(table.shape, bf16),
        ),
        in_specs=[hbm, vmem, vmem, hbm, hbm],
        out_specs=(vmem, vmem),
        scratch_shapes=[
            pltpu.VMEM(own.shape, bf16),
            pltpu.VMEM(mask_fine.shape, jnp.int32),
            pltpu.VMEM((8, LANES), f32),
            pltpu.VMEM((row_places(inner_levels)[1], 2 * strip_rows), bf16),
            *section_scratch(inner_levels, width) * 3,
            *pair_scratch(inner_levels),
            pltpu.SemaphoreType.DMA((5,)),
        ],
        compiler_params=params,
        cost_estimate=cost(3 * 10**9),
        name="inner_blocks",
    )(own, near, far, mask_fine, table)
    return pl.pallas_call(
        functools.partial(outer_kernel, outer_levels, cuts, inner, row_at),
        out_shape=(
            jax.ShapeDtypeStruct((1, 2, fine, 4 * outer_levels[0].quads, shifts), f32),
            jax.ShapeDtypeStruct((1, 2, coarse, 4 * outer_levels[1].quads, shifts), f32),
        ),
        in_specs=[hbm] + [vmem] * 5 + [hbm] * 2 + [vmem] * 2,
        out_specs=(hbm, hbm),
        scratch_shapes=[
            pltpu.VMEM(own.shape, bf16),
            pltpu.VMEM(mask_fine.shape, jnp.int32),
            pltpu.VMEM(mask_coarse.shape, jnp.int32),
            pltpu.VMEM((8, LANES), f32),
            pltpu.VMEM((8, LANES), f32),
            *(pltpu.VMEM((2, level.blocks, 4 * level.quads, shifts), f32) for level in outer_levels),
            *section_scratch(outer_levels, width) * 3,
            *pair_scratch(outer_levels),
            pltpu.SemaphoreType.DMA((9,)),
        ],
        compiler_params=params,
        cost_estimate=cost(4 * 10**9),
        name="outer_blocks",
    )(own, near, far, rim, rim_near, rim_far, mask_fine, mask_coarse, handed, maps)


def local(sections, mask_fine, mask_coarse):
    far = from_device(sections, 2, 0)
    near = from_device(sections, 1, 0)
    rims = [from_device(sections, z, 1) for z in range(3)]
    return correlate(sections, near, far, *rims, mask_fine, mask_coarse)


def solution(mesh):
    in_specs = (
        P("sec", "strip", "groups"),
        P("sec", "strip", "groups"),
        P("sec", "strip", "groups"),
    )
    out_specs = (P("sec", None, "strip", "groups", None), P("sec", None, "strip", "groups", None))
    return jax.shard_map(local, mesh=mesh, in_specs=in_specs, out_specs=out_specs, check_vma=False)
```

time: 26.4 us -> 20 us (0.76)
  waiting for transfers between devices: 11.1 us -> 4.36 us
  Pallas kernels: 7.22 us -> 7.56 us
    ppermute x5, waiting for transfers between devices: 11.1 us -> 4.36 us  [from_device(): return lax.ppermute(value, ('sec', 'strip'), pairs)]
    pallas_call x1 -> x2, Pallas kernels: 7.22 us -> 7.56 us  [the longest x1 4.11 us: correlate(): pl.pallas_call(functools.partial(outer_kernel, outer_levels, cuts, inner,...]
  transfers between devices with their start and end apart: 5 -> 5, of which waited for: 5 -> 2; matrix products, arithmetic and copies ran while one was open for 0% -> 0% of each run, Pallas kernels for 0% -> 18%
where the time goes in v3:
time: 20 us; the launch traced here: 19.7 us
  Pallas kernels  7.56 us (38%)
  starting transfers between devices  7.14 us (36%)
  waiting for transfers between devices  4.36 us (22%)
  between operations  0.69 us (3%)
    ppermute x5, starting transfers between devices, from_device(): return lax.ppermute(value, ('sec', 'strip'), pairs)  7.14 us
    ppermute x5, waiting for transfers between devices, from_device(): return lax.ppermute(value, ('sec', 'strip'), pairs)  4.36 us
    pallas_call x1, Pallas kernels, correlate(): pl.pallas_call(functools.partial(outer_kernel, outer_levels, cuts, inner,...  4.11 us
    pallas_call x1, Pallas kernels, correlate(): pl.pallas_call(functools.partial(inner_kernel, inner_levels, cuts), out_s...  3.45 us
  transfers between devices with their start and end apart: 5, of which 2 were waited for; matrix products, arithmetic and copies ran while one was open for 0% of the time, Pallas kernels for 18%

profile of v3, /device:TPU:1, one launch (start us, length us, event | category | flops | bytes accessed | tf_op | source)
XLA Modules:
  0.0 19.7 jit_solution(9711648739232394249)
XLA Ops:
  0.6 1.3 %collective-permute-start.1 = (bf16[1,64,512]{2,1,0:T(8,128)(2,1)}, bf16[1,64,512]{2,1,0:T(8,128)(2,1)S(1)}, u32[]{:S(2)}, u32[]{:S(2)}) collective-permute-start(bf16[1,64,512]{2,1,0:T(8,128)(2,1)} %own_hbm.3), channel_id=1, source_target_pairs={{8,0},{9,1},{10,2},{11,3},{12,4},{13,5},{14,6},{15,7},{24,16},{25,... | collective-permute-start | bytes 196616 | tf_op jit(solution)/shard_map/ppermute | solution.py:28
  1.9 1.3 %collective-permute-start = (bf16[1,64,512]{2,1,0:T(8,128)(2,1)}, bf16[1,64,512]{2,1,0:T(8,128)(2,1)S(1)}, u32[]{:S(2)}, u32[]{:S(2)}) collective-permute-start(bf16[1,64,512]{2,1,0:T(8,128)(2,1)} %own_hbm.3), channel_id=1, source_target_pairs={{4,0},{5,1},{6,2},{7,3},{8,4},{9,5},{10,6},{11,7},{12,8},{13,9},{1... | collective-permute-start | bytes 196616 | tf_op jit(solution)/shard_map/ppermute | solution.py:28
  3.2 1.3 %collective-permute-start.4 = (bf16[1,64,512]{2,1,0:T(8,128)(2,1)}, bf16[1,64,512]{2,1,0:T(8,128)(2,1)S(1)}, u32[]{:S(2)}, u32[]{:S(2)}) collective-permute-start(bf16[1,64,512]{2,1,0:T(8,128)(2,1)} %own_hbm.3), channel_id=1, source_target_pairs={{9,0},{10,1},{11,2},{13,4},{14,5},{15,6},{25,16},{26,17},{27,18},{... | collective-permute-start | bytes 196616 | tf_op jit(solution)/shard_map/ppermute | solution.py:28
  4.5 1.3 %collective-permute-start.3 = (bf16[1,64,512]{2,1,0:T(8,128)(2,1)}, bf16[1,64,512]{2,1,0:T(8,128)(2,1)S(1)}, u32[]{:S(2)}, u32[]{:S(2)}) collective-permute-start(bf16[1,64,512]{2,1,0:T(8,128)(2,1)} %own_hbm.3), channel_id=1, source_target_pairs={{5,0},{6,1},{7,2},{9,4},{10,5},{11,6},{13,8},{14,9},{15,10},{21,16... | collective-permute-start | bytes 196616 | tf_op jit(solution)/shard_map/ppermute | solution.py:28
  5.8 2.0 %collective-permute-start.2 = (bf16[1,64,512]{2,1,0:T(8,128)(2,1)}, bf16[1,64,512]{2,1,0:T(8,128)(2,1)S(1)}, u32[]{:S(2)}, u32[]{:S(2)}) collective-permute-start(bf16[1,64,512]{2,1,0:T(8,128)(2,1)} %own_hbm.3), channel_id=1, source_target_pairs={{1,0},{2,1},{3,2},{5,4},{6,5},{7,6},{9,8},{10,9},{11,10},{13,12},{... | collective-permute-start | bytes 196616 | tf_op jit(solution)/shard_map/ppermute | solution.py:28
  7.8 0.0 collective-permute-done.1.far
  7.8 1.4 %collective-permute-done.near = bf16[1,64,512]{2,1,0:T(8,128)(2,1)S(1)} collective-permute-done((bf16[1,64,512]{2,1,0:T(8,128)(2,1)}, bf16[1,64,512]{2,1,0:T(8,128)(2,1)S(1)}, u32[]{:S(2)}, u32[]{:S(2)}) %collective-permute-start) | collective-permute-done | bytes 65568 | tf_op jit(solution)/shard_map/ppermute | solution.py:28
  9.3 3.4 %inner_blocks.1 = (f32[2,1,16,1024]{3,2,1,0:T(8,128)S(1)}, bf16[2272,256]{1,0:T(8,128)(2,1)S(1)}) custom-call(bf16[1,64,512]{2,1,0:T(8,128)(2,1)} %own_hbm.3, bf16[1,64,512]{2,1,0:T(8,128)(2,1)S(1)} %collective-permute-done.near, bf16[1,64,512]{2,1,0:T(8,128)(2,1)S(1)} %collective-permute-done.1.far, s32[1,2,16]{2,1,0:T(2,128)} %mask_hbm.3, ...), custom_call_target="tpu_custom_call" | custom-call | flops 3000000000 | bytes 4000000 | tf_op jit(solution)/shard_map/inner_blocks/pallas_call | solution.py:545
  12.7 2.9 %collective-permute-done.4.rim_far = bf16[1,64,512]{2,1,0:T(8,128)(2,1)S(1)} collective-permute-done((bf16[1,64,512]{2,1,0:T(8,128)(2,1)}, bf16[1,64,512]{2,1,0:T(8,128)(2,1)S(1)}, u32[]{:S(2)}, u32[]{:S(2)}) %collective-permute-start.4) | collective-permute-done | bytes 65568 | tf_op jit(solution)/shard_map/ppermute | solution.py:28
  15.6 0.0 collective-permute-done.3.rim_near
  15.6 0.0 collective-permute-done.2.rim
  15.6 4.1 %outer_blocks.1 = (f32[1,2,2,16,1024]{4,3,2,1,0:T(8,128)}, f32[1,2,1,8,1024]{4,3,2,1,0:T(8,128)}) custom-call(bf16[1,64,512]{2,1,0:T(8,128)(2,1)} %own_hbm.3, bf16[1,64,512]{2,1,0:T(8,128)(2,1)S(1)} %collective-permute-done.near, bf16[1,64,512]{2,1,0:T(8,128)(2,1)S(1)} %collective-permute-done.1.far, bf16[1,64,512]{2,1,0:T(8,128)(2,1)S(1)} %collective-permute-done.2.rim, ...), custom_call_target="tpu_custom_call" | custom-call | flops 4000000000 | bytes 4000000 | tf_op jit(solution)/shard_map/outer_blocks/pallas_call | solution.py:566
Async XLA Ops:
  0.6 7.2 %collective-permute-start.1 = (bf16[1,64,512]{2,1,0:T(8,128)(2,1)}, bf16[1,64,512]{2,1,0:T(8,128)(2,1)S(1)}, u32[]{:S(2)}, u32[]{:S(2)}) collective-permute-start(bf16[1,64,512]{2,1,0:T(8,128)(2,1)} %own_hbm.3), channel_id=1, source_target_pairs={{8,0},{9,1},{10,2},{11,3},{12,4},{13,5},{14,6},{15,7},{24,16},{25,... | collective-permute-start | bytes 196616 | tf_op jit(solution)/shard_map/ppermute | solution.py:28
  1.9 7.3 %collective-permute-start = (bf16[1,64,512]{2,1,0:T(8,128)(2,1)}, bf16[1,64,512]{2,1,0:T(8,128)(2,1)S(1)}, u32[]{:S(2)}, u32[]{:S(2)}) collective-permute-start(bf16[1,64,512]{2,1,0:T(8,128)(2,1)} %own_hbm.3), channel_id=1, source_target_pairs={{4,0},{5,1},{6,2},{7,3},{8,4},{9,5},{10,6},{11,7},{12,8},{13,9},{1... | collective-permute-start | bytes 196616 | tf_op jit(solution)/shard_map/ppermute | solution.py:28
  3.2 12.4 %collective-permute-start.4 = (bf16[1,64,512]{2,1,0:T(8,128)(2,1)}, bf16[1,64,512]{2,1,0:T(8,128)(2,1)S(1)}, u32[]{:S(2)}, u32[]{:S(2)}) collective-permute-start(bf16[1,64,512]{2,1,0:T(8,128)(2,1)} %own_hbm.3), channel_id=1, source_target_pairs={{9,0},{10,1},{11,2},{13,4},{14,5},{15,6},{25,16},{26,17},{27,18},{... | collective-permute-start | bytes 196616 | tf_op jit(solution)/shard_map/ppermute | solution.py:28
  4.5 11.1 %collective-permute-start.3 = (bf16[1,64,512]{2,1,0:T(8,128)(2,1)}, bf16[1,64,512]{2,1,0:T(8,128)(2,1)S(1)}, u32[]{:S(2)}, u32[]{:S(2)}) collective-permute-start(bf16[1,64,512]{2,1,0:T(8,128)(2,1)} %own_hbm.3), channel_id=1, source_target_pairs={{5,0},{6,1},{7,2},{9,4},{10,5},{11,6},{13,8},{14,9},{15,10},{21,16... | collective-permute-start | bytes 196616 | tf_op jit(solution)/shard_map/ppermute | solution.py:28
  5.8 9.8 %collective-permute-start.2 = (bf16[1,64,512]{2,1,0:T(8,128)(2,1)}, bf16[1,64,512]{2,1,0:T(8,128)(2,1)S(1)}, u32[]{:S(2)}, u32[]{:S(2)}) collective-permute-start(bf16[1,64,512]{2,1,0:T(8,128)(2,1)} %own_hbm.3), channel_id=1, source_target_pairs={{1,0},{2,1},{3,2},{5,4},{6,5},{7,6},{9,8},{10,9},{11,10},{13,12},{... | collective-permute-start | bytes 196616 | tf_op jit(solution)/shard_map/ppermute | solution.py:28

commit v4 on v3

--- a/solution.py
+++ b/solution.py
@@ -191,34 +191,67 @@
     put(nyquist_at, cosine(x * HALF) * inside(x))
 
 
+def write_fine_table(table_ref, at):
+    y = lax.broadcasted_iota(jnp.int32, (PATCH, LANES), 0)
+    lane = lax.broadcasted_iota(jnp.int32, (PATCH, LANES), 1)
+    frequency = lane & (PATCH - 1)
+    c, s = cosine(y * frequency), cosine(y * frequency - PATCH // 4)
+    depth = 4 * PATCH
+    for p in range(2):
+        mine = (lane >= PATCH) if p else (lane < PATCH)
+        cos, minus_cos, minus_sin = (jnp.where(mine, value, 0.0) for value in (c, -c, -s))
+        for number, pair in enumerate(((cos, minus_sin), (minus_sin, minus_cos))):
+            to = at + (2 * number + p) * PATCH
+            for half, value in enumerate(pair):
+                for level, part in enumerate(split(value)):
+                    table_ref[to + level * depth : to + level * depth + PATCH, half * LANES : (half + 1) * LANES] = part
+
+
 def all_rows(value):
     for step in (4, 2, 1):
         value = value + pltpu.roll(value, step, 0)
     return value
 
 
-def gather_windows(level, place, t_ref, halves, left):
+def left_of(level, place, half_ref, odd_ref):
     cos_at, nyquist_at, sin_at = place
-    body, end = level.body, level.tiles * level.body
+    pieces = []
+    for tile in range(level.tiles):
+        if tile % 2:
+            pieces.append(odd_ref[tile // 2 * level.body : (tile // 2 + 1) * level.body])
+        else:
+            columns = []
+            for p in range(level.pool):
+                at = level.window(tile, p)
+                columns += [half_ref[start : start + level.body, at : at + LANES] for start in (cos_at, sin_at)]
+            pieces.append(jnp.concatenate(columns, axis=1))
+    pieces.append(odd_ref[level.quads * level.body :])
+    return jnp.concatenate(pieces, axis=0)
+
+
+def gather_windows(level, place, t_ref, halves, odds):
+    cos_at, nyquist_at, sin_at = place
+    body, end = level.body, level.quads * level.body
+    row = lax.broadcasted_iota(jnp.int32, (2 * level.half, LANES), 0)
     for p in range(level.pool):
-        for source, target in zip(halves, left):
-            for tile in range(level.tiles):
+        for source, target in zip(halves, odds):
+            for tile in range(1, level.tiles, 2):
                 at = level.window(tile, p)
                 for half, start in enumerate((cos_at, sin_at)):
-                    target[tile * body : (tile + 1) * body, (2 * p + half) * LANES : (2 * p + half + 1) * LANES] = (
+                    to = tile // 2 * body
+                    target[to : to + body, (2 * p + half) * LANES : (2 * p + half + 1) * LANES] = (
                         source[start : start + body, at : at + LANES])
-        row = lax.broadcasted_iota(jnp.int32, (2 * level.half, LANES), 0)
         nyquist = jnp.zeros((2 * level.half, LANES), f32)
         for tile in range(level.tiles):
             at, first = level.window(tile, p), level.nyquist_row(tile, 0)
             value = t_ref[nyquist_at : nyquist_at + 2 * level.half, at : at + LANES]
             nyquist = jnp.where((row >= first) & (row < first + level.blocks), value, nyquist)
-        for target, part in zip(left, split(nyquist)):
+        for target, part in zip(odds, split(nyquist)):
             target[end:, 2 * p * LANES : (2 * p + 1) * LANES] = part
             target[end:, (2 * p + 1) * LANES : (2 * p + 2) * LANES] = jnp.zeros(part.shape, bf16)
 
 
-def spectrum_power(level, f_ref):
+def spectrum_power(level, f_ref, sections):
     sub = lax.broadcasted_iota(jnp.int32, (8, LANES), 0)
     lane = lax.broadcasted_iota(jnp.int32, (8, LANES), 1)
     dc = (sub == 0) & (lane % PATCH == 0)
@@ -230,117 +263,112 @@
         re, im = f_ref[at : at + 8, :LANES], f_ref[at : at + 8, LANES:]
         return re * re + im * im
 
-    tails = [square(level.tiles * level.body + at) for at in range(0, 2 * level.half, 8)]
     sums = []
-    for tile in range(level.tiles):
-        for b in range(level.blocks):
-            base = tile * level.body + b * HALF
-            total = jnp.where(dc, 0.0, square(base))
-            head = jnp.where(sub == 0, total, 0.0)
-            for r in range(8, HALF, 8):
-                total = total + square(base + r)
-            row = level.nyquist_row(tile, b)
-            sums.append(2.0 * total - head + jnp.where(sub == row % 8, tails[row // 8], 0.0))
-    if len(sums) % 2:
-        sums.append(jnp.zeros_like(sums[0]))
+    for z in sections:
+        end = z * level.rows + level.tiles * level.body
+        tails = [square(end + at) for at in range(0, 2 * level.half, 8)]
+        for tile in range(level.tiles):
+            for b in range(level.blocks):
+                base = z * level.rows + tile * level.body + b * HALF
+                total = jnp.where(dc, 0.0, square(base))
+                head = jnp.where(sub == 0, total, 0.0)
+                for r in range(8, HALF, 8):
+                    total = total + square(base + r)
+                row = level.nyquist_row(tile, b)
+                sums.append(2.0 * total - head + jnp.where(sub == row % 8, tails[row // 8], 0.0))
     high, low = split(jnp.concatenate(sums, axis=0))
     return dot(jnp.concatenate([high, low], axis=1), jnp.concatenate([ones, ones], axis=0))
 
 
-def scale_spectrum(level, f_ref, sums, spec_ref):
+def scale_spectrum(level, f_ref, sections, sums, spec_ref):
     sub = lax.broadcasted_iota(jnp.int32, (8, 2 * LANES), 0)
     lane = lax.broadcasted_iota(jnp.int32, (8, 2 * LANES), 1)
     dc = (sub == 0) & (lane % PATCH == 0)
-    end = level.tiles * level.body
-    tails = [f_ref[end + at : end + at + 8] for at in range(0, 2 * level.half, 8)]
-    scaled = [jnp.zeros_like(tail) for tail in tails]
-    for tile in range(level.tiles):
-        for b in range(level.blocks):
-            number = (tile * level.blocks + b) * 8
-            scale = lax.rsqrt(all_rows(sums[number : number + 8]) * (1.0 / PATCH**4) + 1e-05)
-            scale = jnp.concatenate([scale, scale], axis=1)
-            for r in range(0, HALF, 16):
-                at = tile * level.body + b * HALF + r
-                head = f_ref[at : at + 8]
-                if r == 0:
-                    head = jnp.where(dc, 0.0, head)
-                both = jnp.concatenate([head * scale, f_ref[at + 8 : at + 16] * scale], axis=0)
-                spec_ref[at : at + 16] = both.astype(bf16)
-            row = level.nyquist_row(tile, b)
-            scaled[row // 8] = jnp.where(sub == row % 8, tails[row // 8] * scale, scaled[row // 8])
-    spec_ref[end:] = jnp.concatenate(scaled, axis=0).astype(bf16)
-
-
-def transform(levels, strips, row_ref, table_ref, ready, scratch, specs):
+    number = 0
+    for z in sections:
+        start = z * level.rows
+        end = start + level.tiles * level.body
+        tails = [f_ref[end + at : end + at + 8] for at in range(0, 2 * level.half, 8)]
+        scaled = [jnp.zeros_like(tail) for tail in tails]
+        for tile in range(level.tiles):
+            for b in range(level.blocks):
+                scale = lax.rsqrt(all_rows(sums[number : number + 8]) * (1.0 / PATCH**4) + 1e-05)
+                number += 8
+                scale = jnp.concatenate([scale, scale], axis=1)
+                for r in range(0, HALF, 16):
+                    at = start + tile * level.body + b * HALF + r
+                    head = f_ref[at : at + 8]
+                    if r == 0:
+                        head = jnp.where(dc, 0.0, head)
+                    both = jnp.concatenate([head * scale, f_ref[at + 8 : at + 16] * scale], axis=0)
+                    spec_ref[at : at + 16] = both.astype(bf16)
+                row = level.nyquist_row(tile, b)
+                scaled[row // 8] = jnp.where(sub == row % 8, tails[row // 8] * scale, scaled[row // 8])
+        spec_ref[end : end + 2 * level.half] = jnp.concatenate(scaled, axis=0).astype(bf16)
+
+
+def transform(levels, sections, strips, row_ref, table_ref, scratch):
     count = len(levels)
-    t_ref, *halves = scratch[:3]
-    lefts = [scratch[3 + 2 * i : 5 + 2 * i] for i in range(count)]
-    f_refs = scratch[3 + 2 * count : 3 + 3 * count]
+    t_ref, high_ref, low_ref = scratch[:3]
+    odd_refs = scratch[3 : 3 + 2 * count]
+    f_refs, spec_refs = scratch[3 + 2 * count : 3 + 3 * count], scratch[3 + 3 * count :]
     places, size = row_places(levels)
-    ready[0]()
-    x = jnp.concatenate([strip[0] for strip in strips], axis=0)
-    width = x.shape[1]
-    t_ref[:, :width] = dot(row_ref[...], jnp.concatenate([x, x], axis=0))
-    t_ref[:, width:] = jnp.zeros((size, LANES), f32)
-    yield
-    for level, place in zip(levels, places):
-        for start in (place[0], place[2]):
-            for r in range(start, start + level.body, 16):
-                for ref, half in zip(halves, split(t_ref[r : r + 16])):
-                    ref[r : r + 16] = half
-    for level, place, left in zip(levels, places, lefts):
-        gather_windows(level, place, t_ref, halves, left)
-        yield
-    for level, left, f_ref, wait in zip(levels, lefts, f_refs, ready[1:]):
-        wait()
-        f_ref[...] = dot3(left[0][...], left[1][...], table_ref, level.table)
-        yield
-    sums = []
-    for level, f_ref in zip(levels, f_refs):
-        sums.append(spectrum_power(level, f_ref))
-        yield
-    for level, f_ref, total, spec_ref in zip(levels, f_refs, sums, specs):
-        scale_spectrum(level, f_ref, total, spec_ref)
-        yield
-
-
-def run_staggered(tasks):
-    active, waiting = [], list(tasks)
-    while waiting or active:
-        if waiting:
-            active.append(waiting.pop(0))
-        for task in list(active):
-            if next(task, True):
-                active.remove(task)
+    for z in sections:
+        x = jnp.concatenate([strip[0] for strip in strips[z]], axis=0)
+        width = x.shape[1]
+        x = jnp.concatenate([x, x], axis=0)
+        for first in range(0, width, 2 * LANES):
+            columns = slice(first, first + 2 * LANES)
+            t = dot(row_ref[...], x[:, columns])
+            for level, (cos_at, nyquist_at, sin_at) in zip(levels, places):
+                for start in (cos_at, sin_at):
+                    for ref, half in zip((high_ref, low_ref), split(t[start : start + level.body])):
+                        ref[z, start : start + level.body, columns] = half
+                rows = slice(nyquist_at, nyquist_at + 2 * level.half)
+                t_ref[z, rows, columns] = t[rows]
+        t_ref[z, :, width:] = jnp.zeros((size, LANES), f32)
+        for ref in (high_ref, low_ref):
+            ref[z, :, width:] = jnp.zeros((size, LANES), bf16)
+    for index, (level, place) in enumerate(zip(levels, places)):
+        odds = odd_refs[2 * index : 2 * index + 2]
+        for z in sections:
+            gather_windows(level, place, t_ref.at[z], (high_ref.at[z], low_ref.at[z]), [ref.at[z] for ref in odds])
+    for index, (level, place) in enumerate(zip(levels, places)):
+        lefts = [
+            jnp.concatenate([left_of(level, place, ref.at[z], odd.at[z]) for z in sections], axis=0)
+            for ref, odd in zip((high_ref, low_ref), odd_refs[2 * index : 2 * index + 2])]
+        rows = slice(sections[0] * level.rows, (sections[-1] + 1) * level.rows)
+        f_refs[index][rows] = dot3(*lefts, table_ref, level.table)
+    for level, f_ref, spec_ref in zip(levels, f_refs, spec_refs):
+        scale_spectrum(level, f_ref, sections, spectrum_power(level, f_ref, sections), spec_ref)
 
 
 def write_maps(levels, specs, masks, table_ref, shift_at, map_at, scratch, outs):
     cross_ref, y_ref, maps_ref, rows_ref, *stacks = scratch
-    pairs = len(specs) - 1
+    pairs = 2
     base = 0
-    for index, level in enumerate(levels):
-        for d in range(pairs):
-            own, other = specs[0][index], specs[d + 1][index]
-
-            def cross(at, rows):
-                a, b = own[at : at + rows].astype(f32), other[at : at + rows].astype(f32)
-                ar, ai, br, bi = a[:, :LANES], a[:, LANES:], b[:, :LANES], b[:, LANES:]
-                return jnp.concatenate([ar * br + ai * bi, ar * bi - ai * br], axis=1)
-
-            for tile in range(level.tiles):
-                quad, odd = divmod(tile, 2)
-                for r in range(0, level.body, 16):
-                    to = base + quad * level.body + r
-                    cross_ref[to : to + 16, 2 * odd * LANES : 2 * (odd + 1) * LANES] = (
-                        cross(tile * level.body + r, 16).astype(bf16))
-            nyquist = cross(level.tiles * level.body, 2 * level.half)
-            nyquist = jnp.concatenate([nyquist[: level.half], nyquist[level.half :]], axis=1)
-            to = base + level.cross_body
+    for level, spec in zip(levels, specs):
+        def cross(at, rows):
+            a = spec[pairs * level.rows + at : pairs * level.rows + at + rows].astype(f32)
+            ar, ai = a[:, :LANES], a[:, LANES:]
+            for d in range(pairs):
+                b = spec[d * level.rows + at : d * level.rows + at + rows].astype(f32)
+                br, bi = b[:, :LANES], b[:, LANES:]
+                yield base + d * level.cross_rows, jnp.concatenate([ar * br + ai * bi, ar * bi - ai * br], axis=1)
+
+        for tile in range(level.tiles):
+            quad, odd = divmod(tile, 2)
+            for r in range(0, level.body, 16):
+                for to, value in cross(tile * level.body + r, 16):
+                    to += quad * level.body + r
+                    cross_ref[to : to + 16, 2 * odd * LANES : 2 * (odd + 1) * LANES] = value.astype(bf16)
+        for to, value in cross(level.tiles * level.body, 2 * level.half):
+            value = jnp.concatenate([value[: level.half], value[level.half :]], axis=1)
             spare = level.cross_rows - level.cross_body - level.half
             if spare:
-                nyquist = jnp.concatenate([nyquist, jnp.zeros((spare, 4 * LANES), f32)], axis=0)
-            cross_ref[to : base + level.cross_rows] = nyquist.astype(bf16)
-            base += level.cross_rows
+                value = jnp.concatenate([value, jnp.zeros((spare, 4 * LANES), f32)], axis=0)
+            cross_ref[to + level.cross_body : to + level.cross_rows] = value.astype(bf16)
+        base += pairs * level.cross_rows
     y_ref[...] = dot(cross_ref[...], table_ref[shift_at : shift_at + 4 * LANES])
     base = tile = 0
     starts = {}
@@ -373,15 +401,22 @@
                     tile += 1
         base += pairs * level.cross_rows
     kept = [jnp.transpose(mask()) for mask in masks]
-    lanes = lax.broadcasted_iota(jnp.int32, (tile, LANES), 1) // WINDOW
+    lane = lax.broadcasted_iota(jnp.int32, (tile, LANES), 1)
+
+    def exchange(low, high, width):
+        even = (lane & width) == 0
+        return (
+            jnp.where(even, low, pltpu.roll(high, width, 1)),
+            jnp.where(even, pltpu.roll(low, LANES - width, 1), high))
+
     for big in range(WINDOW // 4):
         rows = [maps_ref[:, 4 * big + r, :] for r in range(4)]
+        for step in (2, 1):
+            for r in range(4):
+                if not r & step:
+                    rows[r], rows[r + step] = exchange(rows[r], rows[r + step], step * WINDOW)
         for g in range(4):
-            value = None
-            for r in range(4):
-                moved = rows[r] if r == g else pltpu.roll(rows[r], (WINDOW * (r - g)) % LANES, 1)
-                value = moved if value is None else jnp.where(lanes == r, moved, value)
-            rows_ref[big, pl.ds(g, tile, stride=4), :] = value
+            rows_ref[big, pl.ds(g, tile, stride=4), :] = rows[g]
         for index, (level, out) in enumerate(zip(levels, outs)):
             for b in range(level.blocks):
                 column = kept[index][: 4 * level.quads, level.first + b : level.first + b + 1]
@@ -399,12 +434,13 @@
 def section_scratch(levels, width):
     size = row_places(levels)[1]
     return [
-        pltpu.VMEM((size, width + LANES), f32),
-        pltpu.VMEM((size, width + LANES), bf16),
-        pltpu.VMEM((size, width + LANES), bf16),
-        *(pltpu.VMEM((level.rows, 2 * level.pool * LANES), bf16) for level in levels for _ in range(2)),
-        *(pltpu.VMEM((level.rows, 2 * LANES), f32) for level in levels),
-        *(pltpu.VMEM((level.rows, 2 * LANES), bf16) for level in levels),
+        pltpu.VMEM((3, size, width + LANES), f32),
+        pltpu.VMEM((3, size, width + LANES), bf16),
+        pltpu.VMEM((3, size, width + LANES), bf16),
+        *(pltpu.VMEM((3, level.quads * level.body + 2 * level.half, 2 * level.pool * LANES), bf16)
+          for level in levels for _ in range(2)),
+        *(pltpu.VMEM((3 * level.rows, 2 * LANES), f32) for level in levels),
+        *(pltpu.VMEM((3 * level.rows, 2 * LANES), bf16) for level in levels),
     ]
 
 
@@ -420,19 +456,6 @@
     ]
 
 
-def all_maps(levels, strips, first_ready, row_ref, table_ref, tables_ready, shift_ready, places, masks, scratch, outs):
-    size = 3 + 4 * len(levels)
-    sections = [scratch[z * size : (z + 1) * size] for z in range(3)]
-    specs = [section[size - len(levels) :] for section in sections]
-    run_staggered([
-        transform(
-            levels, strips[z], row_ref, table_ref, (first_ready if z == 0 else lambda: None,) + tables_ready,
-            sections[z], specs[z])
-        for z in (1, 2, 0)])
-    shift_ready()
-    write_maps(levels, specs, masks, table_ref, *places, scratch[3 * size :], outs)
-
-
 def copier(sems):
     used = []
 
@@ -448,8 +471,8 @@
 def inner_kernel(
     levels, cuts,
     own_hbm, near, far, mask_hbm, table_hbm,
-    maps, table_ref,
-    own, mask, pad, row_ref, *rest,
+    maps, own, table_ref,
+    mask, pad, row_ref, *rest,
 ):
     *scratch, sems = rest
     start = copier(sems)
@@ -459,56 +482,46 @@
         return start(table_hbm.at[piece], table_ref.at[piece])
 
     fine_at, shift_at, map_at, coarse_at, end = cuts
-    fine_ready = table(fine_at, shift_at)
     own_ready = start(own_hbm, own)
     shift_ready = table(shift_at, coarse_at)
     mask_ready = start(mask_hbm, mask)
     coarse_ready = table(coarse_at, end)
     write_row_table(row_ref, levels[0])
-    waited = []
-
-    def fine_once():
-        if not waited:
-            fine_ready()
-            waited.append(True)
-
-    def mask_rows():
-        mask_ready()
-        return mask_tile(mask, pad)
-
-    all_maps(
-        levels, ((own,), (near,), (far,)), own_ready, row_ref, table_ref, (fine_once,), shift_ready,
-        (shift_at, map_at), (mask_rows,), scratch, (maps,))
+    write_fine_table(table_ref, fine_at)
+    size = 3 + 4 * len(levels)
+    strips = ((near,), (far,), (own,))
+    transform(levels, (0, 1), strips, row_ref, table_ref, scratch[:size])
+    own_ready()
+    transform(levels, (2,), strips, row_ref, table_ref, scratch[:size])
+    shift_ready()
+    mask_ready()
+    write_maps(
+        levels, scratch[size - len(levels) : size], (lambda: mask_tile(mask, pad),), table_ref, shift_at, map_at,
+        scratch[size:], (maps,))
     coarse_ready()
 
 
 def outer_kernel(
     levels, cuts, inner, row_at,
-    own_hbm, near, far, rim, rim_near, rim_far, mask_hbm, mask_coarse_hbm, table_ref, inner_maps,
+    own, near, far, rim, rim_near, rim_far, mask_hbm, mask_coarse_hbm, table_ref, inner_maps,
     out_fine, out_coarse,
-    own, mask, mask_coarse, pad, pad_coarse, maps, maps_coarse, *rest,
+    mask, mask_coarse, pad, pad_coarse, maps, maps_coarse, *rest,
 ):
     *scratch, sems = rest
     start = copier(sems)
-    own_ready = start(own_hbm, own)
-    mask_ready = start(mask_hbm, mask)
-    mask_coarse_ready = start(mask_coarse_hbm, mask_coarse)
+    masks_ready = [start(mask_hbm, mask), start(mask_coarse_hbm, mask_coarse)]
     stores = [start(inner_maps.at[d], out_fine.at[0, d, pl.ds(0, inner)]) for d in range(2)]
-
-    def mask_rows():
-        mask_ready()
-        return mask_tile(mask, pad)
-
-    def mask_coarse_rows():
-        mask_coarse_ready()
-        return mask_tile(mask_coarse, pad_coarse)
-
     fine_at, shift_at, map_at, coarse_at, end = cuts
     row_ref = table_ref.at[pl.ds(row_at, row_places(levels)[1])]
-    all_maps(
-        levels, ((own, rim), (near, rim_near), (far, rim_far)), own_ready, row_ref, table_ref,
-        (lambda: None,) * 2, lambda: None, (shift_at, map_at), (mask_rows, mask_coarse_rows), scratch,
-        (maps, maps_coarse))
+    size = 3 + 4 * len(levels)
+    strips = ((near, rim_near), (far, rim_far), (own, rim))
+    transform(levels, (0, 1, 2), strips, row_ref, table_ref, scratch[:size])
+    for wait in masks_ready:
+        wait()
+    write_maps(
+        levels, scratch[size - len(levels) : size],
+        (lambda: mask_tile(mask, pad), lambda: mask_tile(mask_coarse, pad_coarse)), table_ref, shift_at, map_at,
+        scratch[size:], (maps, maps_coarse))
     for d in range(2):
         stores.append(start(maps.at[d], out_fine.at[0, d, pl.ds(inner, levels[0].blocks)]))
         stores.append(start(maps_coarse.at[d], out_coarse.at[0, d]))
@@ -542,22 +555,22 @@
     def cost(flops):
         return pl.CostEstimate(flops=flops, bytes_accessed=4 * 10**6, transcendentals=0)
 
-    maps, handed = pl.pallas_call(
+    maps, own_kept, handed = pl.pallas_call(
         functools.partial(inner_kernel, inner_levels, cuts),
         out_shape=(
             jax.ShapeDtypeStruct((2, inner, 4 * inner_levels[0].quads, shifts), f32),
+            jax.ShapeDtypeStruct(own.shape, bf16),
             jax.ShapeDtypeStruct(table.shape, bf16),
         ),
         in_specs=[hbm, vmem, vmem, hbm, hbm],
-        out_specs=(vmem, vmem),
+        out_specs=(vmem,) * 3,
         scratch_shapes=[
-            pltpu.VMEM(own.shape, bf16),
             pltpu.VMEM(mask_fine.shape, jnp.int32),
             pltpu.VMEM((8, LANES), f32),
             pltpu.VMEM((row_places(inner_levels)[1], 2 * strip_rows), bf16),
-            *section_scratch(inner_levels, width) * 3,
+            *section_scratch(inner_levels, width),
             *pair_scratch(inner_levels),
-            pltpu.SemaphoreType.DMA((5,)),
+            pltpu.SemaphoreType.DMA((4,)),
         ],
         compiler_params=params,
         cost_estimate=cost(3 * 10**9),
@@ -569,23 +582,22 @@
             jax.ShapeDtypeStruct((1, 2, fine, 4 * outer_levels[0].quads, shifts), f32),
             jax.ShapeDtypeStruct((1, 2, coarse, 4 * outer_levels[1].quads, shifts), f32),
         ),
-        in_specs=[hbm] + [vmem] * 5 + [hbm] * 2 + [vmem] * 2,
+        in_specs=[vmem] * 6 + [hbm] * 2 + [vmem] * 2,
         out_specs=(hbm, hbm),
         scratch_shapes=[
-            pltpu.VMEM(own.shape, bf16),
             pltpu.VMEM(mask_fine.shape, jnp.int32),
             pltpu.VMEM(mask_coarse.shape, jnp.int32),
             pltpu.VMEM((8, LANES), f32),
             pltpu.VMEM((8, LANES), f32),
             *(pltpu.VMEM((2, level.blocks, 4 * level.quads, shifts), f32) for level in outer_levels),
-            *section_scratch(outer_levels, width) * 3,
+            *section_scratch(outer_levels, width),
             *pair_scratch(outer_levels),
-            pltpu.SemaphoreType.DMA((9,)),
+            pltpu.SemaphoreType.DMA((8,)),
         ],
         compiler_params=params,
         cost_estimate=cost(4 * 10**9),
         name="outer_blocks",
-    )(own, near, far, rim, rim_near, rim_far, mask_fine, mask_coarse, handed, maps)
+    )(own_kept, near, far, rim, rim_near, rim_far, mask_fine, mask_coarse, handed, maps)
 
 
 def local(sections, mask_fine, mask_coarse):

time: 20 us -> 20.2 us (1.010)
  the two profiles are of different devices: /device:TPU:1 before, /device:TPU:9 now
where the time goes in v4:
time: 20.2 us; the launch traced here: 20 us
  starting transfers between devices  9.01 us (45%)
  Pallas kernels  7.11 us (35%)
  waiting for transfers between devices  3.19 us (16%)
  between operations  0.7 us (3%)
    ppermute x5, starting transfers between devices, from_device(): return lax.ppermute(value, ('sec', 'strip'), pairs)  9.01 us
    pallas_call x1, Pallas kernels, correlate(): pl.pallas_call(functools.partial(outer_kernel, outer_levels, cuts, inner,...  3.69 us
    pallas_call x1, Pallas kernels, correlate(): pl.pallas_call(functools.partial(inner_kernel, inner_levels, cuts), out_s...  3.42 us
    ppermute x5, waiting for transfers between devices, from_device(): return lax.ppermute(value, ('sec', 'strip'), pairs)  3.19 us
  transfers between devices with their start and end apart: 5, of which 2 were waited for; matrix products, arithmetic and copies ran while one was open for 0% of the time, Pallas kernels for 17%

profile of v4, /device:TPU:9, one launch (start us, length us, event | category | flops | bytes accessed | tf_op | source)
XLA Modules:
  0.0 20.0 jit_solution(14698209169378805530)
XLA Ops:
  0.6 1.3 %collective-permute-start.1 = (bf16[1,64,512]{2,1,0:T(8,128)(2,1)}, bf16[1,64,512]{2,1,0:T(8,128)(2,1)S(1)}, u32[]{:S(2)}, u32[]{:S(2)}) collective-permute-start(bf16[1,64,512]{2,1,0:T(8,128)(2,1)} %own_hbm.1), channel_id=1, source_target_pairs={{8,0},{9,1},{10,2},{11,3},{12,4},{13,5},{14,6},{15,7},{24,16},{25,... | collective-permute-start | bytes 196616 | tf_op jit(solution)/shard_map/ppermute | solution.py:28
  1.9 1.9 %collective-permute-start = (bf16[1,64,512]{2,1,0:T(8,128)(2,1)}, bf16[1,64,512]{2,1,0:T(8,128)(2,1)S(1)}, u32[]{:S(2)}, u32[]{:S(2)}) collective-permute-start(bf16[1,64,512]{2,1,0:T(8,128)(2,1)} %own_hbm.1), channel_id=1, source_target_pairs={{4,0},{5,1},{6,2},{7,3},{8,4},{9,5},{10,6},{11,7},{12,8},{13,9},{1... | collective-permute-start | bytes 196616 | tf_op jit(solution)/shard_map/ppermute | solution.py:28
  3.9 2.6 %collective-permute-start.2 = (bf16[1,64,512]{2,1,0:T(8,128)(2,1)}, bf16[1,64,512]{2,1,0:T(8,128)(2,1)S(1)}, u32[]{:S(2)}, u32[]{:S(2)}) collective-permute-start(bf16[1,64,512]{2,1,0:T(8,128)(2,1)} %own_hbm.1), channel_id=1, source_target_pairs={{1,0},{2,1},{3,2},{5,4},{6,5},{7,6},{9,8},{10,9},{11,10},{13,12},{... | collective-permute-start | bytes 196616 | tf_op jit(solution)/shard_map/ppermute | solution.py:28
  6.4 1.3 %collective-permute-start.4 = (bf16[1,64,512]{2,1,0:T(8,128)(2,1)}, bf16[1,64,512]{2,1,0:T(8,128)(2,1)S(1)}, u32[]{:S(2)}, u32[]{:S(2)}) collective-permute-start(bf16[1,64,512]{2,1,0:T(8,128)(2,1)} %own_hbm.1), channel_id=1, source_target_pairs={{9,0},{10,1},{11,2},{13,4},{14,5},{15,6},{25,16},{26,17},{27,18},{... | collective-permute-start | bytes 196616 | tf_op jit(solution)/shard_map/ppermute | solution.py:28
  7.7 1.9 %collective-permute-start.3 = (bf16[1,64,512]{2,1,0:T(8,128)(2,1)}, bf16[1,64,512]{2,1,0:T(8,128)(2,1)S(1)}, u32[]{:S(2)}, u32[]{:S(2)}) collective-permute-start(bf16[1,64,512]{2,1,0:T(8,128)(2,1)} %own_hbm.1), channel_id=1, source_target_pairs={{5,0},{6,1},{7,2},{9,4},{10,5},{11,6},{13,8},{14,9},{15,10},{21,16... | collective-permute-start | bytes 196616 | tf_op jit(solution)/shard_map/ppermute | solution.py:28
  9.7 0.0 collective-permute-done.1.far
  9.7 0.0 collective-permute-done.near
  9.7 3.4 %inner_blocks.1 = (f32[2,1,16,1024]{3,2,1,0:T(8,128)S(1)}, bf16[1,64,512]{2,1,0:T(8,128)(2,1)S(1)}, bf16[2272,256]{1,0:T(8,128)(2,1)S(1)}) custom-call(bf16[1,64,512]{2,1,0:T(8,128)(2,1)} %own_hbm.1, bf16[1,64,512]{2,1,0:T(8,128)(2,1)S(1)} %collective-permute-done.near, bf16[1,64,512]{2,1,0:T(8,128)(2,1)S(1)} %collective-permute-done.1.far, ...), custom_call_target="tpu_custom_call" | custom-call | flops 3000000000 | bytes 4000000 | tf_op jit(solution)/shard_map/inner_blocks/pallas_call | solution.py:558
  13.1 0.0 collective-permute-done.2.rim
  13.1 1.9 %collective-permute-done.4.rim_far = bf16[1,64,512]{2,1,0:T(8,128)(2,1)S(1)} collective-permute-done((bf16[1,64,512]{2,1,0:T(8,128)(2,1)}, bf16[1,64,512]{2,1,0:T(8,128)(2,1)S(1)}, u32[]{:S(2)}, u32[]{:S(2)}) %collective-permute-start.4) | collective-permute-done | bytes 65568 | tf_op jit(solution)/shard_map/ppermute | solution.py:28
  15.0 1.3 %collective-permute-done.3.rim_near = bf16[1,64,512]{2,1,0:T(8,128)(2,1)S(1)} collective-permute-done((bf16[1,64,512]{2,1,0:T(8,128)(2,1)}, bf16[1,64,512]{2,1,0:T(8,128)(2,1)S(1)}, u32[]{:S(2)}, u32[]{:S(2)}) %collective-permute-start.3) | collective-permute-done | bytes 65568 | tf_op jit(solution)/shard_map/ppermute | solution.py:28
  16.3 3.7 %outer_blocks.1 = (f32[1,2,2,16,1024]{4,3,2,1,0:T(8,128)}, f32[1,2,1,8,1024]{4,3,2,1,0:T(8,128)}) custom-call(bf16[1,64,512]{2,1,0:T(8,128)(2,1)S(1)} %get-tuple-element.5.own, bf16[1,64,512]{2,1,0:T(8,128)(2,1)S(1)} %collective-permute-done.near, bf16[1,64,512]{2,1,0:T(8,128)(2,1)S(1)} %collective-permute-done.1.far, ...), custom_call_target="tpu_custom_call" | custom-call | flops 4000000000 | bytes 4000000 | tf_op jit(solution)/shard_map/outer_blocks/pallas_call | solution.py:579
Async XLA Ops:
  0.6 9.0 %collective-permute-start.1 = (bf16[1,64,512]{2,1,0:T(8,128)(2,1)}, bf16[1,64,512]{2,1,0:T(8,128)(2,1)S(1)}, u32[]{:S(2)}, u32[]{:S(2)}) collective-permute-start(bf16[1,64,512]{2,1,0:T(8,128)(2,1)} %own_hbm.1), channel_id=1, source_target_pairs={{8,0},{9,1},{10,2},{11,3},{12,4},{13,5},{14,6},{15,7},{24,16},{25,... | collective-permute-start | bytes 196616 | tf_op jit(solution)/shard_map/ppermute | solution.py:28
  1.9 7.8 %collective-permute-start = (bf16[1,64,512]{2,1,0:T(8,128)(2,1)}, bf16[1,64,512]{2,1,0:T(8,128)(2,1)S(1)}, u32[]{:S(2)}, u32[]{:S(2)}) collective-permute-start(bf16[1,64,512]{2,1,0:T(8,128)(2,1)} %own_hbm.1), channel_id=1, source_target_pairs={{4,0},{5,1},{6,2},{7,3},{8,4},{9,5},{10,6},{11,7},{12,8},{13,9},{1... | collective-permute-start | bytes 196616 | tf_op jit(solution)/shard_map/ppermute | solution.py:28
  3.9 9.3 %collective-permute-start.2 = (bf16[1,64,512]{2,1,0:T(8,128)(2,1)}, bf16[1,64,512]{2,1,0:T(8,128)(2,1)S(1)}, u32[]{:S(2)}, u32[]{:S(2)}) collective-permute-start(bf16[1,64,512]{2,1,0:T(8,128)(2,1)} %own_hbm.1), channel_id=1, source_target_pairs={{1,0},{2,1},{3,2},{5,4},{6,5},{7,6},{9,8},{10,9},{11,10},{13,12},{... | collective-permute-start | bytes 196616 | tf_op jit(solution)/shard_map/ppermute | solution.py:28
  6.4 8.6 %collective-permute-start.4 = (bf16[1,64,512]{2,1,0:T(8,128)(2,1)}, bf16[1,64,512]{2,1,0:T(8,128)(2,1)S(1)}, u32[]{:S(2)}, u32[]{:S(2)}) collective-permute-start(bf16[1,64,512]{2,1,0:T(8,128)(2,1)} %own_hbm.1), channel_id=1, source_target_pairs={{9,0},{10,1},{11,2},{13,4},{14,5},{15,6},{25,16},{26,17},{27,18},{... | collective-permute-start | bytes 196616 | tf_op jit(solution)/shard_map/ppermute | solution.py:28
  7.7 8.6 %collective-permute-start.3 = (bf16[1,64,512]{2,1,0:T(8,128)(2,1)}, bf16[1,64,512]{2,1,0:T(8,128)(2,1)S(1)}, u32[]{:S(2)}, u32[]{:S(2)}) collective-permute-start(bf16[1,64,512]{2,1,0:T(8,128)(2,1)} %own_hbm.1), channel_id=1, source_target_pairs={{5,0},{6,1},{7,2},{9,4},{10,5},{11,6},{13,8},{14,9},{15,10},{21,16... | collective-permute-start | bytes 196616 | tf_op jit(solution)/shard_map/ppermute | solution.py:28

commit v5 on v4

--- a/solution.py
+++ b/solution.py
@@ -251,7 +251,7 @@
             target[end:, (2 * p + 1) * LANES : (2 * p + 2) * LANES] = jnp.zeros(part.shape, bf16)
 
 
-def spectrum_power(level, f_ref, sections):
+def spectrum_power(level, f_ref):
     sub = lax.broadcasted_iota(jnp.int32, (8, LANES), 0)
     lane = lax.broadcasted_iota(jnp.int32, (8, LANES), 1)
     dc = (sub == 0) & (lane % PATCH == 0)
@@ -264,83 +264,84 @@
         return re * re + im * im
 
     sums = []
-    for z in sections:
-        end = z * level.rows + level.tiles * level.body
-        tails = [square(end + at) for at in range(0, 2 * level.half, 8)]
-        for tile in range(level.tiles):
-            for b in range(level.blocks):
-                base = z * level.rows + tile * level.body + b * HALF
-                total = jnp.where(dc, 0.0, square(base))
-                head = jnp.where(sub == 0, total, 0.0)
-                for r in range(8, HALF, 8):
-                    total = total + square(base + r)
-                row = level.nyquist_row(tile, b)
-                sums.append(2.0 * total - head + jnp.where(sub == row % 8, tails[row // 8], 0.0))
+    tails = [square(level.tiles * level.body + at) for at in range(0, 2 * level.half, 8)]
+    for tile in range(level.tiles):
+        for b in range(level.blocks):
+            base = tile * level.body + b * HALF
+            total = jnp.where(dc, 0.0, square(base))
+            head = jnp.where(sub == 0, total, 0.0)
+            for r in range(8, HALF, 8):
+                total = total + square(base + r)
+            row = level.nyquist_row(tile, b)
+            sums.append(2.0 * total - head + jnp.where(sub == row % 8, tails[row // 8], 0.0))
     high, low = split(jnp.concatenate(sums, axis=0))
     return dot(jnp.concatenate([high, low], axis=1), jnp.concatenate([ones, ones], axis=0))
 
 
-def scale_spectrum(level, f_ref, sections, sums, spec_ref):
+def scale_spectrum(level, f_ref, sums, spec_ref):
     sub = lax.broadcasted_iota(jnp.int32, (8, 2 * LANES), 0)
     lane = lax.broadcasted_iota(jnp.int32, (8, 2 * LANES), 1)
     dc = (sub == 0) & (lane % PATCH == 0)
-    number = 0
-    for z in sections:
-        start = z * level.rows
-        end = start + level.tiles * level.body
-        tails = [f_ref[end + at : end + at + 8] for at in range(0, 2 * level.half, 8)]
-        scaled = [jnp.zeros_like(tail) for tail in tails]
-        for tile in range(level.tiles):
-            for b in range(level.blocks):
-                scale = lax.rsqrt(all_rows(sums[number : number + 8]) * (1.0 / PATCH**4) + 1e-05)
-                number += 8
-                scale = jnp.concatenate([scale, scale], axis=1)
-                for r in range(0, HALF, 16):
-                    at = start + tile * level.body + b * HALF + r
-                    head = f_ref[at : at + 8]
-                    if r == 0:
-                        head = jnp.where(dc, 0.0, head)
-                    both = jnp.concatenate([head * scale, f_ref[at + 8 : at + 16] * scale], axis=0)
-                    spec_ref[at : at + 16] = both.astype(bf16)
-                row = level.nyquist_row(tile, b)
-                scaled[row // 8] = jnp.where(sub == row % 8, tails[row // 8] * scale, scaled[row // 8])
-        spec_ref[end : end + 2 * level.half] = jnp.concatenate(scaled, axis=0).astype(bf16)
-
-
-def transform(levels, sections, strips, row_ref, table_ref, scratch):
+    end = level.tiles * level.body
+    tails = [f_ref[end + at : end + at + 8] for at in range(0, 2 * level.half, 8)]
+    scaled = [jnp.zeros_like(tail) for tail in tails]
+    for tile in range(level.tiles):
+        for b in range(level.blocks):
+            number = 8 * (tile * level.blocks + b)
+            scale = lax.rsqrt(all_rows(sums[number : number + 8]) * (1.0 / PATCH**4) + 1e-05)
+            scale = jnp.concatenate([scale, scale], axis=1)
+            for r in range(0, HALF, 16):
+                at = tile * level.body + b * HALF + r
+                head = f_ref[at : at + 8]
+                if r == 0:
+                    head = jnp.where(dc, 0.0, head)
+                both = jnp.concatenate([head * scale, f_ref[at + 8 : at + 16] * scale], axis=0)
+                spec_ref[at : at + 16] = both.astype(bf16)
+            row = level.nyquist_row(tile, b)
+            scaled[row // 8] = jnp.where(sub == row % 8, tails[row // 8] * scale, scaled[row // 8])
+    spec_ref[end : end + 2 * level.half] = jnp.concatenate(scaled, axis=0).astype(bf16)
+
+
+def transform(levels, z, x_ref, row_ref, table_ref, scratch):
     count = len(levels)
-    t_ref, high_ref, low_ref = scratch[:3]
+    t_ref, *halves = scratch[:3]
     odd_refs = scratch[3 : 3 + 2 * count]
     f_refs, spec_refs = scratch[3 + 2 * count : 3 + 3 * count], scratch[3 + 3 * count :]
     places, size = row_places(levels)
-    for z in sections:
-        x = jnp.concatenate([strip[0] for strip in strips[z]], axis=0)
-        width = x.shape[1]
-        x = jnp.concatenate([x, x], axis=0)
-        for first in range(0, width, 2 * LANES):
-            columns = slice(first, first + 2 * LANES)
-            t = dot(row_ref[...], x[:, columns])
-            for level, (cos_at, nyquist_at, sin_at) in zip(levels, places):
-                for start in (cos_at, sin_at):
-                    for ref, half in zip((high_ref, low_ref), split(t[start : start + level.body])):
-                        ref[z, start : start + level.body, columns] = half
-                rows = slice(nyquist_at, nyquist_at + 2 * level.half)
-                t_ref[z, rows, columns] = t[rows]
-        t_ref[z, :, width:] = jnp.zeros((size, LANES), f32)
-        for ref in (high_ref, low_ref):
-            ref[z, :, width:] = jnp.zeros((size, LANES), bf16)
+    x = x_ref[z]
+    width = x.shape[1]
+    x = jnp.concatenate([x, x], axis=0)
+    for first in range(0, width, 2 * LANES):
+        columns = slice(first, first + 2 * LANES)
+        t = dot(row_ref[...], x[:, columns])
+        for level, (cos_at, nyquist_at, sin_at) in zip(levels, places):
+            for start in (cos_at, sin_at):
+                for ref, half in zip(halves, split(t[start : start + level.body])):
+                    ref[start : start + level.body, columns] = half
+            rows = slice(nyquist_at, nyquist_at + 2 * level.half)
+            t_ref[rows, columns] = t[rows]
     for index, (level, place) in enumerate(zip(levels, places)):
-        odds = odd_refs[2 * index : 2 * index + 2]
-        for z in sections:
-            gather_windows(level, place, t_ref.at[z], (high_ref.at[z], low_ref.at[z]), [ref.at[z] for ref in odds])
+        gather_windows(level, place, t_ref, halves, odd_refs[2 * index : 2 * index + 2])
     for index, (level, place) in enumerate(zip(levels, places)):
-        lefts = [
-            jnp.concatenate([left_of(level, place, ref.at[z], odd.at[z]) for z in sections], axis=0)
-            for ref, odd in zip((high_ref, low_ref), odd_refs[2 * index : 2 * index + 2])]
-        rows = slice(sections[0] * level.rows, (sections[-1] + 1) * level.rows)
-        f_refs[index][rows] = dot3(*lefts, table_ref, level.table)
+        lefts = [left_of(level, place, ref, odd) for ref, odd in zip(halves, odd_refs[2 * index : 2 * index + 2])]
+        f_refs[index][...] = dot3(*lefts, table_ref, level.table)
     for level, f_ref, spec_ref in zip(levels, f_refs, spec_refs):
-        scale_spectrum(level, f_ref, sections, spectrum_power(level, f_ref, sections), spec_ref)
+        scale_spectrum(level, f_ref, spectrum_power(level, f_ref), spec_ref.at[z])
+
+
+def transform_all(levels, x_ref, own_ready, row_ref, table_ref, scratch):
+    t_ref, *halves = scratch[:3]
+    width = x_ref.shape[2]
+    for ref in (t_ref, *halves):
+        ref[:, width:] = jnp.zeros((ref.shape[0], LANES), ref.dtype)
+
+    def one_section(z, carry):
+        if own_ready is not None:
+            pl.when(z == 2)(own_ready)
+        transform(levels, z, x_ref, row_ref, table_ref, scratch)
+        return carry
+
+    lax.fori_loop(0, 3, one_section, 0)
 
 
 def write_maps(levels, specs, masks, table_ref, shift_at, map_at, scratch, outs):
@@ -349,10 +350,10 @@
     base = 0
     for level, spec in zip(levels, specs):
         def cross(at, rows):
-            a = spec[pairs * level.rows + at : pairs * level.rows + at + rows].astype(f32)
+            a = spec[pairs, at : at + rows].astype(f32)
             ar, ai = a[:, :LANES], a[:, LANES:]
             for d in range(pairs):
-                b = spec[d * level.rows + at : d * level.rows + at + rows].astype(f32)
+                b = spec[d, at : at + rows].astype(f32)
                 br, bi = b[:, :LANES], b[:, LANES:]
                 yield base + d * level.cross_rows, jnp.concatenate([ar * br + ai * bi, ar * bi - ai * br], axis=1)
 
@@ -434,13 +435,13 @@
 def section_scratch(levels, width):
     size = row_places(levels)[1]
     return [
-        pltpu.VMEM((3, size, width + LANES), f32),
-        pltpu.VMEM((3, size, width + LANES), bf16),
-        pltpu.VMEM((3, size, width + LANES), bf16),
-        *(pltpu.VMEM((3, level.quads * level.body + 2 * level.half, 2 * level.pool * LANES), bf16)
+        pltpu.VMEM((size, width + LANES), f32),
+        pltpu.VMEM((size, width + LANES), bf16),
+        pltpu.VMEM((size, width + LANES), bf16),
+        *(pltpu.VMEM((level.quads * level.body + 2 * level.half, 2 * level.pool * LANES), bf16)
           for level in levels for _ in range(2)),
-        *(pltpu.VMEM((3 * level.rows, 2 * LANES), f32) for level in levels),
-        *(pltpu.VMEM((3 * level.rows, 2 * LANES), bf16) for level in levels),
+        *(pltpu.VMEM((level.rows, 2 * LANES), f32) for level in levels),
+        *(pltpu.VMEM((3, level.rows, 2 * LANES), bf16) for level in levels),
     ]
 
 
@@ -472,7 +473,7 @@
     levels, cuts,
     own_hbm, near, far, mask_hbm, table_hbm,
     maps, own, table_ref,
-    mask, pad, row_ref, *rest,
+    mask, pad, row_ref, x_ref, *rest,
 ):
     *scratch, sems = rest
     start = copier(sems)
@@ -489,10 +490,13 @@
     write_row_table(row_ref, levels[0])
     write_fine_table(table_ref, fine_at)
     size = 3 + 4 * len(levels)
-    strips = ((near,), (far,), (own,))
-    transform(levels, (0, 1), strips, row_ref, table_ref, scratch[:size])
-    own_ready()
-    transform(levels, (2,), strips, row_ref, table_ref, scratch[:size])
+    x_ref[0], x_ref[1] = near[0], far[0]
+
+    def take_own():
+        own_ready()
+        x_ref[2] = own[0]
+
+    transform_all(levels, x_ref, take_own, row_ref, table_ref, scratch[:size])
     shift_ready()
     mask_ready()
     write_maps(
@@ -505,7 +509,7 @@
     levels, cuts, inner, row_at,
     own, near, far, rim, rim_near, rim_far, mask_hbm, mask_coarse_hbm, table_ref, inner_maps,
     out_fine, out_coarse,
-    mask, mask_coarse, pad, pad_coarse, maps, maps_coarse, *rest,
+    mask, mask_coarse, pad, pad_coarse, maps, maps_coarse, x_ref, *rest,
 ):
     *scratch, sems = rest
     start = copier(sems)
@@ -514,8 +518,11 @@
     fine_at, shift_at, map_at, coarse_at, end = cuts
     row_ref = table_ref.at[pl.ds(row_at, row_places(levels)[1])]
     size = 3 + 4 * len(levels)
-    strips = ((near, rim_near), (far, rim_far), (own, rim))
-    transform(levels, (0, 1, 2), strips, row_ref, table_ref, scratch[:size])
+    rows = own.shape[1]
+    for z, (strip, below) in enumerate(((near, rim_near), (far, rim_far), (own, rim))):
+        x_ref[z, :rows] = strip[0]
+        x_ref[z, rows:] = below[0]
+    transform_all(levels, x_ref, None, row_ref, table_ref, scratch[:size])
     for wait in masks_ready:
         wait()
     write_maps(
@@ -568,6 +575,7 @@
             pltpu.VMEM(mask_fine.shape, jnp.int32),
             pltpu.VMEM((8, LANES), f32),
             pltpu.VMEM((row_places(inner_levels)[1], 2 * strip_rows), bf16),
+            pltpu.VMEM((3, strip_rows, width), bf16),
             *section_scratch(inner_levels, width),
             *pair_scratch(inner_levels),
             pltpu.SemaphoreType.DMA((4,)),
@@ -590,6 +598,7 @@
             pltpu.VMEM((8, LANES), f32),
             pltpu.VMEM((8, LANES), f32),
             *(pltpu.VMEM((2, level.blocks, 4 * level.quads, shifts), f32) for level in outer_levels),
+            pltpu.VMEM((3, strip_rows + PATCH, width), bf16),
             *section_scratch(outer_levels, width),
             *pair_scratch(outer_levels),
             pltpu.SemaphoreType.DMA((8,)),
@@ -603,7 +612,8 @@
 def local(sections, mask_fine, mask_coarse):
     far = from_device(sections, 2, 0)
     near = from_device(sections, 1, 0)
-    rims = [from_device(sections, z, 1) for z in range(3)]
+    last, far = lax.optimization_barrier((sections, far))
+    rims = [from_device(last if z == 0 else sections, z, 1) for z in range(3)]
     return correlate(sections, near, far, *rims, mask_fine, mask_coarse)
 
 

time: 20.2 us -> 21.8 us (1.079)
  the two profiles are of different devices: /device:TPU:9 before, /device:TPU:1 now
where the time goes in v5:
time: 21.8 us; the launch traced here: 21.6 us
  Pallas kernels  9.28 us (43%)
  starting transfers between devices  8.68 us (40%)
  waiting for transfers between devices  2.92 us (13%)
  between operations  0.69 us (3%)
    ppermute x5, starting transfers between devices, from_device(): return lax.ppermute(value, ('sec', 'strip'), pairs)  8.68 us
    pallas_call x1, Pallas kernels, correlate(): pl.pallas_call(functools.partial(outer_kernel, outer_levels, cuts, inner,...  5.24 us
    pallas_call x1, Pallas kernels, correlate(): pl.pallas_call(functools.partial(inner_kernel, inner_levels, cuts), out_s...  4.04 us
    ppermute x5, waiting for transfers between devices, from_device(): return lax.ppermute(value, ('sec', 'strip'), pairs)  2.92 us
  transfers between devices with their start and end apart: 5, of which 3 were waited for; matrix products, arithmetic and copies ran while one was open for 0% of the time, Pallas kernels for 19%

profile of v5, /device:TPU:1, one launch (start us, length us, event | category | flops | bytes accessed | tf_op | source)
XLA Modules:
  0.0 21.6 jit_solution(5610058345599293939)
XLA Ops:
  0.6 1.3 %collective-permute-start.1 = (bf16[1,64,512]{2,1,0:T(8,128)(2,1)}, bf16[1,64,512]{2,1,0:T(8,128)(2,1)S(1)}, u32[]{:S(2)}, u32[]{:S(2)}) collective-permute-start(bf16[1,64,512]{2,1,0:T(8,128)(2,1)} %own_hbm.1), channel_id=1, source_target_pairs={{8,0},{9,1},{10,2},{11,3},{12,4},{13,5},{14,6},{15,7},{24,16},{25,... | collective-permute-start | bytes 196616 | tf_op jit(solution)/shard_map/ppermute | solution.py:28
  1.9 1.3 %collective-permute-start = (bf16[1,64,512]{2,1,0:T(8,128)(2,1)}, bf16[1,64,512]{2,1,0:T(8,128)(2,1)S(1)}, u32[]{:S(2)}, u32[]{:S(2)}) collective-permute-start(bf16[1,64,512]{2,1,0:T(8,128)(2,1)} %own_hbm.1), channel_id=1, source_target_pairs={{4,0},{5,1},{6,2},{7,3},{8,4},{9,5},{10,6},{11,7},{12,8},{13,9},{1... | collective-permute-start | bytes 196616 | tf_op jit(solution)/shard_map/ppermute | solution.py:28
  3.2 1.3 %collective-permute-start.4 = (bf16[1,64,512]{2,1,0:T(8,128)(2,1)}, bf16[1,64,512]{2,1,0:T(8,128)(2,1)S(1)}, u32[]{:S(2)}, u32[]{:S(2)}) collective-permute-start(bf16[1,64,512]{2,1,0:T(8,128)(2,1)} %own_hbm.1), channel_id=1, source_target_pairs={{9,0},{10,1},{11,2},{13,4},{14,5},{15,6},{25,16},{26,17},{27,18},{... | collective-permute-start | bytes 196616 | tf_op jit(solution)/shard_map/ppermute | solution.py:28
  4.5 1.3 %collective-permute-start.3 = (bf16[1,64,512]{2,1,0:T(8,128)(2,1)}, bf16[1,64,512]{2,1,0:T(8,128)(2,1)S(1)}, u32[]{:S(2)}, u32[]{:S(2)}) collective-permute-start(bf16[1,64,512]{2,1,0:T(8,128)(2,1)} %own_hbm.1), channel_id=1, source_target_pairs={{5,0},{6,1},{7,2},{9,4},{10,5},{11,6},{13,8},{14,9},{15,10},{21,16... | collective-permute-start | bytes 196616 | tf_op jit(solution)/shard_map/ppermute | solution.py:28
  5.8 1.1 %collective-permute-done.1.far = bf16[1,64,512]{2,1,0:T(8,128)(2,1)S(1)} collective-permute-done((bf16[1,64,512]{2,1,0:T(8,128)(2,1)}, bf16[1,64,512]{2,1,0:T(8,128)(2,1)S(1)}, u32[]{:S(2)}, u32[]{:S(2)}) %collective-permute-start.1) | collective-permute-done | bytes 65568 | tf_op jit(solution)/shard_map/ppermute | solution.py:28
  6.9 3.5 %collective-permute-start.2 = (bf16[1,64,512]{2,1,0:T(8,128)(2,1)}, bf16[1,64,512]{2,1,0:T(8,128)(2,1)S(1)}, u32[]{:S(2)}, u32[]{:S(2)}) collective-permute-start(bf16[1,64,512]{2,1,0:T(8,128)(2,1)} %own_hbm.1), channel_id=1, source_target_pairs={{1,0},{2,1},{3,2},{5,4},{6,5},{7,6},{9,8},{10,9},{11,10},{13,12},{... | collective-permute-start | bytes 196616 | tf_op jit(solution)/shard_map/ppermute | solution.py:28
  10.4 0.0 collective-permute-done.near
  10.4 4.0 %inner_blocks.1 = (f32[2,1,16,1024]{3,2,1,0:T(8,128)S(1)}, bf16[1,64,512]{2,1,0:T(8,128)(2,1)S(1)}, bf16[2272,256]{1,0:T(8,128)(2,1)S(1)}) custom-call(bf16[1,64,512]{2,1,0:T(8,128)(2,1)} %own_hbm.1, bf16[1,64,512]{2,1,0:T(8,128)(2,1)S(1)} %collective-permute-done.near, bf16[1,64,512]{2,1,0:T(8,128)(2,1)S(1)} %collective-permute-done.1.far, ...), custom_call_target="tpu_custom_call" | custom-call | flops 3000000000 | bytes 4000000 | tf_op jit(solution)/shard_map/inner_blocks/pallas_call | solution.py:565
  14.5 1.1 %collective-permute-done.4.rim_far = bf16[1,64,512]{2,1,0:T(8,128)(2,1)S(1)} collective-permute-done((bf16[1,64,512]{2,1,0:T(8,128)(2,1)}, bf16[1,64,512]{2,1,0:T(8,128)(2,1)S(1)}, u32[]{:S(2)}, u32[]{:S(2)}) %collective-permute-start.4) | collective-permute-done | bytes 65568 | tf_op jit(solution)/shard_map/ppermute | solution.py:28
  15.6 0.0 collective-permute-done.3.rim_near
  15.6 0.7 %collective-permute-done.2.rim = bf16[1,64,512]{2,1,0:T(8,128)(2,1)S(1)} collective-permute-done((bf16[1,64,512]{2,1,0:T(8,128)(2,1)}, bf16[1,64,512]{2,1,0:T(8,128)(2,1)S(1)}, u32[]{:S(2)}, u32[]{:S(2)}) %collective-permute-start.2) | collective-permute-done | bytes 65568 | tf_op jit(solution)/shard_map/ppermute | solution.py:28
  16.3 5.2 %outer_blocks.1 = (f32[1,2,2,16,1024]{4,3,2,1,0:T(8,128)}, f32[1,2,1,8,1024]{4,3,2,1,0:T(8,128)}) custom-call(bf16[1,64,512]{2,1,0:T(8,128)(2,1)S(1)} %get-tuple-element.8.own, bf16[1,64,512]{2,1,0:T(8,128)(2,1)S(1)} %collective-permute-done.near, bf16[1,64,512]{2,1,0:T(8,128)(2,1)S(1)} %collective-permute-done.1.far, ...), custom_call_target="tpu_custom_call" | custom-call | flops 4000000000 | bytes 4000000 | tf_op jit(solution)/shard_map/outer_blocks/pallas_call | solution.py:587
Async XLA Ops:
  0.6 6.3 %collective-permute-start.1 = (bf16[1,64,512]{2,1,0:T(8,128)(2,1)}, bf16[1,64,512]{2,1,0:T(8,128)(2,1)S(1)}, u32[]{:S(2)}, u32[]{:S(2)}) collective-permute-start(bf16[1,64,512]{2,1,0:T(8,128)(2,1)} %own_hbm.1), channel_id=1, source_target_pairs={{8,0},{9,1},{10,2},{11,3},{12,4},{13,5},{14,6},{15,7},{24,16},{25,... | collective-permute-start | bytes 196616 | tf_op jit(solution)/shard_map/ppermute | solution.py:28
  1.9 8.5 %collective-permute-start = (bf16[1,64,512]{2,1,0:T(8,128)(2,1)}, bf16[1,64,512]{2,1,0:T(8,128)(2,1)S(1)}, u32[]{:S(2)}, u32[]{:S(2)}) collective-permute-start(bf16[1,64,512]{2,1,0:T(8,128)(2,1)} %own_hbm.1), channel_id=1, source_target_pairs={{4,0},{5,1},{6,2},{7,3},{8,4},{9,5},{10,6},{11,7},{12,8},{13,9},{1... | collective-permute-start | bytes 196616 | tf_op jit(solution)/shard_map/ppermute | solution.py:28
  3.2 12.4 %collective-permute-start.4 = (bf16[1,64,512]{2,1,0:T(8,128)(2,1)}, bf16[1,64,512]{2,1,0:T(8,128)(2,1)S(1)}, u32[]{:S(2)}, u32[]{:S(2)}) collective-permute-start(bf16[1,64,512]{2,1,0:T(8,128)(2,1)} %own_hbm.1), channel_id=1, source_target_pairs={{9,0},{10,1},{11,2},{13,4},{14,5},{15,6},{25,16},{26,17},{27,18},{... | collective-permute-start | bytes 196616 | tf_op jit(solution)/shard_map/ppermute | solution.py:28
  4.5 11.1 %collective-permute-start.3 = (bf16[1,64,512]{2,1,0:T(8,128)(2,1)}, bf16[1,64,512]{2,1,0:T(8,128)(2,1)S(1)}, u32[]{:S(2)}, u32[]{:S(2)}) collective-permute-start(bf16[1,64,512]{2,1,0:T(8,128)(2,1)} %own_hbm.1), channel_id=1, source_target_pairs={{5,0},{6,1},{7,2},{9,4},{10,5},{11,6},{13,8},{14,9},{15,10},{21,16... | collective-permute-start | bytes 196616 | tf_op jit(solution)/shard_map/ppermute | solution.py:28
  6.9 9.4 %collective-permute-start.2 = (bf16[1,64,512]{2,1,0:T(8,128)(2,1)}, bf16[1,64,512]{2,1,0:T(8,128)(2,1)S(1)}, u32[]{:S(2)}, u32[]{:S(2)}) collective-permute-start(bf16[1,64,512]{2,1,0:T(8,128)(2,1)} %own_hbm.1), channel_id=1, source_target_pairs={{1,0},{2,1},{3,2},{5,4},{6,5},{7,6},{9,8},{10,9},{11,10},{13,12},{... | collective-permute-start | bytes 196616 | tf_op jit(solution)/shard_map/ppermute | solution.py:28

commit v6 on v4

--- a/solution.py
+++ b/solution.py
@@ -470,7 +470,7 @@
 
 def inner_kernel(
     levels, cuts,
-    own_hbm, near, far, mask_hbm, table_hbm,
+    own_hbm, others, mask_hbm, table_hbm,
     maps, own, table_ref,
     mask, pad, row_ref, *rest,
 ):
@@ -489,7 +489,7 @@
     write_row_table(row_ref, levels[0])
     write_fine_table(table_ref, fine_at)
     size = 3 + 4 * len(levels)
-    strips = ((near,), (far,), (own,))
+    strips = ((others.at[0:1],), (others.at[1:2],), (own,))
     transform(levels, (0, 1), strips, row_ref, table_ref, scratch[:size])
     own_ready()
     transform(levels, (2,), strips, row_ref, table_ref, scratch[:size])
@@ -503,7 +503,7 @@
 
 def outer_kernel(
     levels, cuts, inner, row_at,
-    own, near, far, rim, rim_near, rim_far, mask_hbm, mask_coarse_hbm, table_ref, inner_maps,
+    own, others, rim, rims, mask_hbm, mask_coarse_hbm, table_ref, inner_maps,
     out_fine, out_coarse,
     mask, mask_coarse, pad, pad_coarse, maps, maps_coarse, *rest,
 ):
@@ -514,7 +514,7 @@
     fine_at, shift_at, map_at, coarse_at, end = cuts
     row_ref = table_ref.at[pl.ds(row_at, row_places(levels)[1])]
     size = 3 + 4 * len(levels)
-    strips = ((near, rim_near), (far, rim_far), (own, rim))
+    strips = ((others.at[0:1], rims.at[0:1]), (others.at[1:2], rims.at[1:2]), (own, rim))
     transform(levels, (0, 1, 2), strips, row_ref, table_ref, scratch[:size])
     for wait in masks_ready:
         wait()
@@ -529,7 +529,7 @@
         wait()
 
 
-def correlate(own, near, far, rim, rim_near, rim_far, mask_fine, mask_coarse):
+def correlate(own, others, rim, rims, mask_fine, mask_coarse):
     strip_rows, width = own.shape[1:]
     fine, coarse = mask_fine.shape[1], mask_coarse.shape[1]
     inner = fine - 1
@@ -562,7 +562,7 @@
             jax.ShapeDtypeStruct(own.shape, bf16),
             jax.ShapeDtypeStruct(table.shape, bf16),
         ),
-        in_specs=[hbm, vmem, vmem, hbm, hbm],
+        in_specs=[hbm, vmem, hbm, hbm],
         out_specs=(vmem,) * 3,
         scratch_shapes=[
             pltpu.VMEM(mask_fine.shape, jnp.int32),
@@ -575,14 +575,14 @@
         compiler_params=params,
         cost_estimate=cost(3 * 10**9),
         name="inner_blocks",
-    )(own, near, far, mask_fine, table)
+    )(own, others, mask_fine, table)
     return pl.pallas_call(
         functools.partial(outer_kernel, outer_levels, cuts, inner, row_at),
         out_shape=(
             jax.ShapeDtypeStruct((1, 2, fine, 4 * outer_levels[0].quads, shifts), f32),
             jax.ShapeDtypeStruct((1, 2, coarse, 4 * outer_levels[1].quads, shifts), f32),
         ),
-        in_specs=[vmem] * 6 + [hbm] * 2 + [vmem] * 2,
+        in_specs=[vmem] * 4 + [hbm] * 2 + [vmem] * 2,
         out_specs=(hbm, hbm),
         scratch_shapes=[
             pltpu.VMEM(mask_fine.shape, jnp.int32),
@@ -597,14 +597,16 @@
         compiler_params=params,
         cost_estimate=cost(4 * 10**9),
         name="outer_blocks",
-    )(own_kept, near, far, rim, rim_near, rim_far, mask_fine, mask_coarse, handed, maps)
+    )(own_kept, others, rim, rims, mask_fine, mask_coarse, handed, maps)
 
 
 def local(sections, mask_fine, mask_coarse):
     far = from_device(sections, 2, 0)
     near = from_device(sections, 1, 0)
-    rims = [from_device(sections, z, 1) for z in range(3)]
-    return correlate(sections, near, far, *rims, mask_fine, mask_coarse)
+    rim = from_device(sections, 0, 1)
+    others = jnp.concatenate([near, far], axis=0)
+    rims = from_device(others, 0, 1)
+    return correlate(sections, others, rim, rims, mask_fine, mask_coarse)
 
 
 def solution(mesh):

time: 20.2 us -> 21.2 us (1.050)
  the two profiles are of different devices: /device:TPU:9 before, /device:TPU:1 now
where the time goes in v6:
time: 21.2 us; the launch traced here: 21 us
  starting transfers between devices  8.17 us (39%)
  Pallas kernels  7.11 us (34%)
  waiting for transfers between devices  4.99 us (24%)
  between operations  0.68 us (3%)
    ppermute x4, starting transfers between devices, from_device(): return lax.ppermute(value, ('sec', 'strip'), pairs)  8.17 us
    ppermute x4, waiting for transfers between devices, from_device(): return lax.ppermute(value, ('sec', 'strip'), pairs)  4.99 us
    pallas_call x1, Pallas kernels, correlate(): pl.pallas_call(functools.partial(outer_kernel, outer_levels, cuts, inner,...  3.69 us
    pallas_call x1, Pallas kernels, correlate(): pl.pallas_call(functools.partial(inner_kernel, inner_levels, cuts), out_s...  3.42 us
  transfers between devices with their start and end apart: 4, of which 3 were waited for; matrix products, arithmetic and copies ran while one was open for 0% of the time, Pallas kernels for 16%

profile of v6, /device:TPU:1, one launch (start us, length us, event | category | flops | bytes accessed | tf_op | source)
XLA Modules:
  0.0 21.0 jit_solution(4227766404678636410)
XLA Ops:
  0.6 1.3 %collective-permute-start = (bf16[1,64,512]{2,1,0:T(8,128)(2,1)}, bf16[1,64,512]{2,1,0:T(8,128)(2,1)S(1)}, u32[]{:S(2)}, u32[]{:S(2)}) collective-permute-start(bf16[1,64,512]{2,1,0:T(8,128)(2,1)} %own_hbm.1), channel_id=1, source_target_pairs={{4,0},{5,1},{6,2},{7,3},{8,4},{9,5},{10,6},{11,7},{12,8},{13,9},{1... | collective-permute-start | bytes 196616 | tf_op jit(solution)/shard_map/ppermute | solution.py:28
  1.9 1.3 %collective-permute-start.1 = (bf16[1,64,512]{2,1,0:T(8,128)(2,1)}, bf16[1,64,512]{2,1,0:T(8,128)(2,1)S(1)}, u32[]{:S(2)}, u32[]{:S(2)}) collective-permute-start(bf16[1,64,512]{2,1,0:T(8,128)(2,1)} %own_hbm.1), channel_id=1, source_target_pairs={{8,0},{9,1},{10,2},{11,3},{12,4},{13,5},{14,6},{15,7},{24,16},{25,... | collective-permute-start | bytes 196616 | tf_op jit(solution)/shard_map/ppermute | solution.py:28
  3.2 2.0 %collective-permute-start.2 = (bf16[1,64,512]{2,1,0:T(8,128)(2,1)}, bf16[1,64,512]{2,1,0:T(8,128)(2,1)S(1)}, u32[]{:S(2)}, u32[]{:S(2)}) collective-permute-start(bf16[1,64,512]{2,1,0:T(8,128)(2,1)} %own_hbm.1), channel_id=1, source_target_pairs={{1,0},{2,1},{3,2},{5,4},{6,5},{7,6},{9,8},{10,9},{11,10},{13,12},{... | collective-permute-start | bytes 196616 | tf_op jit(solution)/shard_map/ppermute | solution.py:28
  5.2 1.3 %collective-permute-done = bf16[1,64,512]{2,1,0:T(8,128)(2,1)S(1)} collective-permute-done((bf16[1,64,512]{2,1,0:T(8,128)(2,1)}, bf16[1,64,512]{2,1,0:T(8,128)(2,1)S(1)}, u32[]{:S(2)}, u32[]{:S(2)}) %collective-permute-start) | collective-permute-done | bytes 65568 | tf_op jit(solution)/shard_map/ppermute | solution.py:28
  6.5 3.4 %collective-permute-done.1 = bf16[1,64,512]{2,1,0:T(8,128)(2,1)S(1)} collective-permute-done((bf16[1,64,512]{2,1,0:T(8,128)(2,1)}, bf16[1,64,512]{2,1,0:T(8,128)(2,1)S(1)}, u32[]{:S(2)}, u32[]{:S(2)}) %collective-permute-start.1) | collective-permute-done | bytes 65568 | tf_op jit(solution)/shard_map/ppermute | solution.py:28
  9.9 3.6 %collective-permute-start.3 = (bf16[2,64,512]{2,1,0:T(8,128)(2,1)S(1)}, bf16[2,64,512]{2,1,0:T(8,128)(2,1)S(1)}, u32[]{:S(2)}, u32[]{:S(2)}) collective-permute-start(bf16[2,64,512]{2,1,0:T(8,128)(2,1)S(1)} %constant_dynamic-update-slice_fusion.others), channel_id=1, source_target_pairs={{1,0},{2,1},{3,2},{5,4},{6,5},{7,6},{9,8},{10,9},{11,10},{13,12},{... | collective-permute-start | bytes 393224 | tf_op jit(solution)/shard_map/ppermute | solution.py:28
  13.5 3.4 %inner_blocks.1 = (f32[2,1,16,1024]{3,2,1,0:T(8,128)S(1)}, bf16[1,64,512]{2,1,0:T(8,128)(2,1)S(1)}, bf16[2272,256]{1,0:T(8,128)(2,1)S(1)}) custom-call(bf16[1,64,512]{2,1,0:T(8,128)(2,1)} %own_hbm.1, bf16[2,64,512]{2,1,0:T(8,128)(2,1)S(1)} %constant_dynamic-update-slice_fusion.others, s32[1,2,16]{2,1,0:T(2,128)} %mask_hbm.3, ...), custom_call_target="tpu_custom_call" | custom-call | flops 3000000000 | bytes 4000000 | tf_op jit(solution)/shard_map/inner_blocks/pallas_call | solution.py:558
  17.0 0.0 collective-permute-done.2.rim
  17.0 0.3 %collective-permute-done.3.rims = bf16[2,64,512]{2,1,0:T(8,128)(2,1)S(1)} collective-permute-done((bf16[2,64,512]{2,1,0:T(8,128)(2,1)S(1)}, bf16[2,64,512]{2,1,0:T(8,128)(2,1)S(1)}, u32[]{:S(2)}, u32[]{:S(2)}) %collective-permute-start.3) | collective-permute-done | bytes 131104 | tf_op jit(solution)/shard_map/ppermute | solution.py:28
  17.3 3.7 %outer_blocks.1 = (f32[1,2,2,16,1024]{4,3,2,1,0:T(8,128)}, f32[1,2,1,8,1024]{4,3,2,1,0:T(8,128)}) custom-call(bf16[1,64,512]{2,1,0:T(8,128)(2,1)S(1)} %get-tuple-element.5.own, bf16[2,64,512]{2,1,0:T(8,128)(2,1)S(1)} %constant_dynamic-update-slice_fusion.others, bf16[1,64,512]{2,1,0:T(8,128)(2,1)S(1)} %collective-permute-done.2.rim, ...), custom_call_target="tpu_custom_call" | custom-call | flops 4000000000 | bytes 4000000 | tf_op jit(solution)/shard_map/outer_blocks/pallas_call | solution.py:579
  (2 shorter events, 0.0 us)
Async XLA Ops:
  0.6 5.9 %collective-permute-start = (bf16[1,64,512]{2,1,0:T(8,128)(2,1)}, bf16[1,64,512]{2,1,0:T(8,128)(2,1)S(1)}, u32[]{:S(2)}, u32[]{:S(2)}) collective-permute-start(bf16[1,64,512]{2,1,0:T(8,128)(2,1)} %own_hbm.1), channel_id=1, source_target_pairs={{4,0},{5,1},{6,2},{7,3},{8,4},{9,5},{10,6},{11,7},{12,8},{13,9},{1... | collective-permute-start | bytes 196616 | tf_op jit(solution)/shard_map/ppermute | solution.py:28
  1.9 8.0 %collective-permute-start.1 = (bf16[1,64,512]{2,1,0:T(8,128)(2,1)}, bf16[1,64,512]{2,1,0:T(8,128)(2,1)S(1)}, u32[]{:S(2)}, u32[]{:S(2)}) collective-permute-start(bf16[1,64,512]{2,1,0:T(8,128)(2,1)} %own_hbm.1), channel_id=1, source_target_pairs={{8,0},{9,1},{10,2},{11,3},{12,4},{13,5},{14,6},{15,7},{24,16},{25,... | collective-permute-start | bytes 196616 | tf_op jit(solution)/shard_map/ppermute | solution.py:28
  3.2 13.7 %collective-permute-start.2 = (bf16[1,64,512]{2,1,0:T(8,128)(2,1)}, bf16[1,64,512]{2,1,0:T(8,128)(2,1)S(1)}, u32[]{:S(2)}, u32[]{:S(2)}) collective-permute-start(bf16[1,64,512]{2,1,0:T(8,128)(2,1)} %own_hbm.1), channel_id=1, source_target_pairs={{1,0},{2,1},{3,2},{5,4},{6,5},{7,6},{9,8},{10,9},{11,10},{13,12},{... | collective-permute-start | bytes 196616 | tf_op jit(solution)/shard_map/ppermute | solution.py:28
  9.9 7.4 %collective-permute-start.3 = (bf16[2,64,512]{2,1,0:T(8,128)(2,1)S(1)}, bf16[2,64,512]{2,1,0:T(8,128)(2,1)S(1)}, u32[]{:S(2)}, u32[]{:S(2)}) collective-permute-start(bf16[2,64,512]{2,1,0:T(8,128)(2,1)S(1)} %constant_dynamic-update-slice_fusion.others), channel_id=1, source_target_pairs={{1,0},{2,1},{3,2},{5,4},{6,5},{7,6},{9,8},{10,9},{11,10},{13,12},{... | collective-permute-start | bytes 393224 | tf_op jit(solution)/shard_map/ppermute | solution.py:28

commit v7 on v4

--- a/solution.py
+++ b/solution.py
@@ -307,11 +307,11 @@
         spec_ref[end : end + 2 * level.half] = jnp.concatenate(scaled, axis=0).astype(bf16)
 
 
-def transform(levels, sections, strips, row_ref, table_ref, scratch):
+def transform(levels, sections, strips, row_ref, table_ref, scratch, spec_refs):
     count = len(levels)
     t_ref, high_ref, low_ref = scratch[:3]
     odd_refs = scratch[3 : 3 + 2 * count]
-    f_refs, spec_refs = scratch[3 + 2 * count : 3 + 3 * count], scratch[3 + 3 * count :]
+    f_refs = scratch[3 + 2 * count :]
     places, size = row_places(levels)
     for z in sections:
         x = jnp.concatenate([strip[0] for strip in strips[z]], axis=0)
@@ -343,13 +343,13 @@
         scale_spectrum(level, f_ref, sections, spectrum_power(level, f_ref, sections), spec_ref)
 
 
-def write_maps(levels, specs, masks, table_ref, shift_at, map_at, scratch, outs):
+def write_maps(levels, own_specs, specs, masks, table_ref, shift_at, map_at, scratch, outs):
     cross_ref, y_ref, maps_ref, rows_ref, *stacks = scratch
     pairs = 2
     base = 0
-    for level, spec in zip(levels, specs):
+    for level, own, spec in zip(levels, own_specs, specs):
         def cross(at, rows):
-            a = spec[pairs * level.rows + at : pairs * level.rows + at + rows].astype(f32)
+            a = own[at : at + rows].astype(f32)
             ar, ai = a[:, :LANES], a[:, LANES:]
             for d in range(pairs):
                 b = spec[d * level.rows + at : d * level.rows + at + rows].astype(f32)
@@ -431,17 +431,20 @@
     return pad_ref[...]
 
 
-def section_scratch(levels, width):
+def section_scratch(levels, width, count):
     size = row_places(levels)[1]
     return [
-        pltpu.VMEM((3, size, width + LANES), f32),
-        pltpu.VMEM((3, size, width + LANES), bf16),
-        pltpu.VMEM((3, size, width + LANES), bf16),
-        *(pltpu.VMEM((3, level.quads * level.body + 2 * level.half, 2 * level.pool * LANES), bf16)
+        pltpu.VMEM((count, size, width + LANES), f32),
+        pltpu.VMEM((count, size, width + LANES), bf16),
+        pltpu.VMEM((count, size, width + LANES), bf16),
+        *(pltpu.VMEM((count, level.quads * level.body + 2 * level.half, 2 * level.pool * LANES), bf16)
           for level in levels for _ in range(2)),
-        *(pltpu.VMEM((3 * level.rows, 2 * LANES), f32) for level in levels),
-        *(pltpu.VMEM((3 * level.rows, 2 * LANES), bf16) for level in levels),
+        *(pltpu.VMEM((count * level.rows, 2 * LANES), f32) for level in levels),
     ]
+
+
+def spec_scratch(levels, count):
+    return [pltpu.VMEM((count * level.rows, 2 * LANES), bf16) for level in levels]
 
 
 def pair_scratch(levels):
@@ -488,22 +491,30 @@
     coarse_ready = table(coarse_at, end)
     write_row_table(row_ref, levels[0])
     write_fine_table(table_ref, fine_at)
-    size = 3 + 4 * len(levels)
+    size = 3 + 3 * len(levels)
+    sections, spec_refs, rest = scratch[:size], scratch[size : size + 1], scratch[size + 1 :]
     strips = ((near,), (far,), (own,))
-    transform(levels, (0, 1), strips, row_ref, table_ref, scratch[:size])
+    transform(levels, (0, 1), strips, row_ref, table_ref, sections, spec_refs)
     own_ready()
-    transform(levels, (2,), strips, row_ref, table_ref, scratch[:size])
+    transform(levels, (2,), strips, row_ref, table_ref, sections, spec_refs)
     shift_ready()
     mask_ready()
+    rows = levels[0].rows
     write_maps(
-        levels, scratch[size - len(levels) : size], (lambda: mask_tile(mask, pad),), table_ref, shift_at, map_at,
-        scratch[size:], (maps,))
+        levels, [spec_refs[0].at[pl.ds(2 * rows, rows)]], spec_refs, (lambda: mask_tile(mask, pad),), table_ref,
+        shift_at, map_at, rest, (maps,))
     coarse_ready()
+
+
+def own_kernel(levels, row_at, own, rim, table_ref, *rest):
+    spec_refs, sections = rest[: len(levels)], rest[len(levels) :]
+    row_ref = table_ref.at[pl.ds(row_at, row_places(levels)[1])]
+    transform(levels, (0,), ((own, rim),), row_ref, table_ref, sections, spec_refs)
 
 
 def outer_kernel(
     levels, cuts, inner, row_at,
-    own, near, far, rim, rim_near, rim_far, mask_hbm, mask_coarse_hbm, table_ref, inner_maps,
+    near, far, rim_near, rim_far, mask_hbm, mask_coarse_hbm, table_ref, own_fine, own_coarse, inner_maps,
     out_fine, out_coarse,
     mask, mask_coarse, pad, pad_coarse, maps, maps_coarse, *rest,
 ):
@@ -513,15 +524,16 @@
     stores = [start(inner_maps.at[d], out_fine.at[0, d, pl.ds(0, inner)]) for d in range(2)]
     fine_at, shift_at, map_at, coarse_at, end = cuts
     row_ref = table_ref.at[pl.ds(row_at, row_places(levels)[1])]
-    size = 3 + 4 * len(levels)
-    strips = ((near, rim_near), (far, rim_far), (own, rim))
-    transform(levels, (0, 1, 2), strips, row_ref, table_ref, scratch[:size])
+    size, count = 3 + 3 * len(levels), len(levels)
+    sections, spec_refs, rest = scratch[:size], scratch[size : size + count], scratch[size + count :]
+    strips = ((near, rim_near), (far, rim_far))
+    transform(levels, (0, 1), strips, row_ref, table_ref, sections, spec_refs)
     for wait in masks_ready:
         wait()
     write_maps(
-        levels, scratch[size - len(levels) : size],
+        levels, (own_fine, own_coarse), spec_refs,
         (lambda: mask_tile(mask, pad), lambda: mask_tile(mask_coarse, pad_coarse)), table_ref, shift_at, map_at,
-        scratch[size:], (maps, maps_coarse))
+        rest, (maps, maps_coarse))
     for d in range(2):
         stores.append(start(maps.at[d], out_fine.at[0, d, pl.ds(inner, levels[0].blocks)]))
         stores.append(start(maps_coarse.at[d], out_coarse.at[0, d]))
@@ -568,7 +580,8 @@
             pltpu.VMEM(mask_fine.shape, jnp.int32),
             pltpu.VMEM((8, LANES), f32),
             pltpu.VMEM((row_places(inner_levels)[1], 2 * strip_rows), bf16),
-            *section_scratch(inner_levels, width),
+            *section_scratch(inner_levels, width, 3),
+            *spec_scratch(inner_levels, 3),
             *pair_scratch(inner_levels),
             pltpu.SemaphoreType.DMA((4,)),
         ],
@@ -576,13 +589,23 @@
         cost_estimate=cost(3 * 10**9),
         name="inner_blocks",
     )(own, near, far, mask_fine, table)
+    own_specs = pl.pallas_call(
+        functools.partial(own_kernel, outer_levels, row_at),
+        out_shape=tuple(jax.ShapeDtypeStruct((level.rows, 2 * LANES), bf16) for level in outer_levels),
+        in_specs=[vmem] * 3,
+        out_specs=(vmem,) * 2,
+        scratch_shapes=section_scratch(outer_levels, width, 1),
+        compiler_params=params,
+        cost_estimate=cost(2 * 10**9),
+        name="own_outer_blocks",
+    )(own_kept, rim, handed)
     return pl.pallas_call(
         functools.partial(outer_kernel, outer_levels, cuts, inner, row_at),
         out_shape=(
             jax.ShapeDtypeStruct((1, 2, fine, 4 * outer_levels[0].quads, shifts), f32),
             jax.ShapeDtypeStruct((1, 2, coarse, 4 * outer_levels[1].quads, shifts), f32),
         ),
-        in_specs=[vmem] * 6 + [hbm] * 2 + [vmem] * 2,
+        in_specs=[vmem] * 4 + [hbm] * 2 + [vmem] * 4,
         out_specs=(hbm, hbm),
         scratch_shapes=[
             pltpu.VMEM(mask_fine.shape, jnp.int32),
@@ -590,14 +613,15 @@
             pltpu.VMEM((8, LANES), f32),
             pltpu.VMEM((8, LANES), f32),
             *(pltpu.VMEM((2, level.blocks, 4 * level.quads, shifts), f32) for level in outer_levels),
-            *section_scratch(outer_levels, width),
+            *section_scratch(outer_levels, width, 2),
+            *spec_scratch(outer_levels, 2),
             *pair_scratch(outer_levels),
             pltpu.SemaphoreType.DMA((8,)),
         ],
         compiler_params=params,
         cost_estimate=cost(4 * 10**9),
         name="outer_blocks",
-    )(own_kept, near, far, rim, rim_near, rim_far, mask_fine, mask_coarse, handed, maps)
+    )(near, far, rim_near, rim_far, mask_fine, mask_coarse, handed, *own_specs, maps)
 
 
 def local(sections, mask_fine, mask_coarse):

time: 20.2 us -> 19.1 us (0.946)
  the two profiles are of different devices: /device:TPU:9 before, /device:TPU:1 now
where the time goes in v7:
time: 19.1 us; the launch traced here: 18.9 us
  Pallas kernels  7.95 us (42%)
  starting transfers between devices  7.13 us (37%)
  waiting for transfers between devices  3.14 us (16%)
  between operations  0.7 us (4%)
    ppermute x5, starting transfers between devices, from_device(): return lax.ppermute(value, ('sec', 'strip'), pairs)  7.13 us
    pallas_call x1, Pallas kernels, correlate(): pl.pallas_call(functools.partial(inner_kernel, inner_levels, cuts), out_s...  3.42 us
    pallas_call x1, Pallas kernels, correlate(): pl.pallas_call(functools.partial(outer_kernel, outer_levels, cuts, inner,...  3.3 us
    ppermute x5, waiting for transfers between devices, from_device(): return lax.ppermute(value, ('sec', 'strip'), pairs)  3.14 us
    pallas_call x1, Pallas kernels, correlate(): pl.pallas_call(functools.partial(own_kernel, outer_levels, row_at), out_s...  1.24 us
  transfers between devices with their start and end apart: 5, of which 2 were waited for; matrix products, arithmetic and copies ran while one was open for 0% of the time, Pallas kernels for 25%

profile of v7, /device:TPU:1, one launch (start us, length us, event | category | flops | bytes accessed | tf_op | source)
XLA Modules:
  0.0 18.9 jit_solution(14961149787122633514)
XLA Ops:
  0.6 1.3 %collective-permute-start.1 = (bf16[1,64,512]{2,1,0:T(8,128)(2,1)}, bf16[1,64,512]{2,1,0:T(8,128)(2,1)S(1)}, u32[]{:S(2)}, u32[]{:S(2)}) collective-permute-start(bf16[1,64,512]{2,1,0:T(8,128)(2,1)} %own_hbm.1), channel_id=1, source_target_pairs={{8,0},{9,1},{10,2},{11,3},{12,4},{13,5},{14,6},{15,7},{24,16},{25,... | collective-permute-start | bytes 196616 | tf_op jit(solution)/shard_map/ppermute | solution.py:28
  1.9 1.3 %collective-permute-start = (bf16[1,64,512]{2,1,0:T(8,128)(2,1)}, bf16[1,64,512]{2,1,0:T(8,128)(2,1)S(1)}, u32[]{:S(2)}, u32[]{:S(2)}) collective-permute-start(bf16[1,64,512]{2,1,0:T(8,128)(2,1)} %own_hbm.1), channel_id=1, source_target_pairs={{4,0},{5,1},{6,2},{7,3},{8,4},{9,5},{10,6},{11,7},{12,8},{13,9},{1... | collective-permute-start | bytes 196616 | tf_op jit(solution)/shard_map/ppermute | solution.py:28
  3.2 1.3 %collective-permute-start.3 = (bf16[1,64,512]{2,1,0:T(8,128)(2,1)}, bf16[1,64,512]{2,1,0:T(8,128)(2,1)S(1)}, u32[]{:S(2)}, u32[]{:S(2)}) collective-permute-start(bf16[1,64,512]{2,1,0:T(8,128)(2,1)} %own_hbm.1), channel_id=1, source_target_pairs={{9,0},{10,1},{11,2},{13,4},{14,5},{15,6},{25,16},{26,17},{27,18},{... | collective-permute-start | bytes 196616 | tf_op jit(solution)/shard_map/ppermute | solution.py:28
  4.5 1.3 %collective-permute-start.2 = (bf16[1,64,512]{2,1,0:T(8,128)(2,1)}, bf16[1,64,512]{2,1,0:T(8,128)(2,1)S(1)}, u32[]{:S(2)}, u32[]{:S(2)}) collective-permute-start(bf16[1,64,512]{2,1,0:T(8,128)(2,1)} %own_hbm.1), channel_id=1, source_target_pairs={{5,0},{6,1},{7,2},{9,4},{10,5},{11,6},{13,8},{14,9},{15,10},{21,16... | collective-permute-start | bytes 196616 | tf_op jit(solution)/shard_map/ppermute | solution.py:28
  5.8 2.0 %collective-permute-start.4 = (bf16[1,64,512]{2,1,0:T(8,128)(2,1)}, bf16[1,64,512]{2,1,0:T(8,128)(2,1)S(1)}, u32[]{:S(2)}, u32[]{:S(2)}) collective-permute-start(bf16[1,64,512]{2,1,0:T(8,128)(2,1)} %own_hbm.1), channel_id=1, source_target_pairs={{1,0},{2,1},{3,2},{5,4},{6,5},{7,6},{9,8},{10,9},{11,10},{13,12},{... | collective-permute-start | bytes 196616 | tf_op jit(solution)/shard_map/ppermute | solution.py:28
  7.8 0.0 collective-permute-done.1.far
  7.8 1.4 %collective-permute-done.near = bf16[1,64,512]{2,1,0:T(8,128)(2,1)S(1)} collective-permute-done((bf16[1,64,512]{2,1,0:T(8,128)(2,1)}, bf16[1,64,512]{2,1,0:T(8,128)(2,1)S(1)}, u32[]{:S(2)}, u32[]{:S(2)}) %collective-permute-start) | collective-permute-done | bytes 65568 | tf_op jit(solution)/shard_map/ppermute | solution.py:28
  9.2 3.4 %inner_blocks.1 = (f32[2,1,16,1024]{3,2,1,0:T(8,128)S(1)}, bf16[1,64,512]{2,1,0:T(8,128)(2,1)S(1)}, bf16[2272,256]{1,0:T(8,128)(2,1)S(1)}) custom-call(bf16[1,64,512]{2,1,0:T(8,128)(2,1)} %own_hbm.1, bf16[1,64,512]{2,1,0:T(8,128)(2,1)S(1)} %collective-permute-done.near, bf16[1,64,512]{2,1,0:T(8,128)(2,1)S(1)} %collective-permute-done.1.far, ...), custom_call_target="tpu_custom_call" | custom-call | flops 3000000000 | bytes 4000000 | tf_op jit(solution)/shard_map/inner_blocks/pallas_call | solution.py:570
  12.7 0.0 collective-permute-done.4.rim
  12.7 1.2 %own_outer_blocks.1 = (bf16[272,256]{1,0:T(8,128)(2,1)S(1)}, bf16[144,256]{1,0:T(8,128)(2,1)S(1)}) custom-call(bf16[1,64,512]{2,1,0:T(8,128)(2,1)S(1)} %get-tuple-element.8.own, bf16[1,64,512]{2,1,0:T(8,128)(2,1)S(1)} %collective-permute-done.4.rim, bf16[2272,256]{1,0:T(8,128)(2,1)S(1)} %get-tuple-element.7.table_ref), custom_call_target="tpu_custom_call" | custom-call | flops 2000000000 | bytes 4000000 | tf_op jit(solution)/shard_map/own_outer_blocks/pallas_call | solution.py:592
  13.9 1.7 %collective-permute-done.3.rim_far = bf16[1,64,512]{2,1,0:T(8,128)(2,1)S(1)} collective-permute-done((bf16[1,64,512]{2,1,0:T(8,128)(2,1)}, bf16[1,64,512]{2,1,0:T(8,128)(2,1)S(1)}, u32[]{:S(2)}, u32[]{:S(2)}) %collective-permute-start.3) | collective-permute-done | bytes 65568 | tf_op jit(solution)/shard_map/ppermute | solution.py:28
  15.6 0.0 collective-permute-done.2.rim_near
  15.6 3.3 %outer_blocks.1 = (f32[1,2,2,16,1024]{4,3,2,1,0:T(8,128)}, f32[1,2,1,8,1024]{4,3,2,1,0:T(8,128)}) custom-call(bf16[1,64,512]{2,1,0:T(8,128)(2,1)S(1)} %collective-permute-done.near, bf16[1,64,512]{2,1,0:T(8,128)(2,1)S(1)} %collective-permute-done.1.far, bf16[1,64,512]{2,1,0:T(8,128)(2,1)S(1)} %collective-permute-done.2.rim_near, ...), custom_call_target="tpu_custom_call" | custom-call | flops 4000000000 | bytes 4000000 | tf_op jit(solution)/shard_map/outer_blocks/pallas_call | solution.py:602
Async XLA Ops:
  0.6 7.2 %collective-permute-start.1 = (bf16[1,64,512]{2,1,0:T(8,128)(2,1)}, bf16[1,64,512]{2,1,0:T(8,128)(2,1)S(1)}, u32[]{:S(2)}, u32[]{:S(2)}) collective-permute-start(bf16[1,64,512]{2,1,0:T(8,128)(2,1)} %own_hbm.1), channel_id=1, source_target_pairs={{8,0},{9,1},{10,2},{11,3},{12,4},{13,5},{14,6},{15,7},{24,16},{25,... | collective-permute-start | bytes 196616 | tf_op jit(solution)/shard_map/ppermute | solution.py:28
  1.9 7.3 %collective-permute-start = (bf16[1,64,512]{2,1,0:T(8,128)(2,1)}, bf16[1,64,512]{2,1,0:T(8,128)(2,1)S(1)}, u32[]{:S(2)}, u32[]{:S(2)}) collective-permute-start(bf16[1,64,512]{2,1,0:T(8,128)(2,1)} %own_hbm.1), channel_id=1, source_target_pairs={{4,0},{5,1},{6,2},{7,3},{8,4},{9,5},{10,6},{11,7},{12,8},{13,9},{1... | collective-permute-start | bytes 196616 | tf_op jit(solution)/shard_map/ppermute | solution.py:28
  3.2 12.4 %collective-permute-start.3 = (bf16[1,64,512]{2,1,0:T(8,128)(2,1)}, bf16[1,64,512]{2,1,0:T(8,128)(2,1)S(1)}, u32[]{:S(2)}, u32[]{:S(2)}) collective-permute-start(bf16[1,64,512]{2,1,0:T(8,128)(2,1)} %own_hbm.1), channel_id=1, source_target_pairs={{9,0},{10,1},{11,2},{13,4},{14,5},{15,6},{25,16},{26,17},{27,18},{... | collective-permute-start | bytes 196616 | tf_op jit(solution)/shard_map/ppermute | solution.py:28
  4.5 11.1 %collective-permute-start.2 = (bf16[1,64,512]{2,1,0:T(8,128)(2,1)}, bf16[1,64,512]{2,1,0:T(8,128)(2,1)S(1)}, u32[]{:S(2)}, u32[]{:S(2)}) collective-permute-start(bf16[1,64,512]{2,1,0:T(8,128)(2,1)} %own_hbm.1), channel_id=1, source_target_pairs={{5,0},{6,1},{7,2},{9,4},{10,5},{11,6},{13,8},{14,9},{15,10},{21,16... | collective-permute-start | bytes 196616 | tf_op jit(solution)/shard_map/ppermute | solution.py:28
  5.8 6.8 %collective-permute-start.4 = (bf16[1,64,512]{2,1,0:T(8,128)(2,1)}, bf16[1,64,512]{2,1,0:T(8,128)(2,1)S(1)}, u32[]{:S(2)}, u32[]{:S(2)}) collective-permute-start(bf16[1,64,512]{2,1,0:T(8,128)(2,1)} %own_hbm.1), channel_id=1, source_target_pairs={{1,0},{2,1},{3,2},{5,4},{6,5},{7,6},{9,8},{10,9},{11,10},{13,12},{... | collective-permute-start | bytes 196616 | tf_op jit(solution)/shard_map/ppermute | solution.py:28

commit v8 on v7

--- a/solution.py
+++ b/solution.py
@@ -307,11 +307,9 @@
         spec_ref[end : end + 2 * level.half] = jnp.concatenate(scaled, axis=0).astype(bf16)
 
 
-def transform(levels, sections, strips, row_ref, table_ref, scratch, spec_refs):
-    count = len(levels)
+def transform_rows(levels, sections, strips, row_ref, scratch):
     t_ref, high_ref, low_ref = scratch[:3]
-    odd_refs = scratch[3 : 3 + 2 * count]
-    f_refs = scratch[3 + 2 * count :]
+    odd_refs = scratch[3 : 3 + 2 * len(levels)]
     places, size = row_places(levels)
     for z in sections:
         x = jnp.concatenate([strip[0] for strip in strips[z]], axis=0)
@@ -333,6 +331,12 @@
         odds = odd_refs[2 * index : 2 * index + 2]
         for z in sections:
             gather_windows(level, place, t_ref.at[z], (high_ref.at[z], low_ref.at[z]), [ref.at[z] for ref in odds])
+
+
+def transform_columns(levels, sections, table_ref, scratch, spec_refs):
+    high_ref, low_ref = scratch[1:3]
+    odd_refs, f_refs = scratch[3 : 3 + 2 * len(levels)], scratch[3 + 2 * len(levels) :]
+    places, size = row_places(levels)
     for index, (level, place) in enumerate(zip(levels, places)):
         lefts = [
             jnp.concatenate([left_of(level, place, ref.at[z], odd.at[z]) for z in sections], axis=0)
@@ -343,9 +347,8 @@
         scale_spectrum(level, f_ref, sections, spectrum_power(level, f_ref, sections), spec_ref)
 
 
-def write_maps(levels, own_specs, specs, masks, table_ref, shift_at, map_at, scratch, outs):
+def write_maps(levels, pairs, own_specs, specs, kept, table_ref, shift_at, map_at, scratch, outs):
     cross_ref, y_ref, maps_ref, rows_ref, *stacks = scratch
-    pairs = 2
     base = 0
     for level, own, spec in zip(levels, own_specs, specs):
         def cross(at, rows):
@@ -369,7 +372,7 @@
                 value = jnp.concatenate([value, jnp.zeros((spare, 4 * LANES), f32)], axis=0)
             cross_ref[to + level.cross_body : to + level.cross_rows] = value.astype(bf16)
         base += pairs * level.cross_rows
-    y_ref[...] = dot(cross_ref[...], table_ref[shift_at : shift_at + 4 * LANES])
+    y_ref[:base] = dot(cross_ref[:base], table_ref[shift_at : shift_at + 4 * LANES])
     base = tile = 0
     starts = {}
     row = lax.broadcasted_iota(jnp.int32, (NYQ, LANES), 0)
@@ -391,7 +394,8 @@
                         for half, part in enumerate(split(value)):
                             to = half * (2 * HALF + NYQ) + at
                             stack_ref[to : to + value.shape[0], column : column + LANES] = part
-            both = dot(table_ref[map_at : map_at + 2 * WINDOW, : stack_ref.shape[0]], stack_ref[...])
+            columns = pairs * level.quads * LANES
+            both = dot(table_ref[map_at : map_at + 2 * WINDOW, : stack_ref.shape[0]], stack_ref[:, :columns])
             maps = both[:WINDOW] + both[WINDOW:]
             for d in range(pairs):
                 starts[index, d, b] = tile
@@ -400,7 +404,6 @@
                     maps_ref[tile] = maps[:, column : column + LANES]
                     tile += 1
         base += pairs * level.cross_rows
-    kept = [jnp.transpose(mask()) for mask in masks]
     lane = lax.broadcasted_iota(jnp.int32, (tile, LANES), 1)
 
     def exchange(low, high, width):
@@ -410,7 +413,7 @@
             jnp.where(even, pltpu.roll(low, LANES - width, 1), high))
 
     for big in range(WINDOW // 4):
-        rows = [maps_ref[:, 4 * big + r, :] for r in range(4)]
+        rows = [maps_ref[:tile, 4 * big + r, :] for r in range(4)]
         for step in (2, 1):
             for r in range(4):
                 if not r & step:
@@ -425,10 +428,27 @@
                     out[d, b, :, big * LANES : (big + 1) * LANES] = rows_ref[big, at : at + 4 * level.quads] * column
 
 
-def mask_tile(mask_ref, pad_ref):
+def write_mask_columns(mask_ref, pad_ref, kept_ref):
     pad_ref[...] = jnp.zeros(pad_ref.shape, f32)
     pad_ref[: mask_ref.shape[1], : mask_ref.shape[2]] = mask_ref[0].astype(f32)
-    return pad_ref[...]
+    kept_ref[...] = jnp.transpose(pad_ref[...])
+
+
+def sections_ahead():
+    return lax.axis_size("sec") - 1 - lax.axis_index("sec")
+
+
+def for_pairs(run):
+    ahead = sections_ahead()
+    pl.when(ahead >= 2)(lambda: run(2))
+    pl.when(ahead == 1)(lambda: run(1))
+    pl.when(ahead < 1)(lambda: run(0))
+
+
+def clear_maps(pairs, outs):
+    for out in outs:
+        if pairs < 2:
+            out[pairs:] = jnp.zeros((2 - pairs,) + out.shape[1:], f32)
 
 
 def section_scratch(levels, width, count):
@@ -473,9 +493,9 @@
 
 def inner_kernel(
     levels, cuts,
-    own_hbm, near, far, mask_hbm, table_hbm,
-    maps, own, table_ref,
-    mask, pad, row_ref, *rest,
+    own_hbm, near, far, mask_hbm, mask_coarse_hbm, table_hbm,
+    maps, own, table_ref, kept, kept_coarse,
+    mask, mask_coarse, pad, row_ref, *rest,
 ):
     *scratch, sems = rest
     start = copier(sems)
@@ -485,55 +505,70 @@
         return start(table_hbm.at[piece], table_ref.at[piece])
 
     fine_at, shift_at, map_at, coarse_at, end = cuts
-    own_ready = start(own_hbm, own)
-    shift_ready = table(shift_at, coarse_at)
-    mask_ready = start(mask_hbm, mask)
-    coarse_ready = table(coarse_at, end)
-    write_row_table(row_ref, levels[0])
-    write_fine_table(table_ref, fine_at)
+    copies = [
+        start(own_hbm, own), table(shift_at, coarse_at), start(mask_hbm, mask), start(mask_coarse_hbm, mask_coarse),
+        table(coarse_at, end)]
     size = 3 + 3 * len(levels)
     sections, spec_refs, rest = scratch[:size], scratch[size : size + 1], scratch[size + 1 :]
-    strips = ((near,), (far,), (own,))
-    transform(levels, (0, 1), strips, row_ref, table_ref, sections, spec_refs)
-    own_ready()
-    transform(levels, (2,), strips, row_ref, table_ref, sections, spec_refs)
-    shift_ready()
-    mask_ready()
+    strips = ((own,), (near,), (far,))
     rows = levels[0].rows
-    write_maps(
-        levels, [spec_refs[0].at[pl.ds(2 * rows, rows)]], spec_refs, (lambda: mask_tile(mask, pad),), table_ref,
-        shift_at, map_at, rest, (maps,))
-    coarse_ready()
+
+    def run(pairs):
+        others = range(1, pairs + 1)
+        if pairs:
+            write_row_table(row_ref, levels[0])
+            write_fine_table(table_ref, fine_at)
+            transform_rows(levels, others, strips, row_ref, sections)
+        for wait in copies:
+            wait()
+        if pairs:
+            write_mask_columns(mask, pad, kept)
+            write_mask_columns(mask_coarse, pad, kept_coarse)
+            transform_rows(levels, (0,), strips, row_ref, sections)
+            transform_columns(levels, range(pairs + 1), table_ref, sections, spec_refs)
+            write_maps(
+                levels, pairs, [spec_refs[0].at[pl.ds(0, rows)]], [spec_refs[0].at[pl.ds(rows, pairs * rows)]],
+                (kept,), table_ref, shift_at, map_at, rest, (maps,))
+        clear_maps(pairs, (maps,))
+
+    for_pairs(run)
 
 
 def own_kernel(levels, row_at, own, rim, table_ref, *rest):
     spec_refs, sections = rest[: len(levels)], rest[len(levels) :]
     row_ref = table_ref.at[pl.ds(row_at, row_places(levels)[1])]
-    transform(levels, (0,), ((own, rim),), row_ref, table_ref, sections, spec_refs)
+
+    @pl.when(sections_ahead() >= 1)
+    def _():
+        transform_rows(levels, (0,), ((own, rim),), row_ref, sections)
+        transform_columns(levels, (0,), table_ref, sections, spec_refs)
 
 
 def outer_kernel(
     levels, cuts, inner, row_at,
-    near, far, rim_near, rim_far, mask_hbm, mask_coarse_hbm, table_ref, own_fine, own_coarse, inner_maps,
+    near, far, rim_near, rim_far, table_ref, own_fine, own_coarse, kept, kept_coarse, inner_maps,
     out_fine, out_coarse,
-    mask, mask_coarse, pad, pad_coarse, maps, maps_coarse, *rest,
+    maps, maps_coarse, *rest,
 ):
     *scratch, sems = rest
     start = copier(sems)
-    masks_ready = [start(mask_hbm, mask), start(mask_coarse_hbm, mask_coarse)]
     stores = [start(inner_maps.at[d], out_fine.at[0, d, pl.ds(0, inner)]) for d in range(2)]
     fine_at, shift_at, map_at, coarse_at, end = cuts
     row_ref = table_ref.at[pl.ds(row_at, row_places(levels)[1])]
     size, count = 3 + 3 * len(levels), len(levels)
     sections, spec_refs, rest = scratch[:size], scratch[size : size + count], scratch[size + count :]
     strips = ((near, rim_near), (far, rim_far))
-    transform(levels, (0, 1), strips, row_ref, table_ref, sections, spec_refs)
-    for wait in masks_ready:
-        wait()
-    write_maps(
-        levels, (own_fine, own_coarse), spec_refs,
-        (lambda: mask_tile(mask, pad), lambda: mask_tile(mask_coarse, pad_coarse)), table_ref, shift_at, map_at,
-        rest, (maps, maps_coarse))
+
+    def run(pairs):
+        if pairs:
+            transform_rows(levels, range(pairs), strips, row_ref, sections)
+            transform_columns(levels, range(pairs), table_ref, sections, spec_refs)
+            write_maps(
+                levels, pairs, (own_fine, own_coarse), spec_refs, (kept, kept_coarse), table_ref, shift_at, map_at,
+                rest, (maps, maps_coarse))
+        clear_maps(pairs, (maps, maps_coarse))
+
+    for_pairs(run)
     for d in range(2):
         stores.append(start(maps.at[d], out_fine.at[0, d, pl.ds(inner, levels[0].blocks)]))
         stores.append(start(maps_coarse.at[d], out_coarse.at[0, d]))
@@ -567,28 +602,30 @@
     def cost(flops):
         return pl.CostEstimate(flops=flops, bytes_accessed=4 * 10**6, transcendentals=0)
 
-    maps, own_kept, handed = pl.pallas_call(
+    maps, own_kept, handed, *kept = pl.pallas_call(
         functools.partial(inner_kernel, inner_levels, cuts),
         out_shape=(
             jax.ShapeDtypeStruct((2, inner, 4 * inner_levels[0].quads, shifts), f32),
             jax.ShapeDtypeStruct(own.shape, bf16),
             jax.ShapeDtypeStruct(table.shape, bf16),
+            *(jax.ShapeDtypeStruct((LANES, 8), f32) for _ in range(2)),
         ),
-        in_specs=[hbm, vmem, vmem, hbm, hbm],
-        out_specs=(vmem,) * 3,
+        in_specs=[hbm, vmem, vmem, hbm, hbm, hbm],
+        out_specs=(vmem,) * 5,
         scratch_shapes=[
             pltpu.VMEM(mask_fine.shape, jnp.int32),
+            pltpu.VMEM(mask_coarse.shape, jnp.int32),
             pltpu.VMEM((8, LANES), f32),
             pltpu.VMEM((row_places(inner_levels)[1], 2 * strip_rows), bf16),
             *section_scratch(inner_levels, width, 3),
             *spec_scratch(inner_levels, 3),
             *pair_scratch(inner_levels),
-            pltpu.SemaphoreType.DMA((4,)),
+            pltpu.SemaphoreType.DMA((5,)),
         ],
         compiler_params=params,
         cost_estimate=cost(3 * 10**9),
         name="inner_blocks",
-    )(own, near, far, mask_fine, table)
+    )(own, near, far, mask_fine, mask_coarse, table)
     own_specs = pl.pallas_call(
         functools.partial(own_kernel, outer_levels, row_at),
         out_shape=tuple(jax.ShapeDtypeStruct((level.rows, 2 * LANES), bf16) for level in outer_levels),
@@ -605,23 +642,19 @@
             jax.ShapeDtypeStruct((1, 2, fine, 4 * outer_levels[0].quads, shifts), f32),
             jax.ShapeDtypeStruct((1, 2, coarse, 4 * outer_levels[1].quads, shifts), f32),
         ),
-        in_specs=[vmem] * 4 + [hbm] * 2 + [vmem] * 4,
+        in_specs=[vmem] * 10,
         out_specs=(hbm, hbm),
         scratch_shapes=[
-            pltpu.VMEM(mask_fine.shape, jnp.int32),
-            pltpu.VMEM(mask_coarse.shape, jnp.int32),
-            pltpu.VMEM((8, LANES), f32),
-            pltpu.VMEM((8, LANES), f32),
             *(pltpu.VMEM((2, level.blocks, 4 * level.quads, shifts), f32) for level in outer_levels),
             *section_scratch(outer_levels, width, 2),
             *spec_scratch(outer_levels, 2),
             *pair_scratch(outer_levels),
-            pltpu.SemaphoreType.DMA((8,)),
+            pltpu.SemaphoreType.DMA((6,)),
         ],
         compiler_params=params,
         cost_estimate=cost(4 * 10**9),
         name="outer_blocks",
-    )(near, far, rim_near, rim_far, mask_fine, mask_coarse, handed, *own_specs, maps)
+    )(near, far, rim_near, rim_far, handed, *own_specs, *kept, maps)
 
 
 def local(sections, mask_fine, mask_coarse):

time: 19.1 us -> 19 us (level)
  Pallas kernels: 7.95 us -> 7.67 us
  transfers between devices with their start and end apart: 5 -> 5, of which waited for: 2 -> 2; matrix products, arithmetic and copies ran while one was open for 0% -> 0% of each run, Pallas kernels for 25% -> 24%
where the time goes in v8:
time: 19 us; the launch traced here: 18.8 us
  Pallas kernels  7.67 us (40%)
  starting transfers between devices  7.13 us (38%)
  waiting for transfers between devices  3.28 us (17%)
  between operations  0.7 us (4%)
    ppermute x5, starting transfers between devices, from_device(): return lax.ppermute(value, ('sec', 'strip'), pairs)  7.13 us
    ppermute x5, waiting for transfers between devices, from_device(): return lax.ppermute(value, ('sec', 'strip'), pairs)  3.28 us
    pallas_call x1, Pallas kernels, correlate(): pl.pallas_call(functools.partial(inner_kernel, inner_levels, cuts), out_s...  3.27 us
    pallas_call x1, Pallas kernels, correlate(): pl.pallas_call(functools.partial(outer_kernel, outer_levels, cuts, inner,...  3.16 us
    pallas_call x1, Pallas kernels, correlate(): pl.pallas_call(functools.partial(own_kernel, outer_levels, row_at), out_s...  1.25 us
  transfers between devices with their start and end apart: 5, of which 2 were waited for; matrix products, arithmetic and copies ran while one was open for 0% of the time, Pallas kernels for 24%

profile of v8, /device:TPU:1, one launch (start us, length us, event | category | flops | bytes accessed | tf_op | source)
XLA Modules:
  0.0 18.8 jit_solution(13018713074380277074)
XLA Ops:
  0.6 1.3 %collective-permute-start.1 = (bf16[1,64,512]{2,1,0:T(8,128)(2,1)}, bf16[1,64,512]{2,1,0:T(8,128)(2,1)S(1)}, u32[]{:S(2)}, u32[]{:S(2)}) collective-permute-start(bf16[1,64,512]{2,1,0:T(8,128)(2,1)} %own_hbm.1), channel_id=1, source_target_pairs={{8,0},{9,1},{10,2},{11,3},{12,4},{13,5},{14,6},{15,7},{24,16},{25,... | collective-permute-start | bytes 196616 | tf_op jit(solution)/shard_map/ppermute | solution.py:28
  1.9 1.3 %collective-permute-start = (bf16[1,64,512]{2,1,0:T(8,128)(2,1)}, bf16[1,64,512]{2,1,0:T(8,128)(2,1)S(1)}, u32[]{:S(2)}, u32[]{:S(2)}) collective-permute-start(bf16[1,64,512]{2,1,0:T(8,128)(2,1)} %own_hbm.1), channel_id=1, source_target_pairs={{4,0},{5,1},{6,2},{7,3},{8,4},{9,5},{10,6},{11,7},{12,8},{13,9},{1... | collective-permute-start | bytes 196616 | tf_op jit(solution)/shard_map/ppermute | solution.py:28
  3.2 1.3 %collective-permute-start.3 = (bf16[1,64,512]{2,1,0:T(8,128)(2,1)}, bf16[1,64,512]{2,1,0:T(8,128)(2,1)S(1)}, u32[]{:S(2)}, u32[]{:S(2)}) collective-permute-start(bf16[1,64,512]{2,1,0:T(8,128)(2,1)} %own_hbm.1), channel_id=1, source_target_pairs={{9,0},{10,1},{11,2},{13,4},{14,5},{15,6},{25,16},{26,17},{27,18},{... | collective-permute-start | bytes 196616 | tf_op jit(solution)/shard_map/ppermute | solution.py:28
  4.5 1.3 %collective-permute-start.2 = (bf16[1,64,512]{2,1,0:T(8,128)(2,1)}, bf16[1,64,512]{2,1,0:T(8,128)(2,1)S(1)}, u32[]{:S(2)}, u32[]{:S(2)}) collective-permute-start(bf16[1,64,512]{2,1,0:T(8,128)(2,1)} %own_hbm.1), channel_id=1, source_target_pairs={{5,0},{6,1},{7,2},{9,4},{10,5},{11,6},{13,8},{14,9},{15,10},{21,16... | collective-permute-start | bytes 196616 | tf_op jit(solution)/shard_map/ppermute | solution.py:28
  5.8 2.0 %collective-permute-start.4 = (bf16[1,64,512]{2,1,0:T(8,128)(2,1)}, bf16[1,64,512]{2,1,0:T(8,128)(2,1)S(1)}, u32[]{:S(2)}, u32[]{:S(2)}) collective-permute-start(bf16[1,64,512]{2,1,0:T(8,128)(2,1)} %own_hbm.1), channel_id=1, source_target_pairs={{1,0},{2,1},{3,2},{5,4},{6,5},{7,6},{9,8},{10,9},{11,10},{13,12},{... | collective-permute-start | bytes 196616 | tf_op jit(solution)/shard_map/ppermute | solution.py:28
  7.8 0.0 collective-permute-done.1.far
  7.8 1.4 %collective-permute-done.near = bf16[1,64,512]{2,1,0:T(8,128)(2,1)S(1)} collective-permute-done((bf16[1,64,512]{2,1,0:T(8,128)(2,1)}, bf16[1,64,512]{2,1,0:T(8,128)(2,1)S(1)}, u32[]{:S(2)}, u32[]{:S(2)}) %collective-permute-start) | collective-permute-done | bytes 65568 | tf_op jit(solution)/shard_map/ppermute | solution.py:28
  9.2 3.3 %inner_blocks.1 = (f32[2,1,16,1024]{3,2,1,0:T(8,128)S(1)}, bf16[1,64,512]{2,1,0:T(8,128)(2,1)S(1)}, bf16[2272,256]{1,0:T(8,128)(2,1)S(1)}, f32[128,8]{1,0:T(8,128)S(1)}, f32[128,8]{1,0:T(8,128)S(1)}) custom-call(bf16[1,64,512]{2,1,0:T(8,128)(2,1)} %own_hbm.1, bf16[1,64,512]{2,1,0:T(8,128)(2,1)S(1)} %collective-permute-done.near, ...), custom_call_target="tpu_custom_call" | custom-call | flops 3000000000 | bytes 4000000 | tf_op jit(solution)/shard_map/inner_blocks/pallas_call | solution.py:605
  12.5 0.0 collective-permute-done.4.rim
  12.5 1.2 %own_outer_blocks.1 = (bf16[272,256]{1,0:T(8,128)(2,1)S(1)}, bf16[144,256]{1,0:T(8,128)(2,1)S(1)}) custom-call(bf16[1,64,512]{2,1,0:T(8,128)(2,1)S(1)} %get-tuple-element.10.own, bf16[1,64,512]{2,1,0:T(8,128)(2,1)S(1)} %collective-permute-done.4.rim, bf16[2272,256]{1,0:T(8,128)(2,1)S(1)} %get-tuple-element.9.table_ref), custom_call_target="tpu_custom_call" | custom-call | flops 2000000000 | bytes 4000000 | tf_op jit(solution)/shard_map/own_outer_blocks/pallas_call | solution.py:629
  13.8 1.8 %collective-permute-done.3.rim_far = bf16[1,64,512]{2,1,0:T(8,128)(2,1)S(1)} collective-permute-done((bf16[1,64,512]{2,1,0:T(8,128)(2,1)}, bf16[1,64,512]{2,1,0:T(8,128)(2,1)S(1)}, u32[]{:S(2)}, u32[]{:S(2)}) %collective-permute-start.3) | collective-permute-done | bytes 65568 | tf_op jit(solution)/shard_map/ppermute | solution.py:28
  15.6 0.0 collective-permute-done.2.rim_near
  15.6 3.2 %outer_blocks.1 = (f32[1,2,2,16,1024]{4,3,2,1,0:T(8,128)}, f32[1,2,1,8,1024]{4,3,2,1,0:T(8,128)}) custom-call(bf16[1,64,512]{2,1,0:T(8,128)(2,1)S(1)} %collective-permute-done.near, bf16[1,64,512]{2,1,0:T(8,128)(2,1)S(1)} %collective-permute-done.1.far, bf16[1,64,512]{2,1,0:T(8,128)(2,1)S(1)} %collective-permute-done.2.rim_near, ...), custom_call_target="tpu_custom_call" | custom-call | flops 4000000000 | bytes 4000000 | tf_op jit(solution)/shard_map/outer_blocks/pallas_call | solution.py:639
Async XLA Ops:
  0.6 7.2 %collective-permute-start.1 = (bf16[1,64,512]{2,1,0:T(8,128)(2,1)}, bf16[1,64,512]{2,1,0:T(8,128)(2,1)S(1)}, u32[]{:S(2)}, u32[]{:S(2)}) collective-permute-start(bf16[1,64,512]{2,1,0:T(8,128)(2,1)} %own_hbm.1), channel_id=1, source_target_pairs={{8,0},{9,1},{10,2},{11,3},{12,4},{13,5},{14,6},{15,7},{24,16},{25,... | collective-permute-start | bytes 196616 | tf_op jit(solution)/shard_map/ppermute | solution.py:28
  1.9 7.3 %collective-permute-start = (bf16[1,64,512]{2,1,0:T(8,128)(2,1)}, bf16[1,64,512]{2,1,0:T(8,128)(2,1)S(1)}, u32[]{:S(2)}, u32[]{:S(2)}) collective-permute-start(bf16[1,64,512]{2,1,0:T(8,128)(2,1)} %own_hbm.1), channel_id=1, source_target_pairs={{4,0},{5,1},{6,2},{7,3},{8,4},{9,5},{10,6},{11,7},{12,8},{13,9},{1... | collective-permute-start | bytes 196616 | tf_op jit(solution)/shard_map/ppermute | solution.py:28
  3.2 12.4 %collective-permute-start.3 = (bf16[1,64,512]{2,1,0:T(8,128)(2,1)}, bf16[1,64,512]{2,1,0:T(8,128)(2,1)S(1)}, u32[]{:S(2)}, u32[]{:S(2)}) collective-permute-start(bf16[1,64,512]{2,1,0:T(8,128)(2,1)} %own_hbm.1), channel_id=1, source_target_pairs={{9,0},{10,1},{11,2},{13,4},{14,5},{15,6},{25,16},{26,17},{27,18},{... | collective-permute-start | bytes 196616 | tf_op jit(solution)/shard_map/ppermute | solution.py:28
  4.5 11.1 %collective-permute-start.2 = (bf16[1,64,512]{2,1,0:T(8,128)(2,1)}, bf16[1,64,512]{2,1,0:T(8,128)(2,1)S(1)}, u32[]{:S(2)}, u32[]{:S(2)}) collective-permute-start(bf16[1,64,512]{2,1,0:T(8,128)(2,1)} %own_hbm.1), channel_id=1, source_target_pairs={{5,0},{6,1},{7,2},{9,4},{10,5},{11,6},{13,8},{14,9},{15,10},{21,16... | collective-permute-start | bytes 196616 | tf_op jit(solution)/shard_map/ppermute | solution.py:28
  5.8 6.7 %collective-permute-start.4 = (bf16[1,64,512]{2,1,0:T(8,128)(2,1)}, bf16[1,64,512]{2,1,0:T(8,128)(2,1)S(1)}, u32[]{:S(2)}, u32[]{:S(2)}) collective-permute-start(bf16[1,64,512]{2,1,0:T(8,128)(2,1)} %own_hbm.1), channel_id=1, source_target_pairs={{1,0},{2,1},{3,2},{5,4},{6,5},{7,6},{9,8},{10,9},{11,10},{13,12},{... | collective-permute-start | bytes 196616 | tf_op jit(solution)/shard_map/ppermute | solution.py:28

commit v9 on v8

--- a/solution.py
+++ b/solution.py
@@ -534,38 +534,41 @@
     for_pairs(run)
 
 
-def own_kernel(levels, row_at, own, rim, table_ref, *rest):
-    spec_refs, sections = rest[: len(levels)], rest[len(levels) :]
-    row_ref = table_ref.at[pl.ds(row_at, row_places(levels)[1])]
-
-    @pl.when(sections_ahead() >= 1)
-    def _():
-        transform_rows(levels, (0,), ((own, rim),), row_ref, sections)
-        transform_columns(levels, (0,), table_ref, sections, spec_refs)
-
-
 def outer_kernel(
     levels, cuts, inner, row_at,
-    near, far, rim_near, rim_far, table_ref, own_fine, own_coarse, kept, kept_coarse, inner_maps,
+    own, near, far, gathered_hbm, table_ref, kept, kept_coarse, inner_maps,
     out_fine, out_coarse,
-    maps, maps_coarse, *rest,
+    rims, maps, maps_coarse, *rest,
 ):
     *scratch, sems = rest
     start = copier(sems)
+    secs, strip_count = lax.axis_size("sec"), lax.axis_size("strip")
+    sec, strip = lax.axis_index("sec"), lax.axis_index("strip")
+    below = jnp.minimum(strip + 1, strip_count - 1)
+    loads = [
+        start(gathered_hbm.at[jnp.minimum(sec + z, secs - 1) * strip_count + below], rims.at[z]) for z in range(3)]
     stores = [start(inner_maps.at[d], out_fine.at[0, d, pl.ds(0, inner)]) for d in range(2)]
     fine_at, shift_at, map_at, coarse_at, end = cuts
     row_ref = table_ref.at[pl.ds(row_at, row_places(levels)[1])]
     size, count = 3 + 3 * len(levels), len(levels)
     sections, spec_refs, rest = scratch[:size], scratch[size : size + count], scratch[size + count :]
-    strips = ((near, rim_near), (far, rim_far))
+    strips = ((own, rims.at[0]), (near, rims.at[1]), (far, rims.at[2]))
+    for wait in loads:
+        wait()
+
+    @pl.when(strip == strip_count - 1)
+    def _():
+        rims[...] = jnp.zeros(rims.shape, bf16)
 
     def run(pairs):
         if pairs:
-            transform_rows(levels, range(pairs), strips, row_ref, sections)
-            transform_columns(levels, range(pairs), table_ref, sections, spec_refs)
+            transform_rows(levels, range(pairs + 1), strips, row_ref, sections)
+            transform_columns(levels, range(pairs + 1), table_ref, sections, spec_refs)
             write_maps(
-                levels, pairs, (own_fine, own_coarse), spec_refs, (kept, kept_coarse), table_ref, shift_at, map_at,
-                rest, (maps, maps_coarse))
+                levels, pairs,
+                [spec.at[pl.ds(0, level.rows)] for level, spec in zip(levels, spec_refs)],
+                [spec.at[pl.ds(level.rows, pairs * level.rows)] for level, spec in zip(levels, spec_refs)],
+                (kept, kept_coarse), table_ref, shift_at, map_at, rest, (maps, maps_coarse))
         clear_maps(pairs, (maps, maps_coarse))
 
     for_pairs(run)
@@ -576,7 +579,7 @@
         wait()
 
 
-def correlate(own, near, far, rim, rim_near, rim_far, mask_fine, mask_coarse):
+def correlate(own, near, far, gathered, mask_fine, mask_coarse):
     strip_rows, width = own.shape[1:]
     fine, coarse = mask_fine.shape[1], mask_coarse.shape[1]
     inner = fine - 1
@@ -595,9 +598,9 @@
     hbm = pl.BlockSpec(memory_space=pltpu.HBM)
     vmem = pl.BlockSpec(memory_space=pltpu.VMEM)
     params = pltpu.CompilerParams(vmem_limit_bytes=28 * 1024 * 1024)
-    own, table, mask_fine, mask_coarse = (
+    own, gathered, table, mask_fine, mask_coarse = (
         pltpu.with_memory_space_constraint(value, pltpu.HBM)
-        for value in (own, jnp.asarray(table), mask_fine, mask_coarse))
+        for value in (own, gathered, jnp.asarray(table), mask_fine, mask_coarse))
 
     def cost(flops):
         return pl.CostEstimate(flops=flops, bytes_accessed=4 * 10**6, transcendentals=0)
@@ -626,42 +629,33 @@
         cost_estimate=cost(3 * 10**9),
         name="inner_blocks",
     )(own, near, far, mask_fine, mask_coarse, table)
-    own_specs = pl.pallas_call(
-        functools.partial(own_kernel, outer_levels, row_at),
-        out_shape=tuple(jax.ShapeDtypeStruct((level.rows, 2 * LANES), bf16) for level in outer_levels),
-        in_specs=[vmem] * 3,
-        out_specs=(vmem,) * 2,
-        scratch_shapes=section_scratch(outer_levels, width, 1),
-        compiler_params=params,
-        cost_estimate=cost(2 * 10**9),
-        name="own_outer_blocks",
-    )(own_kept, rim, handed)
     return pl.pallas_call(
         functools.partial(outer_kernel, outer_levels, cuts, inner, row_at),
         out_shape=(
             jax.ShapeDtypeStruct((1, 2, fine, 4 * outer_levels[0].quads, shifts), f32),
             jax.ShapeDtypeStruct((1, 2, coarse, 4 * outer_levels[1].quads, shifts), f32),
         ),
-        in_specs=[vmem] * 10,
+        in_specs=[vmem] * 3 + [hbm] + [vmem] * 4,
         out_specs=(hbm, hbm),
         scratch_shapes=[
+            pltpu.VMEM((3,) + own.shape, bf16),
             *(pltpu.VMEM((2, level.blocks, 4 * level.quads, shifts), f32) for level in outer_levels),
-            *section_scratch(outer_levels, width, 2),
-            *spec_scratch(outer_levels, 2),
+            *section_scratch(outer_levels, width, 3),
+            *spec_scratch(outer_levels, 3),
             *pair_scratch(outer_levels),
-            pltpu.SemaphoreType.DMA((6,)),
+            pltpu.SemaphoreType.DMA((9,)),
         ],
         compiler_params=params,
         cost_estimate=cost(4 * 10**9),
         name="outer_blocks",
-    )(near, far, rim_near, rim_far, handed, *own_specs, *kept, maps)
+    )(own_kept, near, far, gathered, handed, *kept, maps)
 
 
 def local(sections, mask_fine, mask_coarse):
     far = from_device(sections, 2, 0)
     near = from_device(sections, 1, 0)
-    rims = [from_device(sections, z, 1) for z in range(3)]
-    return correlate(sections, near, far, *rims, mask_fine, mask_coarse)
+    gathered = lax.all_gather(sections, ("sec", "strip"))
+    return correlate(sections, near, far, gathered, mask_fine, mask_coarse)
 
 
 def solution(mesh):

time: 19 us -> 62.4 us (3.28)
  waiting for transfers between devices: 3.28 us -> 37.6 us
  between operations: 0.7 us -> 14.1 us
  starting transfers between devices: 7.13 us -> 2.62 us
    all_gather x0 -> x1, waiting for transfers between devices: none -> 30.9 us  [local(): gathered = lax.all_gather(sections, ('sec', 'strip'))]
    ppermute x5 -> x2, starting transfers between devices: 7.13 us -> 2.58 us  [from_device(): return lax.ppermute(value, ('sec', 'strip'), pairs)]
    ppermute x5 -> x2, waiting for transfers between devices: 3.28 us -> 6.02 us  [from_device(): return lax.ppermute(value, ('sec', 'strip'), pairs)]
    pallas_call x1, Pallas kernels: 3.16 us -> 4.51 us  [correlate(): pl.pallas_call(functools.partial(outer_kernel, outer_levels, cuts, inner,...]
    pallas_call x1 -> x0, Pallas kernels: 1.25 us -> none  [correlate(): pl.pallas_call(functools.partial(own_kernel, outer_levels, row_at), out_s...]
    unnamed x0 -> x1, waiting for transfers between devices: none -> 0.68 us
  transfers between devices with their start and end apart: 5 -> 3, of which waited for: 2 -> 3; matrix products, arithmetic and copies ran while one was open for 0% -> 0% of each run, Pallas kernels for 24% -> 5%
where the time goes in v9:
time: 62.4 us; the launch traced here: 62 us
  waiting for transfers between devices  37.6 us (60%)
  between operations  14.1 us (23%)
  Pallas kernels  7.77 us (12%)
  starting transfers between devices  2.62 us (4%)
    all_gather x1, waiting for transfers between devices, local(): gathered = lax.all_gather(sections, ('sec', 'strip'))  30.9 us
    ppermute x2, waiting for transfers between devices, from_device(): return lax.ppermute(value, ('sec', 'strip'), pairs)  6.02 us
    pallas_call x1, Pallas kernels, correlate(): pl.pallas_call(functools.partial(outer_kernel, outer_levels, cuts, inner,...  4.51 us
    pallas_call x1, Pallas kernels, correlate(): pl.pallas_call(functools.partial(inner_kernel, inner_levels, cuts), out_s...  3.26 us
    ppermute x2, starting transfers between devices, from_device(): return lax.ppermute(value, ('sec', 'strip'), pairs)  2.58 us
  transfers between devices with their start and end apart: 3, of which 3 were waited for; matrix products, arithmetic and copies ran while one was open for 0% of the time, Pallas kernels for 5%

profile of v9, /device:TPU:1, one launch (start us, length us, event | category | flops | bytes accessed | tf_op | source)
XLA Modules:
  0.0 62.0 jit_solution(7707375332254026895)
XLA Ops:
  7.2 0.0 all-gather.3.cloned.1.call-start
  7.2 0.7 %all-gather.3.cloned.1.call-update = ((bf16[1,64,512]{2,1,0:T(8,128)(2,1)}), bf16[16,64,512]{2,1,0:T(8,128)(2,1)}) async-update(((), (), s32[]{:S(2)}) %all-gather.3.cloned.1.call-start, bf16[1,64,512]{2,1,0:T(8,128)(2,1)} %own_hbm.1) | async-update | bytes 1179672
  7.9 1.3 %collective-permute-start.1 = (bf16[1,64,512]{2,1,0:T(8,128)(2,1)}, bf16[1,64,512]{2,1,0:T(8,128)(2,1)S(1)}, u32[]{:S(2)}, u32[]{:S(2)}) collective-permute-start(bf16[1,64,512]{2,1,0:T(8,128)(2,1)} %own_hbm.1), channel_id=1, source_target_pairs={{8,0},{9,1},{10,2},{11,3},{12,4},{13,5},{14,6},{15,7},{24,16},{25,... | collective-permute-start | bytes 196616 | tf_op jit(solution)/shard_map/ppermute | solution.py:28
  9.2 1.3 %collective-permute-start = (bf16[1,64,512]{2,1,0:T(8,128)(2,1)}, bf16[1,64,512]{2,1,0:T(8,128)(2,1)S(1)}, u32[]{:S(2)}, u32[]{:S(2)}) collective-permute-start(bf16[1,64,512]{2,1,0:T(8,128)(2,1)} %own_hbm.1), channel_id=1, source_target_pairs={{4,0},{5,1},{6,2},{7,3},{8,4},{9,5},{10,6},{11,7},{12,8},{13,9},{1... | collective-permute-start | bytes 196616 | tf_op jit(solution)/shard_map/ppermute | solution.py:28
  10.5 3.7 %collective-permute-done.1.far = bf16[1,64,512]{2,1,0:T(8,128)(2,1)S(1)} collective-permute-done((bf16[1,64,512]{2,1,0:T(8,128)(2,1)}, bf16[1,64,512]{2,1,0:T(8,128)(2,1)S(1)}, u32[]{:S(2)}, u32[]{:S(2)}) %collective-permute-start.1) | collective-permute-done | bytes 65568 | tf_op jit(solution)/shard_map/ppermute | solution.py:28
  14.2 2.3 %collective-permute-done.near = bf16[1,64,512]{2,1,0:T(8,128)(2,1)S(1)} collective-permute-done((bf16[1,64,512]{2,1,0:T(8,128)(2,1)}, bf16[1,64,512]{2,1,0:T(8,128)(2,1)S(1)}, u32[]{:S(2)}, u32[]{:S(2)}) %collective-permute-start) | collective-permute-done | bytes 65568 | tf_op jit(solution)/shard_map/ppermute | solution.py:28
  16.5 3.3 %inner_blocks.1 = (f32[2,1,16,1024]{3,2,1,0:T(8,128)S(1)}, bf16[1,64,512]{2,1,0:T(8,128)(2,1)S(1)}, bf16[2272,256]{1,0:T(8,128)(2,1)S(1)}, f32[128,8]{1,0:T(8,128)S(1)}, f32[128,8]{1,0:T(8,128)S(1)}) custom-call(bf16[1,64,512]{2,1,0:T(8,128)(2,1)} %own_hbm.1, bf16[1,64,512]{2,1,0:T(8,128)(2,1)S(1)} %collective-permute-done.near, ...), custom_call_target="tpu_custom_call" | custom-call | flops 3000000000 | bytes 4000000 | tf_op jit(solution)/shard_map/inner_blocks/pallas_call | solution.py:608
  19.8 30.9 %all-gather.3.cloned.1.call-done = bf16[16,64,512]{2,1,0:T(8,128)(2,1)} async-done(((bf16[1,64,512]{2,1,0:T(8,128)(2,1)}), bf16[16,64,512]{2,1,0:T(8,128)(2,1)}) %all-gather.3.cloned.1.call-update) | async-done | bytes 1048592 | tf_op jit(solution)/shard_map/all_gather | solution.py:657
  50.7 4.5 %outer_blocks.1 = (f32[1,2,2,16,1024]{4,3,2,1,0:T(8,128)}, f32[1,2,1,8,1024]{4,3,2,1,0:T(8,128)}) custom-call(bf16[1,64,512]{2,1,0:T(8,128)(2,1)S(1)} %get-tuple-element.7.own, bf16[1,64,512]{2,1,0:T(8,128)(2,1)S(1)} %collective-permute-done.near, bf16[1,64,512]{2,1,0:T(8,128)(2,1)S(1)} %collective-permute-done.1.far, bf16[16,1,64,512]{3,2,1,0:T(8,128)(2,1)} %bitcast.1, ...), custom_call_target="tpu_custom_call" | custom-call | flops 4000000000 | bytes 4000000 | tf_op jit(solution)/shard_map/outer_blocks/pallas_call | solution.py:632
Async XLA Ops:
  7.2 43.5 %all-gather.3.cloned.1.call-start = ((), (), s32[]{:S(2)}) async-start(), calls=%async_computation | async-start | bytes 1114112 | tf_op jit(solution)/shard_map/all_gather | solution.py:657
  7.9 6.3 %collective-permute-start.1 = (bf16[1,64,512]{2,1,0:T(8,128)(2,1)}, bf16[1,64,512]{2,1,0:T(8,128)(2,1)S(1)}, u32[]{:S(2)}, u32[]{:S(2)}) collective-permute-start(bf16[1,64,512]{2,1,0:T(8,128)(2,1)} %own_hbm.1), channel_id=1, source_target_pairs={{8,0},{9,1},{10,2},{11,3},{12,4},{13,5},{14,6},{15,7},{24,16},{25,... | collective-permute-start | bytes 196616 | tf_op jit(solution)/shard_map/ppermute | solution.py:28
  9.2 7.3 %collective-permute-start = (bf16[1,64,512]{2,1,0:T(8,128)(2,1)}, bf16[1,64,512]{2,1,0:T(8,128)(2,1)S(1)}, u32[]{:S(2)}, u32[]{:S(2)}) collective-permute-start(bf16[1,64,512]{2,1,0:T(8,128)(2,1)} %own_hbm.1), channel_id=1, source_target_pairs={{4,0},{5,1},{6,2},{7,3},{8,4},{9,5},{10,6},{11,7},{12,8},{13,9},{1... | collective-permute-start | bytes 196616 | tf_op jit(solution)/shard_map/ppermute | solution.py:28
Sparse Core Ops, SparseCore 0:
  10.2 40.4 all-gather.2

commit v10 on v8

--- a/solution.py
+++ b/solution.py
@@ -348,16 +348,16 @@
 
 
 def write_maps(levels, pairs, own_specs, specs, kept, table_ref, shift_at, map_at, scratch, outs):
-    cross_ref, y_ref, maps_ref, rows_ref, *stacks = scratch
-    base = 0
-    for level, own, spec in zip(levels, own_specs, specs):
+    count = len(levels)
+    cross_refs, y_refs, maps_refs, rows_refs, stacks = (scratch[i * count : (i + 1) * count] for i in range(5))
+    for level, own, spec, cross_ref, y_ref in zip(levels, own_specs, specs, cross_refs, y_refs):
         def cross(at, rows):
             a = own[at : at + rows].astype(f32)
             ar, ai = a[:, :LANES], a[:, LANES:]
             for d in range(pairs):
                 b = spec[d * level.rows + at : d * level.rows + at + rows].astype(f32)
                 br, bi = b[:, :LANES], b[:, LANES:]
-                yield base + d * level.cross_rows, jnp.concatenate([ar * br + ai * bi, ar * bi - ai * br], axis=1)
+                yield d * level.cross_rows, jnp.concatenate([ar * br + ai * bi, ar * bi - ai * br], axis=1)
 
         for tile in range(level.tiles):
             quad, odd = divmod(tile, 2)
@@ -371,16 +371,13 @@
             if spare:
                 value = jnp.concatenate([value, jnp.zeros((spare, 4 * LANES), f32)], axis=0)
             cross_ref[to + level.cross_body : to + level.cross_rows] = value.astype(bf16)
-        base += pairs * level.cross_rows
-    y_ref[:base] = dot(cross_ref[:base], table_ref[shift_at : shift_at + 4 * LANES])
-    base = tile = 0
-    starts = {}
+        rows = pairs * level.cross_rows
+        y_ref[:rows] = dot(cross_ref[:rows], table_ref[shift_at : shift_at + 4 * LANES])
     row = lax.broadcasted_iota(jnp.int32, (NYQ, LANES), 0)
-    for index, level in enumerate(levels):
+    for level, y_ref, stack_ref, maps_ref in zip(levels, y_refs, stacks, maps_refs):
         for b in range(level.blocks):
-            stack_ref = stacks[index]
             for d in range(pairs):
-                first = base + d * level.cross_rows
+                first = d * level.cross_rows
                 nyq_at = first + level.cross_body
                 nyquist = y_ref[nyq_at : nyq_at + NYQ, :LANES]
                 for quad in range(level.quads):
@@ -397,34 +394,29 @@
             columns = pairs * level.quads * LANES
             both = dot(table_ref[map_at : map_at + 2 * WINDOW, : stack_ref.shape[0]], stack_ref[:, :columns])
             maps = both[:WINDOW] + both[WINDOW:]
-            for d in range(pairs):
-                starts[index, d, b] = tile
-                for quad in range(level.quads):
-                    column = (d * level.quads + quad) * LANES
-                    maps_ref[tile] = maps[:, column : column + LANES]
-                    tile += 1
-        base += pairs * level.cross_rows
-    lane = lax.broadcasted_iota(jnp.int32, (tile, LANES), 1)
+            for tile in range(pairs * level.quads):
+                maps_ref[b * pairs * level.quads + tile] = maps[:, tile * LANES : (tile + 1) * LANES]
 
     def exchange(low, high, width):
-        even = (lane & width) == 0
+        even = (lax.broadcasted_iota(jnp.int32, low.shape, 1) & width) == 0
         return (
             jnp.where(even, low, pltpu.roll(high, width, 1)),
             jnp.where(even, pltpu.roll(low, LANES - width, 1), high))
 
-    for big in range(WINDOW // 4):
-        rows = [maps_ref[:tile, 4 * big + r, :] for r in range(4)]
-        for step in (2, 1):
-            for r in range(4):
-                if not r & step:
-                    rows[r], rows[r + step] = exchange(rows[r], rows[r + step], step * WINDOW)
-        for g in range(4):
-            rows_ref[big, pl.ds(g, tile, stride=4), :] = rows[g]
-        for index, (level, out) in enumerate(zip(levels, outs)):
+    for index, (level, maps_ref, rows_ref, out) in enumerate(zip(levels, maps_refs, rows_refs, outs)):
+        tiles = level.blocks * pairs * level.quads
+        for big in range(WINDOW // 4):
+            rows = [maps_ref[:tiles, 4 * big + r, :] for r in range(4)]
+            for step in (2, 1):
+                for r in range(4):
+                    if not r & step:
+                        rows[r], rows[r + step] = exchange(rows[r], rows[r + step], step * WINDOW)
+            for g in range(4):
+                rows_ref[big, pl.ds(g, tiles, stride=4), :] = rows[g]
             for b in range(level.blocks):
                 column = kept[index][: 4 * level.quads, level.first + b : level.first + b + 1]
                 for d in range(pairs):
-                    at = 4 * starts[index, d, b]
+                    at = 4 * (b * pairs + d) * level.quads
                     out[d, b, :, big * LANES : (big + 1) * LANES] = rows_ref[big, at : at + 4 * level.quads] * column
 
 
@@ -468,14 +460,15 @@
 
 
 def pair_scratch(levels):
-    rows = sum(2 * level.cross_rows for level in levels)
-    tiles = sum(2 * level.blocks * level.quads for level in levels)
+    def each(shape, dtype):
+        return [pltpu.VMEM(shape(level), dtype) for level in levels]
+
     return [
-        pltpu.VMEM((rows, 4 * LANES), bf16),
-        pltpu.VMEM((rows, 2 * LANES), f32),
-        pltpu.VMEM((tiles, WINDOW, LANES), f32),
-        pltpu.VMEM((WINDOW // 4, 4 * tiles, LANES), f32),
-        *(pltpu.VMEM((4 * HALF + 2 * NYQ, 2 * level.quads * LANES), bf16) for level in levels),
+        *each(lambda level: (2 * level.cross_rows, 4 * LANES), bf16),
+        *each(lambda level: (2 * level.cross_rows, 2 * LANES), f32),
+        *each(lambda level: (2 * level.blocks * level.quads, WINDOW, LANES), f32),
+        *each(lambda level: (WINDOW // 4, 8 * level.blocks * level.quads, LANES), f32),
+        *each(lambda level: (4 * HALF + 2 * NYQ, 2 * level.quads * LANES), bf16),
     ]
 
 
@@ -494,10 +487,10 @@
 def inner_kernel(
     levels, cuts,
     own_hbm, near, far, mask_hbm, mask_coarse_hbm, table_hbm,
-    maps, own, table_ref, kept, kept_coarse,
-    mask, mask_coarse, pad, row_ref, *rest,
+    spec, own, table_ref, kept, kept_coarse,
+    mask, mask_coarse, pad, pad_coarse, row_ref, *rest,
 ):
-    *scratch, sems = rest
+    *sections, sems = rest
     start = copier(sems)
 
     def table(first, last):
@@ -505,43 +498,50 @@
         return start(table_hbm.at[piece], table_ref.at[piece])
 
     fine_at, shift_at, map_at, coarse_at, end = cuts
-    copies = [
-        start(own_hbm, own), table(shift_at, coarse_at), start(mask_hbm, mask), start(mask_coarse_hbm, mask_coarse),
-        table(coarse_at, end)]
-    size = 3 + 3 * len(levels)
-    sections, spec_refs, rest = scratch[:size], scratch[size : size + 1], scratch[size + 1 :]
+    copies = [start(own_hbm, own), start(mask_hbm, mask), start(mask_coarse_hbm, mask_coarse)]
+    tables = [table(shift_at, coarse_at), table(coarse_at, end)]
     strips = ((own,), (near,), (far,))
-    rows = levels[0].rows
 
     def run(pairs):
-        others = range(1, pairs + 1)
         if pairs:
             write_row_table(row_ref, levels[0])
             write_fine_table(table_ref, fine_at)
-            transform_rows(levels, others, strips, row_ref, sections)
+            transform_rows(levels, range(1, pairs + 1), strips, row_ref, sections)
         for wait in copies:
             wait()
         if pairs:
             write_mask_columns(mask, pad, kept)
-            write_mask_columns(mask_coarse, pad, kept_coarse)
+            write_mask_columns(mask_coarse, pad_coarse, kept_coarse)
             transform_rows(levels, (0,), strips, row_ref, sections)
-            transform_columns(levels, range(pairs + 1), table_ref, sections, spec_refs)
+            transform_columns(levels, range(pairs + 1), table_ref, sections, [spec])
+        for wait in tables:
+            wait()
+
+    for_pairs(run)
+
+
+def middle_kernel(
+    inner_levels, levels, cuts, row_at,
+    own, rim, table_ref, spec, kept,
+    own_fine, own_coarse, maps,
+    *rest,
+):
+    size = 3 + 3 * len(levels)
+    sections, pair = rest[:size], rest[size:]
+    fine_at, shift_at, map_at, coarse_at, end = cuts
+    row_ref = table_ref.at[pl.ds(row_at, row_places(levels)[1])]
+    rows = inner_levels[0].rows
+
+    def run(pairs):
+        if pairs:
+            transform_rows(levels, (0,), ((own, rim),), row_ref, sections)
+            transform_columns(levels, (0,), table_ref, sections, (own_fine, own_coarse))
             write_maps(
-                levels, pairs, [spec_refs[0].at[pl.ds(0, rows)]], [spec_refs[0].at[pl.ds(rows, pairs * rows)]],
-                (kept,), table_ref, shift_at, map_at, rest, (maps,))
+                inner_levels, pairs, [spec.at[pl.ds(0, rows)]], [spec.at[pl.ds(rows, pairs * rows)]], (kept,),
+                table_ref, shift_at, map_at, pair, (maps,))
         clear_maps(pairs, (maps,))
 
     for_pairs(run)
-
-
-def own_kernel(levels, row_at, own, rim, table_ref, *rest):
-    spec_refs, sections = rest[: len(levels)], rest[len(levels) :]
-    row_ref = table_ref.at[pl.ds(row_at, row_places(levels)[1])]
-
-    @pl.when(sections_ahead() >= 1)
-    def _():
-        transform_rows(levels, (0,), ((own, rim),), row_ref, sections)
-        transform_columns(levels, (0,), table_ref, sections, spec_refs)
 
 
 def outer_kernel(
@@ -552,7 +552,7 @@
 ):
     *scratch, sems = rest
     start = copier(sems)
-    stores = [start(inner_maps.at[d], out_fine.at[0, d, pl.ds(0, inner)]) for d in range(2)]
+    stores = [start(inner_maps, out_fine.at[0, :, pl.ds(0, inner)])]
     fine_at, shift_at, map_at, coarse_at, end = cuts
     row_ref = table_ref.at[pl.ds(row_at, row_places(levels)[1])]
     size, count = 3 + 3 * len(levels), len(levels)
@@ -569,9 +569,8 @@
         clear_maps(pairs, (maps, maps_coarse))
 
     for_pairs(run)
-    for d in range(2):
-        stores.append(start(maps.at[d], out_fine.at[0, d, pl.ds(inner, levels[0].blocks)]))
-        stores.append(start(maps_coarse.at[d], out_coarse.at[0, d]))
+    stores.append(start(maps, out_fine.at[0, :, pl.ds(inner, levels[0].blocks)]))
+    stores.append(start(maps_coarse, out_coarse.at[0]))
     for wait in stores:
         wait()
 
@@ -602,10 +601,10 @@
     def cost(flops):
         return pl.CostEstimate(flops=flops, bytes_accessed=4 * 10**6, transcendentals=0)
 
-    maps, own_kept, handed, *kept = pl.pallas_call(
+    spec, own_kept, handed, *kept = pl.pallas_call(
         functools.partial(inner_kernel, inner_levels, cuts),
         out_shape=(
-            jax.ShapeDtypeStruct((2, inner, 4 * inner_levels[0].quads, shifts), f32),
+            jax.ShapeDtypeStruct((3 * inner_levels[0].rows, 2 * LANES), bf16),
             jax.ShapeDtypeStruct(own.shape, bf16),
             jax.ShapeDtypeStruct(table.shape, bf16),
             *(jax.ShapeDtypeStruct((LANES, 8), f32) for _ in range(2)),
@@ -616,26 +615,28 @@
             pltpu.VMEM(mask_fine.shape, jnp.int32),
             pltpu.VMEM(mask_coarse.shape, jnp.int32),
             pltpu.VMEM((8, LANES), f32),
+            pltpu.VMEM((8, LANES), f32),
             pltpu.VMEM((row_places(inner_levels)[1], 2 * strip_rows), bf16),
             *section_scratch(inner_levels, width, 3),
-            *spec_scratch(inner_levels, 3),
-            *pair_scratch(inner_levels),
             pltpu.SemaphoreType.DMA((5,)),
         ],
         compiler_params=params,
-        cost_estimate=cost(3 * 10**9),
-        name="inner_blocks",
+        cost_estimate=cost(2 * 10**9),
+        name="inner_spectra",
     )(own, near, far, mask_fine, mask_coarse, table)
-    own_specs = pl.pallas_call(
-        functools.partial(own_kernel, outer_levels, row_at),
-        out_shape=tuple(jax.ShapeDtypeStruct((level.rows, 2 * LANES), bf16) for level in outer_levels),
-        in_specs=[vmem] * 3,
-        out_specs=(vmem,) * 2,
-        scratch_shapes=section_scratch(outer_levels, width, 1),
+    *own_specs, maps = pl.pallas_call(
+        functools.partial(middle_kernel, inner_levels, outer_levels, cuts, row_at),
+        out_shape=(
+            *(jax.ShapeDtypeStruct((level.rows, 2 * LANES), bf16) for level in outer_levels),
+            jax.ShapeDtypeStruct((2, inner, 4 * inner_levels[0].quads, shifts), f32),
+        ),
+        in_specs=[vmem] * 5,
+        out_specs=(vmem,) * 3,
+        scratch_shapes=[*section_scratch(outer_levels, width, 1), *pair_scratch(inner_levels)],
         compiler_params=params,
         cost_estimate=cost(2 * 10**9),
-        name="own_outer_blocks",
-    )(own_kept, rim, handed)
+        name="inner_maps",
+    )(own_kept, rim, handed, spec, kept[0])
     return pl.pallas_call(
         functools.partial(outer_kernel, outer_levels, cuts, inner, row_at),
         out_shape=(
@@ -649,7 +650,7 @@
             *section_scratch(outer_levels, width, 2),
             *spec_scratch(outer_levels, 2),
             *pair_scratch(outer_levels),
-            pltpu.SemaphoreType.DMA((6,)),
+            pltpu.SemaphoreType.DMA((3,)),
         ],
         compiler_params=params,
         cost_estimate=cost(4 * 10**9),

time: 19 us -> 20.1 us (1.058)
  waiting for transfers between devices: 3.28 us -> 4.95 us
  Pallas kernels: 7.67 us -> 7.09 us
    ppermute x5, waiting for transfers between devices: 3.28 us -> 4.95 us  [from_device(): return lax.ppermute(value, ('sec', 'strip'), pairs)]
    pallas_call x1, Pallas kernels: 3.27 us -> 2.29 us  [correlate(): pl.pallas_call(functools.partial(inner_kernel, inner_levels, cuts), out_s...]
    pallas_call x1, Pallas kernels: 1.25 us -> 1.8 us  [correlate(): pl.pallas_call(functools.partial(middle_kernel, inner_levels, outer_level...]
  transfers between devices with their start and end apart: 5 -> 5, of which waited for: 2 -> 2; matrix products, arithmetic and copies ran while one was open for 0% -> 0% of each run, Pallas kernels for 24% -> 21%
where the time goes in v10:
time: 20.1 us; the launch traced here: 19.9 us
  starting transfers between devices  7.13 us (35%)
  Pallas kernels  7.09 us (35%)
  waiting for transfers between devices  4.95 us (25%)
  between operations  0.71 us (4%)
    ppermute x5, starting transfers between devices, from_device(): return lax.ppermute(value, ('sec', 'strip'), pairs)  7.13 us
    ppermute x5, waiting for transfers between devices, from_device(): return lax.ppermute(value, ('sec', 'strip'), pairs)  4.95 us
    pallas_call x1, Pallas kernels, correlate(): pl.pallas_call(functools.partial(outer_kernel, outer_levels, cuts, inner,...  3 us
    pallas_call x1, Pallas kernels, correlate(): pl.pallas_call(functools.partial(inner_kernel, inner_levels, cuts), out_s...  2.29 us
    pallas_call x1, Pallas kernels, correlate(): pl.pallas_call(functools.partial(middle_kernel, inner_levels, outer_level...  1.8 us
  transfers between devices with their start and end apart: 5, of which 2 were waited for; matrix products, arithmetic and copies ran while one was open for 0% of the time, Pallas kernels for 21%

profile of v10, /device:TPU:1, one launch (start us, length us, event | category | flops | bytes accessed | tf_op | source)
XLA Modules:
  0.0 19.9 jit_solution(5311513880018072702)
XLA Ops:
  0.6 1.3 %collective-permute-start = (bf16[1,64,512]{2,1,0:T(8,128)(2,1)}, bf16[1,64,512]{2,1,0:T(8,128)(2,1)S(1)}, u32[]{:S(2)}, u32[]{:S(2)}) collective-permute-start(bf16[1,64,512]{2,1,0:T(8,128)(2,1)} %own_hbm.1), channel_id=1, source_target_pairs={{4,0},{5,1},{6,2},{7,3},{8,4},{9,5},{10,6},{11,7},{12,8},{13,9},{1... | collective-permute-start | bytes 196616 | tf_op jit(solution)/shard_map/ppermute | solution.py:28
  1.9 1.3 %collective-permute-start.1 = (bf16[1,64,512]{2,1,0:T(8,128)(2,1)}, bf16[1,64,512]{2,1,0:T(8,128)(2,1)S(1)}, u32[]{:S(2)}, u32[]{:S(2)}) collective-permute-start(bf16[1,64,512]{2,1,0:T(8,128)(2,1)} %own_hbm.1), channel_id=1, source_target_pairs={{8,0},{9,1},{10,2},{11,3},{12,4},{13,5},{14,6},{15,7},{24,16},{25,... | collective-permute-start | bytes 196616 | tf_op jit(solution)/shard_map/ppermute | solution.py:28
  3.2 2.0 %collective-permute-start.4 = (bf16[1,64,512]{2,1,0:T(8,128)(2,1)}, bf16[1,64,512]{2,1,0:T(8,128)(2,1)S(1)}, u32[]{:S(2)}, u32[]{:S(2)}) collective-permute-start(bf16[1,64,512]{2,1,0:T(8,128)(2,1)} %own_hbm.1), channel_id=1, source_target_pairs={{1,0},{2,1},{3,2},{5,4},{6,5},{7,6},{9,8},{10,9},{11,10},{13,12},{... | collective-permute-start | bytes 196616 | tf_op jit(solution)/shard_map/ppermute | solution.py:28
  5.2 1.3 %collective-permute-start.2 = (bf16[1,64,512]{2,1,0:T(8,128)(2,1)}, bf16[1,64,512]{2,1,0:T(8,128)(2,1)S(1)}, u32[]{:S(2)}, u32[]{:S(2)}) collective-permute-start(bf16[1,64,512]{2,1,0:T(8,128)(2,1)} %own_hbm.1), channel_id=1, source_target_pairs={{5,0},{6,1},{7,2},{9,4},{10,5},{11,6},{13,8},{14,9},{15,10},{21,16... | collective-permute-start | bytes 196616 | tf_op jit(solution)/shard_map/ppermute | solution.py:28
  6.5 1.3 %collective-permute-start.3 = (bf16[1,64,512]{2,1,0:T(8,128)(2,1)}, bf16[1,64,512]{2,1,0:T(8,128)(2,1)S(1)}, u32[]{:S(2)}, u32[]{:S(2)}) collective-permute-start(bf16[1,64,512]{2,1,0:T(8,128)(2,1)} %own_hbm.1), channel_id=1, source_target_pairs={{9,0},{10,1},{11,2},{13,4},{14,5},{15,6},{25,16},{26,17},{27,18},{... | collective-permute-start | bytes 196616 | tf_op jit(solution)/shard_map/ppermute | solution.py:28
  7.8 0.0 collective-permute-done.near
  7.8 2.1 %collective-permute-done.1.far = bf16[1,64,512]{2,1,0:T(8,128)(2,1)S(1)} collective-permute-done((bf16[1,64,512]{2,1,0:T(8,128)(2,1)}, bf16[1,64,512]{2,1,0:T(8,128)(2,1)S(1)}, u32[]{:S(2)}, u32[]{:S(2)}) %collective-permute-start.1) | collective-permute-done | bytes 65568 | tf_op jit(solution)/shard_map/ppermute | solution.py:28
  9.9 2.3 %inner_spectra.1 = (bf16[816,256]{1,0:T(8,128)(2,1)S(1)}, bf16[1,64,512]{2,1,0:T(8,128)(2,1)S(1)}, bf16[2272,256]{1,0:T(8,128)(2,1)S(1)}, f32[128,8]{1,0:T(8,128)S(1)}, f32[128,8]{1,0:T(8,128)S(1)}) custom-call(bf16[1,64,512]{2,1,0:T(8,128)(2,1)} %own_hbm.1, bf16[1,64,512]{2,1,0:T(8,128)(2,1)S(1)} %collective-permute-done.near, ...), custom_call_target="tpu_custom_call" | custom-call | flops 2000000000 | bytes 4000000 | tf_op jit(solution)/shard_map/inner_spectra/pallas_call | solution.py:604
  12.2 0.0 collective-permute-done.4.rim
  12.2 1.8 %inner_maps.1 = (bf16[272,256]{1,0:T(8,128)(2,1)S(1)}, bf16[144,256]{1,0:T(8,128)(2,1)S(1)}, f32[2,1,16,1024]{3,2,1,0:T(8,128)S(1)}) custom-call(bf16[1,64,512]{2,1,0:T(8,128)(2,1)S(1)} %get-tuple-element.11.own, bf16[1,64,512]{2,1,0:T(8,128)(2,1)S(1)} %collective-permute-done.4.rim, bf16[2272,256]{1,0:T(8,128)(2,1)S(1)} %get-tuple-element.10.table_ref, ...), custom_call_target="tpu_custom_call" | custom-call | flops 2000000000 | bytes 4000000 | tf_op jit(solution)/shard_map/inner_maps/pallas_call | solution.py:627
  14.0 0.0 collective-permute-done.2.rim_near
  14.0 2.8 %collective-permute-done.3.rim_far = bf16[1,64,512]{2,1,0:T(8,128)(2,1)S(1)} collective-permute-done((bf16[1,64,512]{2,1,0:T(8,128)(2,1)}, bf16[1,64,512]{2,1,0:T(8,128)(2,1)S(1)}, u32[]{:S(2)}, u32[]{:S(2)}) %collective-permute-start.3) | collective-permute-done | bytes 65568 | tf_op jit(solution)/shard_map/ppermute | solution.py:28
  16.9 3.0 %outer_blocks.1 = (f32[1,2,2,16,1024]{4,3,2,1,0:T(8,128)}, f32[1,2,1,8,1024]{4,3,2,1,0:T(8,128)}) custom-call(bf16[1,64,512]{2,1,0:T(8,128)(2,1)S(1)} %collective-permute-done.near, bf16[1,64,512]{2,1,0:T(8,128)(2,1)S(1)} %collective-permute-done.1.far, bf16[1,64,512]{2,1,0:T(8,128)(2,1)S(1)} %collective-permute-done.2.rim_near, ...), custom_call_target="tpu_custom_call" | custom-call | flops 4000000000 | bytes 4000000 | tf_op jit(solution)/shard_map/outer_blocks/pallas_call | solution.py:640
Async XLA Ops:
  0.6 7.2 %collective-permute-start = (bf16[1,64,512]{2,1,0:T(8,128)(2,1)}, bf16[1,64,512]{2,1,0:T(8,128)(2,1)S(1)}, u32[]{:S(2)}, u32[]{:S(2)}) collective-permute-start(bf16[1,64,512]{2,1,0:T(8,128)(2,1)} %own_hbm.1), channel_id=1, source_target_pairs={{4,0},{5,1},{6,2},{7,3},{8,4},{9,5},{10,6},{11,7},{12,8},{13,9},{1... | collective-permute-start | bytes 196616 | tf_op jit(solution)/shard_map/ppermute | solution.py:28
  1.9 8.0 %collective-permute-start.1 = (bf16[1,64,512]{2,1,0:T(8,128)(2,1)}, bf16[1,64,512]{2,1,0:T(8,128)(2,1)S(1)}, u32[]{:S(2)}, u32[]{:S(2)}) collective-permute-start(bf16[1,64,512]{2,1,0:T(8,128)(2,1)} %own_hbm.1), channel_id=1, source_target_pairs={{8,0},{9,1},{10,2},{11,3},{12,4},{13,5},{14,6},{15,7},{24,16},{25,... | collective-permute-start | bytes 196616 | tf_op jit(solution)/shard_map/ppermute | solution.py:28
  3.2 9.0 %collective-permute-start.4 = (bf16[1,64,512]{2,1,0:T(8,128)(2,1)}, bf16[1,64,512]{2,1,0:T(8,128)(2,1)S(1)}, u32[]{:S(2)}, u32[]{:S(2)}) collective-permute-start(bf16[1,64,512]{2,1,0:T(8,128)(2,1)} %own_hbm.1), channel_id=1, source_target_pairs={{1,0},{2,1},{3,2},{5,4},{6,5},{7,6},{9,8},{10,9},{11,10},{13,12},{... | collective-permute-start | bytes 196616 | tf_op jit(solution)/shard_map/ppermute | solution.py:28
  5.2 8.8 %collective-permute-start.2 = (bf16[1,64,512]{2,1,0:T(8,128)(2,1)}, bf16[1,64,512]{2,1,0:T(8,128)(2,1)S(1)}, u32[]{:S(2)}, u32[]{:S(2)}) collective-permute-start(bf16[1,64,512]{2,1,0:T(8,128)(2,1)} %own_hbm.1), channel_id=1, source_target_pairs={{5,0},{6,1},{7,2},{9,4},{10,5},{11,6},{13,8},{14,9},{15,10},{21,16... | collective-permute-start | bytes 196616 | tf_op jit(solution)/shard_map/ppermute | solution.py:28
  6.5 10.4 %collective-permute-start.3 = (bf16[1,64,512]{2,1,0:T(8,128)(2,1)}, bf16[1,64,512]{2,1,0:T(8,128)(2,1)S(1)}, u32[]{:S(2)}, u32[]{:S(2)}) collective-permute-start(bf16[1,64,512]{2,1,0:T(8,128)(2,1)} %own_hbm.1), channel_id=1, source_target_pairs={{9,0},{10,1},{11,2},{13,4},{14,5},{15,6},{25,16},{26,17},{27,18},{... | collective-permute-start | bytes 196616 | tf_op jit(solution)/shard_map/ppermute | solution.py:28

commit v11 on v10

--- a/solution.py
+++ b/solution.py
@@ -347,7 +347,7 @@
         scale_spectrum(level, f_ref, sections, spectrum_power(level, f_ref, sections), spec_ref)
 
 
-def write_maps(levels, pairs, own_specs, specs, kept, table_ref, shift_at, map_at, scratch, outs):
+def write_maps(levels, pairs, own_specs, specs, kept, table_ref, shift_at, map_at, scratch, outs, finished=()):
     count = len(levels)
     cross_refs, y_refs, maps_refs, rows_refs, stacks = (scratch[i * count : (i + 1) * count] for i in range(5))
     for level, own, spec, cross_ref, y_ref in zip(levels, own_specs, specs, cross_refs, y_refs):
@@ -418,6 +418,8 @@
                 for d in range(pairs):
                     at = 4 * (b * pairs + d) * level.quads
                     out[d, b, :, big * LANES : (big + 1) * LANES] = rows_ref[big, at : at + 4 * level.quads] * column
+        if finished:
+            finished[index]()
 
 
 def write_mask_columns(mask_ref, pad_ref, kept_ref):
@@ -551,8 +553,7 @@
     maps, maps_coarse, *rest,
 ):
     *scratch, sems = rest
-    start = copier(sems)
-    stores = [start(inner_maps, out_fine.at[0, :, pl.ds(0, inner)])]
+    inner_stored = copier(sems)(inner_maps, out_fine.at[0, :, pl.ds(0, inner)])
     fine_at, shift_at, map_at, coarse_at, end = cuts
     row_ref = table_ref.at[pl.ds(row_at, row_places(levels)[1])]
     size, count = 3 + 3 * len(levels), len(levels)
@@ -560,19 +561,24 @@
     strips = ((near, rim_near), (far, rim_far))
 
     def run(pairs):
+        stores = [
+            pltpu.make_async_copy(maps, out_fine.at[0, :, pl.ds(inner, levels[0].blocks)], sems.at[1]),
+            pltpu.make_async_copy(maps_coarse, out_coarse.at[0], sems.at[2])]
+        clear_maps(pairs, (maps, maps_coarse))
         if pairs:
             transform_rows(levels, range(pairs), strips, row_ref, sections)
             transform_columns(levels, range(pairs), table_ref, sections, spec_refs)
             write_maps(
                 levels, pairs, (own_fine, own_coarse), spec_refs, (kept, kept_coarse), table_ref, shift_at, map_at,
-                rest, (maps, maps_coarse))
-        clear_maps(pairs, (maps, maps_coarse))
+                rest, (maps, maps_coarse), [store.start for store in stores])
+        else:
+            for store in stores:
+                store.start()
+        for store in stores:
+            store.wait()
 
     for_pairs(run)
-    stores.append(start(maps, out_fine.at[0, :, pl.ds(inner, levels[0].blocks)]))
-    stores.append(start(maps_coarse, out_coarse.at[0]))
-    for wait in stores:
-        wait()
+    inner_stored()
 
 
 def correlate(own, near, far, rim, rim_near, rim_far, mask_fine, mask_coarse):
@@ -621,7 +627,7 @@
             pltpu.SemaphoreType.DMA((5,)),
         ],
         compiler_params=params,
-        cost_estimate=cost(2 * 10**9),
+        cost_estimate=cost(3 * 10**9),
         name="inner_spectra",
     )(own, near, far, mask_fine, mask_coarse, table)
     *own_specs, maps = pl.pallas_call(

time: 20.1 us -> 20.1 us (level)
  no operation moved by 1% of the time
where the time goes in v11:
time: 20.1 us; the launch traced here: 19.8 us
  starting transfers between devices  7.13 us (35%)
  Pallas kernels  7.05 us (35%)
  waiting for transfers between devices  4.95 us (25%)
  between operations  0.71 us (4%)
    ppermute x5, starting transfers between devices, from_device(): return lax.ppermute(value, ('sec', 'strip'), pairs)  7.13 us
    ppermute x5, waiting for transfers between devices, from_device(): return lax.ppermute(value, ('sec', 'strip'), pairs)  4.95 us
    pallas_call x1, Pallas kernels, correlate(): pl.pallas_call(functools.partial(outer_kernel, outer_levels, cuts, inner,...  2.96 us
    pallas_call x1, Pallas kernels, correlate(): pl.pallas_call(functools.partial(inner_kernel, inner_levels, cuts), out_s...  2.29 us
    pallas_call x1, Pallas kernels, correlate(): pl.pallas_call(functools.partial(middle_kernel, inner_levels, outer_level...  1.8 us
  transfers between devices with their start and end apart: 5, of which 2 were waited for; matrix products, arithmetic and copies ran while one was open for 0% of the time, Pallas kernels for 21%

profile of v11, /device:TPU:1, one launch (start us, length us, event | category | flops | bytes accessed | tf_op | source)
XLA Modules:
  0.0 19.8 jit_solution(6792749088198083390)
XLA Ops:
  0.6 1.3 %collective-permute-start = (bf16[1,64,512]{2,1,0:T(8,128)(2,1)}, bf16[1,64,512]{2,1,0:T(8,128)(2,1)S(1)}, u32[]{:S(2)}, u32[]{:S(2)}) collective-permute-start(bf16[1,64,512]{2,1,0:T(8,128)(2,1)} %own_hbm.1), channel_id=1, source_target_pairs={{4,0},{5,1},{6,2},{7,3},{8,4},{9,5},{10,6},{11,7},{12,8},{13,9},{1... | collective-permute-start | bytes 196616 | tf_op jit(solution)/shard_map/ppermute | solution.py:28
  1.9 1.3 %collective-permute-start.1 = (bf16[1,64,512]{2,1,0:T(8,128)(2,1)}, bf16[1,64,512]{2,1,0:T(8,128)(2,1)S(1)}, u32[]{:S(2)}, u32[]{:S(2)}) collective-permute-start(bf16[1,64,512]{2,1,0:T(8,128)(2,1)} %own_hbm.1), channel_id=1, source_target_pairs={{8,0},{9,1},{10,2},{11,3},{12,4},{13,5},{14,6},{15,7},{24,16},{25,... | collective-permute-start | bytes 196616 | tf_op jit(solution)/shard_map/ppermute | solution.py:28
  3.2 2.0 %collective-permute-start.4 = (bf16[1,64,512]{2,1,0:T(8,128)(2,1)}, bf16[1,64,512]{2,1,0:T(8,128)(2,1)S(1)}, u32[]{:S(2)}, u32[]{:S(2)}) collective-permute-start(bf16[1,64,512]{2,1,0:T(8,128)(2,1)} %own_hbm.1), channel_id=1, source_target_pairs={{1,0},{2,1},{3,2},{5,4},{6,5},{7,6},{9,8},{10,9},{11,10},{13,12},{... | collective-permute-start | bytes 196616 | tf_op jit(solution)/shard_map/ppermute | solution.py:28
  5.2 1.3 %collective-permute-start.2 = (bf16[1,64,512]{2,1,0:T(8,128)(2,1)}, bf16[1,64,512]{2,1,0:T(8,128)(2,1)S(1)}, u32[]{:S(2)}, u32[]{:S(2)}) collective-permute-start(bf16[1,64,512]{2,1,0:T(8,128)(2,1)} %own_hbm.1), channel_id=1, source_target_pairs={{5,0},{6,1},{7,2},{9,4},{10,5},{11,6},{13,8},{14,9},{15,10},{21,16... | collective-permute-start | bytes 196616 | tf_op jit(solution)/shard_map/ppermute | solution.py:28
  6.5 1.3 %collective-permute-start.3 = (bf16[1,64,512]{2,1,0:T(8,128)(2,1)}, bf16[1,64,512]{2,1,0:T(8,128)(2,1)S(1)}, u32[]{:S(2)}, u32[]{:S(2)}) collective-permute-start(bf16[1,64,512]{2,1,0:T(8,128)(2,1)} %own_hbm.1), channel_id=1, source_target_pairs={{9,0},{10,1},{11,2},{13,4},{14,5},{15,6},{25,16},{26,17},{27,18},{... | collective-permute-start | bytes 196616 | tf_op jit(solution)/shard_map/ppermute | solution.py:28
  7.8 0.0 collective-permute-done.near
  7.8 2.1 %collective-permute-done.1.far = bf16[1,64,512]{2,1,0:T(8,128)(2,1)S(1)} collective-permute-done((bf16[1,64,512]{2,1,0:T(8,128)(2,1)}, bf16[1,64,512]{2,1,0:T(8,128)(2,1)S(1)}, u32[]{:S(2)}, u32[]{:S(2)}) %collective-permute-start.1) | collective-permute-done | bytes 65568 | tf_op jit(solution)/shard_map/ppermute | solution.py:28
  9.9 2.3 %inner_spectra.1 = (bf16[816,256]{1,0:T(8,128)(2,1)S(1)}, bf16[1,64,512]{2,1,0:T(8,128)(2,1)S(1)}, bf16[2272,256]{1,0:T(8,128)(2,1)S(1)}, f32[128,8]{1,0:T(8,128)S(1)}, f32[128,8]{1,0:T(8,128)S(1)}) custom-call(bf16[1,64,512]{2,1,0:T(8,128)(2,1)} %own_hbm.1, bf16[1,64,512]{2,1,0:T(8,128)(2,1)S(1)} %collective-permute-done.near, ...), custom_call_target="tpu_custom_call" | custom-call | flops 3000000000 | bytes 4000000 | tf_op jit(solution)/shard_map/inner_spectra/pallas_call | solution.py:610
  12.2 0.0 collective-permute-done.4.rim
  12.2 1.8 %inner_maps.1 = (bf16[272,256]{1,0:T(8,128)(2,1)S(1)}, bf16[144,256]{1,0:T(8,128)(2,1)S(1)}, f32[2,1,16,1024]{3,2,1,0:T(8,128)S(1)}) custom-call(bf16[1,64,512]{2,1,0:T(8,128)(2,1)S(1)} %get-tuple-element.11.own, bf16[1,64,512]{2,1,0:T(8,128)(2,1)S(1)} %collective-permute-done.4.rim, bf16[2272,256]{1,0:T(8,128)(2,1)S(1)} %get-tuple-element.10.table_ref, ...), custom_call_target="tpu_custom_call" | custom-call | flops 2000000000 | bytes 4000000 | tf_op jit(solution)/shard_map/inner_maps/pallas_call | solution.py:633
  14.0 0.0 collective-permute-done.2.rim_near
  14.0 2.8 %collective-permute-done.3.rim_far = bf16[1,64,512]{2,1,0:T(8,128)(2,1)S(1)} collective-permute-done((bf16[1,64,512]{2,1,0:T(8,128)(2,1)}, bf16[1,64,512]{2,1,0:T(8,128)(2,1)S(1)}, u32[]{:S(2)}, u32[]{:S(2)}) %collective-permute-start.3) | collective-permute-done | bytes 65568 | tf_op jit(solution)/shard_map/ppermute | solution.py:28
  16.9 3.0 %outer_blocks.1 = (f32[1,2,2,16,1024]{4,3,2,1,0:T(8,128)}, f32[1,2,1,8,1024]{4,3,2,1,0:T(8,128)}) custom-call(bf16[1,64,512]{2,1,0:T(8,128)(2,1)S(1)} %collective-permute-done.near, bf16[1,64,512]{2,1,0:T(8,128)(2,1)S(1)} %collective-permute-done.1.far, bf16[1,64,512]{2,1,0:T(8,128)(2,1)S(1)} %collective-permute-done.2.rim_near, ...), custom_call_target="tpu_custom_call" | custom-call | flops 4000000000 | bytes 4000000 | tf_op jit(solution)/shard_map/outer_blocks/pallas_call | solution.py:646
Async XLA Ops:
  0.6 7.2 %collective-permute-start = (bf16[1,64,512]{2,1,0:T(8,128)(2,1)}, bf16[1,64,512]{2,1,0:T(8,128)(2,1)S(1)}, u32[]{:S(2)}, u32[]{:S(2)}) collective-permute-start(bf16[1,64,512]{2,1,0:T(8,128)(2,1)} %own_hbm.1), channel_id=1, source_target_pairs={{4,0},{5,1},{6,2},{7,3},{8,4},{9,5},{10,6},{11,7},{12,8},{13,9},{1... | collective-permute-start | bytes 196616 | tf_op jit(solution)/shard_map/ppermute | solution.py:28
  1.9 8.0 %collective-permute-start.1 = (bf16[1,64,512]{2,1,0:T(8,128)(2,1)}, bf16[1,64,512]{2,1,0:T(8,128)(2,1)S(1)}, u32[]{:S(2)}, u32[]{:S(2)}) collective-permute-start(bf16[1,64,512]{2,1,0:T(8,128)(2,1)} %own_hbm.1), channel_id=1, source_target_pairs={{8,0},{9,1},{10,2},{11,3},{12,4},{13,5},{14,6},{15,7},{24,16},{25,... | collective-permute-start | bytes 196616 | tf_op jit(solution)/shard_map/ppermute | solution.py:28
  3.2 9.0 %collective-permute-start.4 = (bf16[1,64,512]{2,1,0:T(8,128)(2,1)}, bf16[1,64,512]{2,1,0:T(8,128)(2,1)S(1)}, u32[]{:S(2)}, u32[]{:S(2)}) collective-permute-start(bf16[1,64,512]{2,1,0:T(8,128)(2,1)} %own_hbm.1), channel_id=1, source_target_pairs={{1,0},{2,1},{3,2},{5,4},{6,5},{7,6},{9,8},{10,9},{11,10},{13,12},{... | collective-permute-start | bytes 196616 | tf_op jit(solution)/shard_map/ppermute | solution.py:28
  5.2 8.8 %collective-permute-start.2 = (bf16[1,64,512]{2,1,0:T(8,128)(2,1)}, bf16[1,64,512]{2,1,0:T(8,128)(2,1)S(1)}, u32[]{:S(2)}, u32[]{:S(2)}) collective-permute-start(bf16[1,64,512]{2,1,0:T(8,128)(2,1)} %own_hbm.1), channel_id=1, source_target_pairs={{5,0},{6,1},{7,2},{9,4},{10,5},{11,6},{13,8},{14,9},{15,10},{21,16... | collective-permute-start | bytes 196616 | tf_op jit(solution)/shard_map/ppermute | solution.py:28
  6.5 10.4 %collective-permute-start.3 = (bf16[1,64,512]{2,1,0:T(8,128)(2,1)}, bf16[1,64,512]{2,1,0:T(8,128)(2,1)S(1)}, u32[]{:S(2)}, u32[]{:S(2)}) collective-permute-start(bf16[1,64,512]{2,1,0:T(8,128)(2,1)} %own_hbm.1), channel_id=1, source_target_pairs={{9,0},{10,1},{11,2},{13,4},{14,5},{15,6},{25,16},{26,17},{27,18},{... | collective-permute-start | bytes 196616 | tf_op jit(solution)/shard_map/ppermute | solution.py:28

commit v12 on v11

--- a/solution.py
+++ b/solution.py
@@ -155,56 +155,6 @@
     return dot(
         jnp.concatenate([high, low, high], axis=1),
         jnp.concatenate([table_high, table_high, table_low], axis=0))
-
-
-def cosine(turns):
-    turns = turns + PATCH // 4
-    part = (turns & (HALF - 1)) - PATCH // 4
-    angle = part.astype(f32) * (2 * np.pi / PATCH)
-    square = angle * angle
-    value = jnp.full(square.shape, 1.0 / 479001600, f32)
-    for term in (-1.0 / 3628800, 1.0 / 40320, -1.0 / 720, 1.0 / 24, -0.5, 1.0):
-        value = value * square + term
-    return jnp.where((turns & HALF) == 0, value, -value)
-
-
-def write_row_table(row_ref, level):
-    (cos_at, nyquist_at, sin_at), = row_places([level])[0]
-    ext = row_ref.shape[1] // 2
-
-    def put(at, value):
-        high, low = split(value)
-        row_ref[at : at + value.shape[0], :ext] = high
-        row_ref[at : at + value.shape[0], ext:] = low
-
-    def inside(x):
-        return jnp.where((x >= 0) & (x < PATCH), 1.0, 0.0)
-
-    k = lax.broadcasted_iota(jnp.int32, (HALF, ext), 0)
-    for b in range(level.blocks):
-        x = lax.broadcasted_iota(jnp.int32, (HALF, ext), 1) - (level.first + b) * STRIDE
-        put(cos_at + b * HALF, cosine(k * x) * inside(x))
-        put(sin_at + b * HALF, cosine(k * x - PATCH // 4) * inside(x))
-    row = lax.broadcasted_iota(jnp.int32, (2 * level.half, ext), 0)
-    x = lax.broadcasted_iota(jnp.int32, (2 * level.half, ext), 1)
-    x = x - (level.first + lax.rem(lax.rem(row, level.half), level.blocks)) * STRIDE
-    put(nyquist_at, cosine(x * HALF) * inside(x))
-
-
-def write_fine_table(table_ref, at):
-    y = lax.broadcasted_iota(jnp.int32, (PATCH, LANES), 0)
-    lane = lax.broadcasted_iota(jnp.int32, (PATCH, LANES), 1)
-    frequency = lane & (PATCH - 1)
-    c, s = cosine(y * frequency), cosine(y * frequency - PATCH // 4)
-    depth = 4 * PATCH
-    for p in range(2):
-        mine = (lane >= PATCH) if p else (lane < PATCH)
-        cos, minus_cos, minus_sin = (jnp.where(mine, value, 0.0) for value in (c, -c, -s))
-        for number, pair in enumerate(((cos, minus_sin), (minus_sin, minus_cos))):
-            to = at + (2 * number + p) * PATCH
-            for half, value in enumerate(pair):
-                for level, part in enumerate(split(value)):
-                    table_ref[to + level * depth : to + level * depth + PATCH, half * LANES : (half + 1) * LANES] = part
 
 
 def all_rows(value):
@@ -474,6 +424,11 @@
     ]
 
 
+def pieces(rows, count=6):
+    cuts = [rows * i // count // 16 * 16 for i in range(count)] + [rows]
+    return list(zip(cuts[:-1], cuts[1:]))
+
+
 def copier(sems):
     used = []
 
@@ -486,38 +441,30 @@
     return start
 
 
-def inner_kernel(
-    levels, cuts,
-    own_hbm, near, far, mask_hbm, mask_coarse_hbm, table_hbm,
-    spec, own, table_ref, kept, kept_coarse,
-    mask, mask_coarse, pad, pad_coarse, row_ref, *rest,
+def load_kernel(
+    own_hbm, mask_hbm, mask_coarse_hbm, table_hbm,
+    own, table_ref, kept, kept_coarse,
+    mask, mask_coarse, pad, pad_coarse, sems,
 ):
-    *sections, sems = rest
     start = copier(sems)
-
-    def table(first, last):
+    waits = [start(own_hbm, own), start(mask_hbm, mask), start(mask_coarse_hbm, mask_coarse)]
+    for first, last in pieces(table_hbm.shape[0]):
         piece = pl.ds(first, last - first)
-        return start(table_hbm.at[piece], table_ref.at[piece])
-
-    fine_at, shift_at, map_at, coarse_at, end = cuts
-    copies = [start(own_hbm, own), start(mask_hbm, mask), start(mask_coarse_hbm, mask_coarse)]
-    tables = [table(shift_at, coarse_at), table(coarse_at, end)]
+        waits.append(start(table_hbm.at[piece], table_ref.at[piece]))
+    for wait in waits:
+        wait()
+    write_mask_columns(mask, pad, kept)
+    write_mask_columns(mask_coarse, pad_coarse, kept_coarse)
+
+
+def inner_kernel(levels, row_at, own, far, near, table_ref, spec, *sections):
     strips = ((own,), (near,), (far,))
+    row_ref = table_ref.at[pl.ds(row_at, row_places(levels)[1]), pl.ds(0, 2 * own.shape[1])]
 
     def run(pairs):
         if pairs:
-            write_row_table(row_ref, levels[0])
-            write_fine_table(table_ref, fine_at)
-            transform_rows(levels, range(1, pairs + 1), strips, row_ref, sections)
-        for wait in copies:
-            wait()
-        if pairs:
-            write_mask_columns(mask, pad, kept)
-            write_mask_columns(mask_coarse, pad_coarse, kept_coarse)
-            transform_rows(levels, (0,), strips, row_ref, sections)
+            transform_rows(levels, range(pairs + 1), strips, row_ref, sections)
             transform_columns(levels, range(pairs + 1), table_ref, sections, [spec])
-        for wait in tables:
-            wait()
 
     for_pairs(run)
 
@@ -548,7 +495,7 @@
 
 def outer_kernel(
     levels, cuts, inner, row_at,
-    near, far, rim_near, rim_far, table_ref, own_fine, own_coarse, kept, kept_coarse, inner_maps,
+    far, near, rim_far, rim_near, table_ref, own_fine, own_coarse, kept, kept_coarse, inner_maps,
     out_fine, out_coarse,
     maps, maps_coarse, *rest,
 ):
@@ -581,7 +528,7 @@
     inner_stored()
 
 
-def correlate(own, near, far, rim, rim_near, rim_far, mask_fine, mask_coarse):
+def correlate(own, near, far, rim_of, rim_near, rim_far, mask_fine, mask_coarse):
     strip_rows, width = own.shape[1:]
     fine, coarse = mask_fine.shape[1], mask_coarse.shape[1]
     inner = fine - 1
@@ -592,6 +539,8 @@
     outer_levels = [Level(1, range(inner, fine), width, cuts[0]), Level(2, range(coarse), width, cuts[3])]
     row_at = cuts[4]
     tables.append(row_table(outer_levels, strip_rows + PATCH))
+    row_inner_at = row_at + tables[-1].shape[0]
+    tables.append(row_table(inner_levels, strip_rows))
     columns = max(table.shape[1] for table in tables)
     table = np.concatenate([np.pad(table, ((0, 0), (0, columns - table.shape[1]))) for table in tables])
     cuts[4] = table.shape[0]
@@ -607,29 +556,37 @@
     def cost(flops):
         return pl.CostEstimate(flops=flops, bytes_accessed=4 * 10**6, transcendentals=0)
 
-    spec, own_kept, handed, *kept = pl.pallas_call(
-        functools.partial(inner_kernel, inner_levels, cuts),
+    kept_own, handed, *kept = pl.pallas_call(
+        load_kernel,
         out_shape=(
-            jax.ShapeDtypeStruct((3 * inner_levels[0].rows, 2 * LANES), bf16),
             jax.ShapeDtypeStruct(own.shape, bf16),
             jax.ShapeDtypeStruct(table.shape, bf16),
             *(jax.ShapeDtypeStruct((LANES, 8), f32) for _ in range(2)),
         ),
-        in_specs=[hbm, vmem, vmem, hbm, hbm, hbm],
-        out_specs=(vmem,) * 5,
+        in_specs=[hbm] * 4,
+        out_specs=(vmem,) * 4,
         scratch_shapes=[
             pltpu.VMEM(mask_fine.shape, jnp.int32),
             pltpu.VMEM(mask_coarse.shape, jnp.int32),
             pltpu.VMEM((8, LANES), f32),
             pltpu.VMEM((8, LANES), f32),
-            pltpu.VMEM((row_places(inner_levels)[1], 2 * strip_rows), bf16),
-            *section_scratch(inner_levels, width, 3),
-            pltpu.SemaphoreType.DMA((5,)),
+            pltpu.SemaphoreType.DMA((3 + len(pieces(table.shape[0])),)),
         ],
+        compiler_params=params,
+        cost_estimate=cost(10**9),
+        name="load",
+    )(own, mask_fine, mask_coarse, table)
+    rim = rim_of(kept_own)
+    spec = pl.pallas_call(
+        functools.partial(inner_kernel, inner_levels, row_inner_at),
+        out_shape=jax.ShapeDtypeStruct((3 * inner_levels[0].rows, 2 * LANES), bf16),
+        in_specs=[vmem] * 4,
+        out_specs=vmem,
+        scratch_shapes=section_scratch(inner_levels, width, 3),
         compiler_params=params,
         cost_estimate=cost(3 * 10**9),
         name="inner_spectra",
-    )(own, near, far, mask_fine, mask_coarse, table)
+    )(kept_own, far, near, handed)
     *own_specs, maps = pl.pallas_call(
         functools.partial(middle_kernel, inner_levels, outer_levels, cuts, row_at),
         out_shape=(
@@ -642,7 +599,7 @@
         compiler_params=params,
         cost_estimate=cost(2 * 10**9),
         name="inner_maps",
-    )(own_kept, rim, handed, spec, kept[0])
+    )(kept_own, rim, handed, spec, kept[0])
     return pl.pallas_call(
         functools.partial(outer_kernel, outer_levels, cuts, inner, row_at),
         out_shape=(
@@ -661,14 +618,15 @@
         compiler_params=params,
         cost_estimate=cost(4 * 10**9),
         name="outer_blocks",
-    )(near, far, rim_near, rim_far, handed, *own_specs, *kept, maps)
+    )(far, near, rim_far, rim_near, handed, *own_specs, *kept, maps)
 
 
 def local(sections, mask_fine, mask_coarse):
     far = from_device(sections, 2, 0)
     near = from_device(sections, 1, 0)
-    rims = [from_device(sections, z, 1) for z in range(3)]
-    return correlate(sections, near, far, *rims, mask_fine, mask_coarse)
+    rim_near, rim_far = from_device(sections, 1, 1), from_device(sections, 2, 1)
+    return correlate(
+        sections, near, far, lambda own: from_device(own, 0, 1), rim_near, rim_far, mask_fine, mask_coarse)
 
 
 def solution(mesh):

time: 20.1 us -> 20.3 us (level)
  the two profiles are of different devices: /device:TPU:1 before, /device:TPU:9 now
where the time goes in v12:
time: 20.3 us; the launch traced here: 20.1 us
  starting transfers between devices  8.38 us (41%)
  Pallas kernels  7.9 us (39%)
  waiting for transfers between devices  3.09 us (15%)
  between operations  0.73 us (4%)
    ppermute x5, starting transfers between devices, from_device(): return lax.ppermute(value, ('sec', 'strip'), pairs)  8.38 us
    ppermute x5, waiting for transfers between devices, from_device(): return lax.ppermute(value, ('sec', 'strip'), pairs)  3.09 us
    pallas_call x1, Pallas kernels, correlate(): pl.pallas_call(functools.partial(outer_kernel, outer_levels, cuts, inner,...  2.95 us
    pallas_call x1, Pallas kernels, correlate(): pl.pallas_call(functools.partial(middle_kernel, inner_levels, outer_level...  1.77 us
    pallas_call x1, Pallas kernels, correlate(): pl.pallas_call(load_kernel, out_shape=(jax.ShapeDtypeStruct(own.shape, bf...  1.63 us
    pallas_call x1, Pallas kernels, correlate(): pl.pallas_call(functools.partial(inner_kernel, inner_levels, row_inner_at...  1.54 us
  transfers between devices with their start and end apart: 5, of which 1 were waited for; matrix products, arithmetic and copies ran while one was open for 0% of the time, Pallas kernels for 25%

profile of v12, /device:TPU:9, one launch (start us, length us, event | category | flops | bytes accessed | tf_op | source)
XLA Modules:
  0.0 20.1 jit_solution(11479095951479944407)
XLA Ops:
  0.6 1.3 %collective-permute-start = (bf16[1,64,512]{2,1,0:T(8,128)(2,1)}, bf16[1,64,512]{2,1,0:T(8,128)(2,1)S(1)}, u32[]{:S(2)}, u32[]{:S(2)}) collective-permute-start(bf16[1,64,512]{2,1,0:T(8,128)(2,1)} %own_hbm.1), channel_id=1, source_target_pairs={{8,0},{9,1},{10,2},{11,3},{12,4},{13,5},{14,6},{15,7},{24,16},{25,... | collective-permute-start | bytes 196616 | tf_op jit(solution)/shard_map/ppermute | solution.py:28
  1.9 1.9 %collective-permute-start.1 = (bf16[1,64,512]{2,1,0:T(8,128)(2,1)}, bf16[1,64,512]{2,1,0:T(8,128)(2,1)S(1)}, u32[]{:S(2)}, u32[]{:S(2)}) collective-permute-start(bf16[1,64,512]{2,1,0:T(8,128)(2,1)} %own_hbm.1), channel_id=1, source_target_pairs={{4,0},{5,1},{6,2},{7,3},{8,4},{9,5},{10,6},{11,7},{12,8},{13,9},{1... | collective-permute-start | bytes 196616 | tf_op jit(solution)/shard_map/ppermute | solution.py:28
  3.9 1.3 %collective-permute-start.2 = (bf16[1,64,512]{2,1,0:T(8,128)(2,1)}, bf16[1,64,512]{2,1,0:T(8,128)(2,1)S(1)}, u32[]{:S(2)}, u32[]{:S(2)}) collective-permute-start(bf16[1,64,512]{2,1,0:T(8,128)(2,1)} %own_hbm.1), channel_id=1, source_target_pairs={{9,0},{10,1},{11,2},{13,4},{14,5},{15,6},{25,16},{26,17},{27,18},{... | collective-permute-start | bytes 196616 | tf_op jit(solution)/shard_map/ppermute | solution.py:28
  5.2 1.9 %collective-permute-start.3 = (bf16[1,64,512]{2,1,0:T(8,128)(2,1)}, bf16[1,64,512]{2,1,0:T(8,128)(2,1)S(1)}, u32[]{:S(2)}, u32[]{:S(2)}) collective-permute-start(bf16[1,64,512]{2,1,0:T(8,128)(2,1)} %own_hbm.1), channel_id=1, source_target_pairs={{5,0},{6,1},{7,2},{9,4},{10,5},{11,6},{13,8},{14,9},{15,10},{21,16... | collective-permute-start | bytes 196616 | tf_op jit(solution)/shard_map/ppermute | solution.py:28
  7.1 1.6 %load.1 = (bf16[1,64,512]{2,1,0:T(8,128)(2,1)S(1)}, bf16[2352,256]{1,0:T(8,128)(2,1)S(1)}, f32[128,8]{1,0:T(8,128)S(1)}, f32[128,8]{1,0:T(8,128)S(1)}) custom-call(bf16[1,64,512]{2,1,0:T(8,128)(2,1)} %own_hbm.1, s32[1,2,16]{2,1,0:T(2,128)} %mask_hbm.1, s32[1,1,8]{2,1,0:T(1,128)} %mask_coarse_hbm.1, bf16[2352,256]{1,0:T(8,128)(2,1)} %constant.2.clone.table_hbm), custom_call_target="tpu_custom_call" | custom-call | flops 1000000000 | bytes 4000000 | tf_op jit(solution)/shard_map/load/pallas_call | solution.py:559
  8.7 2.0 %collective-permute-start.4 = (bf16[1,64,512]{2,1,0:T(8,128)(2,1)S(1)}, bf16[1,64,512]{2,1,0:T(8,128)(2,1)S(1)}, u32[]{:S(2)}, u32[]{:S(2)}) collective-permute-start(bf16[1,64,512]{2,1,0:T(8,128)(2,1)S(1)} %get-tuple-element.10.own), channel_id=1, source_target_pairs={{1,0},{2,1},{3,2},{5,4},{6,5},{7,6},{9,8},{10,9},{11,10},{13,12},{... | collective-permute-start | bytes 196616 | tf_op jit(solution)/shard_map/ppermute | solution.py:28
  10.7 0.0 collective-permute-done.far
  10.7 0.0 collective-permute-done.1.near
  10.7 1.5 %inner_spectra.1.spec = bf16[816,256]{1,0:T(8,128)(2,1)S(1)} custom-call(bf16[1,64,512]{2,1,0:T(8,128)(2,1)S(1)} %get-tuple-element.10.own, bf16[1,64,512]{2,1,0:T(8,128)(2,1)S(1)} %collective-permute-done.far, bf16[1,64,512]{2,1,0:T(8,128)(2,1)S(1)} %collective-permute-done.1.near, bf16[2352,256]{1,0:T(8,128)(2,1)S(1)} %get-tuple-element.9.table_ref), custom_call_target="tpu_custom_call" | custom-call | flops 3000000000 | bytes 4000000 | tf_op jit(solution)/shard_map/inner_spectra/pallas_call | solution.py:580
  12.3 3.1 %collective-permute-done.4.rim = bf16[1,64,512]{2,1,0:T(8,128)(2,1)S(1)} collective-permute-done((bf16[1,64,512]{2,1,0:T(8,128)(2,1)S(1)}, bf16[1,64,512]{2,1,0:T(8,128)(2,1)S(1)}, u32[]{:S(2)}, u32[]{:S(2)}) %collective-permute-start.4) | collective-permute-done | bytes 65568 | tf_op jit(solution)/shard_map/ppermute | solution.py:28
  15.3 1.8 %inner_maps.1 = (bf16[272,256]{1,0:T(8,128)(2,1)S(1)}, bf16[144,256]{1,0:T(8,128)(2,1)S(1)}, f32[2,1,16,1024]{3,2,1,0:T(8,128)S(1)}) custom-call(bf16[1,64,512]{2,1,0:T(8,128)(2,1)S(1)} %get-tuple-element.10.own, bf16[1,64,512]{2,1,0:T(8,128)(2,1)S(1)} %collective-permute-done.4.rim, bf16[2352,256]{1,0:T(8,128)(2,1)S(1)} %get-tuple-element.9.table_ref, ...), custom_call_target="tpu_custom_call" | custom-call | flops 2000000000 | bytes 4000000 | tf_op jit(solution)/shard_map/inner_maps/pallas_call | solution.py:590
  17.1 0.0 collective-permute-done.2.rim_far
  17.1 0.0 collective-permute-done.3.rim_near
  17.1 3.0 %outer_blocks.1 = (f32[1,2,2,16,1024]{4,3,2,1,0:T(8,128)}, f32[1,2,1,8,1024]{4,3,2,1,0:T(8,128)}) custom-call(bf16[1,64,512]{2,1,0:T(8,128)(2,1)S(1)} %collective-permute-done.far, bf16[1,64,512]{2,1,0:T(8,128)(2,1)S(1)} %collective-permute-done.1.near, bf16[1,64,512]{2,1,0:T(8,128)(2,1)S(1)} %collective-permute-done.2.rim_far, ...), custom_call_target="tpu_custom_call" | custom-call | flops 4000000000 | bytes 4000000 | tf_op jit(solution)/shard_map/outer_blocks/pallas_call | solution.py:603
Async XLA Ops:
  0.6 10.1 %collective-permute-start = (bf16[1,64,512]{2,1,0:T(8,128)(2,1)}, bf16[1,64,512]{2,1,0:T(8,128)(2,1)S(1)}, u32[]{:S(2)}, u32[]{:S(2)}) collective-permute-start(bf16[1,64,512]{2,1,0:T(8,128)(2,1)} %own_hbm.1), channel_id=1, source_target_pairs={{8,0},{9,1},{10,2},{11,3},{12,4},{13,5},{14,6},{15,7},{24,16},{25,... | collective-permute-start | bytes 196616 | tf_op jit(solution)/shard_map/ppermute | solution.py:28
  1.9 8.8 %collective-permute-start.1 = (bf16[1,64,512]{2,1,0:T(8,128)(2,1)}, bf16[1,64,512]{2,1,0:T(8,128)(2,1)S(1)}, u32[]{:S(2)}, u32[]{:S(2)}) collective-permute-start(bf16[1,64,512]{2,1,0:T(8,128)(2,1)} %own_hbm.1), channel_id=1, source_target_pairs={{4,0},{5,1},{6,2},{7,3},{8,4},{9,5},{10,6},{11,7},{12,8},{13,9},{1... | collective-permute-start | bytes 196616 | tf_op jit(solution)/shard_map/ppermute | solution.py:28
  3.9 13.3 %collective-permute-start.2 = (bf16[1,64,512]{2,1,0:T(8,128)(2,1)}, bf16[1,64,512]{2,1,0:T(8,128)(2,1)S(1)}, u32[]{:S(2)}, u32[]{:S(2)}) collective-permute-start(bf16[1,64,512]{2,1,0:T(8,128)(2,1)} %own_hbm.1), channel_id=1, source_target_pairs={{9,0},{10,1},{11,2},{13,4},{14,5},{15,6},{25,16},{26,17},{27,18},{... | collective-permute-start | bytes 196616 | tf_op jit(solution)/shard_map/ppermute | solution.py:28
  5.2 12.0 %collective-permute-start.3 = (bf16[1,64,512]{2,1,0:T(8,128)(2,1)}, bf16[1,64,512]{2,1,0:T(8,128)(2,1)S(1)}, u32[]{:S(2)}, u32[]{:S(2)}) collective-permute-start(bf16[1,64,512]{2,1,0:T(8,128)(2,1)} %own_hbm.1), channel_id=1, source_target_pairs={{5,0},{6,1},{7,2},{9,4},{10,5},{11,6},{13,8},{14,9},{15,10},{21,16... | collective-permute-start | bytes 196616 | tf_op jit(solution)/shard_map/ppermute | solution.py:28
  8.7 6.6 %collective-permute-start.4 = (bf16[1,64,512]{2,1,0:T(8,128)(2,1)S(1)}, bf16[1,64,512]{2,1,0:T(8,128)(2,1)S(1)}, u32[]{:S(2)}, u32[]{:S(2)}) collective-permute-start(bf16[1,64,512]{2,1,0:T(8,128)(2,1)S(1)} %get-tuple-element.10.own), channel_id=1, source_target_pairs={{1,0},{2,1},{3,2},{5,4},{6,5},{7,6},{9,8},{10,9},{11,10},{13,12},{... | collective-permute-start | bytes 196616 | tf_op jit(solution)/shard_map/ppermute | solution.py:28

commit v13 on v11

--- a/solution.py
+++ b/solution.py
@@ -486,13 +486,19 @@
     return start
 
 
+def copy_kernel(own_hbm, own, sem):
+    copy = pltpu.make_async_copy(own_hbm, own, sem)
+    copy.start()
+    copy.wait()
+
+
 def inner_kernel(
     levels, cuts,
-    own_hbm, near, far, mask_hbm, mask_coarse_hbm, table_hbm,
-    spec, own, table_ref, kept, kept_coarse,
+    own, far, near, mask_hbm, mask_coarse_hbm, table_hbm,
+    maps, table_ref, kept, kept_coarse,
     mask, mask_coarse, pad, pad_coarse, row_ref, *rest,
 ):
-    *sections, sems = rest
+    *scratch, sems = rest
     start = copier(sems)
 
     def table(first, last):
@@ -500,55 +506,36 @@
         return start(table_hbm.at[piece], table_ref.at[piece])
 
     fine_at, shift_at, map_at, coarse_at, end = cuts
-    copies = [start(own_hbm, own), start(mask_hbm, mask), start(mask_coarse_hbm, mask_coarse)]
-    tables = [table(shift_at, coarse_at), table(coarse_at, end)]
+    copies = [table(shift_at, coarse_at), start(mask_hbm, mask), start(mask_coarse_hbm, mask_coarse)]
+    outer_ready = table(coarse_at, end)
+    size = 3 + 3 * len(levels)
+    sections, spec_refs, rest = scratch[:size], scratch[size : size + 1], scratch[size + 1 :]
     strips = ((own,), (near,), (far,))
+    rows = levels[0].rows
 
     def run(pairs):
         if pairs:
             write_row_table(row_ref, levels[0])
             write_fine_table(table_ref, fine_at)
-            transform_rows(levels, range(1, pairs + 1), strips, row_ref, sections)
+            transform_rows(levels, range(pairs + 1), strips, row_ref, sections)
+            transform_columns(levels, range(pairs + 1), table_ref, sections, spec_refs)
         for wait in copies:
             wait()
         if pairs:
             write_mask_columns(mask, pad, kept)
             write_mask_columns(mask_coarse, pad_coarse, kept_coarse)
-            transform_rows(levels, (0,), strips, row_ref, sections)
-            transform_columns(levels, range(pairs + 1), table_ref, sections, [spec])
-        for wait in tables:
-            wait()
-
-    for_pairs(run)
-
-
-def middle_kernel(
-    inner_levels, levels, cuts, row_at,
-    own, rim, table_ref, spec, kept,
-    own_fine, own_coarse, maps,
-    *rest,
-):
-    size = 3 + 3 * len(levels)
-    sections, pair = rest[:size], rest[size:]
-    fine_at, shift_at, map_at, coarse_at, end = cuts
-    row_ref = table_ref.at[pl.ds(row_at, row_places(levels)[1])]
-    rows = inner_levels[0].rows
-
-    def run(pairs):
-        if pairs:
-            transform_rows(levels, (0,), ((own, rim),), row_ref, sections)
-            transform_columns(levels, (0,), table_ref, sections, (own_fine, own_coarse))
             write_maps(
-                inner_levels, pairs, [spec.at[pl.ds(0, rows)]], [spec.at[pl.ds(rows, pairs * rows)]], (kept,),
-                table_ref, shift_at, map_at, pair, (maps,))
+                levels, pairs, [spec_refs[0].at[pl.ds(0, rows)]], [spec_refs[0].at[pl.ds(rows, pairs * rows)]],
+                (kept,), table_ref, shift_at, map_at, rest, (maps,))
         clear_maps(pairs, (maps,))
+        outer_ready()
 
     for_pairs(run)
 
 
 def outer_kernel(
     levels, cuts, inner, row_at,
-    near, far, rim_near, rim_far, table_ref, own_fine, own_coarse, kept, kept_coarse, inner_maps,
+    own, far, near, rim_far, rim_near, rim, table_ref, kept, kept_coarse, inner_maps,
     out_fine, out_coarse,
     maps, maps_coarse, *rest,
 ):
@@ -558,7 +545,8 @@
     row_ref = table_ref.at[pl.ds(row_at, row_places(levels)[1])]
     size, count = 3 + 3 * len(levels), len(levels)
     sections, spec_refs, rest = scratch[:size], scratch[size : size + count], scratch[size + count :]
-    strips = ((near, rim_near), (far, rim_far))
+    strips = ((own, rim), (near, rim_near), (far, rim_far))
+    own_specs = [spec.at[pl.ds(0, level.rows)] for level, spec in zip(levels, spec_refs)]
 
     def run(pairs):
         stores = [
@@ -566,10 +554,12 @@
             pltpu.make_async_copy(maps_coarse, out_coarse.at[0], sems.at[2])]
         clear_maps(pairs, (maps, maps_coarse))
         if pairs:
-            transform_rows(levels, range(pairs), strips, row_ref, sections)
-            transform_columns(levels, range(pairs), table_ref, sections, spec_refs)
+            transform_rows(levels, range(pairs + 1), strips, row_ref, sections)
+            transform_columns(levels, range(pairs + 1), table_ref, sections, spec_refs)
+            other_specs = [
+                spec.at[pl.ds(level.rows, pairs * level.rows)] for level, spec in zip(levels, spec_refs)]
             write_maps(
-                levels, pairs, (own_fine, own_coarse), spec_refs, (kept, kept_coarse), table_ref, shift_at, map_at,
+                levels, pairs, own_specs, other_specs, (kept, kept_coarse), table_ref, shift_at, map_at,
                 rest, (maps, maps_coarse), [store.start for store in stores])
         else:
             for store in stores:
@@ -581,7 +571,7 @@
     inner_stored()
 
 
-def correlate(own, near, far, rim, rim_near, rim_far, mask_fine, mask_coarse):
+def correlate(own, near, far, rim_of, rim_near, rim_far, mask_fine, mask_coarse):
     strip_rows, width = own.shape[1:]
     fine, coarse = mask_fine.shape[1], mask_coarse.shape[1]
     inner = fine - 1
@@ -607,16 +597,25 @@
     def cost(flops):
         return pl.CostEstimate(flops=flops, bytes_accessed=4 * 10**6, transcendentals=0)
 
-    spec, own_kept, handed, *kept = pl.pallas_call(
+    kept_own = pl.pallas_call(
+        copy_kernel,
+        out_shape=jax.ShapeDtypeStruct(own.shape, bf16),
+        in_specs=[hbm],
+        out_specs=vmem,
+        scratch_shapes=[pltpu.SemaphoreType.DMA],
+        cost_estimate=cost(10**9),
+        name="own_pixels",
+    )(own)
+    rim = rim_of(kept_own)
+    maps, handed, *kept = pl.pallas_call(
         functools.partial(inner_kernel, inner_levels, cuts),
         out_shape=(
-            jax.ShapeDtypeStruct((3 * inner_levels[0].rows, 2 * LANES), bf16),
-            jax.ShapeDtypeStruct(own.shape, bf16),
+            jax.ShapeDtypeStruct((2, inner, 4 * inner_levels[0].quads, shifts), f32),
             jax.ShapeDtypeStruct(table.shape, bf16),
             *(jax.ShapeDtypeStruct((LANES, 8), f32) for _ in range(2)),
         ),
-        in_specs=[hbm, vmem, vmem, hbm, hbm, hbm],
-        out_specs=(vmem,) * 5,
+        in_specs=[vmem] * 3 + [hbm] * 3,
+        out_specs=(vmem,) * 4,
         scratch_shapes=[
             pltpu.VMEM(mask_fine.shape, jnp.int32),
             pltpu.VMEM(mask_coarse.shape, jnp.int32),
@@ -624,25 +623,14 @@
             pltpu.VMEM((8, LANES), f32),
             pltpu.VMEM((row_places(inner_levels)[1], 2 * strip_rows), bf16),
             *section_scratch(inner_levels, width, 3),
-            pltpu.SemaphoreType.DMA((5,)),
+            *spec_scratch(inner_levels, 3),
+            *pair_scratch(inner_levels),
+            pltpu.SemaphoreType.DMA((4,)),
         ],
         compiler_params=params,
         cost_estimate=cost(3 * 10**9),
-        name="inner_spectra",
-    )(own, near, far, mask_fine, mask_coarse, table)
-    *own_specs, maps = pl.pallas_call(
-        functools.partial(middle_kernel, inner_levels, outer_levels, cuts, row_at),
-        out_shape=(
-            *(jax.ShapeDtypeStruct((level.rows, 2 * LANES), bf16) for level in outer_levels),
-            jax.ShapeDtypeStruct((2, inner, 4 * inner_levels[0].quads, shifts), f32),
-        ),
-        in_specs=[vmem] * 5,
-        out_specs=(vmem,) * 3,
-        scratch_shapes=[*section_scratch(outer_levels, width, 1), *pair_scratch(inner_levels)],
-        compiler_params=params,
-        cost_estimate=cost(2 * 10**9),
-        name="inner_maps",
-    )(own_kept, rim, handed, spec, kept[0])
+        name="inner_blocks",
+    )(kept_own, far, near, mask_fine, mask_coarse, table)
     return pl.pallas_call(
         functools.partial(outer_kernel, outer_levels, cuts, inner, row_at),
         out_shape=(
@@ -653,22 +641,23 @@
         out_specs=(hbm, hbm),
         scratch_shapes=[
             *(pltpu.VMEM((2, level.blocks, 4 * level.quads, shifts), f32) for level in outer_levels),
-            *section_scratch(outer_levels, width, 2),
-            *spec_scratch(outer_levels, 2),
+            *section_scratch(outer_levels, width, 3),
+            *spec_scratch(outer_levels, 3),
             *pair_scratch(outer_levels),
             pltpu.SemaphoreType.DMA((3,)),
         ],
         compiler_params=params,
         cost_estimate=cost(4 * 10**9),
         name="outer_blocks",
-    )(near, far, rim_near, rim_far, handed, *own_specs, *kept, maps)
+    )(kept_own, far, near, rim_far, rim_near, rim, handed, *kept, maps)
 
 
 def local(sections, mask_fine, mask_coarse):
     far = from_device(sections, 2, 0)
     near = from_device(sections, 1, 0)
-    rims = [from_device(sections, z, 1) for z in range(3)]
-    return correlate(sections, near, far, *rims, mask_fine, mask_coarse)
+    rim_near, rim_far = from_device(sections, 1, 1), from_device(sections, 2, 1)
+    return correlate(
+        sections, near, far, lambda own: from_device(own, 0, 1), rim_near, rim_far, mask_fine, mask_coarse)
 
 
 def solution(mesh):

time: 20.1 us -> 20.8 us (1.035)
  local copies, waits for them, and re-layouts: 0 us -> 0.84 us
  waiting for transfers between devices: 4.95 us -> 4.42 us
  Pallas kernels: 7.05 us -> 7.37 us
    unnamed x0 -> x4, local copies, waits for them, and re-layouts: none -> 0.84 us
    ppermute x5, waiting for transfers between devices: 4.95 us -> 4.42 us  [from_device(): return lax.ppermute(value, ('sec', 'strip'), pairs)]
    pallas_call x1, Pallas kernels: 2.96 us -> 3.41 us  [correlate(): pl.pallas_call(functools.partial(outer_kernel, outer_levels, cuts, inner,...]
    pallas_call x1, Pallas kernels: 1.8 us -> 1.48 us  [correlate(): pl.pallas_call(copy_kernel, out_shape=jax.ShapeDtypeStruct(own.shape, bf1...]
  transfers between devices with their start and end apart: 5 -> 5, of which waited for: 2 -> 3; matrix products, arithmetic and copies ran while one was open for 0% -> 0% of each run, Pallas kernels for 21% -> 19%
where the time goes in v13:
time: 20.8 us; the launch traced here: 20.5 us
  Pallas kernels  7.37 us (35%)
  starting transfers between devices  7.13 us (34%)
  waiting for transfers between devices  4.42 us (21%)
  local copies, waits for them, and re-layouts  0.84 us (4%)
  between operations  0.7 us (3%)
    ppermute x5, starting transfers between devices, from_device(): return lax.ppermute(value, ('sec', 'strip'), pairs)  7.13 us
    ppermute x5, waiting for transfers between devices, from_device(): return lax.ppermute(value, ('sec', 'strip'), pairs)  4.42 us
    pallas_call x1, Pallas kernels, correlate(): pl.pallas_call(functools.partial(outer_kernel, outer_levels, cuts, inner,...  3.41 us
    pallas_call x1, Pallas kernels, correlate(): pl.pallas_call(functools.partial(inner_kernel, inner_levels, cuts), out_s...  2.49 us
    pallas_call x1, Pallas kernels, correlate(): pl.pallas_call(copy_kernel, out_shape=jax.ShapeDtypeStruct(own.shape, bf1...  1.48 us
    unnamed x4, local copies, waits for them, and re-layouts  0.84 us
  transfers between devices with their start and end apart: 5, of which 3 were waited for; matrix products, arithmetic and copies ran while one was open for 0% of the time, Pallas kernels for 19%

profile of v13, /device:TPU:1, one launch (start us, length us, event | category | flops | bytes accessed | tf_op | source)
XLA Modules:
  0.0 20.5 jit_solution(12010315553306960928)
XLA Ops:
  0.6 1.3 %collective-permute-start.1 = (bf16[1,64,512]{2,1,0:T(8,128)(2,1)}, bf16[1,64,512]{2,1,0:T(8,128)(2,1)S(1)}, u32[]{:S(2)}, u32[]{:S(2)}) collective-permute-start(bf16[1,64,512]{2,1,0:T(8,128)(2,1)} %own_hbm.1), channel_id=1, source_target_pairs={{4,0},{5,1},{6,2},{7,3},{8,4},{9,5},{10,6},{11,7},{12,8},{13,9},{1... | collective-permute-start | bytes 196616 | tf_op jit(solution)/shard_map/ppermute | solution.py:28
  1.9 1.3 %collective-permute-start = (bf16[1,64,512]{2,1,0:T(8,128)(2,1)}, bf16[1,64,512]{2,1,0:T(8,128)(2,1)S(1)}, u32[]{:S(2)}, u32[]{:S(2)}) collective-permute-start(bf16[1,64,512]{2,1,0:T(8,128)(2,1)} %own_hbm.1), channel_id=1, source_target_pairs={{8,0},{9,1},{10,2},{11,3},{12,4},{13,5},{14,6},{15,7},{24,16},{25,... | collective-permute-start | bytes 196616 | tf_op jit(solution)/shard_map/ppermute | solution.py:28
  3.2 1.3 %collective-permute-start.3 = (bf16[1,64,512]{2,1,0:T(8,128)(2,1)}, bf16[1,64,512]{2,1,0:T(8,128)(2,1)S(1)}, u32[]{:S(2)}, u32[]{:S(2)}) collective-permute-start(bf16[1,64,512]{2,1,0:T(8,128)(2,1)} %own_hbm.1), channel_id=1, source_target_pairs={{5,0},{6,1},{7,2},{9,4},{10,5},{11,6},{13,8},{14,9},{15,10},{21,16... | collective-permute-start | bytes 196616 | tf_op jit(solution)/shard_map/ppermute | solution.py:28
  4.5 1.3 %collective-permute-start.2 = (bf16[1,64,512]{2,1,0:T(8,128)(2,1)}, bf16[1,64,512]{2,1,0:T(8,128)(2,1)S(1)}, u32[]{:S(2)}, u32[]{:S(2)}) collective-permute-start(bf16[1,64,512]{2,1,0:T(8,128)(2,1)} %own_hbm.1), channel_id=1, source_target_pairs={{9,0},{10,1},{11,2},{13,4},{14,5},{15,6},{25,16},{26,17},{27,18},{... | collective-permute-start | bytes 196616 | tf_op jit(solution)/shard_map/ppermute | solution.py:28
  5.8 1.5 %own_pixels.1.own = bf16[1,64,512]{2,1,0:T(8,128)(2,1)} custom-call(bf16[1,64,512]{2,1,0:T(8,128)(2,1)} %own_hbm.1), custom_call_target="tpu_custom_call" | custom-call | flops 1000000000 | bytes 4000000 | tf_op jit(solution)/shard_map/own_pixels/pallas_call | solution.py:600
  7.3 2.0 %collective-permute-start.4 = (bf16[1,64,512]{2,1,0:T(8,128)(2,1)}, bf16[1,64,512]{2,1,0:T(8,128)(2,1)S(1)}, u32[]{:S(2)}, u32[]{:S(2)}) collective-permute-start(bf16[1,64,512]{2,1,0:T(8,128)(2,1)} %own_pixels.1.own), channel_id=1, source_target_pairs={{1,0},{2,1},{3,2},{5,4},{6,5},{7,6},{9,8},{10,9},{11,10},{13,12},{... | collective-permute-start | bytes 196616 | tf_op jit(solution)/shard_map/ppermute | solution.py:28
  9.3 0.0 collective-permute-done.1.near
  9.3 0.6 %collective-permute-done.far = bf16[1,64,512]{2,1,0:T(8,128)(2,1)S(1)} collective-permute-done((bf16[1,64,512]{2,1,0:T(8,128)(2,1)}, bf16[1,64,512]{2,1,0:T(8,128)(2,1)S(1)}, u32[]{:S(2)}, u32[]{:S(2)}) %collective-permute-start) | collective-permute-done | bytes 65568 | tf_op jit(solution)/shard_map/ppermute | solution.py:28
  9.9 0.0 copy-start
  9.9 0.8 %copy-done = bf16[1,64,512]{2,1,0:T(8,128)(2,1)S(1)} copy-done((bf16[1,64,512]{2,1,0:T(8,128)(2,1)S(1)}, bf16[1,64,512]{2,1,0:T(8,128)(2,1)}, u32[]{:S(2)}) %copy-start) | copy-done | bytes 65560
  10.7 0.0 copy-start.1
  10.7 2.5 %inner_blocks.1 = (f32[2,1,16,1024]{3,2,1,0:T(8,128)S(1)}, bf16[2272,256]{1,0:T(8,128)(2,1)S(1)}, f32[128,8]{1,0:T(8,128)S(1)}, f32[128,8]{1,0:T(8,128)S(1)}) custom-call(bf16[1,64,512]{2,1,0:T(8,128)(2,1)S(1)} %copy-done, bf16[1,64,512]{2,1,0:T(8,128)(2,1)S(1)} %collective-permute-done.far, bf16[1,64,512]{2,1,0:T(8,128)(2,1)S(1)} %collective-permute-done.1.near, ...), custom_call_target="tpu_custom_call" | custom-call | flops 3000000000 | bytes 4000000 | tf_op jit(solution)/shard_map/inner_blocks/pallas_call | solution.py:610
  13.2 0.7 %collective-permute-done.4.rim = bf16[1,64,512]{2,1,0:T(8,128)(2,1)S(1)} collective-permute-done((bf16[1,64,512]{2,1,0:T(8,128)(2,1)}, bf16[1,64,512]{2,1,0:T(8,128)(2,1)S(1)}, u32[]{:S(2)}, u32[]{:S(2)}) %collective-permute-start.4) | collective-permute-done | bytes 65568 | tf_op jit(solution)/shard_map/ppermute | solution.py:28
  14.0 0.0 collective-permute-done.3.rim_near
  14.0 3.1 %collective-permute-done.2.rim_far = bf16[1,64,512]{2,1,0:T(8,128)(2,1)S(1)} collective-permute-done((bf16[1,64,512]{2,1,0:T(8,128)(2,1)}, bf16[1,64,512]{2,1,0:T(8,128)(2,1)S(1)}, u32[]{:S(2)}, u32[]{:S(2)}) %collective-permute-start.2) | collective-permute-done | bytes 65568 | tf_op jit(solution)/shard_map/ppermute | solution.py:28
  17.1 0.0 copy-done.1
  17.1 3.4 %outer_blocks.1 = (f32[1,2,2,16,1024]{4,3,2,1,0:T(8,128)}, f32[1,2,1,8,1024]{4,3,2,1,0:T(8,128)}) custom-call(bf16[1,64,512]{2,1,0:T(8,128)(2,1)S(1)} %copy-done.1, bf16[1,64,512]{2,1,0:T(8,128)(2,1)S(1)} %collective-permute-done.far, bf16[1,64,512]{2,1,0:T(8,128)(2,1)S(1)} %collective-permute-done.1.near, ...), custom_call_target="tpu_custom_call" | custom-call | flops 4000000000 | bytes 4000000 | tf_op jit(solution)/shard_map/outer_blocks/pallas_call | solution.py:634
Async XLA Ops:
  0.6 8.7 %collective-permute-start.1 = (bf16[1,64,512]{2,1,0:T(8,128)(2,1)}, bf16[1,64,512]{2,1,0:T(8,128)(2,1)S(1)}, u32[]{:S(2)}, u32[]{:S(2)}) collective-permute-start(bf16[1,64,512]{2,1,0:T(8,128)(2,1)} %own_hbm.1), channel_id=1, source_target_pairs={{4,0},{5,1},{6,2},{7,3},{8,4},{9,5},{10,6},{11,7},{12,8},{13,9},{1... | collective-permute-start | bytes 196616 | tf_op jit(solution)/shard_map/ppermute | solution.py:28
  1.9 8.0 %collective-permute-start = (bf16[1,64,512]{2,1,0:T(8,128)(2,1)}, bf16[1,64,512]{2,1,0:T(8,128)(2,1)S(1)}, u32[]{:S(2)}, u32[]{:S(2)}) collective-permute-start(bf16[1,64,512]{2,1,0:T(8,128)(2,1)} %own_hbm.1), channel_id=1, source_target_pairs={{8,0},{9,1},{10,2},{11,3},{12,4},{13,5},{14,6},{15,7},{24,16},{25,... | collective-permute-start | bytes 196616 | tf_op jit(solution)/shard_map/ppermute | solution.py:28
  3.2 10.8 %collective-permute-start.3 = (bf16[1,64,512]{2,1,0:T(8,128)(2,1)}, bf16[1,64,512]{2,1,0:T(8,128)(2,1)S(1)}, u32[]{:S(2)}, u32[]{:S(2)}) collective-permute-start(bf16[1,64,512]{2,1,0:T(8,128)(2,1)} %own_hbm.1), channel_id=1, source_target_pairs={{5,0},{6,1},{7,2},{9,4},{10,5},{11,6},{13,8},{14,9},{15,10},{21,16... | collective-permute-start | bytes 196616 | tf_op jit(solution)/shard_map/ppermute | solution.py:28
  4.5 12.5 %collective-permute-start.2 = (bf16[1,64,512]{2,1,0:T(8,128)(2,1)}, bf16[1,64,512]{2,1,0:T(8,128)(2,1)S(1)}, u32[]{:S(2)}, u32[]{:S(2)}) collective-permute-start(bf16[1,64,512]{2,1,0:T(8,128)(2,1)} %own_hbm.1), channel_id=1, source_target_pairs={{9,0},{10,1},{11,2},{13,4},{14,5},{15,6},{25,16},{26,17},{27,18},{... | collective-permute-start | bytes 196616 | tf_op jit(solution)/shard_map/ppermute | solution.py:28
  7.3 6.7 %collective-permute-start.4 = (bf16[1,64,512]{2,1,0:T(8,128)(2,1)}, bf16[1,64,512]{2,1,0:T(8,128)(2,1)S(1)}, u32[]{:S(2)}, u32[]{:S(2)}) collective-permute-start(bf16[1,64,512]{2,1,0:T(8,128)(2,1)} %own_pixels.1.own), channel_id=1, source_target_pairs={{1,0},{2,1},{3,2},{5,4},{6,5},{7,6},{9,8},{10,9},{11,10},{13,12},{... | collective-permute-start | bytes 196616 | tf_op jit(solution)/shard_map/ppermute | solution.py:28
  9.9 0.8 %copy-start = (bf16[1,64,512]{2,1,0:T(8,128)(2,1)S(1)}, bf16[1,64,512]{2,1,0:T(8,128)(2,1)}, u32[]{:S(2)}) copy-start(bf16[1,64,512]{2,1,0:T(8,128)(2,1)} %own_pixels.1.own) | copy-start | bytes 196612
  10.7 6.3 %copy-start.1 = (bf16[1,64,512]{2,1,0:T(8,128)(2,1)S(1)}, bf16[1,64,512]{2,1,0:T(8,128)(2,1)}, u32[]{:S(2)}) copy-start(bf16[1,64,512]{2,1,0:T(8,128)(2,1)} %own_pixels.1.own) | copy-start | bytes 196612

commit v14 on v11

--- a/solution.py
+++ b/solution.py
@@ -489,10 +489,10 @@
 def inner_kernel(
     levels, cuts,
     own_hbm, near, far, mask_hbm, mask_coarse_hbm, table_hbm,
-    spec, own, table_ref, kept, kept_coarse,
+    maps, own, table_ref, kept, kept_coarse,
     mask, mask_coarse, pad, pad_coarse, row_ref, *rest,
 ):
-    *sections, sems = rest
+    *scratch, sems = rest
     start = copier(sems)
 
     def table(first, last):
@@ -500,50 +500,45 @@
         return start(table_hbm.at[piece], table_ref.at[piece])
 
     fine_at, shift_at, map_at, coarse_at, end = cuts
-    copies = [start(own_hbm, own), start(mask_hbm, mask), start(mask_coarse_hbm, mask_coarse)]
-    tables = [table(shift_at, coarse_at), table(coarse_at, end)]
+    own_ready = start(own_hbm, own)
+    copies = [table(shift_at, coarse_at), start(mask_hbm, mask), start(mask_coarse_hbm, mask_coarse)]
+    outer_ready = table(coarse_at, end)
+    size = 3 + 3 * len(levels)
+    sections, spec_refs, rest = scratch[:size], scratch[size : size + 1], scratch[size + 1 :]
     strips = ((own,), (near,), (far,))
+    rows = levels[0].rows
 
     def run(pairs):
         if pairs:
             write_row_table(row_ref, levels[0])
             write_fine_table(table_ref, fine_at)
             transform_rows(levels, range(1, pairs + 1), strips, row_ref, sections)
+        own_ready()
+        if pairs:
+            transform_rows(levels, (0,), strips, row_ref, sections)
+            transform_columns(levels, range(pairs + 1), table_ref, sections, spec_refs)
         for wait in copies:
             wait()
         if pairs:
             write_mask_columns(mask, pad, kept)
             write_mask_columns(mask_coarse, pad_coarse, kept_coarse)
-            transform_rows(levels, (0,), strips, row_ref, sections)
-            transform_columns(levels, range(pairs + 1), table_ref, sections, [spec])
-        for wait in tables:
-            wait()
+            write_maps(
+                levels, pairs, [spec_refs[0].at[pl.ds(0, rows)]], [spec_refs[0].at[pl.ds(rows, pairs * rows)]],
+                (kept,), table_ref, shift_at, map_at, rest, (maps,))
+        clear_maps(pairs, (maps,))
+        outer_ready()
 
     for_pairs(run)
 
 
-def middle_kernel(
-    inner_levels, levels, cuts, row_at,
-    own, rim, table_ref, spec, kept,
-    own_fine, own_coarse, maps,
-    *rest,
-):
-    size = 3 + 3 * len(levels)
-    sections, pair = rest[:size], rest[size:]
-    fine_at, shift_at, map_at, coarse_at, end = cuts
+def own_kernel(levels, row_at, own, rim, table_ref, *rest):
+    spec_refs, sections = rest[: len(levels)], rest[len(levels) :]
     row_ref = table_ref.at[pl.ds(row_at, row_places(levels)[1])]
-    rows = inner_levels[0].rows
-
-    def run(pairs):
-        if pairs:
-            transform_rows(levels, (0,), ((own, rim),), row_ref, sections)
-            transform_columns(levels, (0,), table_ref, sections, (own_fine, own_coarse))
-            write_maps(
-                inner_levels, pairs, [spec.at[pl.ds(0, rows)]], [spec.at[pl.ds(rows, pairs * rows)]], (kept,),
-                table_ref, shift_at, map_at, pair, (maps,))
-        clear_maps(pairs, (maps,))
-
-    for_pairs(run)
+
+    @pl.when(sections_ahead() >= 1)
+    def _():
+        transform_rows(levels, (0,), ((own, rim),), row_ref, sections)
+        transform_columns(levels, (0,), table_ref, sections, spec_refs)
 
 
 def outer_kernel(
@@ -607,10 +602,10 @@
     def cost(flops):
         return pl.CostEstimate(flops=flops, bytes_accessed=4 * 10**6, transcendentals=0)
 
-    spec, own_kept, handed, *kept = pl.pallas_call(
+    maps, own_kept, handed, *kept = pl.pallas_call(
         functools.partial(inner_kernel, inner_levels, cuts),
         out_shape=(
-            jax.ShapeDtypeStruct((3 * inner_levels[0].rows, 2 * LANES), bf16),
+            jax.ShapeDtypeStruct((2, inner, 4 * inner_levels[0].quads, shifts), f32),
             jax.ShapeDtypeStruct(own.shape, bf16),
             jax.ShapeDtypeStruct(table.shape, bf16),
             *(jax.ShapeDtypeStruct((LANES, 8), f32) for _ in range(2)),
@@ -624,25 +619,24 @@
             pltpu.VMEM((8, LANES), f32),
             pltpu.VMEM((row_places(inner_levels)[1], 2 * strip_rows), bf16),
             *section_scratch(inner_levels, width, 3),
+            *spec_scratch(inner_levels, 3),
+            *pair_scratch(inner_levels),
             pltpu.SemaphoreType.DMA((5,)),
         ],
         compiler_params=params,
         cost_estimate=cost(3 * 10**9),
-        name="inner_spectra",
+        name="inner_blocks",
     )(own, near, far, mask_fine, mask_coarse, table)
-    *own_specs, maps = pl.pallas_call(
-        functools.partial(middle_kernel, inner_levels, outer_levels, cuts, row_at),
-        out_shape=(
-            *(jax.ShapeDtypeStruct((level.rows, 2 * LANES), bf16) for level in outer_levels),
-            jax.ShapeDtypeStruct((2, inner, 4 * inner_levels[0].quads, shifts), f32),
-        ),
-        in_specs=[vmem] * 5,
-        out_specs=(vmem,) * 3,
-        scratch_shapes=[*section_scratch(outer_levels, width, 1), *pair_scratch(inner_levels)],
+    own_specs = pl.pallas_call(
+        functools.partial(own_kernel, outer_levels, row_at),
+        out_shape=tuple(jax.ShapeDtypeStruct((level.rows, 2 * LANES), bf16) for level in outer_levels),
+        in_specs=[vmem] * 3,
+        out_specs=(vmem,) * 2,
+        scratch_shapes=section_scratch(outer_levels, width, 1),
         compiler_params=params,
         cost_estimate=cost(2 * 10**9),
-        name="inner_maps",
-    )(own_kept, rim, handed, spec, kept[0])
+        name="own_outer_blocks",
+    )(own_kept, rim, handed)
     return pl.pallas_call(
         functools.partial(outer_kernel, outer_levels, cuts, inner, row_at),
         out_shape=(

time: 20.1 us -> 18.8 us (0.935)
  waiting for transfers between devices: 4.95 us -> 3.45 us
  Pallas kernels: 7.05 us -> 7.28 us
    ppermute x5, waiting for transfers between devices: 4.95 us -> 3.45 us  [from_device(): return lax.ppermute(value, ('sec', 'strip'), pairs)]
    pallas_call x1, Pallas kernels: 2.29 us -> 3.11 us  [correlate(): pl.pallas_call(functools.partial(inner_kernel, inner_levels, cuts), out_s...]
    pallas_call x1, Pallas kernels: 1.8 us -> 1.23 us  [correlate(): pl.pallas_call(functools.partial(own_kernel, outer_levels, row_at), out_s...]
  transfers between devices with their start and end apart: 5 -> 5, of which waited for: 2 -> 3; matrix products, arithmetic and copies ran while one was open for 0% -> 0% of each run, Pallas kernels for 21% -> 23%
where the time goes in v14:
time: 18.8 us; the launch traced here: 18.6 us
  Pallas kernels  7.28 us (39%)
  starting transfers between devices  7.13 us (38%)
  waiting for transfers between devices  3.45 us (18%)
  between operations  0.7 us (4%)
    ppermute x5, starting transfers between devices, from_device(): return lax.ppermute(value, ('sec', 'strip'), pairs)  7.13 us
    ppermute x5, waiting for transfers between devices, from_device(): return lax.ppermute(value, ('sec', 'strip'), pairs)  3.45 us
    pallas_call x1, Pallas kernels, correlate(): pl.pallas_call(functools.partial(inner_kernel, inner_levels, cuts), out_s...  3.11 us
    pallas_call x1, Pallas kernels, correlate(): pl.pallas_call(functools.partial(outer_kernel, outer_levels, cuts, inner,...  2.94 us
    pallas_call x1, Pallas kernels, correlate(): pl.pallas_call(functools.partial(own_kernel, outer_levels, row_at), out_s...  1.23 us
  transfers between devices with their start and end apart: 5, of which 3 were waited for; matrix products, arithmetic and copies ran while one was open for 0% of the time, Pallas kernels for 23%

profile of v14, /device:TPU:1, one launch (start us, length us, event | category | flops | bytes accessed | tf_op | source)
XLA Modules:
  0.0 18.6 jit_solution(8243872455488856627)
XLA Ops:
  0.6 1.3 %collective-permute-start.1 = (bf16[1,64,512]{2,1,0:T(8,128)(2,1)}, bf16[1,64,512]{2,1,0:T(8,128)(2,1)S(1)}, u32[]{:S(2)}, u32[]{:S(2)}) collective-permute-start(bf16[1,64,512]{2,1,0:T(8,128)(2,1)} %own_hbm.1), channel_id=1, source_target_pairs={{8,0},{9,1},{10,2},{11,3},{12,4},{13,5},{14,6},{15,7},{24,16},{25,... | collective-permute-start | bytes 196616 | tf_op jit(solution)/shard_map/ppermute | solution.py:28
  1.9 1.3 %collective-permute-start = (bf16[1,64,512]{2,1,0:T(8,128)(2,1)}, bf16[1,64,512]{2,1,0:T(8,128)(2,1)S(1)}, u32[]{:S(2)}, u32[]{:S(2)}) collective-permute-start(bf16[1,64,512]{2,1,0:T(8,128)(2,1)} %own_hbm.1), channel_id=1, source_target_pairs={{4,0},{5,1},{6,2},{7,3},{8,4},{9,5},{10,6},{11,7},{12,8},{13,9},{1... | collective-permute-start | bytes 196616 | tf_op jit(solution)/shard_map/ppermute | solution.py:28
  3.2 1.3 %collective-permute-start.3 = (bf16[1,64,512]{2,1,0:T(8,128)(2,1)}, bf16[1,64,512]{2,1,0:T(8,128)(2,1)S(1)}, u32[]{:S(2)}, u32[]{:S(2)}) collective-permute-start(bf16[1,64,512]{2,1,0:T(8,128)(2,1)} %own_hbm.1), channel_id=1, source_target_pairs={{9,0},{10,1},{11,2},{13,4},{14,5},{15,6},{25,16},{26,17},{27,18},{... | collective-permute-start | bytes 196616 | tf_op jit(solution)/shard_map/ppermute | solution.py:28
  4.5 1.3 %collective-permute-start.2 = (bf16[1,64,512]{2,1,0:T(8,128)(2,1)}, bf16[1,64,512]{2,1,0:T(8,128)(2,1)S(1)}, u32[]{:S(2)}, u32[]{:S(2)}) collective-permute-start(bf16[1,64,512]{2,1,0:T(8,128)(2,1)} %own_hbm.1), channel_id=1, source_target_pairs={{5,0},{6,1},{7,2},{9,4},{10,5},{11,6},{13,8},{14,9},{15,10},{21,16... | collective-permute-start | bytes 196616 | tf_op jit(solution)/shard_map/ppermute | solution.py:28
  5.8 2.0 %collective-permute-start.4 = (bf16[1,64,512]{2,1,0:T(8,128)(2,1)}, bf16[1,64,512]{2,1,0:T(8,128)(2,1)S(1)}, u32[]{:S(2)}, u32[]{:S(2)}) collective-permute-start(bf16[1,64,512]{2,1,0:T(8,128)(2,1)} %own_hbm.1), channel_id=1, source_target_pairs={{1,0},{2,1},{3,2},{5,4},{6,5},{7,6},{9,8},{10,9},{11,10},{13,12},{... | collective-permute-start | bytes 196616 | tf_op jit(solution)/shard_map/ppermute | solution.py:28
  7.8 0.0 collective-permute-done.1.far
  7.8 1.4 %collective-permute-done.near = bf16[1,64,512]{2,1,0:T(8,128)(2,1)S(1)} collective-permute-done((bf16[1,64,512]{2,1,0:T(8,128)(2,1)}, bf16[1,64,512]{2,1,0:T(8,128)(2,1)S(1)}, u32[]{:S(2)}, u32[]{:S(2)}) %collective-permute-start) | collective-permute-done | bytes 65568 | tf_op jit(solution)/shard_map/ppermute | solution.py:28
  9.2 3.1 %inner_blocks.1 = (f32[2,1,16,1024]{3,2,1,0:T(8,128)S(1)}, bf16[1,64,512]{2,1,0:T(8,128)(2,1)S(1)}, bf16[2272,256]{1,0:T(8,128)(2,1)S(1)}, f32[128,8]{1,0:T(8,128)S(1)}, f32[128,8]{1,0:T(8,128)S(1)}) custom-call(bf16[1,64,512]{2,1,0:T(8,128)(2,1)} %own_hbm.1, bf16[1,64,512]{2,1,0:T(8,128)(2,1)S(1)} %collective-permute-done.near, ...), custom_call_target="tpu_custom_call" | custom-call | flops 3000000000 | bytes 4000000 | tf_op jit(solution)/shard_map/inner_blocks/pallas_call | solution.py:605
  12.4 0.1 collective-permute-done.4.rim
  12.5 1.2 %own_outer_blocks.1 = (bf16[272,256]{1,0:T(8,128)(2,1)S(1)}, bf16[144,256]{1,0:T(8,128)(2,1)S(1)}) custom-call(bf16[1,64,512]{2,1,0:T(8,128)(2,1)S(1)} %get-tuple-element.10.own, bf16[1,64,512]{2,1,0:T(8,128)(2,1)S(1)} %collective-permute-done.4.rim, bf16[2272,256]{1,0:T(8,128)(2,1)S(1)} %get-tuple-element.9.table_ref), custom_call_target="tpu_custom_call" | custom-call | flops 2000000000 | bytes 4000000 | tf_op jit(solution)/shard_map/own_outer_blocks/pallas_call | solution.py:630
  13.7 1.9 %collective-permute-done.3.rim_far = bf16[1,64,512]{2,1,0:T(8,128)(2,1)S(1)} collective-permute-done((bf16[1,64,512]{2,1,0:T(8,128)(2,1)}, bf16[1,64,512]{2,1,0:T(8,128)(2,1)S(1)}, u32[]{:S(2)}, u32[]{:S(2)}) %collective-permute-start.3) | collective-permute-done | bytes 65568 | tf_op jit(solution)/shard_map/ppermute | solution.py:28
  15.6 0.0 collective-permute-done.2.rim_near
  15.6 2.9 %outer_blocks.1 = (f32[1,2,2,16,1024]{4,3,2,1,0:T(8,128)}, f32[1,2,1,8,1024]{4,3,2,1,0:T(8,128)}) custom-call(bf16[1,64,512]{2,1,0:T(8,128)(2,1)S(1)} %collective-permute-done.near, bf16[1,64,512]{2,1,0:T(8,128)(2,1)S(1)} %collective-permute-done.1.far, bf16[1,64,512]{2,1,0:T(8,128)(2,1)S(1)} %collective-permute-done.2.rim_near, ...), custom_call_target="tpu_custom_call" | custom-call | flops 4000000000 | bytes 4000000 | tf_op jit(solution)/shard_map/outer_blocks/pallas_call | solution.py:640
Async XLA Ops:
  0.6 7.2 %collective-permute-start.1 = (bf16[1,64,512]{2,1,0:T(8,128)(2,1)}, bf16[1,64,512]{2,1,0:T(8,128)(2,1)S(1)}, u32[]{:S(2)}, u32[]{:S(2)}) collective-permute-start(bf16[1,64,512]{2,1,0:T(8,128)(2,1)} %own_hbm.1), channel_id=1, source_target_pairs={{8,0},{9,1},{10,2},{11,3},{12,4},{13,5},{14,6},{15,7},{24,16},{25,... | collective-permute-start | bytes 196616 | tf_op jit(solution)/shard_map/ppermute | solution.py:28
  1.9 7.3 %collective-permute-start = (bf16[1,64,512]{2,1,0:T(8,128)(2,1)}, bf16[1,64,512]{2,1,0:T(8,128)(2,1)S(1)}, u32[]{:S(2)}, u32[]{:S(2)}) collective-permute-start(bf16[1,64,512]{2,1,0:T(8,128)(2,1)} %own_hbm.1), channel_id=1, source_target_pairs={{4,0},{5,1},{6,2},{7,3},{8,4},{9,5},{10,6},{11,7},{12,8},{13,9},{1... | collective-permute-start | bytes 196616 | tf_op jit(solution)/shard_map/ppermute | solution.py:28
  3.2 12.4 %collective-permute-start.3 = (bf16[1,64,512]{2,1,0:T(8,128)(2,1)}, bf16[1,64,512]{2,1,0:T(8,128)(2,1)S(1)}, u32[]{:S(2)}, u32[]{:S(2)}) collective-permute-start(bf16[1,64,512]{2,1,0:T(8,128)(2,1)} %own_hbm.1), channel_id=1, source_target_pairs={{9,0},{10,1},{11,2},{13,4},{14,5},{15,6},{25,16},{26,17},{27,18},{... | collective-permute-start | bytes 196616 | tf_op jit(solution)/shard_map/ppermute | solution.py:28
  4.5 11.1 %collective-permute-start.2 = (bf16[1,64,512]{2,1,0:T(8,128)(2,1)}, bf16[1,64,512]{2,1,0:T(8,128)(2,1)S(1)}, u32[]{:S(2)}, u32[]{:S(2)}) collective-permute-start(bf16[1,64,512]{2,1,0:T(8,128)(2,1)} %own_hbm.1), channel_id=1, source_target_pairs={{5,0},{6,1},{7,2},{9,4},{10,5},{11,6},{13,8},{14,9},{15,10},{21,16... | collective-permute-start | bytes 196616 | tf_op jit(solution)/shard_map/ppermute | solution.py:28
  5.8 6.7 %collective-permute-start.4 = (bf16[1,64,512]{2,1,0:T(8,128)(2,1)}, bf16[1,64,512]{2,1,0:T(8,128)(2,1)S(1)}, u32[]{:S(2)}, u32[]{:S(2)}) collective-permute-start(bf16[1,64,512]{2,1,0:T(8,128)(2,1)} %own_hbm.1), channel_id=1, source_target_pairs={{1,0},{2,1},{3,2},{5,4},{6,5},{7,6},{9,8},{10,9},{11,10},{13,12},{... | collective-permute-start | bytes 196616 | tf_op jit(solution)/shard_map/ppermute | solution.py:28

commit v15 on v14

--- a/solution.py
+++ b/solution.py
@@ -213,42 +213,31 @@
     return value
 
 
-def left_of(level, place, half_ref, odd_ref):
+def left_of(level, place, half_ref, nyquist_ref):
     cos_at, nyquist_at, sin_at = place
     pieces = []
     for tile in range(level.tiles):
-        if tile % 2:
-            pieces.append(odd_ref[tile // 2 * level.body : (tile // 2 + 1) * level.body])
-        else:
-            columns = []
-            for p in range(level.pool):
-                at = level.window(tile, p)
-                columns += [half_ref[start : start + level.body, at : at + LANES] for start in (cos_at, sin_at)]
-            pieces.append(jnp.concatenate(columns, axis=1))
-    pieces.append(odd_ref[level.quads * level.body :])
+        columns = []
+        for p in range(level.pool):
+            at = level.window(tile, p)
+            columns += [half_ref[start : start + level.body, at : at + LANES] for start in (cos_at, sin_at)]
+        pieces.append(jnp.concatenate(columns, axis=1))
+    pieces.append(nyquist_ref[...])
     return jnp.concatenate(pieces, axis=0)
 
 
-def gather_windows(level, place, t_ref, halves, odds):
+def gather_nyquist(level, place, t_ref, targets):
     cos_at, nyquist_at, sin_at = place
-    body, end = level.body, level.quads * level.body
     row = lax.broadcasted_iota(jnp.int32, (2 * level.half, LANES), 0)
     for p in range(level.pool):
-        for source, target in zip(halves, odds):
-            for tile in range(1, level.tiles, 2):
-                at = level.window(tile, p)
-                for half, start in enumerate((cos_at, sin_at)):
-                    to = tile // 2 * body
-                    target[to : to + body, (2 * p + half) * LANES : (2 * p + half + 1) * LANES] = (
-                        source[start : start + body, at : at + LANES])
         nyquist = jnp.zeros((2 * level.half, LANES), f32)
         for tile in range(level.tiles):
             at, first = level.window(tile, p), level.nyquist_row(tile, 0)
             value = t_ref[nyquist_at : nyquist_at + 2 * level.half, at : at + LANES]
             nyquist = jnp.where((row >= first) & (row < first + level.blocks), value, nyquist)
-        for target, part in zip(odds, split(nyquist)):
-            target[end:, 2 * p * LANES : (2 * p + 1) * LANES] = part
-            target[end:, (2 * p + 1) * LANES : (2 * p + 2) * LANES] = jnp.zeros(part.shape, bf16)
+        for target, part in zip(targets, split(nyquist)):
+            target[:, 2 * p * LANES : (2 * p + 1) * LANES] = part
+            target[:, (2 * p + 1) * LANES : (2 * p + 2) * LANES] = jnp.zeros(part.shape, bf16)
 
 
 def spectrum_power(level, f_ref, sections):
@@ -330,7 +319,7 @@
     for index, (level, place) in enumerate(zip(levels, places)):
         odds = odd_refs[2 * index : 2 * index + 2]
         for z in sections:
-            gather_windows(level, place, t_ref.at[z], (high_ref.at[z], low_ref.at[z]), [ref.at[z] for ref in odds])
+            gather_nyquist(level, place, t_ref.at[z], [ref.at[z] for ref in odds])
 
 
 def transform_columns(levels, sections, table_ref, scratch, spec_refs):
@@ -343,8 +332,8 @@
             for ref, odd in zip((high_ref, low_ref), odd_refs[2 * index : 2 * index + 2])]
         rows = slice(sections[0] * level.rows, (sections[-1] + 1) * level.rows)
         f_refs[index][rows] = dot3(*lefts, table_ref, level.table)
-    for level, f_ref, spec_ref in zip(levels, f_refs, spec_refs):
-        scale_spectrum(level, f_ref, sections, spectrum_power(level, f_ref, sections), spec_ref)
+        sums = spectrum_power(level, f_refs[index], sections)
+        scale_spectrum(level, f_refs[index], sections, sums, spec_refs[index])
 
 
 def write_maps(levels, pairs, own_specs, specs, kept, table_ref, shift_at, map_at, scratch, outs, finished=()):
@@ -451,7 +440,7 @@
         pltpu.VMEM((count, size, width + LANES), f32),
         pltpu.VMEM((count, size, width + LANES), bf16),
         pltpu.VMEM((count, size, width + LANES), bf16),
-        *(pltpu.VMEM((count, level.quads * level.body + 2 * level.half, 2 * level.pool * LANES), bf16)
+        *(pltpu.VMEM((count, 2 * level.half, 2 * level.pool * LANES), bf16)
           for level in levels for _ in range(2)),
         *(pltpu.VMEM((count * level.rows, 2 * LANES), f32) for level in levels),
     ]

time: 18.8 us -> 19.1 us (1.016)
  Pallas kernels: 7.28 us -> 7.6 us
    pallas_call x1, Pallas kernels: 2.94 us -> 3.28 us  [correlate(): pl.pallas_call(functools.partial(outer_kernel, outer_levels, cuts, inner,...]
where the time goes in v15:
time: 19.1 us; the launch traced here: 18.9 us
  Pallas kernels  7.6 us (40%)
  starting transfers between devices  7.13 us (37%)
  waiting for transfers between devices  3.48 us (18%)
  between operations  0.7 us (4%)
    ppermute x5, starting transfers between devices, from_device(): return lax.ppermute(value, ('sec', 'strip'), pairs)  7.13 us
    ppermute x5, waiting for transfers between devices, from_device(): return lax.ppermute(value, ('sec', 'strip'), pairs)  3.48 us
    pallas_call x1, Pallas kernels, correlate(): pl.pallas_call(functools.partial(outer_kernel, outer_levels, cuts, inner,...  3.28 us
    pallas_call x1, Pallas kernels, correlate(): pl.pallas_call(functools.partial(inner_kernel, inner_levels, cuts), out_s...  3.1 us
    pallas_call x1, Pallas kernels, correlate(): pl.pallas_call(functools.partial(own_kernel, outer_levels, row_at), out_s...  1.22 us
  transfers between devices with their start and end apart: 5, of which 3 were waited for; matrix products, arithmetic and copies ran while one was open for 0% of the time, Pallas kernels for 23%

profile of v15, /device:TPU:1, one launch (start us, length us, event | category | flops | bytes accessed | tf_op | source)
XLA Modules:
  0.0 18.9 jit_solution(7259496892653839530)
XLA Ops:
  0.6 1.3 %collective-permute-start.1 = (bf16[1,64,512]{2,1,0:T(8,128)(2,1)}, bf16[1,64,512]{2,1,0:T(8,128)(2,1)S(1)}, u32[]{:S(2)}, u32[]{:S(2)}) collective-permute-start(bf16[1,64,512]{2,1,0:T(8,128)(2,1)} %own_hbm.1), channel_id=1, source_target_pairs={{8,0},{9,1},{10,2},{11,3},{12,4},{13,5},{14,6},{15,7},{24,16},{25,... | collective-permute-start | bytes 196616 | tf_op jit(solution)/shard_map/ppermute | solution.py:28
  1.9 1.3 %collective-permute-start = (bf16[1,64,512]{2,1,0:T(8,128)(2,1)}, bf16[1,64,512]{2,1,0:T(8,128)(2,1)S(1)}, u32[]{:S(2)}, u32[]{:S(2)}) collective-permute-start(bf16[1,64,512]{2,1,0:T(8,128)(2,1)} %own_hbm.1), channel_id=1, source_target_pairs={{4,0},{5,1},{6,2},{7,3},{8,4},{9,5},{10,6},{11,7},{12,8},{13,9},{1... | collective-permute-start | bytes 196616 | tf_op jit(solution)/shard_map/ppermute | solution.py:28
  3.2 1.3 %collective-permute-start.3 = (bf16[1,64,512]{2,1,0:T(8,128)(2,1)}, bf16[1,64,512]{2,1,0:T(8,128)(2,1)S(1)}, u32[]{:S(2)}, u32[]{:S(2)}) collective-permute-start(bf16[1,64,512]{2,1,0:T(8,128)(2,1)} %own_hbm.1), channel_id=1, source_target_pairs={{9,0},{10,1},{11,2},{13,4},{14,5},{15,6},{25,16},{26,17},{27,18},{... | collective-permute-start | bytes 196616 | tf_op jit(solution)/shard_map/ppermute | solution.py:28
  4.5 1.3 %collective-permute-start.2 = (bf16[1,64,512]{2,1,0:T(8,128)(2,1)}, bf16[1,64,512]{2,1,0:T(8,128)(2,1)S(1)}, u32[]{:S(2)}, u32[]{:S(2)}) collective-permute-start(bf16[1,64,512]{2,1,0:T(8,128)(2,1)} %own_hbm.1), channel_id=1, source_target_pairs={{5,0},{6,1},{7,2},{9,4},{10,5},{11,6},{13,8},{14,9},{15,10},{21,16... | collective-permute-start | bytes 196616 | tf_op jit(solution)/shard_map/ppermute | solution.py:28
  5.8 2.0 %collective-permute-start.4 = (bf16[1,64,512]{2,1,0:T(8,128)(2,1)}, bf16[1,64,512]{2,1,0:T(8,128)(2,1)S(1)}, u32[]{:S(2)}, u32[]{:S(2)}) collective-permute-start(bf16[1,64,512]{2,1,0:T(8,128)(2,1)} %own_hbm.1), channel_id=1, source_target_pairs={{1,0},{2,1},{3,2},{5,4},{6,5},{7,6},{9,8},{10,9},{11,10},{13,12},{... | collective-permute-start | bytes 196616 | tf_op jit(solution)/shard_map/ppermute | solution.py:28
  7.8 0.0 collective-permute-done.1.far
  7.8 1.4 %collective-permute-done.near = bf16[1,64,512]{2,1,0:T(8,128)(2,1)S(1)} collective-permute-done((bf16[1,64,512]{2,1,0:T(8,128)(2,1)}, bf16[1,64,512]{2,1,0:T(8,128)(2,1)S(1)}, u32[]{:S(2)}, u32[]{:S(2)}) %collective-permute-start) | collective-permute-done | bytes 65568 | tf_op jit(solution)/shard_map/ppermute | solution.py:28
  9.2 3.1 %inner_blocks.1 = (f32[2,1,16,1024]{3,2,1,0:T(8,128)S(1)}, bf16[1,64,512]{2,1,0:T(8,128)(2,1)S(1)}, bf16[2272,256]{1,0:T(8,128)(2,1)S(1)}, f32[128,8]{1,0:T(8,128)S(1)}, f32[128,8]{1,0:T(8,128)S(1)}) custom-call(bf16[1,64,512]{2,1,0:T(8,128)(2,1)} %own_hbm.1, bf16[1,64,512]{2,1,0:T(8,128)(2,1)S(1)} %collective-permute-done.near, ...), custom_call_target="tpu_custom_call" | custom-call | flops 3000000000 | bytes 4000000 | tf_op jit(solution)/shard_map/inner_blocks/pallas_call | solution.py:594
  12.4 0.1 collective-permute-done.4.rim
  12.5 1.2 %own_outer_blocks.1 = (bf16[272,256]{1,0:T(8,128)(2,1)S(1)}, bf16[144,256]{1,0:T(8,128)(2,1)S(1)}) custom-call(bf16[1,64,512]{2,1,0:T(8,128)(2,1)S(1)} %get-tuple-element.10.own, bf16[1,64,512]{2,1,0:T(8,128)(2,1)S(1)} %collective-permute-done.4.rim, bf16[2272,256]{1,0:T(8,128)(2,1)S(1)} %get-tuple-element.9.table_ref), custom_call_target="tpu_custom_call" | custom-call | flops 2000000000 | bytes 4000000 | tf_op jit(solution)/shard_map/own_outer_blocks/pallas_call | solution.py:619
  13.7 1.9 %collective-permute-done.3.rim_far = bf16[1,64,512]{2,1,0:T(8,128)(2,1)S(1)} collective-permute-done((bf16[1,64,512]{2,1,0:T(8,128)(2,1)}, bf16[1,64,512]{2,1,0:T(8,128)(2,1)S(1)}, u32[]{:S(2)}, u32[]{:S(2)}) %collective-permute-start.3) | collective-permute-done | bytes 65568 | tf_op jit(solution)/shard_map/ppermute | solution.py:28
  15.6 0.0 collective-permute-done.2.rim_near
  15.6 3.3 %outer_blocks.1 = (f32[1,2,2,16,1024]{4,3,2,1,0:T(8,128)}, f32[1,2,1,8,1024]{4,3,2,1,0:T(8,128)}) custom-call(bf16[1,64,512]{2,1,0:T(8,128)(2,1)S(1)} %collective-permute-done.near, bf16[1,64,512]{2,1,0:T(8,128)(2,1)S(1)} %collective-permute-done.1.far, bf16[1,64,512]{2,1,0:T(8,128)(2,1)S(1)} %collective-permute-done.2.rim_near, ...), custom_call_target="tpu_custom_call" | custom-call | flops 4000000000 | bytes 4000000 | tf_op jit(solution)/shard_map/outer_blocks/pallas_call | solution.py:629
Async XLA Ops:
  0.6 7.2 %collective-permute-start.1 = (bf16[1,64,512]{2,1,0:T(8,128)(2,1)}, bf16[1,64,512]{2,1,0:T(8,128)(2,1)S(1)}, u32[]{:S(2)}, u32[]{:S(2)}) collective-permute-start(bf16[1,64,512]{2,1,0:T(8,128)(2,1)} %own_hbm.1), channel_id=1, source_target_pairs={{8,0},{9,1},{10,2},{11,3},{12,4},{13,5},{14,6},{15,7},{24,16},{25,... | collective-permute-start | bytes 196616 | tf_op jit(solution)/shard_map/ppermute | solution.py:28
  1.9 7.3 %collective-permute-start = (bf16[1,64,512]{2,1,0:T(8,128)(2,1)}, bf16[1,64,512]{2,1,0:T(8,128)(2,1)S(1)}, u32[]{:S(2)}, u32[]{:S(2)}) collective-permute-start(bf16[1,64,512]{2,1,0:T(8,128)(2,1)} %own_hbm.1), channel_id=1, source_target_pairs={{4,0},{5,1},{6,2},{7,3},{8,4},{9,5},{10,6},{11,7},{12,8},{13,9},{1... | collective-permute-start | bytes 196616 | tf_op jit(solution)/shard_map/ppermute | solution.py:28
  3.2 12.4 %collective-permute-start.3 = (bf16[1,64,512]{2,1,0:T(8,128)(2,1)}, bf16[1,64,512]{2,1,0:T(8,128)(2,1)S(1)}, u32[]{:S(2)}, u32[]{:S(2)}) collective-permute-start(bf16[1,64,512]{2,1,0:T(8,128)(2,1)} %own_hbm.1), channel_id=1, source_target_pairs={{9,0},{10,1},{11,2},{13,4},{14,5},{15,6},{25,16},{26,17},{27,18},{... | collective-permute-start | bytes 196616 | tf_op jit(solution)/shard_map/ppermute | solution.py:28
  4.5 11.1 %collective-permute-start.2 = (bf16[1,64,512]{2,1,0:T(8,128)(2,1)}, bf16[1,64,512]{2,1,0:T(8,128)(2,1)S(1)}, u32[]{:S(2)}, u32[]{:S(2)}) collective-permute-start(bf16[1,64,512]{2,1,0:T(8,128)(2,1)} %own_hbm.1), channel_id=1, source_target_pairs={{5,0},{6,1},{7,2},{9,4},{10,5},{11,6},{13,8},{14,9},{15,10},{21,16... | collective-permute-start | bytes 196616 | tf_op jit(solution)/shard_map/ppermute | solution.py:28
  5.8 6.7 %collective-permute-start.4 = (bf16[1,64,512]{2,1,0:T(8,128)(2,1)}, bf16[1,64,512]{2,1,0:T(8,128)(2,1)S(1)}, u32[]{:S(2)}, u32[]{:S(2)}) collective-permute-start(bf16[1,64,512]{2,1,0:T(8,128)(2,1)} %own_hbm.1), channel_id=1, source_target_pairs={{1,0},{2,1},{3,2},{5,4},{6,5},{7,6},{9,8},{10,9},{11,10},{13,12},{... | collective-permute-start | bytes 196616 | tf_op jit(solution)/shard_map/ppermute | solution.py:28

commit v16 on v14

--- a/solution.py
+++ b/solution.py
@@ -208,8 +208,9 @@
 
 
 def all_rows(value):
+    value = value.reshape(value.shape[0] // 8, 8, value.shape[1])
     for step in (4, 2, 1):
-        value = value + pltpu.roll(value, step, 0)
+        value = value + pltpu.roll(value, step, 1)
     return value
 
 
@@ -281,6 +282,7 @@
 
 
 def scale_spectrum(level, f_ref, sections, sums, spec_ref):
+    scales = lax.rsqrt(all_rows(sums) * (1.0 / PATCH**4) + 1e-05)
     sub = lax.broadcasted_iota(jnp.int32, (8, 2 * LANES), 0)
     lane = lax.broadcasted_iota(jnp.int32, (8, 2 * LANES), 1)
     dc = (sub == 0) & (lane % PATCH == 0)
@@ -292,9 +294,8 @@
         scaled = [jnp.zeros_like(tail) for tail in tails]
         for tile in range(level.tiles):
             for b in range(level.blocks):
-                scale = lax.rsqrt(all_rows(sums[number : number + 8]) * (1.0 / PATCH**4) + 1e-05)
-                number += 8
-                scale = jnp.concatenate([scale, scale], axis=1)
+                scale = jnp.concatenate([scales[number], scales[number]], axis=1)
+                number += 1
                 for r in range(0, HALF, 16):
                     at = start + tile * level.body + b * HALF + r
                     head = f_ref[at : at + 8]
@@ -311,6 +312,16 @@
     t_ref, high_ref, low_ref = scratch[:3]
     odd_refs = scratch[3 : 3 + 2 * len(levels)]
     places, size = row_places(levels)
+
+    def keep(z, columns, t):
+        for level, (cos_at, nyquist_at, sin_at) in zip(levels, places):
+            for start in (cos_at, sin_at):
+                for ref, half in zip((high_ref, low_ref), split(t[start : start + level.body])):
+                    ref[z, start : start + level.body, columns] = half
+            rows = slice(nyquist_at, nyquist_at + 2 * level.half)
+            t_ref[z, rows, columns] = t[rows]
+
+    waiting = None
     for z in sections:
         x = jnp.concatenate([strip[0] for strip in strips[z]], axis=0)
         width = x.shape[1]
@@ -318,15 +329,13 @@
         for first in range(0, width, 2 * LANES):
             columns = slice(first, first + 2 * LANES)
             t = dot(row_ref[...], x[:, columns])
-            for level, (cos_at, nyquist_at, sin_at) in zip(levels, places):
-                for start in (cos_at, sin_at):
-                    for ref, half in zip((high_ref, low_ref), split(t[start : start + level.body])):
-                        ref[z, start : start + level.body, columns] = half
-                rows = slice(nyquist_at, nyquist_at + 2 * level.half)
-                t_ref[z, rows, columns] = t[rows]
+            if waiting is not None:
+                keep(*waiting)
+            waiting = (z, columns, t)
         t_ref[z, :, width:] = jnp.zeros((size, LANES), f32)
         for ref in (high_ref, low_ref):
             ref[z, :, width:] = jnp.zeros((size, LANES), bf16)
+    keep(*waiting)
     for index, (level, place) in enumerate(zip(levels, places)):
         odds = odd_refs[2 * index : 2 * index + 2]
         for z in sections:
@@ -343,8 +352,9 @@
             for ref, odd in zip((high_ref, low_ref), odd_refs[2 * index : 2 * index + 2])]
         rows = slice(sections[0] * level.rows, (sections[-1] + 1) * level.rows)
         f_refs[index][rows] = dot3(*lefts, table_ref, level.table)
-    for level, f_ref, spec_ref in zip(levels, f_refs, spec_refs):
-        scale_spectrum(level, f_ref, sections, spectrum_power(level, f_ref, sections), spec_ref)
+    sums = [spectrum_power(level, f_ref, sections) for level, f_ref in zip(levels, f_refs)]
+    for level, f_ref, total, spec_ref in zip(levels, f_refs, sums, spec_refs):
+        scale_spectrum(level, f_ref, sections, total, spec_ref)
 
 
 def write_maps(levels, pairs, own_specs, specs, kept, table_ref, shift_at, map_at, scratch, outs, finished=()):
@@ -403,20 +413,25 @@
             jnp.where(even, low, pltpu.roll(high, width, 1)),
             jnp.where(even, pltpu.roll(low, LANES - width, 1), high))
 
+    bigs = range(WINDOW // 4)
     for index, (level, maps_ref, rows_ref, out) in enumerate(zip(levels, maps_refs, rows_refs, outs)):
         tiles = level.blocks * pairs * level.quads
-        for big in range(WINDOW // 4):
-            rows = [maps_ref[:tiles, 4 * big + r, :] for r in range(4)]
-            for step in (2, 1):
-                for r in range(4):
-                    if not r & step:
-                        rows[r], rows[r + step] = exchange(rows[r], rows[r + step], step * WINDOW)
+        rows = [[maps_ref[:tiles, 4 * big + r, :] for r in range(4)] for big in bigs]
+        for step in (2, 1):
+            for r in range(4):
+                if not r & step:
+                    for big in bigs:
+                        rows[big][r], rows[big][r + step] = exchange(
+                            rows[big][r], rows[big][r + step], step * WINDOW)
+        for big in bigs:
             for g in range(4):
-                rows_ref[big, pl.ds(g, tiles, stride=4), :] = rows[g]
-            for b in range(level.blocks):
-                column = kept[index][: 4 * level.quads, level.first + b : level.first + b + 1]
-                for d in range(pairs):
-                    at = 4 * (b * pairs + d) * level.quads
+                rows_ref[big, pl.ds(g, tiles, stride=4), :] = rows[big][g]
+        for b in range(level.blocks):
+            column = kept[index][: 4 * level.quads, level.first + b : level.first + b + 1]
+            column = jnp.broadcast_to(column, (4 * level.quads, LANES))
+            for d in range(pairs):
+                at = 4 * (b * pairs + d) * level.quads
+                for big in bigs:
                     out[d, b, :, big * LANES : (big + 1) * LANES] = rows_ref[big, at : at + 4 * level.quads] * column
         if finished:
             finished[index]()

time: 18.8 us -> 18.8 us (level)
  no operation moved by 1% of the time
where the time goes in v16:
time: 18.8 us; the launch traced here: 18.6 us
  Pallas kernels  7.3 us (39%)
  starting transfers between devices  7.13 us (38%)
  waiting for transfers between devices  3.46 us (18%)
  between operations  0.7 us (4%)
    ppermute x5, starting transfers between devices, from_device(): return lax.ppermute(value, ('sec', 'strip'), pairs)  7.13 us
    ppermute x5, waiting for transfers between devices, from_device(): return lax.ppermute(value, ('sec', 'strip'), pairs)  3.46 us
    pallas_call x1, Pallas kernels, correlate(): pl.pallas_call(functools.partial(inner_kernel, inner_levels, cuts), out_s...  3.1 us
    pallas_call x1, Pallas kernels, correlate(): pl.pallas_call(functools.partial(outer_kernel, outer_levels, cuts, inner,...  2.97 us
    pallas_call x1, Pallas kernels, correlate(): pl.pallas_call(functools.partial(own_kernel, outer_levels, row_at), out_s...  1.23 us
  transfers between devices with their start and end apart: 5, of which 3 were waited for; matrix products, arithmetic and copies ran while one was open for 0% of the time, Pallas kernels for 23%

profile of v16, /device:TPU:1, one launch (start us, length us, event | category | flops | bytes accessed | tf_op | source)
XLA Modules:
  0.0 18.6 jit_solution(1931743137073557044)
XLA Ops:
  0.6 1.3 %collective-permute-start.1 = (bf16[1,64,512]{2,1,0:T(8,128)(2,1)}, bf16[1,64,512]{2,1,0:T(8,128)(2,1)S(1)}, u32[]{:S(2)}, u32[]{:S(2)}) collective-permute-start(bf16[1,64,512]{2,1,0:T(8,128)(2,1)} %own_hbm.1), channel_id=1, source_target_pairs={{8,0},{9,1},{10,2},{11,3},{12,4},{13,5},{14,6},{15,7},{24,16},{25,... | collective-permute-start | bytes 196616 | tf_op jit(solution)/shard_map/ppermute | solution.py:28
  1.9 1.3 %collective-permute-start = (bf16[1,64,512]{2,1,0:T(8,128)(2,1)}, bf16[1,64,512]{2,1,0:T(8,128)(2,1)S(1)}, u32[]{:S(2)}, u32[]{:S(2)}) collective-permute-start(bf16[1,64,512]{2,1,0:T(8,128)(2,1)} %own_hbm.1), channel_id=1, source_target_pairs={{4,0},{5,1},{6,2},{7,3},{8,4},{9,5},{10,6},{11,7},{12,8},{13,9},{1... | collective-permute-start | bytes 196616 | tf_op jit(solution)/shard_map/ppermute | solution.py:28
  3.2 1.3 %collective-permute-start.3 = (bf16[1,64,512]{2,1,0:T(8,128)(2,1)}, bf16[1,64,512]{2,1,0:T(8,128)(2,1)S(1)}, u32[]{:S(2)}, u32[]{:S(2)}) collective-permute-start(bf16[1,64,512]{2,1,0:T(8,128)(2,1)} %own_hbm.1), channel_id=1, source_target_pairs={{9,0},{10,1},{11,2},{13,4},{14,5},{15,6},{25,16},{26,17},{27,18},{... | collective-permute-start | bytes 196616 | tf_op jit(solution)/shard_map/ppermute | solution.py:28
  4.5 1.3 %collective-permute-start.2 = (bf16[1,64,512]{2,1,0:T(8,128)(2,1)}, bf16[1,64,512]{2,1,0:T(8,128)(2,1)S(1)}, u32[]{:S(2)}, u32[]{:S(2)}) collective-permute-start(bf16[1,64,512]{2,1,0:T(8,128)(2,1)} %own_hbm.1), channel_id=1, source_target_pairs={{5,0},{6,1},{7,2},{9,4},{10,5},{11,6},{13,8},{14,9},{15,10},{21,16... | collective-permute-start | bytes 196616 | tf_op jit(solution)/shard_map/ppermute | solution.py:28
  5.8 2.0 %collective-permute-start.4 = (bf16[1,64,512]{2,1,0:T(8,128)(2,1)}, bf16[1,64,512]{2,1,0:T(8,128)(2,1)S(1)}, u32[]{:S(2)}, u32[]{:S(2)}) collective-permute-start(bf16[1,64,512]{2,1,0:T(8,128)(2,1)} %own_hbm.1), channel_id=1, source_target_pairs={{1,0},{2,1},{3,2},{5,4},{6,5},{7,6},{9,8},{10,9},{11,10},{13,12},{... | collective-permute-start | bytes 196616 | tf_op jit(solution)/shard_map/ppermute | solution.py:28
  7.8 0.0 collective-permute-done.1.far
  7.8 1.4 %collective-permute-done.near = bf16[1,64,512]{2,1,0:T(8,128)(2,1)S(1)} collective-permute-done((bf16[1,64,512]{2,1,0:T(8,128)(2,1)}, bf16[1,64,512]{2,1,0:T(8,128)(2,1)S(1)}, u32[]{:S(2)}, u32[]{:S(2)}) %collective-permute-start) | collective-permute-done | bytes 65568 | tf_op jit(solution)/shard_map/ppermute | solution.py:28
  9.2 3.1 %inner_blocks.1 = (f32[2,1,16,1024]{3,2,1,0:T(8,128)S(1)}, bf16[1,64,512]{2,1,0:T(8,128)(2,1)S(1)}, bf16[2272,256]{1,0:T(8,128)(2,1)S(1)}, f32[128,8]{1,0:T(8,128)S(1)}, f32[128,8]{1,0:T(8,128)S(1)}) custom-call(bf16[1,64,512]{2,1,0:T(8,128)(2,1)} %own_hbm.1, bf16[1,64,512]{2,1,0:T(8,128)(2,1)S(1)} %collective-permute-done.near, ...), custom_call_target="tpu_custom_call" | custom-call | flops 3000000000 | bytes 4000000 | tf_op jit(solution)/shard_map/inner_blocks/pallas_call | solution.py:620
  12.4 0.1 collective-permute-done.4.rim
  12.5 1.2 %own_outer_blocks.1 = (bf16[272,256]{1,0:T(8,128)(2,1)S(1)}, bf16[144,256]{1,0:T(8,128)(2,1)S(1)}) custom-call(bf16[1,64,512]{2,1,0:T(8,128)(2,1)S(1)} %get-tuple-element.10.own, bf16[1,64,512]{2,1,0:T(8,128)(2,1)S(1)} %collective-permute-done.4.rim, bf16[2272,256]{1,0:T(8,128)(2,1)S(1)} %get-tuple-element.9.table_ref), custom_call_target="tpu_custom_call" | custom-call | flops 2000000000 | bytes 4000000 | tf_op jit(solution)/shard_map/own_outer_blocks/pallas_call | solution.py:645
  13.7 1.9 %collective-permute-done.3.rim_far = bf16[1,64,512]{2,1,0:T(8,128)(2,1)S(1)} collective-permute-done((bf16[1,64,512]{2,1,0:T(8,128)(2,1)}, bf16[1,64,512]{2,1,0:T(8,128)(2,1)S(1)}, u32[]{:S(2)}, u32[]{:S(2)}) %collective-permute-start.3) | collective-permute-done | bytes 65568 | tf_op jit(solution)/shard_map/ppermute | solution.py:28
  15.6 0.0 collective-permute-done.2.rim_near
  15.6 3.0 %outer_blocks.1 = (f32[1,2,2,16,1024]{4,3,2,1,0:T(8,128)}, f32[1,2,1,8,1024]{4,3,2,1,0:T(8,128)}) custom-call(bf16[1,64,512]{2,1,0:T(8,128)(2,1)S(1)} %collective-permute-done.near, bf16[1,64,512]{2,1,0:T(8,128)(2,1)S(1)} %collective-permute-done.1.far, bf16[1,64,512]{2,1,0:T(8,128)(2,1)S(1)} %collective-permute-done.2.rim_near, ...), custom_call_target="tpu_custom_call" | custom-call | flops 4000000000 | bytes 4000000 | tf_op jit(solution)/shard_map/outer_blocks/pallas_call | solution.py:655
Async XLA Ops:
  0.6 7.2 %collective-permute-start.1 = (bf16[1,64,512]{2,1,0:T(8,128)(2,1)}, bf16[1,64,512]{2,1,0:T(8,128)(2,1)S(1)}, u32[]{:S(2)}, u32[]{:S(2)}) collective-permute-start(bf16[1,64,512]{2,1,0:T(8,128)(2,1)} %own_hbm.1), channel_id=1, source_target_pairs={{8,0},{9,1},{10,2},{11,3},{12,4},{13,5},{14,6},{15,7},{24,16},{25,... | collective-permute-start | bytes 196616 | tf_op jit(solution)/shard_map/ppermute | solution.py:28
  1.9 7.3 %collective-permute-start = (bf16[1,64,512]{2,1,0:T(8,128)(2,1)}, bf16[1,64,512]{2,1,0:T(8,128)(2,1)S(1)}, u32[]{:S(2)}, u32[]{:S(2)}) collective-permute-start(bf16[1,64,512]{2,1,0:T(8,128)(2,1)} %own_hbm.1), channel_id=1, source_target_pairs={{4,0},{5,1},{6,2},{7,3},{8,4},{9,5},{10,6},{11,7},{12,8},{13,9},{1... | collective-permute-start | bytes 196616 | tf_op jit(solution)/shard_map/ppermute | solution.py:28
  3.2 12.4 %collective-permute-start.3 = (bf16[1,64,512]{2,1,0:T(8,128)(2,1)}, bf16[1,64,512]{2,1,0:T(8,128)(2,1)S(1)}, u32[]{:S(2)}, u32[]{:S(2)}) collective-permute-start(bf16[1,64,512]{2,1,0:T(8,128)(2,1)} %own_hbm.1), channel_id=1, source_target_pairs={{9,0},{10,1},{11,2},{13,4},{14,5},{15,6},{25,16},{26,17},{27,18},{... | collective-permute-start | bytes 196616 | tf_op jit(solution)/shard_map/ppermute | solution.py:28
  4.5 11.1 %collective-permute-start.2 = (bf16[1,64,512]{2,1,0:T(8,128)(2,1)}, bf16[1,64,512]{2,1,0:T(8,128)(2,1)S(1)}, u32[]{:S(2)}, u32[]{:S(2)}) collective-permute-start(bf16[1,64,512]{2,1,0:T(8,128)(2,1)} %own_hbm.1), channel_id=1, source_target_pairs={{5,0},{6,1},{7,2},{9,4},{10,5},{11,6},{13,8},{14,9},{15,10},{21,16... | collective-permute-start | bytes 196616 | tf_op jit(solution)/shard_map/ppermute | solution.py:28
  5.8 6.7 %collective-permute-start.4 = (bf16[1,64,512]{2,1,0:T(8,128)(2,1)}, bf16[1,64,512]{2,1,0:T(8,128)(2,1)S(1)}, u32[]{:S(2)}, u32[]{:S(2)}) collective-permute-start(bf16[1,64,512]{2,1,0:T(8,128)(2,1)} %own_hbm.1), channel_id=1, source_target_pairs={{1,0},{2,1},{3,2},{5,4},{6,5},{7,6},{9,8},{10,9},{11,10},{13,12},{... | collective-permute-start | bytes 196616 | tf_op jit(solution)/shard_map/ppermute | solution.py:28

commit v17 on v14

--- a/solution.py
+++ b/solution.py
@@ -59,13 +59,13 @@
 
 def coarse_table():
     c, s = wave((np.arange(2 * PATCH) // 2)[:, None] * np.arange(PATCH)[None, :])
-    table = np.zeros((2, 2, 2 * PATCH, 2, 2, PATCH))
-    for p in range(2):
-        table[p, 0, :, 0, p] = 0.5 * c
-        table[p, 1, :, 0, p] = -0.5 * s
-        table[p, 0, :, 1, p] = -0.5 * s
-        table[p, 1, :, 1, p] = -0.5 * c
-    return stacked(table.reshape(8 * PATCH, 4 * PATCH))
+    re = np.concatenate([0.5 * c, -0.5 * s], axis=0)
+    im = np.concatenate([-0.5 * s, -0.5 * c], axis=0)
+    rows = []
+    for pair in ((re, im), (im, re)):
+        high, low = split_table(np.concatenate(pair, axis=1))
+        rows += [np.concatenate([high, low], axis=1), np.concatenate([high, np.zeros_like(low)], axis=1)]
+    return np.concatenate(rows, axis=0)
 
 
 def shift_tables():
@@ -333,6 +333,21 @@
             gather_windows(level, place, t_ref.at[z], (high_ref.at[z], low_ref.at[z]), [ref.at[z] for ref in odds])
 
 
+def coarse_columns(high, low, table_ref, at):
+    depth = 2 * LANES
+    parts = []
+    for p in range(2):
+        columns = slice(p * depth, (p + 1) * depth)
+        value = dot(
+            jnp.concatenate([high[:, columns], low[:, columns]], axis=1),
+            table_ref[at + 2 * p * depth : at + 2 * (p + 1) * depth])
+        parts.append(value[:, :LANES] + value[:, LANES:])
+    first = lax.broadcasted_iota(jnp.int32, parts[0].shape, 1) < PATCH
+    re = jnp.where(first, parts[0], parts[1])
+    im = pltpu.roll(jnp.where(first, parts[1], parts[0]), PATCH, 1)
+    return jnp.concatenate([re, im], axis=1)
+
+
 def transform_columns(levels, sections, table_ref, scratch, spec_refs):
     high_ref, low_ref = scratch[1:3]
     odd_refs, f_refs = scratch[3 : 3 + 2 * len(levels)], scratch[3 + 2 * len(levels) :]
@@ -342,7 +357,10 @@
             jnp.concatenate([left_of(level, place, ref.at[z], odd.at[z]) for z in sections], axis=0)
             for ref, odd in zip((high_ref, low_ref), odd_refs[2 * index : 2 * index + 2])]
         rows = slice(sections[0] * level.rows, (sections[-1] + 1) * level.rows)
-        f_refs[index][rows] = dot3(*lefts, table_ref, level.table)
+        if level.pool == 1:
+            f_refs[index][rows] = dot3(*lefts, table_ref, level.table)
+        else:
+            f_refs[index][rows] = coarse_columns(*lefts, table_ref, level.table)
     for level, f_ref, spec_ref in zip(levels, f_refs, spec_refs):
         scale_spectrum(level, f_ref, sections, spectrum_power(level, f_ref, sections), spec_ref)
 

time: 18.8 us -> 18.9 us (level)
  transfers between devices with their start and end apart: 5 -> 5, of which waited for: 3 -> 3; matrix products, arithmetic and copies ran while one was open for 0% -> 0% of each run, Pallas kernels for 23% -> 24%
where the time goes in v17:
time: 18.9 us; the launch traced here: 18.7 us
  Pallas kernels  7.46 us (39%)
  starting transfers between devices  7.13 us (38%)
  waiting for transfers between devices  3.39 us (18%)
  between operations  0.7 us (4%)
    ppermute x5, starting transfers between devices, from_device(): return lax.ppermute(value, ('sec', 'strip'), pairs)  7.13 us
    ppermute x5, waiting for transfers between devices, from_device(): return lax.ppermute(value, ('sec', 'strip'), pairs)  3.39 us
    pallas_call x1, Pallas kernels, correlate(): pl.pallas_call(functools.partial(inner_kernel, inner_levels, cuts), out_s...  3.11 us
    pallas_call x1, Pallas kernels, correlate(): pl.pallas_call(functools.partial(outer_kernel, outer_levels, cuts, inner,...  3.05 us
    pallas_call x1, Pallas kernels, correlate(): pl.pallas_call(functools.partial(own_kernel, outer_levels, row_at), out_s...  1.29 us
  transfers between devices with their start and end apart: 5, of which 3 were waited for; matrix products, arithmetic and copies ran while one was open for 0% of the time, Pallas kernels for 24%

profile of v17, /device:TPU:1, one launch (start us, length us, event | category | flops | bytes accessed | tf_op | source)
XLA Modules:
  0.0 18.7 jit_solution(15782706020461344238)
XLA Ops:
  0.6 1.3 %collective-permute-start.1 = (bf16[1,64,512]{2,1,0:T(8,128)(2,1)}, bf16[1,64,512]{2,1,0:T(8,128)(2,1)S(1)}, u32[]{:S(2)}, u32[]{:S(2)}) collective-permute-start(bf16[1,64,512]{2,1,0:T(8,128)(2,1)} %own_hbm.1), channel_id=1, source_target_pairs={{8,0},{9,1},{10,2},{11,3},{12,4},{13,5},{14,6},{15,7},{24,16},{25,... | collective-permute-start | bytes 196616 | tf_op jit(solution)/shard_map/ppermute | solution.py:28
  1.9 1.3 %collective-permute-start = (bf16[1,64,512]{2,1,0:T(8,128)(2,1)}, bf16[1,64,512]{2,1,0:T(8,128)(2,1)S(1)}, u32[]{:S(2)}, u32[]{:S(2)}) collective-permute-start(bf16[1,64,512]{2,1,0:T(8,128)(2,1)} %own_hbm.1), channel_id=1, source_target_pairs={{4,0},{5,1},{6,2},{7,3},{8,4},{9,5},{10,6},{11,7},{12,8},{13,9},{1... | collective-permute-start | bytes 196616 | tf_op jit(solution)/shard_map/ppermute | solution.py:28
  3.2 1.3 %collective-permute-start.3 = (bf16[1,64,512]{2,1,0:T(8,128)(2,1)}, bf16[1,64,512]{2,1,0:T(8,128)(2,1)S(1)}, u32[]{:S(2)}, u32[]{:S(2)}) collective-permute-start(bf16[1,64,512]{2,1,0:T(8,128)(2,1)} %own_hbm.1), channel_id=1, source_target_pairs={{9,0},{10,1},{11,2},{13,4},{14,5},{15,6},{25,16},{26,17},{27,18},{... | collective-permute-start | bytes 196616 | tf_op jit(solution)/shard_map/ppermute | solution.py:28
  4.5 1.3 %collective-permute-start.2 = (bf16[1,64,512]{2,1,0:T(8,128)(2,1)}, bf16[1,64,512]{2,1,0:T(8,128)(2,1)S(1)}, u32[]{:S(2)}, u32[]{:S(2)}) collective-permute-start(bf16[1,64,512]{2,1,0:T(8,128)(2,1)} %own_hbm.1), channel_id=1, source_target_pairs={{5,0},{6,1},{7,2},{9,4},{10,5},{11,6},{13,8},{14,9},{15,10},{21,16... | collective-permute-start | bytes 196616 | tf_op jit(solution)/shard_map/ppermute | solution.py:28
  5.8 2.0 %collective-permute-start.4 = (bf16[1,64,512]{2,1,0:T(8,128)(2,1)}, bf16[1,64,512]{2,1,0:T(8,128)(2,1)S(1)}, u32[]{:S(2)}, u32[]{:S(2)}) collective-permute-start(bf16[1,64,512]{2,1,0:T(8,128)(2,1)} %own_hbm.1), channel_id=1, source_target_pairs={{1,0},{2,1},{3,2},{5,4},{6,5},{7,6},{9,8},{10,9},{11,10},{13,12},{... | collective-permute-start | bytes 196616 | tf_op jit(solution)/shard_map/ppermute | solution.py:28
  7.8 0.0 collective-permute-done.1.far
  7.8 1.4 %collective-permute-done.near = bf16[1,64,512]{2,1,0:T(8,128)(2,1)S(1)} collective-permute-done((bf16[1,64,512]{2,1,0:T(8,128)(2,1)}, bf16[1,64,512]{2,1,0:T(8,128)(2,1)S(1)}, u32[]{:S(2)}, u32[]{:S(2)}) %collective-permute-start) | collective-permute-done | bytes 65568 | tf_op jit(solution)/shard_map/ppermute | solution.py:28
  9.2 3.1 %inner_blocks.1 = (f32[2,1,16,1024]{3,2,1,0:T(8,128)S(1)}, bf16[1,64,512]{2,1,0:T(8,128)(2,1)S(1)}, bf16[2272,256]{1,0:T(8,128)(2,1)S(1)}, f32[128,8]{1,0:T(8,128)S(1)}, f32[128,8]{1,0:T(8,128)S(1)}) custom-call(bf16[1,64,512]{2,1,0:T(8,128)(2,1)} %own_hbm.1, bf16[1,64,512]{2,1,0:T(8,128)(2,1)S(1)} %collective-permute-done.near, ...), custom_call_target="tpu_custom_call" | custom-call | flops 3000000000 | bytes 4000000 | tf_op jit(solution)/shard_map/inner_blocks/pallas_call | solution.py:623
  12.4 0.1 collective-permute-done.4.rim
  12.5 1.3 %own_outer_blocks.1 = (bf16[272,256]{1,0:T(8,128)(2,1)S(1)}, bf16[144,256]{1,0:T(8,128)(2,1)S(1)}) custom-call(bf16[1,64,512]{2,1,0:T(8,128)(2,1)S(1)} %get-tuple-element.10.own, bf16[1,64,512]{2,1,0:T(8,128)(2,1)S(1)} %collective-permute-done.4.rim, bf16[2272,256]{1,0:T(8,128)(2,1)S(1)} %get-tuple-element.9.table_ref), custom_call_target="tpu_custom_call" | custom-call | flops 2000000000 | bytes 4000000 | tf_op jit(solution)/shard_map/own_outer_blocks/pallas_call | solution.py:648
  13.8 1.8 %collective-permute-done.3.rim_far = bf16[1,64,512]{2,1,0:T(8,128)(2,1)S(1)} collective-permute-done((bf16[1,64,512]{2,1,0:T(8,128)(2,1)}, bf16[1,64,512]{2,1,0:T(8,128)(2,1)S(1)}, u32[]{:S(2)}, u32[]{:S(2)}) %collective-permute-start.3) | collective-permute-done | bytes 65568 | tf_op jit(solution)/shard_map/ppermute | solution.py:28
  15.6 0.0 collective-permute-done.2.rim_near
  15.6 3.1 %outer_blocks.1 = (f32[1,2,2,16,1024]{4,3,2,1,0:T(8,128)}, f32[1,2,1,8,1024]{4,3,2,1,0:T(8,128)}) custom-call(bf16[1,64,512]{2,1,0:T(8,128)(2,1)S(1)} %collective-permute-done.near, bf16[1,64,512]{2,1,0:T(8,128)(2,1)S(1)} %collective-permute-done.1.far, bf16[1,64,512]{2,1,0:T(8,128)(2,1)S(1)} %collective-permute-done.2.rim_near, ...), custom_call_target="tpu_custom_call" | custom-call | flops 4000000000 | bytes 4000000 | tf_op jit(solution)/shard_map/outer_blocks/pallas_call | solution.py:658
Async XLA Ops:
  0.6 7.2 %collective-permute-start.1 = (bf16[1,64,512]{2,1,0:T(8,128)(2,1)}, bf16[1,64,512]{2,1,0:T(8,128)(2,1)S(1)}, u32[]{:S(2)}, u32[]{:S(2)}) collective-permute-start(bf16[1,64,512]{2,1,0:T(8,128)(2,1)} %own_hbm.1), channel_id=1, source_target_pairs={{8,0},{9,1},{10,2},{11,3},{12,4},{13,5},{14,6},{15,7},{24,16},{25,... | collective-permute-start | bytes 196616 | tf_op jit(solution)/shard_map/ppermute | solution.py:28
  1.9 7.3 %collective-permute-start = (bf16[1,64,512]{2,1,0:T(8,128)(2,1)}, bf16[1,64,512]{2,1,0:T(8,128)(2,1)S(1)}, u32[]{:S(2)}, u32[]{:S(2)}) collective-permute-start(bf16[1,64,512]{2,1,0:T(8,128)(2,1)} %own_hbm.1), channel_id=1, source_target_pairs={{4,0},{5,1},{6,2},{7,3},{8,4},{9,5},{10,6},{11,7},{12,8},{13,9},{1... | collective-permute-start | bytes 196616 | tf_op jit(solution)/shard_map/ppermute | solution.py:28
  3.2 12.4 %collective-permute-start.3 = (bf16[1,64,512]{2,1,0:T(8,128)(2,1)}, bf16[1,64,512]{2,1,0:T(8,128)(2,1)S(1)}, u32[]{:S(2)}, u32[]{:S(2)}) collective-permute-start(bf16[1,64,512]{2,1,0:T(8,128)(2,1)} %own_hbm.1), channel_id=1, source_target_pairs={{9,0},{10,1},{11,2},{13,4},{14,5},{15,6},{25,16},{26,17},{27,18},{... | collective-permute-start | bytes 196616 | tf_op jit(solution)/shard_map/ppermute | solution.py:28
  4.5 11.1 %collective-permute-start.2 = (bf16[1,64,512]{2,1,0:T(8,128)(2,1)}, bf16[1,64,512]{2,1,0:T(8,128)(2,1)S(1)}, u32[]{:S(2)}, u32[]{:S(2)}) collective-permute-start(bf16[1,64,512]{2,1,0:T(8,128)(2,1)} %own_hbm.1), channel_id=1, source_target_pairs={{5,0},{6,1},{7,2},{9,4},{10,5},{11,6},{13,8},{14,9},{15,10},{21,16... | collective-permute-start | bytes 196616 | tf_op jit(solution)/shard_map/ppermute | solution.py:28
  5.8 6.7 %collective-permute-start.4 = (bf16[1,64,512]{2,1,0:T(8,128)(2,1)}, bf16[1,64,512]{2,1,0:T(8,128)(2,1)S(1)}, u32[]{:S(2)}, u32[]{:S(2)}) collective-permute-start(bf16[1,64,512]{2,1,0:T(8,128)(2,1)} %own_hbm.1), channel_id=1, source_target_pairs={{1,0},{2,1},{3,2},{5,4},{6,5},{7,6},{9,8},{10,9},{11,10},{13,12},{... | collective-permute-start | bytes 196616 | tf_op jit(solution)/shard_map/ppermute | solution.py:28
